TPU v7x, 32 devices: a whole 2x2x4 slice. The times are simulated.
32 devices in a mesh: gx: 8 (over z, x), gy: 4 (over y, core).
Axes of the slice: x: 2, y: 2, z: 4, core: 2. Of those that a mesh axis runs over, the one named last changes fastest.
Arguments:
- density: float32 [8, 4, 8, 64, 1024], P('gx', 'gy'), may hold values from -0.07 to 1.15
- moves: int32 [8, 4, 8], P('gx', 'gy'), may hold values from 0 to 255, as said below
- cols: int32 [8, 4, 8, 16], P('gx', 'gy'), may hold values from 0 to 39, as said below
- halo_rows: int32 [8, 4, 4], P('gx', 'gy'), may hold values from 0 to 7, as said below
Outputs:
- purified: float32 [8, 4, 8, 64, 1024], P('gx', 'gy')
- occupation: float32 [4], replicated
Inputs may be any that keep to these rules, and one draw needn't show every extreme that they name: moves is a permutation of the 256 row ids. Rows leave in 8 waves: in each wave every brick sends one row to the brick beside it (periodic, among the eight around it) in that wave's direction, the waves' directions all differ, and the row lands in the slot that the receiving brick emptied in the same wave; all other rows keep their id. cols[i, j, r, 0] is r; the 16 entries of a row are distinct. `halo_rows`: the 4 entries of a brick are distinct.
All inputs are finite; a program needn't handle non-finite values.
Results may differ from a plain program's by a relative error of at most 0.0003.
Values sent between devices are 32-bit elements; how exact they have to be, the bound alone decides.
No kernel may reach another device: no remote copies, remote signals or barrier semaphores. Data moves between devices by JAX's collectives and lax.ppermute only.
A program may use at most 192 MiB of HBM per device.

v0:
```python
import jax
import jax.numpy as jnp
import numpy as np
from jax import lax
from jax.sharding import PartitionSpec as P

WAVES = 8
STEPS = 2


step_x = np.array([-1, -1, -1, 0, 0, 1, 1, 1])
step_y = np.array([-1, 0, 1, -1, 1, -1, 0, 1])
highest = lax.Precision.HIGHEST


def extended_2(block, sides, width):
    for axis, dim in sides:
        count = lax.axis_size(axis)
        forward = [(i, i + 1) for i in range(count - 1)]
        forward.append((count - 1, 0))
        backward = [(target, source) for source, target in forward]
        low = lax.ppermute(
            lax.slice_in_dim(block, block.shape[dim] - width, None, axis=dim), axis, forward
        )
        high = lax.ppermute(lax.slice_in_dim(block, 0, width, axis=dim), axis, backward)
        block = jnp.concatenate([low, block, high], axis=dim)
    return block


def neighbour_rows(extended):
    inner = extended.shape[2:]
    nine = extended.reshape((9,) + inner)
    picked = jnp.concatenate([nine[:4], nine[5:]], 0)
    return picked.reshape((8 * inner[0],) + inner[1:])


def slot_trace(current):
    block = current.shape[1]
    return jnp.sum(jnp.diagonal(current[:, :, :block], axis1=1, axis2=2))


def square_rows(current, local_cols, own_ids, candidates, candidate_ids):
    row_count, block, strip = current.shape
    slots = local_cols.shape[1]
    group = min(4, row_count)

    def one_group(pieces):
        mine, my_cols, my_ids = pieces
        width = mine.shape[0]
        far = jnp.take(candidates, my_cols, axis=0)
        far_ids = jnp.take(candidate_ids, my_cols, axis=0)
        match = far_ids[:, :, :, None] == my_ids[:, None, None, :]
        picked = jnp.argmax(match.astype(jnp.int32), axis=2)
        found = jnp.any(match, axis=2)
        far_blocks = far.reshape(width, slots, block, slots, block)
        aligned = jnp.take_along_axis(far_blocks, picked[:, :, None, :, None], axis=3)
        aligned = jnp.where(found[:, :, None, :, None], aligned, 0.0).reshape(
            width, slots, block, strip
        )
        return jnp.einsum("gatb,gtbx->gax", mine, aligned, precision=highest)

    grouped = (
        current.reshape(row_count // group, group, block, slots, block),
        local_cols.reshape(row_count // group, group, slots),
        own_ids.reshape(row_count // group, group, slots),
    )
    return lax.map(one_group, grouped).reshape(row_count, block, strip)


def shards(density, moves, cols, halo_rows):
    row_count = density.shape[2]
    block = density.shape[3]
    strip = density.shape[4]
    slots = cols.shape[3]
    rim_count = halo_rows.shape[2]
    count_x = lax.axis_size("gx")
    count_y = lax.axis_size("gy")
    index_x = lax.axis_index("gx")
    index_y = lax.axis_index("gy")
    myself = index_x * count_y + index_y
    offsets_x = jnp.asarray(step_x, dtype=jnp.int32)
    offsets_y = jnp.asarray(step_y, dtype=jnp.int32)
    neighbours = (index_x + offsets_x) % count_x * count_y + (index_y + offsets_y) % count_y
    previous = density.reshape(row_count, block * strip)
    target = moves.reshape(row_count)
    dest_dev = target // row_count
    dest_slot = target % row_count
    leaving = dest_dev != myself
    slot_ids = jnp.arange(row_count, dtype=jnp.int32)
    labels = (target + 1).astype(jnp.float32)
    rank = jnp.cumsum(leaving.astype(jnp.int32)) - 1
    waves = jnp.arange(WAVES, dtype=jnp.int32)
    chosen = (leaving[None, :] & (rank[None, :] == waves[:, None])).astype(jnp.float32)
    outgoing = jnp.dot(chosen, previous, precision=highest).reshape(1, 1, WAVES, block * strip)
    outgoing_marks = jnp.dot(chosen, labels, precision=highest).reshape(1, 1, WAVES)
    extended, extended_marks = (
        extended_2(outgoing, (("gx", 0), ("gy", 1)), 1),
        extended_2(outgoing_marks, (("gx", 0), ("gy", 1)), 1),
    )
    arrived = extended.reshape(9 * WAVES, block * strip)
    arrived_marks = extended_marks.reshape(9 * WAVES)
    wanted = (myself * row_count + slot_ids + 1).astype(jnp.float32)
    keep = ((~leaving)[None, :] & (dest_slot[None, :] == slot_ids[:, None])).astype(jnp.float32)
    take_in = (arrived_marks[None, :] == wanted[:, None]).astype(jnp.float32)
    current = jnp.dot(
        jnp.concatenate([keep, take_in], 1),
        jnp.concatenate([previous, arrived], 0),
        precision=highest,
    ).reshape(row_count, block, strip)
    local_cols = cols.reshape(row_count, slots)
    own_rims = halo_rows.reshape(rim_count)
    near_lists = neighbour_rows(extended_2(halo_rows, (("gx", 0), ("gy", 1)), 1))
    near_firsts = jnp.repeat(neighbours * row_count, rim_count)
    table = jnp.concatenate([myself * row_count + slot_ids, near_firsts + near_lists])
    pool = table.shape[0]
    own_ids = jnp.sum(
        jnp.where(local_cols[:, :, None] == jnp.arange(pool, dtype=jnp.int32), table, 0), axis=2
    )
    rim_ids = jnp.take(own_ids, own_rims, axis=0).reshape(1, 1, rim_count, slots)
    near_ids = neighbour_rows(extended_2(rim_ids, (("gx", 0), ("gy", 1)), 1))
    candidate_ids = jnp.concatenate([own_ids, near_ids], 0)
    scale = 1.0 / (count_x * count_y * row_count * block)
    results = []
    for step in range(STEPS):
        rims = jnp.take(current, own_rims, axis=0).reshape(1, 1, rim_count, block, strip)
        near_strips = neighbour_rows(extended_2(rims, (("gx", 0), ("gy", 1)), 1))
        candidates = jnp.concatenate([current, near_strips], 0)
        squared = square_rows(current, local_cols, own_ids, candidates, candidate_ids)
        pair = jnp.stack([slot_trace(current), slot_trace(squared)]) * scale
        results.append(lax.psum(pair, ("gx", "gy")))
        if step % 2 == 1:
            current = 2.0 * current - squared
        else:
            current = squared
    occupation = jnp.concatenate(results)
    return (current.reshape(density.shape), occupation)


def solution(mesh):
    in_specs = (
        P("gx", "gy", None, None, None),
        P("gx", "gy", None),
        P("gx", "gy", None, None),
        P("gx", "gy", None),
    )
    out_specs = (P("gx", "gy", None, None, None), P())
    return jax.shard_map(shards, mesh=mesh, in_specs=in_specs, out_specs=out_specs, check_vma=False)
```

profile of v0, /device:TPU:0, one launch (start us, length us, event | category | flops | bytes accessed | tf_op | source)
XLA Modules:
  0.0 1465.2 jit_solution(16250803813605956835)
XLA Ops:
  7.4 6.0 collective-permute-start.5
  13.4 87.5 %collective-permute-done.5 = f32[1,1,8,65536]{3,2,1,0:T(8,128)S(1)} collective-permute-done((f32[1,1,8,65536]{3,2,1,0:T(8,128)S(1)}, f32[1,1,8,65536]{3,2,1,0:T(8,128)S(1)}, u32[]{:S(2)}, u32[]{:S(2)}) %collective-permute-start.5) | collective-permute-done | bytes 2097184 | tf_op jit(solution)/shard_map/ppermute | solution.py:25
  106.1 3.7 collective-permute-start.1
  111.2 4.9 collective-permute-done
  117.1 124.2 %collective-permute-done.3 = f32[3,1,8]{2,1,0:T(1,128)S(1)} collective-permute-done((f32[3,1,8]{2,1,0:T(1,128)S(1)}, f32[3,1,8]{2,1,0:T(1,128)S(1)}, u32[]{:S(2)}, u32[]{:S(2)}) %collective-permute-start.3) | collective-permute-done | bytes 128 | tf_op jit(solution)/shard_map/ppermute | solution.py:25
  244.1 7.1 pad_maximum_fusion
  251.3 8.5 fusion.8
  267.0 3.4 collective-permute-start.17
  270.3 44.3 %collective-permute-done.17 = f32[1,1,4,64,1024]{4,3,2,1,0:T(8,128)S(1)} collective-permute-done((f32[1,1,4,64,1024]{4,3,2,1,0:T(8,128)S(1)}, f32[1,1,4,64,1024]{4,3,2,1,0:T(8,128)S(1)}, u32[]{:S(2)}, u32[]{:S(2)}) %collective-permute-start.17) | collective-permute-done | bytes 1048608 | tf_op jit(solution)/shard_map/ppermute | solution.py:25
  318.2 3.8 collective-permute-start.9
  322.1 6.2 collective-permute-done.8
  328.9 57.3 %collective-permute-done.11 = s32[3,1,4]{2,1,0:T(1,128)S(1)} collective-permute-done((s32[3,1,4]{2,1,0:T(1,128)S(1)}, s32[3,1,4]{2,1,0:T(1,128)S(1)}, u32[]{:S(2)}, u32[]{:S(2)}) %collective-permute-start.11) | collective-permute-done | bytes 80 | tf_op jit(solution)/shard_map/ppermute | solution.py:25
  389.4 3.5 collective-permute-start.13
  394.2 5.0 collective-permute-done.12
  402.7 3.8 reshape_reshape.10
  406.5 3.9 pad_maximum_fusion.3
  412.1 4.1 pad_maximum_fusion.5
  416.2 9.3 pad_maximum_fusion.1
  427.1 424.0 %while.20 = (s32[]{:T(128)}, f32[2,4,64,1024]{3,2,1,0:T(8,128)}, f32[2,4,64,16,64]{4,3,2,1,0:T(8,128)}, s32[2,4,16]{2,1,0:T(4,128)S(1)}, s32[40,16]{1,0:T(8,128)...) while((s32[]{:T(128)}, f32[2,4,64,1024]{3,2,1,0:T(8,128)}, ...), condition=%wide.region_5.10_spmd, body=%wide.region_2.9_spmd.sunk | while | flops 3234000384 | bytes 289483808 | solution.py:67
  431.1 12.8 gather_fusion
  443.9 12.4 broadcast_select_fusion.8
  456.3 25.8 %reshape.567 = f32[4,16,64,16,64]{4,3,2,1,0:T(8,128)} reshape(f32[4,16,64,1024]{3,2,1,0:T(8,128)} %broadcast_select_fusion.8) | data formatting | bytes 33554432 | tf_op jit(solution)/shard_map/while/body/eval_jaxpr/reshape | solution.py:55
  482.1 30.5 %copy.122 = f32[4,16,64,16,64]{4,2,3,1,0:T(8,128)} copy(f32[4,16,64,16,64]{4,3,2,1,0:T(8,128)} %reshape.567) | data formatting | bytes 33554432 | tf_op jit(solution)/shard_map/while/body/eval_jaxpr/reshape | solution.py:55
  512.7 43.2 %gather_fusion.2 = f32[1024,64,64]{2,1,0:T(8,128)} fusion(f32[4,16,64,16,64]{4,2,3,1,0:T(8,128)} %copy.122, s32[1024]{0:T(1024)S(1)} %reshape.568), kind=kCustom, calls=%fused_computation.3.clone.clone.1 | custom fusion | bytes 33566720 | tf_op jit(solution)/shard_map/while/body/eval_jaxpr/jit(take_along_axis)/gather | solution.py:56
  555.9 12.8 bitcast_select_fusion.5
  568.7 25.5 %copy.123 = f32[4,16,64,16,64]{4,3,2,1,0:T(8,128)} copy(f32[4,16,64,16,64]{4,2,3,1,0:T(8,128)S(1)} %bitcast_select_fusion.5) | data formatting | bytes 33554432 | tf_op jit(solution)/shard_map/while/body/eval_jaxpr/jit(_where)/select_n | solution.py:57
  594.1 28.3 %reshape.569 = f32[4,16,64,1024]{3,2,1,0:T(8,128)} reshape(f32[4,16,64,16,64]{4,3,2,1,0:T(8,128)} %copy.123) | data formatting | bytes 33554432 | tf_op jit(solution)/shard_map/while/body/eval_jaxpr/reshape | solution.py:57
  622.4 16.2 %fusion.54 = f32[2,4,64,1024]{3,2,1,0:T(8,128)} fusion(f32[2,4,64,1024]{3,2,1,0:T(8,128)} %get-tuple-element.314, s32[]{:T(128)S(6)} %copy.133, f32[4,16,64,1024]{3,2,1,0:T(8,128)} %reshape.569, f32[1,4,64,16,64]{4,3,2,1,0:T(8,128)S(1)} %constant_dynamic-slice_fusion.4), kind=kOutput, calls=%fused_computation.17.clone.1 | convolution fusion | flops 3221225472 | bytes 18874372 | tf_op jit(solution)/shard_map/while/body/eval_jaxpr/gatb,gtbx->gax/dot_general | solution.py:60
  642.6 12.8 gather_fusion
  655.4 12.4 broadcast_select_fusion.8
  667.8 25.8 %reshape.567 = f32[4,16,64,16,64]{4,3,2,1,0:T(8,128)} reshape(f32[4,16,64,1024]{3,2,1,0:T(8,128)} %broadcast_select_fusion.8) | data formatting | bytes 33554432 | tf_op jit(solution)/shard_map/while/body/eval_jaxpr/reshape | solution.py:55
  693.6 30.5 %copy.122 = f32[4,16,64,16,64]{4,2,3,1,0:T(8,128)} copy(f32[4,16,64,16,64]{4,3,2,1,0:T(8,128)} %reshape.567) | data formatting | bytes 33554432 | tf_op jit(solution)/shard_map/while/body/eval_jaxpr/reshape | solution.py:55
  724.2 43.8 %gather_fusion.2 = f32[1024,64,64]{2,1,0:T(8,128)} fusion(f32[4,16,64,16,64]{4,2,3,1,0:T(8,128)} %copy.122, s32[1024]{0:T(1024)S(1)} %reshape.568), kind=kCustom, calls=%fused_computation.3.clone.clone.1 | custom fusion | bytes 33566720 | tf_op jit(solution)/shard_map/while/body/eval_jaxpr/jit(take_along_axis)/gather | solution.py:56
  767.9 12.8 bitcast_select_fusion.5
  780.7 25.5 %copy.123 = f32[4,16,64,16,64]{4,3,2,1,0:T(8,128)} copy(f32[4,16,64,16,64]{4,2,3,1,0:T(8,128)S(1)} %bitcast_select_fusion.5) | data formatting | bytes 33554432 | tf_op jit(solution)/shard_map/while/body/eval_jaxpr/jit(_where)/select_n | solution.py:57
  806.2 28.3 %reshape.569 = f32[4,16,64,1024]{3,2,1,0:T(8,128)} reshape(f32[4,16,64,16,64]{4,3,2,1,0:T(8,128)} %copy.123) | data formatting | bytes 33554432 | tf_op jit(solution)/shard_map/while/body/eval_jaxpr/reshape | solution.py:57
  834.5 16.2 %fusion.54 = f32[2,4,64,1024]{3,2,1,0:T(8,128)} fusion(f32[2,4,64,1024]{3,2,1,0:T(8,128)} %get-tuple-element.314, s32[]{:T(128)S(6)} %copy.133, f32[4,16,64,1024]{3,2,1,0:T(8,128)} %reshape.569, f32[1,4,64,16,64]{4,3,2,1,0:T(8,128)S(1)} %constant_dynamic-slice_fusion.4), kind=kOutput, calls=%fused_computation.17.clone.1 | convolution fusion | flops 3221225472 | bytes 18874372 | tf_op jit(solution)/shard_map/while/body/eval_jaxpr/gatb,gtbx->gax/dot_general | solution.py:60
  851.1 3.4 gather_fusion.11
  858.0 44.8 %collective-permute-done.21 = f32[1,1,4,64,1024]{4,3,2,1,0:T(8,128)S(1)} collective-permute-done((f32[1,1,4,64,1024]{4,3,2,1,0:T(8,128)S(1)}, f32[1,1,4,64,1024]{4,3,2,1,0:T(8,128)S(1)}, u32[]{:S(2)}, u32[]{:S(2)}) %collective-permute-start.21) | collective-permute-done | bytes 1048608 | tf_op jit(solution)/shard_map/ppermute | solution.py:25
  917.3 56.2 %collective-permute-done.23 = f32[3,1,4,64,1024]{4,3,2,1,0:T(8,128)} collective-permute-done((f32[3,1,4,64,1024]{4,3,2,1,0:T(8,128)}, f32[3,1,4,64,1024]{4,3,2,1,0:T(8,128)}, u32[]{:S(2)}, u32[]{:S(2)}) %collective-permute-start.23) | collective-permute-done | bytes 3145760 | tf_op jit(solution)/shard_map/ppermute | solution.py:25
  974.1 3.9 pad_maximum_fusion.4
  979.6 4.1 pad_maximum_fusion.6
  983.7 9.3 pad_maximum_fusion.2
  994.6 423.8 %while.21 = (s32[]{:T(128)}, f32[2,4,64,1024]{3,2,1,0:T(8,128)}, f32[2,4,64,16,64]{4,3,2,1,0:T(8,128)}, s32[2,4,16]{2,1,0:T(4,128)S(1)}, s32[40,16]{1,0:T(8,128)...) while((s32[]{:T(128)}, f32[2,4,64,1024]{3,2,1,0:T(8,128)}, ...), condition=%wide.region_9.14_spmd, body=%wide.region_6.13_spmd.sunk | while | flops 3234000384 | bytes 289483808 | solution.py:67
  998.8 12.8 gather_fusion.3
  1011.6 12.4 broadcast_select_fusion.10
  1024.0 25.8 %reshape.577 = f32[4,16,64,16,64]{4,3,2,1,0:T(8,128)} reshape(f32[4,16,64,1024]{3,2,1,0:T(8,128)} %broadcast_select_fusion.10) | data formatting | bytes 33554432 | tf_op jit(solution)/shard_map/while/body/eval_jaxpr/reshape | solution.py:55
  1049.8 30.5 %copy.125 = f32[4,16,64,16,64]{4,2,3,1,0:T(8,128)} copy(f32[4,16,64,16,64]{4,3,2,1,0:T(8,128)} %reshape.577) | data formatting | bytes 33554432 | tf_op jit(solution)/shard_map/while/body/eval_jaxpr/reshape | solution.py:55
  1080.3 43.2 %gather_fusion.5 = f32[1024,64,64]{2,1,0:T(8,128)} fusion(f32[4,16,64,16,64]{4,2,3,1,0:T(8,128)} %copy.125, s32[1024]{0:T(1024)S(1)} %reshape.578), kind=kCustom, calls=%fused_computation.7.clone.clone.1 | custom fusion | bytes 33566720 | tf_op jit(solution)/shard_map/while/body/eval_jaxpr/jit(take_along_axis)/gather | solution.py:56
  1123.5 12.8 bitcast_select_fusion.6
  1136.3 25.5 %copy.126 = f32[4,16,64,16,64]{4,3,2,1,0:T(8,128)} copy(f32[4,16,64,16,64]{4,2,3,1,0:T(8,128)S(1)} %bitcast_select_fusion.6) | data formatting | bytes 33554432 | tf_op jit(solution)/shard_map/while/body/eval_jaxpr/jit(_where)/select_n | solution.py:57
  1161.8 28.3 %reshape.579 = f32[4,16,64,1024]{3,2,1,0:T(8,128)} reshape(f32[4,16,64,16,64]{4,3,2,1,0:T(8,128)} %copy.126) | data formatting | bytes 33554432 | tf_op jit(solution)/shard_map/while/body/eval_jaxpr/reshape | solution.py:57
  1190.1 16.2 %fusion.57 = f32[2,4,64,1024]{3,2,1,0:T(8,128)} fusion(f32[2,4,64,1024]{3,2,1,0:T(8,128)} %get-tuple-element.338, s32[]{:T(128)S(6)} %copy.139, f32[4,16,64,1024]{3,2,1,0:T(8,128)} %reshape.579, f32[1,4,64,16,64]{4,3,2,1,0:T(8,128)S(1)} %constant_dynamic-slice_fusion.5), kind=kOutput, calls=%fused_computation.35.clone.1 | convolution fusion | flops 3221225472 | bytes 18874372 | tf_op jit(solution)/shard_map/while/body/eval_jaxpr/gatb,gtbx->gax/dot_general | solution.py:60
  1210.3 12.8 gather_fusion.3
  1223.1 12.4 broadcast_select_fusion.10
  1235.5 25.8 %reshape.577 = f32[4,16,64,16,64]{4,3,2,1,0:T(8,128)} reshape(f32[4,16,64,1024]{3,2,1,0:T(8,128)} %broadcast_select_fusion.10) | data formatting | bytes 33554432 | tf_op jit(solution)/shard_map/while/body/eval_jaxpr/reshape | solution.py:55
  1261.3 30.5 %copy.125 = f32[4,16,64,16,64]{4,2,3,1,0:T(8,128)} copy(f32[4,16,64,16,64]{4,3,2,1,0:T(8,128)} %reshape.577) | data formatting | bytes 33554432 | tf_op jit(solution)/shard_map/while/body/eval_jaxpr/reshape | solution.py:55
  1291.9 43.8 %gather_fusion.5 = f32[1024,64,64]{2,1,0:T(8,128)} fusion(f32[4,16,64,16,64]{4,2,3,1,0:T(8,128)} %copy.125, s32[1024]{0:T(1024)S(1)} %reshape.578), kind=kCustom, calls=%fused_computation.7.clone.clone.1 | custom fusion | bytes 33566720 | tf_op jit(solution)/shard_map/while/body/eval_jaxpr/jit(take_along_axis)/gather | solution.py:56
  1335.6 12.8 bitcast_select_fusion.6
  1348.4 25.5 %copy.126 = f32[4,16,64,16,64]{4,3,2,1,0:T(8,128)} copy(f32[4,16,64,16,64]{4,2,3,1,0:T(8,128)S(1)} %bitcast_select_fusion.6) | data formatting | bytes 33554432 | tf_op jit(solution)/shard_map/while/body/eval_jaxpr/jit(_where)/select_n | solution.py:57
  1373.9 28.3 %reshape.579 = f32[4,16,64,1024]{3,2,1,0:T(8,128)} reshape(f32[4,16,64,16,64]{4,3,2,1,0:T(8,128)} %copy.126) | data formatting | bytes 33554432 | tf_op jit(solution)/shard_map/while/body/eval_jaxpr/reshape | solution.py:57
  1402.2 16.2 %fusion.57 = f32[2,4,64,1024]{3,2,1,0:T(8,128)} fusion(f32[2,4,64,1024]{3,2,1,0:T(8,128)} %get-tuple-element.338, s32[]{:T(128)S(6)} %copy.139, f32[4,16,64,1024]{3,2,1,0:T(8,128)} %reshape.579, f32[1,4,64,16,64]{4,3,2,1,0:T(8,128)S(1)} %constant_dynamic-slice_fusion.5), kind=kOutput, calls=%fused_computation.35.clone.1 | convolution fusion | flops 3221225472 | bytes 18874372 | tf_op jit(solution)/shard_map/while/body/eval_jaxpr/gatb,gtbx->gax/dot_general | solution.py:60
  1418.4 4.2 multiply_subtract_fusion
  1427.6 36.8 %all-reduce = (f32[2]{0:T(128)S(1)}, f32[2]{0:T(128)S(1)}) all-reduce(f32[2]{0:T(128)S(1)} %get-tuple-element.206, f32[2]{0:T(128)S(1)} %get-tuple-element.205), channel_id=1, replica_groups=mesh['gx'=8,'gy'=4] {'gx','gy'}, use_global_device_ids=true, to_apply=%region_14.19 | all-reduce | flops 4 | bytes 32 | tf_op jit(solution)/shard_map/psum | solution.py:130
  (193 shorter events, 82.9 us)
Async XLA Ops:
  5.0 1.3 copy-start.2
  6.3 99.7 %copy-start.18 = (s32[1,1,8]{2,1,0:T(1,128)S(1)}, s32[1,1,8]{2,1,0:T(1,128)}, u32[]{:S(2)}) copy-start(s32[1,1,8]{2,1,0:T(1,128)} %param.19) | copy-start | bytes 100
  6.3 103.6 %copy-start.19 = (s32[1,1,4]{2,1,0:T(1,128)S(1)}, s32[1,1,4]{2,1,0:T(1,128)}, u32[]{:S(2)}) copy-start(s32[1,1,4]{2,1,0:T(1,128)} %param.21) | copy-start | bytes 52
  7.4 93.6 %collective-permute-start.5 = (f32[1,1,8,65536]{3,2,1,0:T(8,128)S(1)}, f32[1,1,8,65536]{3,2,1,0:T(8,128)S(1)}, u32[]{:S(2)}, u32[]{:S(2)}) collective-permute-start(f32[1,1,8,65536]{3,2,1,0:T(8,128)S(1)} %convolution_bitcast_fusion), channel_id=1, source_target_pairs={{4,0},{8,4},{12,8},{16,12},{20,16},{24,20},{28,24},{0,28},{5,1},{9... | collective-permute-start | bytes 6291464 | tf_op jit(solution)/shard_map/ppermute | solution.py:25
  13.4 87.7 %collective-permute-start.4 = (f32[1,1,8,65536]{3,2,1,0:T(8,128)S(1)}, f32[1,1,8,65536]{3,2,1,0:T(8,128)S(1)}, u32[]{:S(2)}, u32[]{:S(2)}) collective-permute-start(f32[1,1,8,65536]{3,2,1,0:T(8,128)S(1)} %convolution_bitcast_fusion), channel_id=1, source_target_pairs={{0,4},{4,8},{8,12},{12,16},{16,20},{20,24},{24,28},{28,0},{1,5},{5... | collective-permute-start | bytes 6291464 | tf_op jit(solution)/shard_map/ppermute | solution.py:22
  100.9 1.3 copy-start.6
  102.3 3.2 copy-start.7
  105.5 138.6 %collective-permute-start.7 = (f32[3,1,8,65536]{3,2,1,0:T(8,128)}, f32[3,1,8,65536]{3,2,1,0:T(8,128)}, u32[]{:S(2)}, u32[]{:S(2)}) collective-permute-start(f32[3,1,8,65536]{3,2,1,0:T(8,128)} %pad_maximum_fusion.7), channel_id=1, source_target_pairs={{1,0},{2,1},{3,2},{0,3},{5,4},{6,5},{7,6},{4,7},{9,8},{10,9},{11,1... | collective-permute-start | bytes 18874376 | tf_op jit(solution)/shard_map/ppermute | solution.py:25
  105.8 138.3 %collective-permute-start.6 = (f32[3,1,8,65536]{3,2,1,0:T(8,128)}, f32[3,1,8,65536]{3,2,1,0:T(8,128)}, u32[]{:S(2)}, u32[]{:S(2)}) collective-permute-start(f32[3,1,8,65536]{3,2,1,0:T(8,128)} %pad_maximum_fusion.7), channel_id=1, source_target_pairs={{0,1},{1,2},{2,3},{3,0},{4,5},{5,6},{6,7},{7,4},{8,9},{9,10},{10,1... | collective-permute-start | bytes 18874376 | tf_op jit(solution)/shard_map/ppermute | solution.py:22
  106.1 5.0 collective-permute-start.1
  109.9 6.2 collective-permute-start
  109.9 152.5 %copy-start.13 = (s32[1024]{0:T(1024)}, s32[1024]{0:T(1024)S(1)}, u32[]{:S(2)}) copy-start(s32[1024]{0:T(1024)S(1)} %pad_clamp_fusion.2) | copy-start | bytes 12292
  109.9 279.4 %copy-start.14 = (pred[4]{0:T(512)(128)(4,1)}, pred[4]{0:T(512)(128)(4,1)S(1)}, u32[]{:S(2)}) copy-start(pred[4]{0:T(512)(128)(4,1)S(1)} %compare_and_fusion.2) | copy-start | bytes 16
  116.1 125.1 %collective-permute-start.3 = (f32[3,1,8]{2,1,0:T(1,128)S(1)}, f32[3,1,8]{2,1,0:T(1,128)S(1)}, u32[]{:S(2)}, u32[]{:S(2)}) collective-permute-start(f32[3,1,8]{2,1,0:T(1,128)S(1)} %pad_maximum_fusion.11), channel_id=1, source_target_pairs={{1,0},{2,1},{3,2},{0,3},{5,4},{6,5},{7,6},{4,7},{9,8},{10,9},{11,1... | collective-permute-start | bytes 296 | tf_op jit(solution)/shard_map/ppermute | solution.py:25
  116.1 127.8 %collective-permute-start.2 = (f32[3,1,8]{2,1,0:T(1,128)S(1)}, f32[3,1,8]{2,1,0:T(1,128)S(1)}, u32[]{:S(2)}, u32[]{:S(2)}) collective-permute-start(f32[3,1,8]{2,1,0:T(1,128)S(1)} %pad_maximum_fusion.11), channel_id=1, source_target_pairs={{0,1},{1,2},{2,3},{3,0},{4,5},{5,6},{6,7},{7,4},{8,9},{9,10},{10,1... | collective-permute-start | bytes 296 | tf_op jit(solution)/shard_map/ppermute | solution.py:22
  259.8 146.7 %copy-start.1 = (f32[8,65536]{1,0:T(8,128)}, f32[8,65536]{1,0:T(8,128)S(1)}, u32[]{:S(2)}) copy-start(f32[8,65536]{1,0:T(8,128)S(1)} %fusion.8) | copy-start | bytes 6291460
  259.8 62.3 %copy-start.16 = (s32[8]{0:T(128)S(1)}, s32[8]{0:T(128)}, u32[]{:S(2)}) copy-start(s32[8]{0:T(128)} %constant.173.clone) | copy-start | bytes 100
  259.8 62.3 %copy-start.17 = (s32[8]{0:T(128)S(1)}, s32[8]{0:T(128)}, u32[]{:S(2)}) copy-start(s32[8]{0:T(128)} %constant.172.clone) | copy-start | bytes 100
  259.8 128.6 %copy-start.12 = (s32[1,1,8,16]{3,2,1,0:T(8,128)S(1)}, s32[1,1,8,16]{3,2,1,0:T(8,128)}, u32[]{:S(2)}) copy-start(s32[1,1,8,16]{3,2,1,0:T(8,128)} %param.20) | copy-start | bytes 1540
  267.0 47.7 %collective-permute-start.17 = (f32[1,1,4,64,1024]{4,3,2,1,0:T(8,128)S(1)}, f32[1,1,4,64,1024]{4,3,2,1,0:T(8,128)S(1)}, u32[]{:S(2)}, u32[]{:S(2)}) collective-permute-start(f32[1,1,4,64,1024]{4,3,2,1,0:T(8,128)S(1)} %select_bitcast_fusion.1), channel_id=1, source_target_pairs={{4,0},{8,4},{12,8},{16,12},{20,16},{24,20},{28,24},{0,28},{5,1},{9... | collective-permute-start | bytes 3145736 | tf_op jit(solution)/shard_map/ppermute | solution.py:25
  270.3 44.3 %collective-permute-start.16 = (f32[1,1,4,64,1024]{4,3,2,1,0:T(8,128)S(1)}, f32[1,1,4,64,1024]{4,3,2,1,0:T(8,128)S(1)}, u32[]{:S(2)}, u32[]{:S(2)}) collective-permute-start(f32[1,1,4,64,1024]{4,3,2,1,0:T(8,128)S(1)} %select_bitcast_fusion.1), channel_id=1, source_target_pairs={{0,4},{4,8},{8,12},{12,16},{16,20},{20,24},{24,28},{28,0},{1,5},{5... | collective-permute-start | bytes 3145736 | tf_op jit(solution)/shard_map/ppermute | solution.py:22
  314.7 1.0 copy-start.8
  315.6 2.1 copy-start.9
  317.7 88.8 %collective-permute-start.19 = (f32[3,1,4,64,1024]{4,3,2,1,0:T(8,128)}, f32[3,1,4,64,1024]{4,3,2,1,0:T(8,128)}, u32[]{:S(2)}, u32[]{:S(2)}) collective-permute-start(f32[3,1,4,64,1024]{4,3,2,1,0:T(8,128)} %pad_maximum_fusion.8), channel_id=1, source_target_pairs={{1,0},{2,1},{3,2},{0,3},{5,4},{6,5},{7,6},{4,7},{9,8},{10,9},{11,1... | collective-permute-start | bytes 9437192 | tf_op jit(solution)/shard_map/ppermute | solution.py:25
  317.7 88.8 %collective-permute-start.18 = (f32[3,1,4,64,1024]{4,3,2,1,0:T(8,128)}, f32[3,1,4,64,1024]{4,3,2,1,0:T(8,128)}, u32[]{:S(2)}, u32[]{:S(2)}) collective-permute-start(f32[3,1,4,64,1024]{4,3,2,1,0:T(8,128)} %pad_maximum_fusion.8), channel_id=1, source_target_pairs={{0,1},{1,2},{2,3},{3,0},{4,5},{5,6},{6,7},{7,4},{8,9},{9,10},{10,1... | collective-permute-start | bytes 9437192 | tf_op jit(solution)/shard_map/ppermute | solution.py:22
  318.2 10.1 collective-permute-start.9
  322.0 6.2 collective-permute-start.8
  328.3 57.9 %collective-permute-start.11 = (s32[3,1,4]{2,1,0:T(1,128)S(1)}, s32[3,1,4]{2,1,0:T(1,128)S(1)}, u32[]{:S(2)}, u32[]{:S(2)}) collective-permute-start(s32[3,1,4]{2,1,0:T(1,128)S(1)} %constant_dynamic-update-slice_fusion), channel_id=1, source_target_pairs={{1,0},{2,1},{3,2},{0,3},{5,4},{6,5},{7,6},{4,7},{9,8},{10,9},{11,1... | collective-permute-start | bytes 152 | tf_op jit(solution)/shard_map/ppermute | solution.py:25
  328.4 59.5 %collective-permute-start.10 = (s32[3,1,4]{2,1,0:T(1,128)S(1)}, s32[3,1,4]{2,1,0:T(1,128)S(1)}, u32[]{:S(2)}, u32[]{:S(2)}) collective-permute-start(s32[3,1,4]{2,1,0:T(1,128)S(1)} %constant_dynamic-update-slice_fusion), channel_id=1, source_target_pairs={{0,1},{1,2},{2,3},{3,0},{4,5},{5,6},{6,7},{7,4},{8,9},{9,10},{10,1... | collective-permute-start | bytes 152 | tf_op jit(solution)/shard_map/ppermute | solution.py:22
  389.4 4.8 collective-permute-start.13
  392.9 6.3 collective-permute-start.12
  399.2 1.4 collective-permute-start.15
  399.2 3.3 collective-permute-start.14
  412.1 4.1 copy-start.5
  427.1 427.4 %copy-start.15 = (pred[4]{0:T(512)(128)(4,1)S(1)}, pred[4]{0:T(512)(128)(4,1)}, u32[]{:S(2)}) copy-start(pred[4]{0:T(512)(128)(4,1)} %copy-done.14) | copy-start | bytes 16
  851.1 59.4 %copy-start = (f32[2,4,64,1024]{3,2,1,0:T(8,128)S(1)}, f32[2,4,64,1024]{3,2,1,0:T(8,128)}, u32[]{:S(2)}) copy-start(f32[2,4,64,1024]{3,2,1,0:T(8,128)} %get-tuple-element.82) | copy-start | bytes 6291460
  855.9 46.8 %collective-permute-start.21 = (f32[1,1,4,64,1024]{4,3,2,1,0:T(8,128)S(1)}, f32[1,1,4,64,1024]{4,3,2,1,0:T(8,128)S(1)}, u32[]{:S(2)}, u32[]{:S(2)}) collective-permute-start(f32[1,1,4,64,1024]{4,3,2,1,0:T(8,128)S(1)} %select_bitcast_fusion), channel_id=1, source_target_pairs={{4,0},{8,4},{12,8},{16,12},{20,16},{24,20},{28,24},{0,28},{5,1},{9... | collective-permute-start | bytes 3145736 | tf_op jit(solution)/shard_map/ppermute | solution.py:25
  856.0 46.8 %collective-permute-start.20 = (f32[1,1,4,64,1024]{4,3,2,1,0:T(8,128)S(1)}, f32[1,1,4,64,1024]{4,3,2,1,0:T(8,128)S(1)}, u32[]{:S(2)}, u32[]{:S(2)}) collective-permute-start(f32[1,1,4,64,1024]{4,3,2,1,0:T(8,128)S(1)} %select_bitcast_fusion), channel_id=1, source_target_pairs={{0,4},{4,8},{8,12},{12,16},{16,20},{20,24},{24,28},{28,0},{1,5},{5... | collective-permute-start | bytes 3145736 | tf_op jit(solution)/shard_map/ppermute | solution.py:22
  902.8 2.1 copy-start.10
  902.8 2.6 copy-start.11
  904.9 68.6 %collective-permute-start.23 = (f32[3,1,4,64,1024]{4,3,2,1,0:T(8,128)}, f32[3,1,4,64,1024]{4,3,2,1,0:T(8,128)}, u32[]{:S(2)}, u32[]{:S(2)}) collective-permute-start(f32[3,1,4,64,1024]{4,3,2,1,0:T(8,128)} %pad_maximum_fusion.9), channel_id=1, source_target_pairs={{1,0},{2,1},{3,2},{0,3},{5,4},{6,5},{7,6},{4,7},{9,8},{10,9},{11,1... | collective-permute-start | bytes 9437192 | tf_op jit(solution)/shard_map/ppermute | solution.py:25
  904.9 69.2 %collective-permute-start.22 = (f32[3,1,4,64,1024]{4,3,2,1,0:T(8,128)}, f32[3,1,4,64,1024]{4,3,2,1,0:T(8,128)}, u32[]{:S(2)}, u32[]{:S(2)}) collective-permute-start(f32[3,1,4,64,1024]{4,3,2,1,0:T(8,128)} %pad_maximum_fusion.9), channel_id=1, source_target_pairs={{0,1},{1,2},{2,3},{3,0},{4,5},{5,6},{6,7},{7,4},{8,9},{9,10},{10,1... | collective-permute-start | bytes 9437192 | tf_op jit(solution)/shard_map/ppermute | solution.py:22
  905.4 72.6 %copy-start.3 = (s32[64]{0:T(128)}, s32[64]{0:T(128)S(1)}, u32[]{:S(2)}) copy-start(s32[64]{0:T(128)S(1)} %or_bitcast_fusion) | copy-start | bytes 772
  1418.4 5.8 copy-start.4
where the time goes:
time: 1480 us; the launch traced here: 1470 us
  local copies, waits for them, and re-layouts  716 us (48%)
  waiting for transfers between devices  441 us (30%)
  other arithmetic  169 us (11%)
  matrix products  74.5 us (5%)
  blocking collectives  36.8 us (2%)
  starting transfers between devices  26.2 us (2%)
    ppermute x12, waiting for transfers between devices, extended_2(): lax.ppermute(lax.slice_in_dim(block, 0, width, axis=dim), axis, backward)  417 us
    reshape x8, local copies, waits for them, and re-layouts, one_group(): far_blocks = far.reshape(width, slots, block, slots, block)  225 us
    gather x8, local copies, waits for them, and re-layouts, one_group(): jnp.take_along_axis(far_blocks, picked[:, :, None, :, None], axis=3)  174 us
    reshape x4, local copies, waits for them, and re-layouts, one_group(): jnp.where(found[:, :, None, :, None], aligned, 0.0)  113 us
    select_n x4, local copies, waits for them, and re-layouts, one_group(): jnp.where(found[:, :, None, :, None], aligned, 0.0)  102 us
    dot_general x4, matrix products, one_group(): return jnp.einsum('gatb,gtbx->gax', mine, aligned, precision=highest)  64.8 us
    gather x4, local copies, waits for them, and re-layouts, one_group(): far = jnp.take(candidates, my_cols, axis=0)  51.3 us
    select_n x4, other arithmetic, one_group(): jnp.where(found[:, :, None, :, None], aligned, 0.0)  51.2 us
  transfers between devices with their start and end apart: 24, of which 17 were waited for; matrix products, arithmetic and copies ran while one was open for 1% of the time, Pallas kernels for 0%

commit v1 on v0

v1 whole, which is shorter than its diff:
```python
import functools

import jax
import jax.numpy as jnp
import numpy as np
from jax import lax
from jax.experimental import pallas as pl
from jax.experimental.pallas import tpu as pltpu
from jax.sharding import PartitionSpec as P

STEPS = 2
AXES = ("gx", "gy")
LANES = 128
TILE = 256

step_x = np.array([-1, -1, -1, 0, 0, 1, 1, 1])
step_y = np.array([-1, 0, 1, -1, 1, -1, 0, 1])

GROUPS = ("C", "A", "Y", "CA", "B", "YA", "CB", "YB")
FRAME = {
    "C": (0, 1),
    "A": (1, 0),
    "Y": (0, -1),
    "CA": (1, 1),
    "B": (-1, 0),
    "YA": (1, -1),
    "CB": (-1, 1),
    "YB": (-1, -1),
}


def flat_perm(count_x, count_y, move):
    pairs = []
    for i in range(count_x):
        for j in range(count_y):
            x, y = move(i, j)
            pairs.append((i * count_y + j, (x % count_x) * count_y + y % count_y))
    return pairs


def toward_a(i, j):
    return i ^ 1, j


def along_b(i, j):
    return (i + 2 if i % 2 == 0 else i - 2), j


def toward_c(i, j):
    return i, j ^ 1


def toward_y(i, j):
    return i, (j - 1 if j % 2 == 0 else j + 1)


def half_pair(ref_rows, left, right):
    lane = lax.broadcasted_iota(jnp.int32, (64, LANES), 1)
    one = jnp.maximum(left, 0)
    two = jnp.maximum(right, 0)
    low = ref_rows(one >> 1)
    high = ref_rows(two >> 1)
    low = pltpu.roll(low, (one & 1) * 64, 1)
    high = pltpu.roll(high, (1 - (two & 1)) * 64, 1)
    low_end = jnp.where(left >= 0, 64, 0)
    high_start = jnp.where(right >= 0, 64, 128)
    return jnp.where(lane < low_end, low, jnp.where(lane >= high_start, high, 0.0))


def split(value):
    high = value.astype(jnp.bfloat16)
    low = (value - high.astype(jnp.float32)).astype(jnp.bfloat16)
    return high, low


def trace_of(block):
    row = lax.broadcasted_iota(jnp.int32, block.shape, 0)
    lane = lax.broadcasted_iota(jnp.int32, block.shape, 1)
    return jnp.sum(jnp.where(row == lane, block, 0.0))


def place(slots, rims, arrived):
    rows = len(arrived)
    block, strip = arrived[0].shape
    half = rims.shape[0] // 2

    def kernel(slots_ref, rims_ref, *refs):
        ins, (current_ref, first_ref, second_ref, trace_ref) = refs[:rows], refs[rows:]
        total = jnp.float32(0.0)
        for d in range(rows):
            current_ref[slots_ref[d]] = ins[d][...]
            total += trace_of(ins[d][:, :LANES])
        trace_ref[0, 0] = total
        for m in range(half):
            first_ref[m] = current_ref[rims_ref[m]]
            second_ref[m] = current_ref[rims_ref[half + m]]

    vmem = pl.BlockSpec(memory_space=pltpu.VMEM)
    smem = pl.BlockSpec(memory_space=pltpu.SMEM)
    return pl.pallas_call(
        kernel,
        out_shape=(
            jax.ShapeDtypeStruct((rows, block, strip), jnp.float32),
            jax.ShapeDtypeStruct((half, block, strip), jnp.float32),
            jax.ShapeDtypeStruct((half, block, strip), jnp.float32),
            jax.ShapeDtypeStruct((1, 1), jnp.float32),
        ),
        in_specs=[smem, smem] + [vmem] * rows,
        out_specs=(vmem, vmem, vmem, smem),
        compiler_params=pltpu.CompilerParams(vmem_limit_bytes=32 * 2**20),
        name="place_rows",
    )(slots, rims, *arrived)


def product_kernel(spec, *refs):
    first, counts, has_total, last, blend, pool = spec
    refs = list(refs)
    slot_ref = refs.pop(0)
    if last:
        where_ref, rims_ref = refs.pop(0), refs.pop(0)
    own_ref = refs.pop(0)
    parts = [refs.pop(0) for _ in counts] if counts else [own_ref]
    total_ref = refs.pop(0) if has_total else None
    if last:
        out_ref, rim_a_ref, rim_b_ref, trace_ref = (refs.pop(0) for _ in range(4))
    else:
        total_out = refs.pop(0)
    a_high, a_low, d_high, d_low = (refs.pop(0) for _ in range(4))
    rows = own_ref.shape[0]
    members = sum(ref.shape[0] for ref in parts)
    n = pl.program_id(0)

    @pl.when(n == 0)
    def _():
        def one_row(g, carry):
            at = pl.ds(pl.multiple_of(g * 64, 64), 64)
            for k in range(members // 2):
                spot = first + 2 * k
                value = half_pair(
                    lambda s: own_ref[g, :, pl.ds(pl.multiple_of(s * LANES, LANES), LANES)],
                    slot_ref[g, spot],
                    slot_ref[g, spot + 1],
                )
                high, low = split(value)
                a_high[at, pl.ds(k * LANES, LANES)] = high
                a_low[at, pl.ds(k * LANES, LANES)] = low
            return carry

        lax.fori_loop(0, rows, one_row, 0)

    base = 0
    for ref in parts:

        def one_member(c, carry, ref=ref, base=base):
            at = pl.ds(pl.multiple_of((base + c) * 64, 64), 64)
            for q in range(TILE // LANES):
                spot = n * (TILE // 64) + 2 * q
                left = slot_ref[first + base + c, spot]
                right = slot_ref[first + base + c, spot + 1]
                to = pl.ds(q * LANES, LANES)

                @pl.when(jnp.maximum(left, right) >= 0)
                def _():
                    value = half_pair(
                        lambda s: ref[c, :, pl.ds(pl.multiple_of(s * LANES, LANES), LANES)],
                        left,
                        right,
                    )
                    high, low = split(value)
                    d_high[at, to] = high
                    d_low[at, to] = low

                @pl.when(jnp.maximum(left, right) < 0)
                def _():
                    d_high[at, to] = jnp.zeros((64, LANES), jnp.bfloat16)
                    d_low[at, to] = jnp.zeros((64, LANES), jnp.bfloat16)

            return carry

        lax.fori_loop(0, ref.shape[0], one_member, 0)
        base += ref.shape[0]

    dot = functools.partial(jnp.dot, preferred_element_type=jnp.float32)
    result = dot(a_high[...], d_high[...])
    result += dot(a_high[...], d_low[...])
    result += dot(a_low[...], d_high[...])
    if has_total:
        result += total_ref[...]
    if not last:
        total_out[...] = result
        return
    dense_ref = refs.pop(0)
    dense_ref[:, pl.ds(pl.multiple_of(n * TILE, TILE), TILE)] = result

    @pl.when(n == pl.num_programs(0) - 1)
    def _():
        trace_ref[0, 0] = jnp.float32(0.0)

        def one_row(g, carry):
            at = pl.ds(pl.multiple_of(g * 64, 64), 64)
            for k in range(own_ref.shape[2] // LANES):
                value = half_pair(
                    lambda s: dense_ref[at, pl.ds(pl.multiple_of(s * LANES, LANES), LANES)],
                    where_ref[g, 2 * k],
                    where_ref[g, 2 * k + 1],
                )
                if k == 0:
                    trace_ref[0, 0] += trace_of(value)
                to = pl.ds(k * LANES, LANES)
                if blend:
                    value = 2.0 * own_ref[g, :, to] - value
                out_ref[g, :, to] = value
            return carry

        lax.fori_loop(0, rows, one_row, 0)
        if rim_a_ref is not None:
            half = rim_a_ref.shape[0]
            for m in range(half):
                rim_a_ref[m] = out_ref[rims_ref[m]]
                rim_b_ref[m] = out_ref[rims_ref[half + m]]


def product(first, slot_table, own, parts, total, last=None, name="product"):
    rows, block, strip = own.shape
    pool = slot_table.shape[0]
    members = sum(p.shape[0] for p in parts) if parts else rows
    depth = members * block
    width = pool * block
    whole = lambda a: pl.BlockSpec(a.shape, lambda n: (0,) * a.ndim, pipeline_mode=pl.Buffered(1))
    smem = pl.BlockSpec(memory_space=pltpu.SMEM)
    tile = pl.BlockSpec((rows * block, TILE), lambda n: (0, n))
    ins = [slot_table]
    in_specs = [smem]
    if last is not None:
        where, rims, blend = last
        ins += [where, rims]
        in_specs += [smem, smem]
    ins += [own, *parts]
    in_specs += [whole(own), *(whole(p) for p in parts)]
    if total is not None:
        ins.append(total)
        in_specs.append(tile)
    scratch = [
        pltpu.VMEM((rows * block, depth), jnp.bfloat16),
        pltpu.VMEM((rows * block, depth), jnp.bfloat16),
        pltpu.VMEM((depth, TILE), jnp.bfloat16),
        pltpu.VMEM((depth, TILE), jnp.bfloat16),
    ]
    if last is None:
        out_shape = jax.ShapeDtypeStruct((rows * block, width), jnp.float32)
        out_specs = tile
    else:
        half = rims.shape[0] // 2
        rim = jax.ShapeDtypeStruct((half, block, strip), jnp.float32)
        out_shape = (
            jax.ShapeDtypeStruct(own.shape, jnp.float32),
            rim,
            rim,
            jax.ShapeDtypeStruct((1, 1), jnp.float32),
        )
        fixed = lambda a: pl.BlockSpec(a.shape, lambda n: (0, 0, 0))
        out_specs = (fixed(own), fixed(rim), fixed(rim), smem)
        scratch.append(pltpu.VMEM((rows * block, width), jnp.float32))
    spec = (
        first,
        tuple(p.shape[0] for p in parts),
        total is not None,
        last is not None,
        last is not None and last[2],
        pool,
    )
    return pl.pallas_call(
        functools.partial(product_kernel, spec),
        grid=(width // TILE,),
        out_shape=out_shape,
        in_specs=in_specs,
        out_specs=out_specs,
        scratch_shapes=scratch,
        compiler_params=pltpu.CompilerParams(
            dimension_semantics=("arbitrary",), vmem_limit_bytes=48 * 2**20
        ),
        cost_estimate=pl.CostEstimate(
            flops=6 * rows * block * depth * width,
            bytes_accessed=4 * (rows + members) * block * strip + 8 * rows * block * width,
            transcendentals=0,
        ),
        name=name,
    )(*ins)


def butterfly(value, count_x, count_y):
    for bit in [1 << b for b in range(count_y.bit_length() - 1)]:
        perm = flat_perm(count_x, count_y, lambda i, j: (i, j ^ bit))
        value = value + lax.ppermute(value, AXES, perm)
    for bit in [1 << b for b in range(count_x.bit_length() - 1)]:
        perm = flat_perm(count_x, count_y, lambda i, j: (i ^ bit, j))
        value = value + lax.ppermute(value, AXES, perm)
    return value


def tables(cols, halo, index_x, index_y, count_x, count_y):
    rows, slots = cols.shape
    rims = halo.shape[0]
    sign_x = 1 - 2 * (index_x % 2)
    sign_y = 1 - 2 * (index_y % 2)
    frame = np.array([FRAME[name] for name in GROUPS])
    away = cols - rows
    direction = away // rims
    listed = away % rims
    linear = direction + (direction >= 4).astype(jnp.int32)
    in_list = halo[None, None, :] == cols[:, :, None]
    spot = jnp.sum(jnp.where(in_list, jnp.arange(rims, dtype=jnp.int32), 0), axis=2)
    inner = jnp.where(jnp.any(in_list, axis=2), 4 * rims + spot, -1)
    code = jnp.where(cols < rows, inner, linear * rims + listed)
    mine = jnp.sum(
        jnp.where((halo[:, None] == jnp.arange(rows, dtype=jnp.int32))[:, :, None], code[None], 0),
        axis=1,
    )
    codes = lax.all_gather(mine, AXES).reshape(count_x * count_y, rims, slots)
    other_x = (index_x + jnp.asarray(frame[:, 0], jnp.int32) * sign_x) % count_x
    other_y = (index_y + jnp.asarray(frame[:, 1], jnp.int32) * sign_y) % count_y
    near = jnp.take(codes, other_x * count_y + other_y, axis=0)

    base_of = np.zeros((9,), np.int32)
    for g, name in enumerate(GROUPS):
        x, y = FRAME[name]
        base_of[3 * (x + 1) + y + 1] = rows + g * rims

    def locate(place, index, shift_x, shift_y):
        x = (place // 3 - 1) * sign_x + shift_x
        y = (place % 3 - 1) * sign_y + shift_y
        inside = (jnp.abs(x) <= 1) & (jnp.abs(y) <= 1)
        at = 3 * (x + 1) + y + 1
        spot = index
        for k in range(9):
            if k != 4:
                spot = spot + jnp.where(at == k, int(base_of[k]), 0)
        own = index * 0
        for m in range(rims):
            own = own + jnp.where(index == m, halo[m], 0)
        return jnp.where(inside, jnp.where(at == 4, own, spot), -1)

    own_spots = jnp.where(cols < rows, cols, locate(linear, listed, 0, 0))
    shift_x = frame[:, 0].astype(np.int32)[:, None, None]
    shift_y = frame[:, 1].astype(np.int32)[:, None, None]
    near_spots = locate(near // rims, near % rims, shift_x, shift_y)
    near_spots = jnp.where(near < 0, -1, near_spots)
    spots = jnp.concatenate([own_spots, near_spots.reshape(-1, slots)], 0)
    pool = spots.shape[0]
    hit = spots[:, :, None] == jnp.arange(pool, dtype=jnp.int32)
    slot_table = (
        jnp.sum(jnp.where(hit, jnp.arange(1, slots + 1, dtype=jnp.int32)[:, None], 0), axis=1) - 1
    )
    return own_spots.astype(jnp.int32), slot_table.astype(jnp.int32)


def shards(density, moves, cols, halo_rows):
    row_count, block, strip = density.shape[2:]
    rim_count = halo_rows.shape[2]
    count_x = lax.axis_size("gx")
    count_y = lax.axis_size("gy")
    index_x = lax.axis_index("gx")
    index_y = lax.axis_index("gy")
    rows = density.reshape(row_count, block, strip)
    rims = halo_rows.reshape(rim_count)

    owner = moves.reshape(row_count) // row_count
    other = (index_x + jnp.asarray(step_x, jnp.int32)) % count_x * count_y
    other = other + (index_y + jnp.asarray(step_y, jnp.int32)) % count_y
    slot_ids = jnp.arange(row_count, dtype=jnp.int32)
    slots = jnp.sum(jnp.where(owner[None, :] == other[:, None], slot_ids, 0), axis=1)
    arrived = []
    for d in range(len(step_x)):
        dx, dy = int(step_x[d]), int(step_y[d])
        perm = flat_perm(count_x, count_y, lambda i, j: (i + dx, j + dy))
        leaving = lax.dynamic_index_in_dim(rows, slots[d], 0, keepdims=False)
        arrived.append(lax.ppermute(leaving, AXES, perm))

    own_spots, slot_table = tables(
        cols.reshape(row_count, -1), rims, index_x, index_y, count_x, count_y
    )
    current, rim_0, rim_1, trace = place(slots, rims, arrived)
    swap = {
        "A": flat_perm(count_x, count_y, toward_a),
        "B": flat_perm(count_x, count_y, along_b),
        "C": flat_perm(count_x, count_y, toward_c),
        "Y": flat_perm(count_x, count_y, toward_y),
    }
    go = lambda value, way: lax.ppermute(value, AXES, swap[way])
    traces = [trace]
    for step in range(STEPS):
        y_0, a_0 = go(rim_0, "Y"), go(rim_0, "A")
        y_1, a_1 = go(rim_1, "Y"), go(rim_1, "A")
        c_0, c_1 = go(rim_0, "C"), go(rim_1, "C")
        b_0, b_1 = go(a_0, "B"), go(a_1, "B")
        ya_0, ya_1 = go(y_0, "A"), go(a_1, "Y")
        ca_0, ca_1 = go(a_0, "C"), go(a_1, "C")
        yb_0, yb_1 = go(ya_0, "B"), go(b_1, "Y")
        cb_0, cb_1 = go(b_0, "C"), go(b_1, "C")
        four = 2 * rim_0.shape[0]
        total = product(0, slot_table, current, [], None, name="own_rows")
        total = product(
            row_count, slot_table, current, [c_0, c_1, a_0, a_1, y_0, y_1], total, name="near_rows"
        )
        total = product(
            row_count + 3 * four,
            slot_table,
            current,
            [ca_0, ca_1, b_0, b_1, ya_0, ya_1],
            total,
            name="corner_rows",
        )
        current, rim_0, rim_1, trace = product(
            row_count + 6 * four,
            slot_table,
            current,
            [cb_0, cb_1, yb_0, yb_1],
            total,
            last=(own_spots, rims, step % 2 == 1),
            name="last_rows",
        )
        traces.append(trace)
    scale = 1.0 / (count_x * count_y * row_count * block)
    early = butterfly(jnp.concatenate([traces[0], traces[1]], axis=0), count_x, count_y)
    late = butterfly(traces[2], count_x, count_y)
    occupation = jnp.stack([early[0, 0], early[1, 0], early[1, 0], late[0, 0]]) * scale
    return (current.reshape(density.shape), occupation)


def solution(mesh):
    in_specs = (
        P("gx", "gy", None, None, None),
        P("gx", "gy", None),
        P("gx", "gy", None, None),
        P("gx", "gy", None),
    )
    out_specs = (P("gx", "gy", None, None, None), P())
    return jax.shard_map(shards, mesh=mesh, in_specs=in_specs, out_specs=out_specs, check_vma=False)
```

time: 1480 us -> 365 us (0.25)
  local copies, waits for them, and re-layouts: 716 us -> 7.38 us
  waiting for transfers between devices: 441 us -> 49.8 us
  Pallas kernels: 0 us -> 179 us
  other arithmetic: 169 us -> 15.8 us
  matrix products: 74.5 us -> 0 us
  starting transfers between devices: 26.2 us -> 52.5 us
  between operations: 1.19 us -> 19.2 us
    ppermute x24 -> x50, waiting for transfers between devices: 441 us -> 49.8 us  [the longest x10 27.4 us: butterfly(): value = value + lax.ppermute(value, AXES, perm)]
    reshape x15 -> x0, local copies, waits for them, and re-layouts: 341 us -> none  [the longest x8 225 us: one_group(): far_blocks = far.reshape(width, slots, block, slots, block)]
    gather x22 -> x1, local copies, waits for them, and re-layouts: 239 us -> 0.57 us  [tables(): near = jnp.take(codes, other_x * count_y + other_y, axis=0)]
    pallas_call x0 -> x9, Pallas kernels: none -> 179 us  [the longest x8 177 us: product(): pl.pallas_call(functools.partial(product_kernel, spec), grid=(width // TI...]
    select_n x4 -> x0, local copies, waits for them, and re-layouts: 102 us -> none  [one_group(): jnp.where(found[:, :, None, :, None], aligned, 0.0)]
    select_n x16 -> x3, other arithmetic: 101 us -> 6.48 us  [the longest x1 3.18 us: tables(): own_spots = jnp.where(cols < rows, cols, locate(linear, listed, 0, 0))]
    dot_general x7 -> x0, matrix products: 74.5 us -> none  [the longest x4 64.8 us: one_group(): return jnp.einsum('gatb,gtbx->gax', mine, aligned, precision=highest)]
    concatenate x20 -> x2, other arithmetic: 49.8 us -> 1.34 us  [the longest x1 1.33 us: shards(): jnp.concatenate([traces[0], traces[1]], axis=0)]
  transfers between devices with their start and end apart: 24 -> 50, of which waited for: 17 -> 13; matrix products, arithmetic and copies ran while one was open for 1% -> 5% of each run, Pallas kernels for 0% -> 38%
where the time goes in v1:
time: 365 us; the launch traced here: 364 us
  Pallas kernels  179 us (49%)
  starting transfers between devices  52.5 us (14%)
  waiting for transfers between devices  49.8 us (14%)
  blocking collectives  40.7 us (11%)
  between operations  19.2 us (5%)
  other arithmetic  15.8 us (4%)
  local copies, waits for them, and re-layouts  7.38 us (2%)
    pallas_call x8, Pallas kernels, product(): pl.pallas_call(functools.partial(product_kernel, spec), grid=(width // TI...  177 us
    all_gather x1, blocking collectives, tables(): codes = lax.all_gather(mine, AXES).reshape(count_x * count_y, rims, slots)  40.7 us
    ppermute x10, waiting for transfers between devices, butterfly(): value = value + lax.ppermute(value, AXES, perm)  27.4 us
    ppermute x32, starting transfers between devices, shards(): go = lambda value, way: lax.ppermute(value, AXES, swap[way])  22.5 us
    ppermute x10, starting transfers between devices, butterfly(): value = value + lax.ppermute(value, AXES, perm)  16.6 us
    ppermute x8, starting transfers between devices, shards(): arrived.append(lax.ppermute(leaving, AXES, perm))  13.3 us
    ppermute x8, waiting for transfers between devices, shards(): arrived.append(lax.ppermute(leaving, AXES, perm))  13.3 us
    ppermute x32, waiting for transfers between devices, shards(): go = lambda value, way: lax.ppermute(value, AXES, swap[way])  9.01 us
  transfers between devices with their start and end apart: 50, of which 13 were waited for; matrix products, arithmetic and copies ran while one was open for 5% of the time, Pallas kernels for 38%

profile of v1, /device:TPU:0, one launch (start us, length us, event | category | flops | bytes accessed | tf_op | source)
XLA Modules:
  0.0 363.8 jit_solution(15778528673666393597)
XLA Ops:
  0.6 0.7 and_select_fusion.2
  1.5 0.7 fusion.29
  16.9 1.7 dynamic-slice_bitcast_fusion
  18.6 6.4 %collective-permute-start = (f32[64,1024]{1,0:T(8,128)S(1)}, f32[64,1024]{1,0:T(8,128)S(1)}, u32[]{:S(2)}, u32[]{:S(2)}) collective-permute-start(f32[64,1024]{1,0:T(8,128)S(1)} %get-tuple-element.30), channel_id=1, source_target_pairs={{0,31},{1,28},{2,29},{3,30},{4,3},{5,0},{6,1},{7,2},{8,7},{9,4},{1... | collective-permute-start | bytes 786440 | tf_op jit(solution)/shard_map/ppermute | solution.py:377
  25.0 0.5 collective-permute-start.1
  26.0 2.1 collective-permute-start.3
  28.1 0.8 fusion
  28.9 0.8 compare_reduce_fusion
  29.7 0.7 compare_and_fusion
  30.3 1.5 fusion.30
  31.8 3.2 compare_select_fusion.2
  35.0 1.9 collective-permute-start.5
  36.9 0.5 collective-permute-done.1.refs_1_
  37.3 1.9 collective-permute-start.6
  39.3 12.8 %collective-permute-done.2.refs_2_ = f32[64,1024]{1,0:T(8,128)S(1)} collective-permute-done((f32[64,1024]{1,0:T(8,128)S(1)}, f32[64,1024]{1,0:T(8,128)S(1)}, u32[]{:S(2)}, u32[]{:S(2)}) %collective-permute-start.2) | collective-permute-done | bytes 262176 | tf_op jit(solution)/shard_map/ppermute | solution.py:377
  52.1 0.7 iota_compare_fusion.1
  53.0 0.7 add.346
  53.8 0.7 add.352
  54.7 40.7 %all-gather.1 = s32[32,4,16]{2,1,0:T(4,128)S(1)} all-gather(s32[1,4,16]{2,1,0:T(4,128)S(1)} %bitcast.55), channel_id=2, replica_groups=mesh['gx'=8,'gy'=4] {'gx','gy'}, dimensions={0}, use_global_device_ids=true | all-gather | bytes 8448 | tf_op jit(solution)/shard_map/all_gather | solution.py:319
  95.4 0.6 gather_fusion
  96.1 0.6 copy-done
  96.7 1.2 place_rows.1
  98.1 2.6 select_select_fusion
  101.5 1.7 collective-permute-start.23
  103.3 8.9 %collective-permute-done.11.refs_5_ = f32[2,64,1024]{2,1,0:T(8,128)S(1)} collective-permute-done((f32[2,64,1024]{2,1,0:T(8,128)S(1)}, f32[2,64,1024]{2,1,0:T(8,128)S(1)}, u32[]{:S(2)}, u32[]{:S(2)}) %collective-permute-start.11) | collective-permute-done | bytes 524320 | tf_op jit(solution)/shard_map/ppermute | solution.py:389
  112.5 21.4 %own_rows.2.refs_8_ = f32[512,2560]{1,0:T(8,128)} custom-call(s32[40,40]{1,0:T(8,128)S(1)} %broadcast_add_fusion.refs_0_, f32[8,64,1024]{2,1,0:T(8,128)S(1)} %get-tuple-element.12.refs_1_.refs_3_), custom_call_target="tpu_custom_call" | custom-call | flops 4026531840 | bytes 14680064 | tf_op jit(solution)/shard_map/own_rows/pallas_call | solution.py:272
  134.7 2.1 collective-permute-start.15
  136.8 24.8 %near_rows.2.refs_8_ = f32[512,2560]{1,0:T(8,128)} custom-call(s32[40,40]{1,0:T(8,128)S(1)} %broadcast_add_fusion.refs_0_, f32[8,64,1024]{2,1,0:T(8,128)S(1)} %get-tuple-element.12.refs_1_.refs_3_, f32[2,64,1024]{2,1,0:T(8,128)S(1)} %collective-permute-done.21.refs_2_, f32[2,64,1024]{2,1,0:T(8,128)S(1)} %collective-permute-done.22.refs_3_, ...), custom_call_target="tpu_custom_call" | custom-call | flops 6039797760 | bytes 15728640 | tf_op jit(solution)/shard_map/near_rows/pallas_call | solution.py:272
  161.8 0.8 collective-permute-start.17
  163.1 3.1 collective-permute-start.16
  166.2 23.1 %corner_rows.2.refs_8_ = f32[512,2560]{1,0:T(8,128)} custom-call(s32[40,40]{1,0:T(8,128)S(1)} %broadcast_add_fusion.refs_0_, f32[8,64,1024]{2,1,0:T(8,128)S(1)} %get-tuple-element.12.refs_1_.refs_3_, f32[2,64,1024]{2,1,0:T(8,128)S(1)} %collective-permute-done.18.refs_2_, f32[2,64,1024]{2,1,0:T(8,128)S(1)} %collective-permute-done.19.refs_3_, ...), custom_call_target="tpu_custom_call" | custom-call | flops 6039797760 | bytes 15728640 | tf_op jit(solution)/shard_map/corner_rows/pallas_call | solution.py:272
  189.3 19.2 %last_rows.2 = (f32[8,64,1024]{2,1,0:T(8,128)S(1)}, f32[2,64,1024]{2,1,0:T(8,128)S(1)}, f32[2,64,1024]{2,1,0:T(8,128)S(1)}, f32[1,1]{1,0:T(1,128)}) custom-call(s32[40,40]{1,0:T(8,128)S(1)} %broadcast_add_fusion.refs_0_, s32[8,16]{1,0:T(8,128)S(1)} %get-tuple-element.32.refs_1_, s32[4]{0:T(128)S(1)} %bitcast.50, f32[8,64,1024]{2,1,0:T(8,128)} %copy-done.2, ...), custom_call_target="tpu_custom_call" | custom-call | flops 4026531840 | bytes 14680064 | tf_op jit(solution)/shard_map/last_rows/pallas_call | solution.py:272
  208.4 2.8 collective-permute-start.24
  211.6 1.3 pad_maximum_fusion
  213.2 0.9 collective-permute-done.40
  214.1 1.3 fusion.27
  215.5 1.9 collective-permute-start.41
  217.4 6.2 %collective-permute-done.41 = f32[2,1]{1,0:T(2,128)S(1)} collective-permute-done((f32[2,1]{1,0:T(2,128)S(1)}, f32[2,1]{1,0:T(2,128)S(1)}, u32[]{:S(2)}, u32[]{:S(2)}) %collective-permute-start.41) | collective-permute-done | bytes 40 | tf_op jit(solution)/shard_map/ppermute | solution.py:294
  223.6 1.3 fusion.31
  224.9 0.7 collective-permute-start.42
  225.7 8.1 %collective-permute-done.42 = f32[2,1]{1,0:T(2,128)S(1)} collective-permute-done((f32[2,1]{1,0:T(2,128)S(1)}, f32[2,1]{1,0:T(2,128)S(1)}, u32[]{:S(2)}, u32[]{:S(2)}) %collective-permute-start.42) | collective-permute-done | bytes 40 | tf_op jit(solution)/shard_map/ppermute | solution.py:297
  233.8 1.6 collective-permute-start.43
  235.4 2.0 collective-permute-done.43
  237.4 1.7 collective-permute-start.44
  239.0 2.8 collective-permute-done.44
  241.8 1.0 collective-permute-start.39
  242.9 0.9 collective-permute-start.25
  243.8 21.4 %own_rows.3.refs_8_ = f32[512,2560]{1,0:T(8,128)} custom-call(s32[40,40]{1,0:T(8,128)S(1)} %broadcast_add_fusion.refs_0_, f32[8,64,1024]{2,1,0:T(8,128)S(1)} %get-tuple-element.15.refs_1_.refs_3_), custom_call_target="tpu_custom_call" | custom-call | flops 4026531840 | bytes 14680064 | tf_op jit(solution)/shard_map/own_rows/pallas_call | solution.py:272
  265.2 0.6 fusion.28
  265.8 1.3 collective-permute-start.28
  267.1 1.4 collective-permute-start.36
  268.6 0.9 collective-permute-start.31
  269.5 24.8 %near_rows.3.refs_8_ = f32[512,2560]{1,0:T(8,128)} custom-call(s32[40,40]{1,0:T(8,128)S(1)} %broadcast_add_fusion.refs_0_, f32[8,64,1024]{2,1,0:T(8,128)S(1)} %get-tuple-element.15.refs_1_.refs_3_, f32[2,64,1024]{2,1,0:T(8,128)S(1)} %collective-permute-done.37.refs_2_, f32[2,64,1024]{2,1,0:T(8,128)S(1)} %collective-permute-done.38.refs_3_, ...), custom_call_target="tpu_custom_call" | custom-call | flops 6039797760 | bytes 15728640 | tf_op jit(solution)/shard_map/near_rows/pallas_call | solution.py:272
  295.4 2.5 collective-permute-start.32
  297.9 23.0 %corner_rows.3.refs_8_ = f32[512,2560]{1,0:T(8,128)} custom-call(s32[40,40]{1,0:T(8,128)S(1)} %broadcast_add_fusion.refs_0_, f32[8,64,1024]{2,1,0:T(8,128)S(1)} %get-tuple-element.15.refs_1_.refs_3_, f32[2,64,1024]{2,1,0:T(8,128)S(1)} %collective-permute-done.34.refs_2_, f32[2,64,1024]{2,1,0:T(8,128)S(1)} %collective-permute-done.35.refs_3_, ...), custom_call_target="tpu_custom_call" | custom-call | flops 6039797760 | bytes 15728640 | tf_op jit(solution)/shard_map/corner_rows/pallas_call | solution.py:272
  321.0 19.6 %last_rows.3 = (f32[8,64,1024]{2,1,0:T(8,128)}, f32[2,64,1024]{2,1,0:T(8,128)}, f32[2,64,1024]{2,1,0:T(8,128)}, f32[1,1]{1,0:T(1,128)}) custom-call(s32[40,40]{1,0:T(8,128)S(1)} %broadcast_add_fusion.refs_0_, s32[8,16]{1,0:T(8,128)S(1)} %get-tuple-element.32.refs_1_, s32[4]{0:T(128)S(1)} %bitcast.51, f32[8,64,1024]{2,1,0:T(8,128)S(1)} %get-tuple-element.15.refs_1_.refs_3_, ...), custom_call_target="tpu_custom_call" | custom-call | flops 4026531840 | bytes 14680064 | tf_op jit(solution)/shard_map/last_rows/pallas_call | solution.py:272
  340.7 1.4 collective-permute-done.45
  343.2 3.5 collective-permute-start.46
  347.6 3.9 %collective-permute-start.47 = (f32[1,1]{1,0:T(1,128)}, f32[1,1]{1,0:T(1,128)}, u32[]{:S(2)}, u32[]{:S(2)}) collective-permute-start(f32[1,1]{1,0:T(1,128)} %add.391), channel_id=1, source_target_pairs={{0,4},{1,5},{2,6},{3,7},{4,0},{5,1},{6,2},{7,3},{8,12},{9,13},{10,... | collective-permute-start | bytes 20 | tf_op jit(solution)/shard_map/ppermute | solution.py:297
  352.4 1.5 collective-permute-start.48
  353.9 2.2 collective-permute-done.48
  356.7 1.4 collective-permute-start.49
  358.1 3.2 collective-permute-done.49
  362.0 1.9 maximum_multiply_fusion
  (84 shorter events, 6.2 us)
Async XLA Ops:
  18.6 16.4 %collective-permute-start = (f32[64,1024]{1,0:T(8,128)S(1)}, f32[64,1024]{1,0:T(8,128)S(1)}, u32[]{:S(2)}, u32[]{:S(2)}) collective-permute-start(f32[64,1024]{1,0:T(8,128)S(1)} %get-tuple-element.30), channel_id=1, source_target_pairs={{0,31},{1,28},{2,29},{3,30},{4,3},{5,0},{6,1},{7,2},{8,7},{9,4},{1... | collective-permute-start | bytes 786440 | tf_op jit(solution)/shard_map/ppermute | solution.py:377
  25.0 12.3 %collective-permute-start.1 = (f32[64,1024]{1,0:T(8,128)S(1)}, f32[64,1024]{1,0:T(8,128)S(1)}, u32[]{:S(2)}, u32[]{:S(2)}) collective-permute-start(f32[64,1024]{1,0:T(8,128)S(1)} %get-tuple-element.29), channel_id=1, source_target_pairs={{0,28},{1,29},{2,30},{3,31},{4,0},{5,1},{6,2},{7,3},{8,4},{9,5},{1... | collective-permute-start | bytes 786440 | tf_op jit(solution)/shard_map/ppermute | solution.py:377
  25.6 26.5 %collective-permute-start.2 = (f32[64,1024]{1,0:T(8,128)S(1)}, f32[64,1024]{1,0:T(8,128)S(1)}, u32[]{:S(2)}, u32[]{:S(2)}) collective-permute-start(f32[64,1024]{1,0:T(8,128)S(1)} %get-tuple-element.28), channel_id=1, source_target_pairs={{0,29},{1,30},{2,31},{3,28},{4,1},{5,2},{6,3},{7,0},{8,5},{9,6},{1... | collective-permute-start | bytes 786440 | tf_op jit(solution)/shard_map/ppermute | solution.py:377
  26.0 70.0 %collective-permute-start.3 = (f32[64,1024]{1,0:T(8,128)S(1)}, f32[64,1024]{1,0:T(8,128)S(1)}, u32[]{:S(2)}, u32[]{:S(2)}) collective-permute-start(f32[64,1024]{1,0:T(8,128)S(1)} %get-tuple-element.27), channel_id=1, source_target_pairs={{0,3},{1,0},{2,1},{3,2},{4,7},{5,4},{6,5},{7,6},{8,11},{9,8},{10,9... | collective-permute-start | bytes 786440 | tf_op jit(solution)/shard_map/ppermute | solution.py:377
  28.1 67.9 %collective-permute-start.4 = (f32[64,1024]{1,0:T(8,128)S(1)}, f32[64,1024]{1,0:T(8,128)S(1)}, u32[]{:S(2)}, u32[]{:S(2)}) collective-permute-start(f32[64,1024]{1,0:T(8,128)S(1)} %get-tuple-element.26), channel_id=1, source_target_pairs={{0,1},{1,2},{2,3},{3,0},{4,5},{5,6},{6,7},{7,4},{8,9},{9,10},{10,1... | collective-permute-start | bytes 786440 | tf_op jit(solution)/shard_map/ppermute | solution.py:377
  35.0 61.0 %collective-permute-start.5 = (f32[64,1024]{1,0:T(8,128)S(1)}, f32[64,1024]{1,0:T(8,128)S(1)}, u32[]{:S(2)}, u32[]{:S(2)}) collective-permute-start(f32[64,1024]{1,0:T(8,128)S(1)} %get-tuple-element.25), channel_id=1, source_target_pairs={{0,7},{1,4},{2,5},{3,6},{4,11},{5,8},{6,9},{7,10},{8,15},{9,12},{1... | collective-permute-start | bytes 786440 | tf_op jit(solution)/shard_map/ppermute | solution.py:377
  37.3 58.7 %collective-permute-start.6 = (f32[64,1024]{1,0:T(8,128)S(1)}, f32[64,1024]{1,0:T(8,128)S(1)}, u32[]{:S(2)}, u32[]{:S(2)}) collective-permute-start(f32[64,1024]{1,0:T(8,128)S(1)} %get-tuple-element.31), channel_id=1, source_target_pairs={{0,4},{1,5},{2,6},{3,7},{4,8},{5,9},{6,10},{7,11},{8,12},{9,13},{1... | collective-permute-start | bytes 786440 | tf_op jit(solution)/shard_map/ppermute | solution.py:377
  52.1 44.0 %collective-permute-start.7 = (f32[64,1024]{1,0:T(8,128)S(1)}, f32[64,1024]{1,0:T(8,128)S(1)}, u32[]{:S(2)}, u32[]{:S(2)}) collective-permute-start(f32[64,1024]{1,0:T(8,128)S(1)} %get-tuple-element.24), channel_id=1, source_target_pairs={{0,5},{1,6},{2,7},{3,4},{4,9},{5,10},{6,11},{7,8},{8,13},{9,14},{1... | collective-permute-start | bytes 786440 | tf_op jit(solution)/shard_map/ppermute | solution.py:377
  96.0 0.7 copy-start
  97.9 68.2 %copy-start.2 = (f32[8,64,1024]{2,1,0:T(8,128)}, f32[8,64,1024]{2,1,0:T(8,128)S(1)}, u32[]{:S(2)}) copy-start(f32[8,64,1024]{2,1,0:T(8,128)S(1)} %get-tuple-element.12.refs_1_.refs_3_) | copy-start | bytes 6291460
  98.0 14.2 %collective-permute-start.11 = (f32[2,64,1024]{2,1,0:T(8,128)S(1)}, f32[2,64,1024]{2,1,0:T(8,128)S(1)}, u32[]{:S(2)}, u32[]{:S(2)}) collective-permute-start(f32[2,64,1024]{2,1,0:T(8,128)S(1)} %get-tuple-element.14), channel_id=1, source_target_pairs={{0,4},{1,5},{2,6},{3,7},{4,0},{5,1},{6,2},{7,3},{8,12},{9,13},{10,... | collective-permute-start | bytes 1572872 | tf_op jit(solution)/shard_map/ppermute | solution.py:389
  98.0 14.4 %collective-permute-start.14 = (f32[2,64,1024]{2,1,0:T(8,128)S(1)}, f32[2,64,1024]{2,1,0:T(8,128)S(1)}, u32[]{:S(2)}, u32[]{:S(2)}) collective-permute-start(f32[2,64,1024]{2,1,0:T(8,128)S(1)} %get-tuple-element.13), channel_id=1, source_target_pairs={{0,3},{1,2},{2,1},{3,0},{4,7},{5,6},{6,5},{7,4},{8,11},{9,10},{10,... | collective-permute-start | bytes 1572872 | tf_op jit(solution)/shard_map/ppermute | solution.py:389
  101.0 32.9 %collective-permute-start.21 = (f32[2,64,1024]{2,1,0:T(8,128)S(1)}, f32[2,64,1024]{2,1,0:T(8,128)S(1)}, u32[]{:S(2)}, u32[]{:S(2)}) collective-permute-start(f32[2,64,1024]{2,1,0:T(8,128)S(1)} %get-tuple-element.13), channel_id=1, source_target_pairs={{0,1},{1,0},{2,3},{3,2},{4,5},{5,4},{6,7},{7,6},{8,9},{9,8},{10,11... | collective-permute-start | bytes 1572872 | tf_op jit(solution)/shard_map/ppermute | solution.py:389
  101.4 32.6 %collective-permute-start.22 = (f32[2,64,1024]{2,1,0:T(8,128)S(1)}, f32[2,64,1024]{2,1,0:T(8,128)S(1)}, u32[]{:S(2)}, u32[]{:S(2)}) collective-permute-start(f32[2,64,1024]{2,1,0:T(8,128)S(1)} %get-tuple-element.14), channel_id=1, source_target_pairs={{0,1},{1,0},{2,3},{3,2},{4,5},{5,4},{6,7},{7,6},{8,9},{9,8},{10,11... | collective-permute-start | bytes 1572872 | tf_op jit(solution)/shard_map/ppermute | solution.py:389
  101.5 33.1 %collective-permute-start.23 = (f32[2,64,1024]{2,1,0:T(8,128)S(1)}, f32[2,64,1024]{2,1,0:T(8,128)S(1)}, u32[]{:S(2)}, u32[]{:S(2)}) collective-permute-start(f32[2,64,1024]{2,1,0:T(8,128)S(1)} %get-tuple-element.14), channel_id=1, source_target_pairs={{0,3},{1,2},{2,1},{3,0},{4,7},{5,6},{6,5},{7,4},{8,11},{9,10},{10,... | collective-permute-start | bytes 1572872 | tf_op jit(solution)/shard_map/ppermute | solution.py:389
  112.2 22.0 %collective-permute-start.8 = (f32[2,64,1024]{2,1,0:T(8,128)S(1)}, f32[2,64,1024]{2,1,0:T(8,128)S(1)}, u32[]{:S(2)}, u32[]{:S(2)}) collective-permute-start(f32[2,64,1024]{2,1,0:T(8,128)S(1)} %get-tuple-element.13), channel_id=1, source_target_pairs={{0,4},{1,5},{2,6},{3,7},{4,0},{5,1},{6,2},{7,3},{8,12},{9,13},{10,... | collective-permute-start | bytes 1572872 | tf_op jit(solution)/shard_map/ppermute | solution.py:389
  112.5 22.2 %collective-permute-start.12 = (f32[2,64,1024]{2,1,0:T(8,128)S(1)}, f32[2,64,1024]{2,1,0:T(8,128)S(1)}, u32[]{:S(2)}, u32[]{:S(2)}) collective-permute-start(f32[2,64,1024]{2,1,0:T(8,128)S(1)} %collective-permute-done.11.refs_5_), channel_id=1, source_target_pairs={{0,8},{1,9},{2,10},{3,11},{4,28},{5,29},{6,30},{7,31},{8,16},{9,17... | collective-permute-start | bytes 1572872 | tf_op jit(solution)/shard_map/ppermute | solution.py:389
  133.9 29.2 %collective-permute-start.19 = (f32[2,64,1024]{2,1,0:T(8,128)S(1)}, f32[2,64,1024]{2,1,0:T(8,128)S(1)}, u32[]{:S(2)}, u32[]{:S(2)}) collective-permute-start(f32[2,64,1024]{2,1,0:T(8,128)S(1)} %collective-permute-done.11.refs_5_), channel_id=1, source_target_pairs={{0,1},{1,0},{2,3},{3,2},{4,5},{5,4},{6,7},{7,6},{8,9},{9,8},{10,11... | collective-permute-start | bytes 1572872 | tf_op jit(solution)/shard_map/ppermute | solution.py:389
  133.9 32.3 %collective-permute-start.20 = (f32[2,64,1024]{2,1,0:T(8,128)S(1)}, f32[2,64,1024]{2,1,0:T(8,128)S(1)}, u32[]{:S(2)}, u32[]{:S(2)}) collective-permute-start(f32[2,64,1024]{2,1,0:T(8,128)S(1)} %collective-permute-done.11.refs_5_), channel_id=1, source_target_pairs={{0,3},{1,2},{2,1},{3,0},{4,7},{5,6},{6,5},{7,4},{8,11},{9,10},{10,... | collective-permute-start | bytes 1572872 | tf_op jit(solution)/shard_map/ppermute | solution.py:389
  134.2 27.6 %collective-permute-start.18 = (f32[2,64,1024]{2,1,0:T(8,128)S(1)}, f32[2,64,1024]{2,1,0:T(8,128)S(1)}, u32[]{:S(2)}, u32[]{:S(2)}) collective-permute-start(f32[2,64,1024]{2,1,0:T(8,128)S(1)} %collective-permute-done.8.refs_4_), channel_id=1, source_target_pairs={{0,1},{1,0},{2,3},{3,2},{4,5},{5,4},{6,7},{7,6},{8,9},{9,8},{10,11... | collective-permute-start | bytes 1572872 | tf_op jit(solution)/shard_map/ppermute | solution.py:389
  134.7 28.0 %collective-permute-start.9 = (f32[2,64,1024]{2,1,0:T(8,128)S(1)}, f32[2,64,1024]{2,1,0:T(8,128)S(1)}, u32[]{:S(2)}, u32[]{:S(2)}) collective-permute-start(f32[2,64,1024]{2,1,0:T(8,128)S(1)} %collective-permute-done.8.refs_4_), channel_id=1, source_target_pairs={{0,8},{1,9},{2,10},{3,11},{4,28},{5,29},{6,30},{7,31},{8,16},{9,17... | collective-permute-start | bytes 1572872 | tf_op jit(solution)/shard_map/ppermute | solution.py:389
  134.7 26.9 %collective-permute-start.15 = (f32[2,64,1024]{2,1,0:T(8,128)S(1)}, f32[2,64,1024]{2,1,0:T(8,128)S(1)}, u32[]{:S(2)}, u32[]{:S(2)}) collective-permute-start(f32[2,64,1024]{2,1,0:T(8,128)S(1)} %collective-permute-done.14.refs_6_), channel_id=1, source_target_pairs={{0,4},{1,5},{2,6},{3,7},{4,0},{5,1},{6,2},{7,3},{8,12},{9,13},{10,... | collective-permute-start | bytes 1572872 | tf_op jit(solution)/shard_map/ppermute | solution.py:389
  161.6 27.7 %copy-start.1 = (s32[1,1,4]{2,1,0:T(1,128)S(1)}, s32[1,1,4]{2,1,0:T(1,128)}, u32[]{:S(2)}) copy-start(s32[1,1,4]{2,1,0:T(1,128)} %param.13) | copy-start | bytes 52
  161.6 27.6 %collective-permute-start.13 = (f32[2,64,1024]{2,1,0:T(8,128)S(1)}, f32[2,64,1024]{2,1,0:T(8,128)S(1)}, u32[]{:S(2)}, u32[]{:S(2)}) collective-permute-start(f32[2,64,1024]{2,1,0:T(8,128)S(1)} %collective-permute-done.12.refs_5_), channel_id=1, source_target_pairs={{0,1},{1,0},{2,3},{3,2},{4,5},{5,4},{6,7},{7,6},{8,9},{9,8},{10,11... | collective-permute-start | bytes 1572872 | tf_op jit(solution)/shard_map/ppermute | solution.py:389
  161.8 27.4 %collective-permute-start.17 = (f32[2,64,1024]{2,1,0:T(8,128)S(1)}, f32[2,64,1024]{2,1,0:T(8,128)S(1)}, u32[]{:S(2)}, u32[]{:S(2)}) collective-permute-start(f32[2,64,1024]{2,1,0:T(8,128)S(1)} %collective-permute-done.12.refs_5_), channel_id=1, source_target_pairs={{0,3},{1,2},{2,1},{3,0},{4,7},{5,6},{6,5},{7,4},{8,11},{9,10},{10,... | collective-permute-start | bytes 1572872 | tf_op jit(solution)/shard_map/ppermute | solution.py:389
  162.7 26.6 %collective-permute-start.10 = (f32[2,64,1024]{2,1,0:T(8,128)S(1)}, f32[2,64,1024]{2,1,0:T(8,128)S(1)}, u32[]{:S(2)}, u32[]{:S(2)}) collective-permute-start(f32[2,64,1024]{2,1,0:T(8,128)S(1)} %collective-permute-done.9.refs_4_), channel_id=1, source_target_pairs={{0,1},{1,0},{2,3},{3,2},{4,5},{5,4},{6,7},{7,6},{8,9},{9,8},{10,11... | collective-permute-start | bytes 1572872 | tf_op jit(solution)/shard_map/ppermute | solution.py:389
  163.1 26.2 %collective-permute-start.16 = (f32[2,64,1024]{2,1,0:T(8,128)S(1)}, f32[2,64,1024]{2,1,0:T(8,128)S(1)}, u32[]{:S(2)}, u32[]{:S(2)}) collective-permute-start(f32[2,64,1024]{2,1,0:T(8,128)S(1)} %collective-permute-done.15.refs_6_), channel_id=1, source_target_pairs={{0,8},{1,9},{2,10},{3,11},{4,28},{5,29},{6,30},{7,31},{8,16},{9,17... | collective-permute-start | bytes 1572872 | tf_op jit(solution)/shard_map/ppermute | solution.py:389
  208.4 33.4 %collective-permute-start.24 = (f32[2,64,1024]{2,1,0:T(8,128)S(1)}, f32[2,64,1024]{2,1,0:T(8,128)S(1)}, u32[]{:S(2)}, u32[]{:S(2)}) collective-permute-start(f32[2,64,1024]{2,1,0:T(8,128)S(1)} %get-tuple-element.16), channel_id=1, source_target_pairs={{0,4},{1,5},{2,6},{3,7},{4,0},{5,1},{6,2},{7,3},{8,12},{9,13},{10,... | collective-permute-start | bytes 1572872 | tf_op jit(solution)/shard_map/ppermute | solution.py:389
  211.2 54.5 %collective-permute-start.30 = (f32[2,64,1024]{2,1,0:T(8,128)S(1)}, f32[2,64,1024]{2,1,0:T(8,128)S(1)}, u32[]{:S(2)}, u32[]{:S(2)}) collective-permute-start(f32[2,64,1024]{2,1,0:T(8,128)S(1)} %get-tuple-element.16), channel_id=1, source_target_pairs={{0,3},{1,2},{2,1},{3,0},{4,7},{5,6},{6,5},{7,4},{8,11},{9,10},{10,... | collective-permute-start | bytes 1572872 | tf_op jit(solution)/shard_map/ppermute | solution.py:389
  211.2 54.5 %collective-permute-start.37 = (f32[2,64,1024]{2,1,0:T(8,128)S(1)}, f32[2,64,1024]{2,1,0:T(8,128)S(1)}, u32[]{:S(2)}, u32[]{:S(2)}) collective-permute-start(f32[2,64,1024]{2,1,0:T(8,128)S(1)} %get-tuple-element.16), channel_id=1, source_target_pairs={{0,1},{1,0},{2,3},{3,2},{4,5},{5,4},{6,7},{7,6},{8,9},{9,8},{10,11... | collective-permute-start | bytes 1572872 | tf_op jit(solution)/shard_map/ppermute | solution.py:389
  211.2 31.6 %collective-permute-start.27 = (f32[2,64,1024]{2,1,0:T(8,128)S(1)}, f32[2,64,1024]{2,1,0:T(8,128)S(1)}, u32[]{:S(2)}, u32[]{:S(2)}) collective-permute-start(f32[2,64,1024]{2,1,0:T(8,128)S(1)} %get-tuple-element.17), channel_id=1, source_target_pairs={{0,4},{1,5},{2,6},{3,7},{4,0},{5,1},{6,2},{7,3},{8,12},{9,13},{10,... | collective-permute-start | bytes 1572872 | tf_op jit(solution)/shard_map/ppermute | solution.py:389
  212.9 1.2 collective-permute-start.40
  215.5 8.1 %collective-permute-start.41 = (f32[2,1]{1,0:T(2,128)S(1)}, f32[2,1]{1,0:T(2,128)S(1)}, u32[]{:S(2)}, u32[]{:S(2)}) collective-permute-start(f32[2,1]{1,0:T(2,128)S(1)} %fusion.27), channel_id=1, source_target_pairs={{0,2},{1,3},{2,0},{3,1},{4,6},{5,7},{6,4},{7,5},{8,10},{9,11},{10,... | collective-permute-start | bytes 32 | tf_op jit(solution)/shard_map/ppermute | solution.py:294
  224.9 8.8 %collective-permute-start.42 = (f32[2,1]{1,0:T(2,128)S(1)}, f32[2,1]{1,0:T(2,128)S(1)}, u32[]{:S(2)}, u32[]{:S(2)}) collective-permute-start(f32[2,1]{1,0:T(2,128)S(1)} %fusion.31), channel_id=1, source_target_pairs={{0,4},{1,5},{2,6},{3,7},{4,0},{5,1},{6,2},{7,3},{8,12},{9,13},{10,... | collective-permute-start | bytes 32 | tf_op jit(solution)/shard_map/ppermute | solution.py:297
  233.8 3.6 collective-permute-start.43
  237.4 4.5 %collective-permute-start.44 = (f32[2,1]{1,0:T(2,128)S(1)}, f32[2,1]{1,0:T(2,128)S(1)}, u32[]{:S(2)}, u32[]{:S(2)}) collective-permute-start(f32[2,1]{1,0:T(2,128)S(1)} %add.388), channel_id=1, source_target_pairs={{0,16},{1,17},{2,18},{3,19},{4,20},{5,21},{6,22},{7,23},{8,24},{9,... | collective-permute-start | bytes 32 | tf_op jit(solution)/shard_map/ppermute | solution.py:297
  241.8 25.3 %collective-permute-start.38 = (f32[2,64,1024]{2,1,0:T(8,128)S(1)}, f32[2,64,1024]{2,1,0:T(8,128)S(1)}, u32[]{:S(2)}, u32[]{:S(2)}) collective-permute-start(f32[2,64,1024]{2,1,0:T(8,128)S(1)} %get-tuple-element.17), channel_id=1, source_target_pairs={{0,1},{1,0},{2,3},{3,2},{4,5},{5,4},{6,7},{7,6},{8,9},{9,8},{10,11... | collective-permute-start | bytes 1572872 | tf_op jit(solution)/shard_map/ppermute | solution.py:389
  241.8 25.3 %collective-permute-start.39 = (f32[2,64,1024]{2,1,0:T(8,128)S(1)}, f32[2,64,1024]{2,1,0:T(8,128)S(1)}, u32[]{:S(2)}, u32[]{:S(2)}) collective-permute-start(f32[2,64,1024]{2,1,0:T(8,128)S(1)} %get-tuple-element.17), channel_id=1, source_target_pairs={{0,3},{1,2},{2,1},{3,0},{4,7},{5,6},{6,5},{7,4},{8,11},{9,10},{10,... | collective-permute-start | bytes 1572872 | tf_op jit(solution)/shard_map/ppermute | solution.py:389
  242.9 25.7 %collective-permute-start.25 = (f32[2,64,1024]{2,1,0:T(8,128)S(1)}, f32[2,64,1024]{2,1,0:T(8,128)S(1)}, u32[]{:S(2)}, u32[]{:S(2)}) collective-permute-start(f32[2,64,1024]{2,1,0:T(8,128)S(1)} %collective-permute-done.24.refs_4_), channel_id=1, source_target_pairs={{0,8},{1,9},{2,10},{3,11},{4,28},{5,29},{6,30},{7,31},{8,16},{9,17... | collective-permute-start | bytes 1572872 | tf_op jit(solution)/shard_map/ppermute | solution.py:389
  265.8 29.2 %collective-permute-start.34 = (f32[2,64,1024]{2,1,0:T(8,128)S(1)}, f32[2,64,1024]{2,1,0:T(8,128)S(1)}, u32[]{:S(2)}, u32[]{:S(2)}) collective-permute-start(f32[2,64,1024]{2,1,0:T(8,128)S(1)} %collective-permute-done.24.refs_4_), channel_id=1, source_target_pairs={{0,1},{1,0},{2,3},{3,2},{4,5},{5,4},{6,7},{7,6},{8,9},{9,8},{10,11... | collective-permute-start | bytes 1572872 | tf_op jit(solution)/shard_map/ppermute | solution.py:389
  265.8 28.5 %collective-permute-start.28 = (f32[2,64,1024]{2,1,0:T(8,128)S(1)}, f32[2,64,1024]{2,1,0:T(8,128)S(1)}, u32[]{:S(2)}, u32[]{:S(2)}) collective-permute-start(f32[2,64,1024]{2,1,0:T(8,128)S(1)} %collective-permute-done.27.refs_5_), channel_id=1, source_target_pairs={{0,8},{1,9},{2,10},{3,11},{4,28},{5,29},{6,30},{7,31},{8,16},{9,17... | collective-permute-start | bytes 1572872 | tf_op jit(solution)/shard_map/ppermute | solution.py:389
  267.1 28.3 %collective-permute-start.35 = (f32[2,64,1024]{2,1,0:T(8,128)S(1)}, f32[2,64,1024]{2,1,0:T(8,128)S(1)}, u32[]{:S(2)}, u32[]{:S(2)}) collective-permute-start(f32[2,64,1024]{2,1,0:T(8,128)S(1)} %collective-permute-done.27.refs_5_), channel_id=1, source_target_pairs={{0,1},{1,0},{2,3},{3,2},{4,5},{5,4},{6,7},{7,6},{8,9},{9,8},{10,11... | collective-permute-start | bytes 1572872 | tf_op jit(solution)/shard_map/ppermute | solution.py:389
  267.1 30.8 %collective-permute-start.36 = (f32[2,64,1024]{2,1,0:T(8,128)S(1)}, f32[2,64,1024]{2,1,0:T(8,128)S(1)}, u32[]{:S(2)}, u32[]{:S(2)}) collective-permute-start(f32[2,64,1024]{2,1,0:T(8,128)S(1)} %collective-permute-done.27.refs_5_), channel_id=1, source_target_pairs={{0,3},{1,2},{2,1},{3,0},{4,7},{5,6},{6,5},{7,4},{8,11},{9,10},{10,... | collective-permute-start | bytes 1572872 | tf_op jit(solution)/shard_map/ppermute | solution.py:389
  268.6 26.0 %collective-permute-start.31 = (f32[2,64,1024]{2,1,0:T(8,128)S(1)}, f32[2,64,1024]{2,1,0:T(8,128)S(1)}, u32[]{:S(2)}, u32[]{:S(2)}) collective-permute-start(f32[2,64,1024]{2,1,0:T(8,128)S(1)} %collective-permute-done.30.refs_6_), channel_id=1, source_target_pairs={{0,4},{1,5},{2,6},{3,7},{4,0},{5,1},{6,2},{7,3},{8,12},{9,13},{10,... | collective-permute-start | bytes 1572872 | tf_op jit(solution)/shard_map/ppermute | solution.py:389
  294.3 26.6 %collective-permute-start.29 = (f32[2,64,1024]{2,1,0:T(8,128)S(1)}, f32[2,64,1024]{2,1,0:T(8,128)S(1)}, u32[]{:S(2)}, u32[]{:S(2)}) collective-permute-start(f32[2,64,1024]{2,1,0:T(8,128)S(1)} %collective-permute-done.28.refs_5_), channel_id=1, source_target_pairs={{0,1},{1,0},{2,3},{3,2},{4,5},{5,4},{6,7},{7,6},{8,9},{9,8},{10,11... | collective-permute-start | bytes 1572872 | tf_op jit(solution)/shard_map/ppermute | solution.py:389
  294.5 26.4 %collective-permute-start.33 = (f32[2,64,1024]{2,1,0:T(8,128)S(1)}, f32[2,64,1024]{2,1,0:T(8,128)S(1)}, u32[]{:S(2)}, u32[]{:S(2)}) collective-permute-start(f32[2,64,1024]{2,1,0:T(8,128)S(1)} %collective-permute-done.28.refs_5_), channel_id=1, source_target_pairs={{0,3},{1,2},{2,1},{3,0},{4,7},{5,6},{6,5},{7,4},{8,11},{9,10},{10,... | collective-permute-start | bytes 1572872 | tf_op jit(solution)/shard_map/ppermute | solution.py:389
  294.9 26.0 %collective-permute-start.26 = (f32[2,64,1024]{2,1,0:T(8,128)S(1)}, f32[2,64,1024]{2,1,0:T(8,128)S(1)}, u32[]{:S(2)}, u32[]{:S(2)}) collective-permute-start(f32[2,64,1024]{2,1,0:T(8,128)S(1)} %collective-permute-done.25.refs_4_), channel_id=1, source_target_pairs={{0,1},{1,0},{2,3},{3,2},{4,5},{5,4},{6,7},{7,6},{8,9},{9,8},{10,11... | collective-permute-start | bytes 1572872 | tf_op jit(solution)/shard_map/ppermute | solution.py:389
  295.4 25.6 %collective-permute-start.32 = (f32[2,64,1024]{2,1,0:T(8,128)S(1)}, f32[2,64,1024]{2,1,0:T(8,128)S(1)}, u32[]{:S(2)}, u32[]{:S(2)}) collective-permute-start(f32[2,64,1024]{2,1,0:T(8,128)S(1)} %collective-permute-done.31.refs_6_), channel_id=1, source_target_pairs={{0,8},{1,9},{2,10},{3,11},{4,28},{5,29},{6,30},{7,31},{8,16},{9,17... | collective-permute-start | bytes 1572872 | tf_op jit(solution)/shard_map/ppermute | solution.py:389
  340.6 1.5 collective-permute-start.45
  343.2 3.8 %collective-permute-start.46 = (f32[1,1]{1,0:T(1,128)}, f32[1,1]{1,0:T(1,128)}, u32[]{:S(2)}, u32[]{:S(2)}) collective-permute-start(f32[1,1]{1,0:T(1,128)} %add.390), channel_id=1, source_target_pairs={{0,2},{1,3},{2,0},{3,1},{4,6},{5,7},{6,4},{7,5},{8,10},{9,11},{10,... | collective-permute-start | bytes 20 | tf_op jit(solution)/shard_map/ppermute | solution.py:294
  347.6 4.2 %collective-permute-start.47 = (f32[1,1]{1,0:T(1,128)}, f32[1,1]{1,0:T(1,128)}, u32[]{:S(2)}, u32[]{:S(2)}) collective-permute-start(f32[1,1]{1,0:T(1,128)} %add.391), channel_id=1, source_target_pairs={{0,4},{1,5},{2,6},{3,7},{4,0},{5,1},{6,2},{7,3},{8,12},{9,13},{10,... | collective-permute-start | bytes 20 | tf_op jit(solution)/shard_map/ppermute | solution.py:297
  352.4 3.7 %collective-permute-start.48 = (f32[1,1]{1,0:T(1,128)}, f32[1,1]{1,0:T(1,128)}, u32[]{:S(2)}, u32[]{:S(2)}) collective-permute-start(f32[1,1]{1,0:T(1,128)} %add.392), channel_id=1, source_target_pairs={{0,8},{1,9},{2,10},{3,11},{4,12},{5,13},{6,14},{7,15},{8,0},{9,1},... | collective-permute-start | bytes 20 | tf_op jit(solution)/shard_map/ppermute | solution.py:297
  356.7 4.6 %collective-permute-start.49 = (f32[1,1]{1,0:T(1,128)}, f32[1,1]{1,0:T(1,128)}, u32[]{:S(2)}, u32[]{:S(2)}) collective-permute-start(f32[1,1]{1,0:T(1,128)} %add.393), channel_id=1, source_target_pairs={{0,16},{1,17},{2,18},{3,19},{4,20},{5,21},{6,22},{7,23},{8,24},{9,... | collective-permute-start | bytes 20 | tf_op jit(solution)/shard_map/ppermute | solution.py:297

commit v2 on v0

v2 whole, which is shorter than its diff:
```python
import functools

import jax
import jax.numpy as jnp
import numpy as np
from jax import lax
from jax.experimental import pallas as pl
from jax.experimental.pallas import tpu as pltpu
from jax.sharding import PartitionSpec as P

STEPS = 2
AXES = ("gx", "gy")
LANES = 128
TILE = 256

step_x = np.array([-1, -1, -1, 0, 0, 1, 1, 1])
step_y = np.array([-1, 0, 1, -1, 1, -1, 0, 1])
send_order = (0, 7, 2, 5, 1, 6, 3, 4)

GROUPS = ("C", "A", "Y", "CA", "B", "YA", "CB", "YB")
FRAME = {
    "C": (0, 1),
    "A": (1, 0),
    "Y": (0, -1),
    "CA": (1, 1),
    "B": (-1, 0),
    "YA": (1, -1),
    "CB": (-1, 1),
    "YB": (-1, -1),
}


def flat_perm(count_x, count_y, move):
    pairs = []
    for i in range(count_x):
        for j in range(count_y):
            x, y = move(i, j)
            pairs.append((i * count_y + j, (x % count_x) * count_y + y % count_y))
    return pairs


def toward_a(i, j):
    return i ^ 1, j


def along_b(i, j):
    return (i + 2 if i % 2 == 0 else i - 2), j


def toward_c(i, j):
    return i, j ^ 1


def toward_y(i, j):
    return i, (j - 1 if j % 2 == 0 else j + 1)


def split(value):
    high = value.astype(jnp.bfloat16)
    low = (value - high.astype(jnp.float32)).astype(jnp.bfloat16)
    return high, low


def trace_of(block):
    row = lax.broadcasted_iota(jnp.int32, block.shape, 0)
    lane = lax.broadcasted_iota(jnp.int32, block.shape, 1)
    return jnp.sum(jnp.where(row == lane, block, 0.0))


def quotient(value, by, most):
    total = jnp.zeros_like(value)
    for k in range(1, most + 1):
        total += (value >= by * k).astype(jnp.int32)
    return total


VMEM = pl.BlockSpec(memory_space=pltpu.VMEM)
SMEM = pl.BlockSpec(memory_space=pltpu.SMEM)


def pack(moves, rims, cols, rows, count_x, count_y):
    row_count, block, strip = rows.shape
    slots = cols.shape[1]
    rim_count = rims.shape[0]
    tiles = strip // LANES
    ways = len(step_x)

    def kernel(moves_ref, rims_ref, cols_ref, rows_ref, *refs):
        outs, (slots_ref, codes_ref, tail_ref) = refs[:ways], refs[ways:]
        index_x = lax.axis_index("gx")
        index_y = lax.axis_index("gy")
        cols = cols_ref[...]
        inner = jnp.full(cols.shape, -1, jnp.int32)
        for m in range(rim_count):
            inner = jnp.where(cols == rims_ref[m], 4 * rim_count + m, inner)
        away = cols - row_count
        direction = quotient(away, rim_count, ways - 1)
        place = direction + (direction >= 4).astype(jnp.int32)
        code = jnp.where(
            cols < row_count, inner, place * rim_count + away - direction * rim_count
        )
        codes_ref[...] = jnp.zeros(codes_ref.shape, jnp.float32)
        tail_ref[...] = jnp.zeros(tail_ref.shape, jnp.float32)
        codes_ref[:, :slots] = code.astype(jnp.float32)
        for m in range(rim_count):
            tail_ref[pl.ds(m, 1), :] = codes_ref[pl.ds(rims_ref[m], 1), :]
        for d in range(ways):
            x = lax.rem(index_x + int(step_x[d]) + count_x, count_x)
            y = lax.rem(index_y + int(step_y[d]) + count_y, count_y)
            first = (x * count_y + y) * row_count
            slot = jnp.int32(0)
            for r in range(1, row_count):
                target = moves_ref[r]
                slot = jnp.where((target >= first) & (target < first + row_count), r, slot)
            slots_ref[d] = slot
            for k in range(tiles):
                outs[d][k * block : (k + 1) * block, :] = rows_ref[
                    slot, :, k * LANES : (k + 1) * LANES
                ]
            outs[d][tiles * block :, :] = tail_ref[...]

    message = jax.ShapeDtypeStruct((tiles * block + 8, LANES), jnp.float32)
    return pl.pallas_call(
        kernel,
        out_shape=(message,) * ways + (jax.ShapeDtypeStruct((ways,), jnp.int32),),
        in_specs=[SMEM, SMEM, VMEM, VMEM],
        out_specs=(VMEM,) * ways + (SMEM,),
        scratch_shapes=[
            pltpu.VMEM((row_count, LANES), jnp.float32),
            pltpu.VMEM((8, LANES), jnp.float32),
        ],
        compiler_params=pltpu.CompilerParams(vmem_limit_bytes=16 * 2**20),
        name="pack_rows",
    )(moves, rims, cols, rows)


def place(slots, rims, arrived, strip):
    rows = len(arrived)
    tiles = strip // LANES
    block = (arrived[0].shape[0] - 8) // tiles
    count = rims.shape[0]
    half = count // 2

    def kernel(slots_ref, rims_ref, *refs):
        ins, outs = refs[:rows], refs[rows:]
        current_ref, rim_ref, first_ref, second_ref, trace_ref = outs
        total = jnp.float32(0.0)
        for d in range(rows):
            for k in range(tiles):
                current_ref[slots_ref[d], :, k * LANES : (k + 1) * LANES] = ins[d][
                    k * block : (k + 1) * block, :
                ]
            total += trace_of(ins[d][:block, :])
        trace_ref[0] = total
        for m in range(count):
            row = current_ref[rims_ref[m]]
            rim_ref[m] = row
            (first_ref if m < half else second_ref)[m % half] = row

    rim = lambda n: jax.ShapeDtypeStruct((n, block, strip), jnp.float32)
    return pl.pallas_call(
        kernel,
        out_shape=(rim(rows), rim(count), rim(half), rim(half))
        + (jax.ShapeDtypeStruct((1,), jnp.float32),),
        in_specs=[SMEM, SMEM] + [VMEM] * rows,
        out_specs=(VMEM, VMEM, VMEM, VMEM, SMEM),
        compiler_params=pltpu.CompilerParams(vmem_limit_bytes=16 * 2**20),
        name="place_rows",
    )(slots, rims, *arrived)


def tables(rims, cols, arrived):
    rows, slots = cols.shape
    rim_count = rims.shape[0]
    pool = rows + len(GROUPS) * rim_count
    tail = arrived[0].shape[0] // 8 - 1
    base_of = [0] * 9
    for g, name in enumerate(GROUPS):
        x, y = FRAME[name]
        base_of[3 * (x + 1) + y + 1] = rows + g * rim_count

    def kernel(rims_ref, cols_ref, *refs):
        tails, (spots_ref, table_ref, all_ref) = refs[: len(arrived)], refs[len(arrived) :]
        sign_x = 1 - 2 * lax.rem(lax.axis_index("gx"), 2)
        sign_y = 1 - 2 * lax.rem(lax.axis_index("gy"), 2)

        def locate(place, index, shift_x, shift_y):
            third = quotient(place, 3, 2)
            x = (third - 1) * sign_x + shift_x
            y = (place - 3 * third - 1) * sign_y + shift_y
            inside = (x >= -1) & (x <= 1) & (y >= -1) & (y <= 1)
            at = 3 * (x + 1) + y + 1
            spot = index
            for k in range(9):
                if k != 4:
                    spot = spot + jnp.where(at == k, base_of[k], 0)
            for m in range(rim_count):
                spot = jnp.where((at == 4) & (index == m), rims_ref[m], spot)
            return jnp.where(inside, spot, -1)

        cols = cols_ref[...]
        away = cols - rows
        direction = quotient(away, rim_count, 7)
        place = direction + (direction >= 4).astype(jnp.int32)
        spots = locate(place, away - direction * rim_count, 0, 0)
        spots = jnp.where(cols < rows, cols, spots)
        spots_ref[...] = spots
        all_ref[...] = jnp.full(all_ref.shape, -1, jnp.int32)
        all_ref[:rows, :slots] = spots
        for d in range(len(arrived)):
            x = -int(step_x[d]) * sign_x
            y = -int(step_y[d]) * sign_y
            at = 3 * (x + 1) + y + 1
            base = jnp.int32(0)
            for k in range(9):
                base = jnp.where(at == k, base_of[k], base)
            near = tails[d][...].astype(jnp.int32)
            place = quotient(near, rim_count, 8)
            spots = locate(place, near - place * rim_count, x, y)
            spots = jnp.where(near < 0, -1, spots)
            for m in range(rim_count):
                all_ref[pl.ds(base + m, 1), :] = spots[m : m + 1, :]
        lane = lax.broadcasted_iota(jnp.int32, (pool, LANES), 1)
        found = jnp.full((pool, LANES), -1, jnp.int32)
        for u in range(slots):
            found = jnp.where(all_ref[:, u : u + 1] == lane, u, found)
        entry = (found >> 1) + 16 * ((found ^ lane) & 1)
        table_ref[...] = jnp.where(found < 0, slots // 2, entry)

    last = pl.BlockSpec((8, LANES), lambda n: (tail, 0))
    full = lambda shape: pl.BlockSpec(shape, lambda n: (0, 0))
    return pl.pallas_call(
        kernel,
        grid=(1,),
        out_shape=(
            jax.ShapeDtypeStruct((rows, slots), jnp.int32),
            jax.ShapeDtypeStruct((pool, LANES), jnp.int32),
        ),
        in_specs=[SMEM, full((rows, slots))] + [last] * len(arrived),
        out_specs=(full((rows, slots)), full((pool, LANES))),
        scratch_shapes=[pltpu.VMEM((pool, LANES), jnp.int32)],
        name="make_tables",
    )(rims, cols, *arrived)


def spread(parts, high_ref, low_ref):
    base = 0
    strip = parts[0].shape[2]
    for ref in parts:

        def one(c, carry, ref=ref, base=base):
            at = pl.ds(pl.multiple_of((base + c) * 64, 64), 64)
            for k in range(strip // LANES):
                to = pl.ds(k * LANES, LANES)
                value = ref[c, :, to]
                for turn in range(2):
                    high, low = split(pltpu.roll(value, 64, 1) if turn else value)
                    high_ref[turn, at, to] = high
                    low_ref[turn, at, to] = low
            zeros = jnp.zeros((64, LANES), jnp.bfloat16)
            high_ref[0, at, pl.ds(strip, LANES)] = zeros
            low_ref[0, at, pl.ds(strip, LANES)] = zeros
            return carry

        lax.fori_loop(0, ref.shape[0], one, 0)
        base += ref.shape[0]


def fill(table_ref, first, member, members, tile, source, targets):
    left_half = lax.broadcasted_iota(jnp.int32, (64, LANES), 1) < 64
    spot = tile * (TILE // 64)
    for c in range(members):
        at = pl.ds(pl.multiple_of((member + c) * 64, 64), 64)
        for q in range(TILE // LANES):
            left = table_ref[first + member + c, spot + 2 * q]
            right = table_ref[first + member + c, spot + 2 * q + 1]
            from_left = pl.ds(pl.multiple_of((left & 15) * LANES, LANES), LANES)
            from_right = pl.ds(pl.multiple_of((right & 15) * LANES, LANES), LANES)
            for k in range(2):
                value = jnp.where(
                    left_half,
                    source[k][left >> 4, at, from_left],
                    source[k][right >> 4, at, from_right],
                )
                for refs, lane in targets:
                    to = pl.ds(pl.multiple_of(lane + q * LANES, LANES), LANES)
                    refs[k][pl.ds(c * 64, 64), to] = value


def three_products(a_high, a_low, d_high, d_low):
    left = jnp.concatenate([a_high, a_high, a_low], axis=1)
    right = jnp.concatenate([d_high, d_low, d_high], axis=0)
    return jnp.dot(left, right, preferred_element_type=jnp.float32)


def wide_scratch(members, strip):
    return [pltpu.VMEM((2, members * 64, strip + LANES), jnp.bfloat16)] * 2


def pipelined(units, fill_one, multiply, buffers):
    even, odd = buffers
    fill_one(jnp.int32(0), even)

    def two(j, carry):
        fill_one(2 * j + 1, odd)
        multiply(2 * j, even)
        fill_one(jnp.minimum(2 * j + 2, units - 1), even)
        multiply(2 * j + 1, odd)
        return carry

    lax.fori_loop(0, units // 2, two, 0)
    if units % 2:
        multiply(units - 1, even)


def own_product(table, current):
    rows, block, strip = current.shape
    width = table.shape[0] * block
    depth = rows * block
    tiles = width // TILE

    def kernel(table_ref, current_ref, high_ref, low_ref, total_ref, *scratch):
        wide, own, even, odd = scratch[0:2], scratch[2:4], scratch[4:6], scratch[6:8]
        spread([current_ref], *wide)
        for n in range(depth // TILE):
            fill(table_ref, 0, 0, rows, n, wide, [(own, n * TILE)])

        def fill_one(n, buffers):
            fill(table_ref, 0, 0, rows, n, wide, [(buffers, 0), ((high_ref, low_ref), n * TILE)])

        def multiply(n, buffers):
            to = pl.ds(pl.multiple_of(n * TILE, TILE), TILE)
            total_ref[:, to] = three_products(
                own[0][...], own[1][...], buffers[0][...], buffers[1][...]
            )

        pipelined(tiles, fill_one, multiply, (even, odd))

    dense = lambda t: jax.ShapeDtypeStruct((depth, width), t)
    return pl.pallas_call(
        kernel,
        out_shape=(dense(jnp.bfloat16), dense(jnp.bfloat16), dense(jnp.float32)),
        in_specs=[SMEM, VMEM],
        out_specs=(VMEM, VMEM, VMEM),
        scratch_shapes=wide_scratch(rows, strip)
        + [pltpu.VMEM((depth, depth), jnp.bfloat16)] * 2
        + [pltpu.VMEM((depth, TILE), jnp.bfloat16)] * 4,
        compiler_params=pltpu.CompilerParams(vmem_limit_bytes=24 * 2**20),
        cost_estimate=cost(2 * tiles),
        name="own_product",
    )(table, current)


def cost(units):
    return pl.CostEstimate(
        flops=units * 3 * 2 * 512 * TILE * TILE * 2, bytes_accessed=12 * 2**20, transcendentals=0
    )


def columns_of(name):
    x, y = FRAME[name]
    tiles = [0, 1]
    for g, other in enumerate(GROUPS):
        if abs(FRAME[other][0] - x) <= 1 and abs(FRAME[other][1] - y) <= 1:
            tiles.append(2 + g)
    return tiles


def add_product(names, table, high, low, parts, total, label, last=None):
    depth_own, width = total.shape
    _, block, strip = parts[0].shape
    rows = depth_own // block
    count = TILE // block
    members = count * len(names)
    start = GROUPS.index(names[0])
    first = rows + start * count
    lists = [columns_of(name) for name in names]
    begins = [sum(len(t) for t in lists[:k]) for k in range(len(lists) + 1)]
    codes = [sum(t << (4 * k) for k, t in enumerate(tiles)) for tiles in lists]

    def unit(i):
        group, begin, code = jnp.int32(0), jnp.int32(0), jnp.int32(codes[0])
        for k in range(1, len(lists)):
            after = i >= begins[k]
            group = jnp.where(after, k, group)
            begin = jnp.where(after, begins[k], begin)
            code = jnp.where(after, codes[k], code)
        return group, (code >> (4 * (i - begin))) & 15

    def kernel(table_ref, high_ref, low_ref, *refs):
        refs = list(refs)
        part_refs = [refs.pop(0) for _ in parts]
        total_in = refs.pop(0)
        if last is not None:
            spots_ref, rims_ref, traces_ref, current_ref = (refs.pop(0) for _ in range(4))
            out_ref, rim_ref, first_ref, second_ref, trace_ref = (refs.pop(0) for _ in range(5))
            total_ref = refs.pop(-1)
        else:
            total_ref = refs.pop(0)
        wide, even, odd = refs[0:2], refs[2:4], refs[4:6]
        spread(part_refs, *wide)

        def fill_one(i, buffers):
            group, tile = unit(i)
            fill(table_ref, first, group * count, count, tile, wide, [(buffers, 0)])

        def multiply(i, buffers):
            group, tile = unit(i)
            at = pl.ds(pl.multiple_of(first * block + group * TILE, TILE), TILE)
            to = pl.ds(pl.multiple_of(tile * TILE, TILE), TILE)
            total_ref[:, to] = total_in[:, to] + three_products(
                high_ref[:, at], low_ref[:, at], buffers[0][...], buffers[1][...]
            )

        if last is not None:
            for n in range(width // TILE):
                if n not in lists[0]:
                    to = pl.ds(n * TILE, TILE)
                    total_ref[:, to] = total_in[:, to]
        pipelined(begins[-1], fill_one, multiply, (even, odd))
        if last is None:
            return
        known = traces_ref.shape[0]
        for k in range(known):
            trace_ref[k] = traces_ref[k]
        lane = lax.broadcasted_iota(jnp.int32, (64, LANES), 1)

        def one_row(g, trace):
            at = pl.ds(pl.multiple_of(g * 64, 64), 64)
            for k in range(strip // LANES):
                sides = []
                for side in range(2):
                    spot = spots_ref[g, 2 * k + side]
                    tile = pl.ds(pl.multiple_of((spot >> 1) * LANES, LANES), LANES)
                    sides.append(pltpu.roll(total_ref[at, tile], ((spot ^ side) & 1) * 64, 1))
                value = jnp.where(lane < 64, *sides)
                if k == 0:
                    trace += trace_of(value)
                to = pl.ds(k * LANES, LANES)
                if blend:
                    value = 2.0 * current_ref[g, :, to] - value
                out_ref[g, :, to] = value
            return trace

        trace_ref[known] = lax.fori_loop(0, rows, one_row, jnp.float32(0.0))
        for m in range(count):
            row = out_ref[rims_ref[m]]
            rim_ref[m] = row
            (first_ref if m < count // 2 else second_ref)[m % (count // 2)] = row

    ins = [table, high, low, *parts, total]
    in_specs = [SMEM] + [VMEM] * (3 + len(parts))
    if last is None:
        out_shape = (jax.ShapeDtypeStruct((depth_own, width), jnp.float32),)
        small = ()
    else:
        spots, rims, traces, current, blend = last
        ins += [spots, rims, traces, current]
        in_specs += [SMEM, SMEM, SMEM, VMEM]
        shape = lambda n: jax.ShapeDtypeStruct((n, block, strip), jnp.float32)
        out_shape = (shape(rows), shape(count), shape(count // 2), shape(count // 2))
        small = (jax.ShapeDtypeStruct((traces.shape[0] + 1,), jnp.float32),)
    scratch = wide_scratch(members, strip) + [pltpu.VMEM((TILE, TILE), jnp.bfloat16)] * 4
    if last is not None:
        scratch.append(pltpu.VMEM((depth_own, width), jnp.float32))
    result = pl.pallas_call(
        kernel,
        out_shape=out_shape + small,
        in_specs=in_specs,
        out_specs=(VMEM,) * len(out_shape) + (SMEM,) * len(small),
        scratch_shapes=scratch,
        input_output_aliases={3 + len(parts): 0} if last is None else {},
        compiler_params=pltpu.CompilerParams(vmem_limit_bytes=24 * 2**20),
        cost_estimate=cost(begins[-1]),
        name=label,
    )(*ins)
    return result[0] if last is None else result


def sum_everywhere(value, count_x, count_y):
    for count, at in ((count_y, 1), (count_x, 0)):
        bit = 1
        while bit < count:
            send = lambda b: lax.ppermute(
                value,
                AXES,
                flat_perm(
                    count_x, count_y, lambda i, j: (i, j ^ b) if at else (i ^ b, j)
                ),
            )
            if 2 * bit < count:
                one, two, three = send(bit), send(2 * bit), send(3 * bit)
                value = (value + one) + (two + three)
                bit *= 4
            else:
                value = value + send(bit)
                bit *= 2
    return value


def shards(density, moves, cols, halo_rows):
    row_count, block, strip = density.shape[2:]
    rim_count = halo_rows.shape[2]
    count_x = lax.axis_size("gx")
    count_y = lax.axis_size("gy")
    rows = density.reshape(row_count, block, strip)
    rims = halo_rows.reshape(rim_count)
    own_cols = cols.reshape(row_count, -1)

    *leaving, slots = pack(moves.reshape(row_count), rims, own_cols, rows, count_x, count_y)
    arrived = [None] * len(step_x)
    for d in send_order:
        dx, dy = int(step_x[d]), int(step_y[d])
        perm = flat_perm(count_x, count_y, lambda i, j: (i + dx, j + dy))
        arrived[d] = lax.ppermute(leaving[d], AXES, perm)

    current, rim, rim_0, rim_1, traces = place(slots, rims, arrived, strip)
    spots, table = tables(rims, own_cols, arrived)
    swap = {
        "A": flat_perm(count_x, count_y, toward_a),
        "B": flat_perm(count_x, count_y, along_b),
        "C": flat_perm(count_x, count_y, toward_c),
        "Y": flat_perm(count_x, count_y, toward_y),
    }
    go = lambda value, way: lax.ppermute(value, AXES, swap[way])
    for step in range(STEPS):
        a_0, y_0 = go(rim_0, "A"), go(rim_0, "Y")
        a_1, y_1 = go(rim_1, "A"), go(rim_1, "Y")
        c = go(rim, "C")
        high, low, total = own_product(table, current)
        a_0, y_0, total = lax.optimization_barrier((a_0, y_0, total))
        b_0, ya_0, ca_0 = go(a_0, "B"), go(y_0, "A"), go(a_0, "C")
        b_1, ya_1, ca_1 = go(a_1, "B"), go(a_1, "Y"), go(a_1, "C")
        add = functools.partial(add_product, table=table, high=high, low=low)
        total = add(
            ("C", "A", "Y"), parts=[c, a_0, a_1, y_0, y_1], total=total, label="near_product"
        )
        b_0, b_1, ya_0, total = lax.optimization_barrier((b_0, b_1, ya_0, total))
        cb_0, cb_1 = go(b_0, "C"), go(b_1, "C")
        yb_0, yb_1 = go(ya_0, "B"), go(b_1, "Y")
        corner = [ca_0, ca_1, b_0, b_1, ya_0, ya_1, cb_0, cb_1]
        total = add(("CA", "B", "YA", "CB"), parts=corner, total=total, label="corner_product")
        last = (spots, rims, traces, current, step % 2 == 1)
        current, rim, rim_0, rim_1, traces = add(
            ("YB",), parts=[yb_0, yb_1], total=total, label="last_product", last=last
        )
    scale = 1.0 / (count_x * count_y * row_count * block)
    sums = sum_everywhere(traces, count_x, count_y) * scale
    occupation = jnp.stack([sums[0], sums[1], sums[1], sums[2]])
    return (current.reshape(density.shape), occupation)


def solution(mesh):
    in_specs = (
        P("gx", "gy", None, None, None),
        P("gx", "gy", None),
        P("gx", "gy", None, None),
        P("gx", "gy", None),
    )
    out_specs = (P("gx", "gy", None, None, None), P())
    return jax.shard_map(shards, mesh=mesh, in_specs=in_specs, out_specs=out_specs, check_vma=False)
```

time: 1480 us -> 217 us (0.15)
  local copies, waits for them, and re-layouts: 716 us -> 5.78 us
  waiting for transfers between devices: 441 us -> 91.1 us
  other arithmetic: 169 us -> 0.6 us
  Pallas kernels: 0 us -> 84 us
  matrix products: 74.5 us -> 0 us
  blocking collectives: 36.8 us -> 0 us
    ppermute x24 -> x45, waiting for transfers between devices: 441 us -> 91.1 us  [the longest x30 49.1 us: shards(): go = lambda value, way: lax.ppermute(value, AXES, swap[way])]
    reshape x15 -> x0, local copies, waits for them, and re-layouts: 341 us -> none  [the longest x8 225 us: one_group(): far_blocks = far.reshape(width, slots, block, slots, block)]
    gather x22 -> x0, local copies, waits for them, and re-layouts: 239 us -> none  [the longest x8 174 us: one_group(): jnp.take_along_axis(far_blocks, picked[:, :, None, :, None], axis=3)]
    select_n x4 -> x0, local copies, waits for them, and re-layouts: 102 us -> none  [one_group(): jnp.where(found[:, :, None, :, None], aligned, 0.0)]
    select_n x16 -> x0, other arithmetic: 101 us -> none  [the longest x4 51.2 us: one_group(): jnp.where(found[:, :, None, :, None], aligned, 0.0)]
    pallas_call x0 -> x11, Pallas kernels: none -> 84 us  [the longest x6 61.1 us: add_product(): pl.pallas_call(kernel, out_shape=out_shape + small, in_specs=in_specs, ou...]
    dot_general x7 -> x0, matrix products: 74.5 us -> none  [the longest x4 64.8 us: one_group(): return jnp.einsum('gatb,gtbx->gax', mine, aligned, precision=highest)]
    concatenate x20 -> x0, other arithmetic: 49.8 us -> none  [the longest x11 22.2 us: extended_2(): block = jnp.concatenate([low, block, high], axis=dim)]
  transfers between devices with their start and end apart: 24 -> 45, of which waited for: 17 -> 19; matrix products, arithmetic and copies ran while one was open for 1% -> 0% of each run, Pallas kernels for 0% -> 31%
where the time goes in v2:
time: 217 us
  waiting for transfers between devices  91.1 us (42%)
  Pallas kernels  84 us (39%)
  starting transfers between devices  34.2 us (16%)
  local copies, waits for them, and re-layouts  5.78 us (3%)
    pallas_call x6, Pallas kernels, add_product(): pl.pallas_call(kernel, out_shape=out_shape + small, in_specs=in_specs, ou...  61.1 us
    ppermute x30, waiting for transfers between devices, shards(): go = lambda value, way: lax.ppermute(value, AXES, swap[way])  49.1 us
    ppermute x8, waiting for transfers between devices, shards(): arrived[d] = lax.ppermute(leaving[d], AXES, perm)  34.7 us
    pallas_call x2, Pallas kernels, own_product(): pl.pallas_call(kernel, out_shape=(dense(jnp.bfloat16), dense(jnp.bfloat16...  17.8 us
    ppermute x30, starting transfers between devices, shards(): go = lambda value, way: lax.ppermute(value, AXES, swap[way])  14.9 us
    ppermute x8, starting transfers between devices, shards(): arrived[d] = lax.ppermute(leaving[d], AXES, perm)  10.6 us
    ppermute x7, starting transfers between devices, sum_everywhere(): lax.ppermute(value, AXES, flat_perm(count_x, count_y, lambda i, j: (i, j...  8.72 us
    ppermute x7, waiting for transfers between devices, sum_everywhere(): lax.ppermute(value, AXES, flat_perm(count_x, count_y, lambda i, j: (i, j...  7.27 us
  transfers between devices with their start and end apart: 45, of which 19 were waited for; matrix products, arithmetic and copies ran while one was open for 0% of the time, Pallas kernels for 31%

profile of v2, /device:TPU:0, one launch (start us, length us, event | category | flops | bytes accessed | tf_op | source)
XLA Modules:
  0.0 216.7 jit_solution(11513595337907548327)
XLA Ops:
  0.6 1.6 copy-done
  2.2 0.7 copy-done.11
  2.9 0.7 copy-done.13
  3.6 0.7 copy-done.16
  4.2 1.3 pack_rows.1
  5.5 6.4 %collective-permute-start = (f32[520,128]{1,0:T(8,128)S(1)}, f32[520,128]{1,0:T(8,128)S(1)}, u32[]{:S(2)}, u32[]{:S(2)}) collective-permute-start(f32[520,128]{1,0:T(8,128)S(1)} %get-tuple-element.45), channel_id=1, source_target_pairs={{0,31},{1,28},{2,29},{3,30},{4,3},{5,0},{6,1},{7,2},{8,7},{9,4},{1... | collective-permute-start | bytes 798728 | tf_op jit(solution)/shard_map/ppermute | solution.py:515
  11.9 0.5 collective-permute-start.1
  12.5 0.4 collective-permute-start.2
  12.9 2.1 collective-permute-start.3
  15.0 3.7 %collective-permute-done.refs_0_ = f32[520,128]{1,0:T(8,128)S(1)} collective-permute-done((f32[520,128]{1,0:T(8,128)S(1)}, f32[520,128]{1,0:T(8,128)S(1)}, u32[]{:S(2)}, u32[]{:S(2)}) %collective-permute-start) | collective-permute-done | bytes 266272 | tf_op jit(solution)/shard_map/ppermute | solution.py:515
  18.7 0.7 collective-permute-start.5
  19.4 5.0 %collective-permute-done.1.refs_1_ = f32[520,128]{1,0:T(8,128)S(1)} collective-permute-done((f32[520,128]{1,0:T(8,128)S(1)}, f32[520,128]{1,0:T(8,128)S(1)}, u32[]{:S(2)}, u32[]{:S(2)}) %collective-permute-start.1) | collective-permute-done | bytes 266272 | tf_op jit(solution)/shard_map/ppermute | solution.py:515
  24.4 0.4 collective-permute-start.6
  24.8 14.6 %collective-permute-done.2.refs_2_ = f32[520,128]{1,0:T(8,128)S(1)} collective-permute-done((f32[520,128]{1,0:T(8,128)S(1)}, f32[520,128]{1,0:T(8,128)S(1)}, u32[]{:S(2)}, u32[]{:S(2)}) %collective-permute-start.2) | collective-permute-done | bytes 266272 | tf_op jit(solution)/shard_map/ppermute | solution.py:515
  39.5 11.4 %collective-permute-done.7.refs_7_ = f32[520,128]{1,0:T(8,128)S(1)} collective-permute-done((f32[520,128]{1,0:T(8,128)S(1)}, f32[520,128]{1,0:T(8,128)S(1)}, u32[]{:S(2)}, u32[]{:S(2)}) %collective-permute-start.7) | collective-permute-done | bytes 266272 | tf_op jit(solution)/shard_map/ppermute | solution.py:515
  50.9 0.7 copy-done.14
  51.5 2.1 place_rows.1
  53.6 0.7 copy-done.6
  54.4 1.9 collective-permute-start.11
  56.4 1.5 collective-permute-start.15
  57.9 1.7 make_tables.1
  59.6 0.7 copy-done.9
  60.3 8.9 %own_product.2 = (bf16[512,2560]{1,0:T(8,128)(2,1)S(1)}, bf16[512,2560]{1,0:T(8,128)(2,1)S(1)}, f32[512,2560]{1,0:T(8,128)S(1)}) custom-call(s32[40,128]{1,0:T(8,128)S(1)} %copy-done.9, f32[8,64,1024]{2,1,0:T(8,128)S(1)} %get-tuple-element.55.current_ref.refs_6_), custom_call_target="tpu_custom_call" | custom-call | flops 8053063680 | bytes 12582912 | tf_op jit(solution)/shard_map/own_product/pallas_call | solution.py:340
  69.2 0.1 collective-permute-done.8.refs_1_
  69.4 0.5 collective-permute-start.18
  69.9 10.3 %collective-permute-done.11.refs_2_ = f32[2,64,1024]{2,1,0:T(8,128)} collective-permute-done((f32[2,64,1024]{2,1,0:T(8,128)}, f32[2,64,1024]{2,1,0:T(8,128)}, u32[]{:S(2)}, u32[]{:S(2)}) %collective-permute-start.11) | collective-permute-done | bytes 524320 | tf_op jit(solution)/shard_map/ppermute | solution.py:525
  80.2 0.3 collective-permute-start.13
  80.6 12.0 %near_product.2.refs_8_ = f32[512,2560]{1,0:T(8,128)S(1)} custom-call(s32[40,128]{1,0:T(8,128)S(1)} %copy-done.9, bf16[512,2560]{1,0:T(8,128)(2,1)S(1)} %get-tuple-element.56.high_ref, bf16[512,2560]{1,0:T(8,128)(2,1)S(1)} %get-tuple-element.57.low_ref, f32[4,64,1024]{2,1,0:T(8,128)} %collective-permute-done.14.refs_0_, ...), custom_call_target="tpu_custom_call", output_to_operand_aliasing={{}: (8, {})} | custom-call | flops 8455716864 | bytes 12582912 | tf_op jit(solution)/shard_map/near_product/pallas_call | solution.py:466
  92.7 1.3 collective-permute-done.13.refs_4_
  94.0 2.9 %collective-permute-done.12.refs_3_ = f32[2,64,1024]{2,1,0:T(8,128)S(1)} collective-permute-done((f32[2,64,1024]{2,1,0:T(8,128)}, f32[2,64,1024]{2,1,0:T(8,128)S(1)}, u32[]{:S(2)}, u32[]{:S(2)}) %collective-permute-start.12) | collective-permute-done | bytes 524320 | tf_op jit(solution)/shard_map/ppermute | solution.py:525
  96.9 0.5 collective-permute-start.22
  97.4 0.2 collective-permute-start.16
  97.7 8.9 %collective-permute-done.20.refs_5_ = f32[2,64,1024]{2,1,0:T(8,128)S(1)} collective-permute-done((f32[2,64,1024]{2,1,0:T(8,128)}, f32[2,64,1024]{2,1,0:T(8,128)S(1)}, u32[]{:S(2)}, u32[]{:S(2)}) %collective-permute-start.20) | collective-permute-done | bytes 524320 | tf_op jit(solution)/shard_map/ppermute | solution.py:525
  106.5 12.0 %corner_product.2.refs_2_ = f32[512,2560]{1,0:T(8,128)S(1)} custom-call(s32[40,128]{1,0:T(8,128)S(1)} %copy-done.9, bf16[512,2560]{1,0:T(8,128)(2,1)S(1)} %get-tuple-element.56.high_ref, bf16[512,2560]{1,0:T(8,128)(2,1)S(1)} %get-tuple-element.57.low_ref, f32[2,64,1024]{2,1,0:T(8,128)S(1)} %collective-permute-done.18.refs_0_, ...), custom_call_target="tpu_custom_call", output_to_operand_aliasing={{}: (11, {})} | custom-call | flops 8858370048 | bytes 12582912 | tf_op jit(solution)/shard_map/corner_product/pallas_call | solution.py:466
  118.6 6.6 %last_product.2 = (f32[8,64,1024]{2,1,0:T(8,128)S(1)}, f32[4,64,1024]{2,1,0:T(8,128)S(1)}, f32[2,64,1024]{2,1,0:T(8,128)S(1)}, f32[2,64,1024]{2,1,0:T(8,128)S(1)}, f32[2]{0:T(128)S(1)}) custom-call(s32[40,128]{1,0:T(8,128)S(1)} %copy-done.10, bf16[512,2560]{1,0:T(8,128)(2,1)S(1)} %get-tuple-element.56.high_ref, ...), custom_call_target="tpu_custom_call" | custom-call | flops 2013265920 | bytes 12582912 | tf_op jit(solution)/shard_map/last_product/pallas_call | solution.py:466
  125.2 1.4 collective-permute-start.29
  126.6 3.5 %collective-permute-start.23 = (f32[2,64,1024]{2,1,0:T(8,128)S(1)}, f32[2,64,1024]{2,1,0:T(8,128)S(1)}, u32[]{:S(2)}, u32[]{:S(2)}) collective-permute-start(f32[2,64,1024]{2,1,0:T(8,128)S(1)} %get-tuple-element.74), channel_id=1, source_target_pairs={{0,4},{1,5},{2,6},{3,7},{4,0},{5,1},{6,2},{7,3},{8,12},{9,13},{10,... | collective-permute-start | bytes 1572872 | tf_op jit(solution)/shard_map/ppermute | solution.py:525
  130.2 1.7 collective-permute-start.30
  131.9 8.9 %own_product.3 = (bf16[512,2560]{1,0:T(8,128)(2,1)S(1)}, bf16[512,2560]{1,0:T(8,128)(2,1)S(1)}, f32[512,2560]{1,0:T(8,128)S(1)}) custom-call(s32[40,128]{1,0:T(8,128)S(1)} %copy-done.10, f32[8,64,1024]{2,1,0:T(8,128)S(1)} %get-tuple-element.71.current_ref.refs_6_), custom_call_target="tpu_custom_call" | custom-call | flops 8053063680 | bytes 12582912 | tf_op jit(solution)/shard_map/own_product/pallas_call | solution.py:340
  140.8 2.1 collective-permute-done.23.refs_1_
  142.8 1.5 collective-permute-done.24.refs_3_
  144.3 0.2 collective-permute-start.25
  144.6 9.0 %collective-permute-done.26.refs_2_ = f32[2,64,1024]{2,1,0:T(8,128)S(1)} collective-permute-done((f32[2,64,1024]{2,1,0:T(8,128)S(1)}, f32[2,64,1024]{2,1,0:T(8,128)S(1)}, u32[]{:S(2)}, u32[]{:S(2)}) %collective-permute-start.26) | collective-permute-done | bytes 524320 | tf_op jit(solution)/shard_map/ppermute | solution.py:525
  153.5 1.7 collective-permute-start.28
  155.3 0.3 collective-permute-done.30.refs_4_
  155.6 0.2 collective-permute-start.27
  155.8 11.0 %near_product.3.refs_8_ = f32[512,2560]{1,0:T(8,128)S(1)} custom-call(s32[40,128]{1,0:T(8,128)S(1)} %copy-done.10, bf16[512,2560]{1,0:T(8,128)(2,1)S(1)} %get-tuple-element.72.high_ref, bf16[512,2560]{1,0:T(8,128)(2,1)S(1)} %get-tuple-element.73.low_ref, f32[4,64,1024]{2,1,0:T(8,128)S(1)} %collective-permute-done.29.refs_0_, ...), custom_call_target="tpu_custom_call", output_to_operand_aliasing={{}: (8, {})} | custom-call | flops 8455716864 | bytes 12582912 | tf_op jit(solution)/shard_map/near_product/pallas_call | solution.py:466
  166.9 4.4 %collective-permute-done.27.refs_3_ = f32[2,64,1024]{2,1,0:T(8,128)S(1)} collective-permute-done((f32[2,64,1024]{2,1,0:T(8,128)S(1)}, f32[2,64,1024]{2,1,0:T(8,128)S(1)}, u32[]{:S(2)}, u32[]{:S(2)}) %collective-permute-start.27) | collective-permute-done | bytes 524320 | tf_op jit(solution)/shard_map/ppermute | solution.py:525
  171.3 0.5 collective-permute-start.37
  171.8 0.2 collective-permute-start.32
  172.0 0.1 collective-permute-start.31
  172.1 8.4 %collective-permute-done.35.refs_5_ = f32[2,64,1024]{2,1,0:T(8,128)S(1)} collective-permute-done((f32[2,64,1024]{2,1,0:T(8,128)S(1)}, f32[2,64,1024]{2,1,0:T(8,128)S(1)}, u32[]{:S(2)}, u32[]{:S(2)}) %collective-permute-start.35) | collective-permute-done | bytes 524320 | tf_op jit(solution)/shard_map/ppermute | solution.py:525
  180.5 12.0 %corner_product.3.refs_2_ = f32[512,2560]{1,0:T(8,128)S(1)} custom-call(s32[40,128]{1,0:T(8,128)S(1)} %copy-done.10, bf16[512,2560]{1,0:T(8,128)(2,1)S(1)} %get-tuple-element.72.high_ref, bf16[512,2560]{1,0:T(8,128)(2,1)S(1)} %get-tuple-element.73.low_ref, f32[2,64,1024]{2,1,0:T(8,128)S(1)} %collective-permute-done.33.refs_0_, ...), custom_call_target="tpu_custom_call", output_to_operand_aliasing={{}: (11, {})} | custom-call | flops 8858370048 | bytes 12582912 | tf_op jit(solution)/shard_map/corner_product/pallas_call | solution.py:466
  192.5 7.5 %last_product.3 = (f32[8,64,1024]{2,1,0:T(8,128)}, f32[4,64,1024]{2,1,0:T(8,128)}, f32[2,64,1024]{2,1,0:T(8,128)}, f32[2,64,1024]{2,1,0:T(8,128)}, f32[3]{0:T(128)S(1)}) custom-call(s32[40,128]{1,0:T(8,128)S(1)} %copy-done.10, bf16[512,2560]{1,0:T(8,128)(2,1)S(1)} %get-tuple-element.72.high_ref, bf16[512,2560]{1,0:T(8,128)(2,1)S(1)} %get-tuple-element.73.low_ref, ...), custom_call_target="tpu_custom_call" | custom-call | flops 2013265920 | bytes 12582912 | tf_op jit(solution)/shard_map/last_product/pallas_call | solution.py:466
  200.0 1.5 collective-permute-start.38
  201.5 1.4 collective-permute-start.40
  202.9 2.1 collective-permute-done.39
  205.0 2.1 collective-permute-start.41
  207.1 1.5 collective-permute-start.43
  208.7 2.0 collective-permute-done.42
  210.6 0.9 collective-permute-done.43
  211.6 2.2 %collective-permute-start.44 = (f32[3]{0:T(128)S(1)}, f32[3]{0:T(128)S(1)}, u32[]{:S(2)}, u32[]{:S(2)}) collective-permute-start(f32[3]{0:T(128)S(1)} %add_add_fusion), channel_id=1, source_target_pairs={{0,16},{1,17},{2,18},{3,19},{4,20},{5,21},{6,22},{7,23},{8,24},{9,... | collective-permute-start | bytes 44 | tf_op jit(solution)/shard_map/ppermute | solution.py:484
  213.7 2.3 %collective-permute-done.44 = f32[3]{0:T(128)S(1)} collective-permute-done((f32[3]{0:T(128)S(1)}, f32[3]{0:T(128)S(1)}, u32[]{:S(2)}, u32[]{:S(2)}) %collective-permute-start.44) | collective-permute-done | bytes 44 | tf_op jit(solution)/shard_map/ppermute | solution.py:484
  216.1 0.6 pad_maximum_fusion
  (76 shorter events, 0.6 us)
Async XLA Ops:
  0.6 1.6 copy-start
  2.2 0.7 copy-start.11
  2.9 0.7 copy-start.13
  3.6 0.7 copy-start.16
  5.5 13.2 %collective-permute-start = (f32[520,128]{1,0:T(8,128)S(1)}, f32[520,128]{1,0:T(8,128)S(1)}, u32[]{:S(2)}, u32[]{:S(2)}) collective-permute-start(f32[520,128]{1,0:T(8,128)S(1)} %get-tuple-element.45), channel_id=1, source_target_pairs={{0,31},{1,28},{2,29},{3,30},{4,3},{5,0},{6,1},{7,2},{8,7},{9,4},{1... | collective-permute-start | bytes 798728 | tf_op jit(solution)/shard_map/ppermute | solution.py:515
  11.9 12.5 %collective-permute-start.1 = (f32[520,128]{1,0:T(8,128)S(1)}, f32[520,128]{1,0:T(8,128)S(1)}, u32[]{:S(2)}, u32[]{:S(2)}) collective-permute-start(f32[520,128]{1,0:T(8,128)S(1)} %get-tuple-element.46), channel_id=1, source_target_pairs={{0,28},{1,29},{2,30},{3,31},{4,0},{5,1},{6,2},{7,3},{8,4},{9,5},{1... | collective-permute-start | bytes 798728 | tf_op jit(solution)/shard_map/ppermute | solution.py:515
  12.5 27.0 %collective-permute-start.2 = (f32[520,128]{1,0:T(8,128)S(1)}, f32[520,128]{1,0:T(8,128)S(1)}, u32[]{:S(2)}, u32[]{:S(2)}) collective-permute-start(f32[520,128]{1,0:T(8,128)S(1)} %get-tuple-element.47), channel_id=1, source_target_pairs={{0,29},{1,30},{2,31},{3,28},{4,1},{5,2},{6,3},{7,0},{8,5},{9,6},{1... | collective-permute-start | bytes 798728 | tf_op jit(solution)/shard_map/ppermute | solution.py:515
  12.9 26.5 %collective-permute-start.3 = (f32[520,128]{1,0:T(8,128)S(1)}, f32[520,128]{1,0:T(8,128)S(1)}, u32[]{:S(2)}, u32[]{:S(2)}) collective-permute-start(f32[520,128]{1,0:T(8,128)S(1)} %get-tuple-element.48), channel_id=1, source_target_pairs={{0,3},{1,0},{2,1},{3,2},{4,7},{5,4},{6,5},{7,6},{8,11},{9,8},{10,9... | collective-permute-start | bytes 798728 | tf_op jit(solution)/shard_map/ppermute | solution.py:515
  15.0 24.4 %collective-permute-start.4 = (f32[520,128]{1,0:T(8,128)S(1)}, f32[520,128]{1,0:T(8,128)S(1)}, u32[]{:S(2)}, u32[]{:S(2)}) collective-permute-start(f32[520,128]{1,0:T(8,128)S(1)} %get-tuple-element.49), channel_id=1, source_target_pairs={{0,1},{1,2},{2,3},{3,0},{4,5},{5,6},{6,7},{7,4},{8,9},{9,10},{10,1... | collective-permute-start | bytes 798728 | tf_op jit(solution)/shard_map/ppermute | solution.py:515
  18.7 39.2 %copy-start.1 = (f32[520,128]{1,0:T(8,128)}, f32[520,128]{1,0:T(8,128)S(1)}, u32[]{:S(2)}) copy-start(f32[520,128]{1,0:T(8,128)S(1)} %collective-permute-done.refs_0_) | copy-start | bytes 798724
  18.7 20.8 %collective-permute-start.5 = (f32[520,128]{1,0:T(8,128)S(1)}, f32[520,128]{1,0:T(8,128)S(1)}, u32[]{:S(2)}, u32[]{:S(2)}) collective-permute-start(f32[520,128]{1,0:T(8,128)S(1)} %get-tuple-element.50), channel_id=1, source_target_pairs={{0,7},{1,4},{2,5},{3,6},{4,11},{5,8},{6,9},{7,10},{8,15},{9,12},{1... | collective-permute-start | bytes 798728 | tf_op jit(solution)/shard_map/ppermute | solution.py:515
  24.4 33.5 %copy-start.2 = (f32[520,128]{1,0:T(8,128)}, f32[520,128]{1,0:T(8,128)S(1)}, u32[]{:S(2)}) copy-start(f32[520,128]{1,0:T(8,128)S(1)} %collective-permute-done.1.refs_1_) | copy-start | bytes 798724
  24.4 15.1 %collective-permute-start.6 = (f32[520,128]{1,0:T(8,128)S(1)}, f32[520,128]{1,0:T(8,128)S(1)}, u32[]{:S(2)}, u32[]{:S(2)}) collective-permute-start(f32[520,128]{1,0:T(8,128)S(1)} %get-tuple-element.51), channel_id=1, source_target_pairs={{0,4},{1,5},{2,6},{3,7},{4,8},{5,9},{6,10},{7,11},{8,12},{9,13},{1... | collective-permute-start | bytes 798728 | tf_op jit(solution)/shard_map/ppermute | solution.py:515
  39.4 18.4 %copy-start.3 = (f32[520,128]{1,0:T(8,128)}, f32[520,128]{1,0:T(8,128)S(1)}, u32[]{:S(2)}) copy-start(f32[520,128]{1,0:T(8,128)S(1)} %collective-permute-done.2.refs_2_) | copy-start | bytes 798724
  39.4 11.4 %collective-permute-start.7 = (f32[520,128]{1,0:T(8,128)S(1)}, f32[520,128]{1,0:T(8,128)S(1)}, u32[]{:S(2)}, u32[]{:S(2)}) collective-permute-start(f32[520,128]{1,0:T(8,128)S(1)} %get-tuple-element.52), channel_id=1, source_target_pairs={{0,5},{1,6},{2,7},{3,4},{4,9},{5,10},{6,11},{7,8},{8,13},{9,14},{1... | collective-permute-start | bytes 798728 | tf_op jit(solution)/shard_map/ppermute | solution.py:515
  39.4 18.4 %copy-start.4 = (f32[520,128]{1,0:T(8,128)}, f32[520,128]{1,0:T(8,128)S(1)}, u32[]{:S(2)}) copy-start(f32[520,128]{1,0:T(8,128)S(1)} %collective-permute-done.3.refs_3_) | copy-start | bytes 798724
  39.4 18.4 %copy-start.5 = (f32[520,128]{1,0:T(8,128)}, f32[520,128]{1,0:T(8,128)S(1)}, u32[]{:S(2)}) copy-start(f32[520,128]{1,0:T(8,128)S(1)} %collective-permute-done.4.refs_4_) | copy-start | bytes 798724
  39.5 14.2 %copy-start.7 = (f32[520,128]{1,0:T(8,128)}, f32[520,128]{1,0:T(8,128)S(1)}, u32[]{:S(2)}) copy-start(f32[520,128]{1,0:T(8,128)S(1)} %collective-permute-done.6.refs_6_) | copy-start | bytes 798724
  50.9 3.5 %copy-start.8 = (f32[520,128]{1,0:T(8,128)}, f32[520,128]{1,0:T(8,128)S(1)}, u32[]{:S(2)}) copy-start(f32[520,128]{1,0:T(8,128)S(1)} %collective-permute-done.7.refs_7_) | copy-start | bytes 798724
  50.9 0.7 copy-start.14
  53.6 0.7 copy-start.6
  54.4 26.2 %collective-permute-start.14 = (f32[4,64,1024]{2,1,0:T(8,128)}, f32[4,64,1024]{2,1,0:T(8,128)}, u32[]{:S(2)}, u32[]{:S(2)}) collective-permute-start(f32[4,64,1024]{2,1,0:T(8,128)} %get-tuple-element.63), channel_id=1, source_target_pairs={{0,1},{1,0},{2,3},{3,2},{4,5},{5,4},{6,7},{7,6},{8,9},{9,8},{10,11... | collective-permute-start | bytes 3145736 | tf_op jit(solution)/shard_map/ppermute | solution.py:525
  54.4 15.0 %collective-permute-start.8 = (f32[2,64,1024]{2,1,0:T(8,128)}, f32[2,64,1024]{2,1,0:T(8,128)}, u32[]{:S(2)}, u32[]{:S(2)}) collective-permute-start(f32[2,64,1024]{2,1,0:T(8,128)} %get-tuple-element.58), channel_id=1, source_target_pairs={{0,4},{1,5},{2,6},{3,7},{4,0},{5,1},{6,2},{7,3},{8,12},{9,13},{10,... | collective-permute-start | bytes 1572872 | tf_op jit(solution)/shard_map/ppermute | solution.py:525
  54.4 15.0 %collective-permute-start.9 = (f32[2,64,1024]{2,1,0:T(8,128)}, f32[2,64,1024]{2,1,0:T(8,128)}, u32[]{:S(2)}, u32[]{:S(2)}) collective-permute-start(f32[2,64,1024]{2,1,0:T(8,128)} %get-tuple-element.58), channel_id=1, source_target_pairs={{0,3},{1,2},{2,1},{3,0},{4,7},{5,6},{6,5},{7,4},{8,11},{9,10},{10,... | collective-permute-start | bytes 1572872 | tf_op jit(solution)/shard_map/ppermute | solution.py:525
  54.4 25.8 %collective-permute-start.11 = (f32[2,64,1024]{2,1,0:T(8,128)}, f32[2,64,1024]{2,1,0:T(8,128)}, u32[]{:S(2)}, u32[]{:S(2)}) collective-permute-start(f32[2,64,1024]{2,1,0:T(8,128)} %get-tuple-element.61), channel_id=1, source_target_pairs={{0,4},{1,5},{2,6},{3,7},{4,0},{5,1},{6,2},{7,3},{8,12},{9,13},{10,... | collective-permute-start | bytes 1572872 | tf_op jit(solution)/shard_map/ppermute | solution.py:525
  56.4 24.1 %collective-permute-start.15 = (f32[2,64,1024]{2,1,0:T(8,128)}, f32[2,64,1024]{2,1,0:T(8,128)}, u32[]{:S(2)}, u32[]{:S(2)}) collective-permute-start(f32[2,64,1024]{2,1,0:T(8,128)} %get-tuple-element.61), channel_id=1, source_target_pairs={{0,3},{1,2},{2,1},{3,0},{4,7},{5,6},{6,5},{7,4},{8,11},{9,10},{10,... | collective-permute-start | bytes 1572872 | tf_op jit(solution)/shard_map/ppermute | solution.py:525
  59.6 0.7 copy-start.9
  69.4 23.3 %collective-permute-start.10 = (f32[2,64,1024]{2,1,0:T(8,128)}, f32[2,64,1024]{2,1,0:T(8,128)S(1)}, u32[]{:S(2)}, u32[]{:S(2)}) collective-permute-start(f32[2,64,1024]{2,1,0:T(8,128)} %collective-permute-done.8.refs_1_), channel_id=1, source_target_pairs={{0,8},{1,9},{2,10},{3,11},{4,28},{5,29},{6,30},{7,31},{8,16},{9,17... | collective-permute-start | bytes 1572872 | tf_op jit(solution)/shard_map/ppermute | solution.py:525
  69.4 28.0 %collective-permute-start.18 = (f32[2,64,1024]{2,1,0:T(8,128)}, f32[2,64,1024]{2,1,0:T(8,128)S(1)}, u32[]{:S(2)}, u32[]{:S(2)}) collective-permute-start(f32[2,64,1024]{2,1,0:T(8,128)} %collective-permute-done.8.refs_1_), channel_id=1, source_target_pairs={{0,1},{1,0},{2,3},{3,2},{4,5},{5,4},{6,7},{7,6},{8,9},{9,8},{10,11... | collective-permute-start | bytes 1572872 | tf_op jit(solution)/shard_map/ppermute | solution.py:525
  80.2 13.8 %collective-permute-start.13 = (f32[2,64,1024]{2,1,0:T(8,128)}, f32[2,64,1024]{2,1,0:T(8,128)S(1)}, u32[]{:S(2)}, u32[]{:S(2)}) collective-permute-start(f32[2,64,1024]{2,1,0:T(8,128)} %collective-permute-done.9.refs_3_), channel_id=1, source_target_pairs={{0,4},{1,5},{2,6},{3,7},{4,0},{5,1},{6,2},{7,3},{8,12},{9,13},{10,... | collective-permute-start | bytes 1572872 | tf_op jit(solution)/shard_map/ppermute | solution.py:525
  80.5 16.4 %collective-permute-start.12 = (f32[2,64,1024]{2,1,0:T(8,128)}, f32[2,64,1024]{2,1,0:T(8,128)S(1)}, u32[]{:S(2)}, u32[]{:S(2)}) collective-permute-start(f32[2,64,1024]{2,1,0:T(8,128)} %collective-permute-done.11.refs_2_), channel_id=1, source_target_pairs={{0,8},{1,9},{2,10},{3,11},{4,28},{5,29},{6,30},{7,31},{8,16},{9,17... | collective-permute-start | bytes 1572872 | tf_op jit(solution)/shard_map/ppermute | solution.py:525
  80.5 16.9 %collective-permute-start.19 = (f32[2,64,1024]{2,1,0:T(8,128)}, f32[2,64,1024]{2,1,0:T(8,128)S(1)}, u32[]{:S(2)}, u32[]{:S(2)}) collective-permute-start(f32[2,64,1024]{2,1,0:T(8,128)} %collective-permute-done.11.refs_2_), channel_id=1, source_target_pairs={{0,1},{1,0},{2,3},{3,2},{4,5},{5,4},{6,7},{7,6},{8,9},{9,8},{10,11... | collective-permute-start | bytes 1572872 | tf_op jit(solution)/shard_map/ppermute | solution.py:525
  92.6 25.9 %copy-start.10 = (s32[40,128]{1,0:T(8,128)S(1)}, s32[40,128]{1,0:T(8,128)}, u32[]{:S(2)}) copy-start(s32[40,128]{1,0:T(8,128)} %get-tuple-element.53.table_ref) | copy-start | bytes 61444
  92.6 25.9 %copy-start.12 = (s32[8,16]{1,0:T(8,128)S(1)}, s32[8,16]{1,0:T(8,128)}, u32[]{:S(2)}) copy-start(s32[8,16]{1,0:T(8,128)} %get-tuple-element.69.refs_3_) | copy-start | bytes 1540
  92.6 25.9 %copy-start.15 = (s32[1,1,4]{2,1,0:T(1,128)S(1)}, s32[1,1,4]{2,1,0:T(1,128)}, u32[]{:S(2)}) copy-start(s32[1,1,4]{2,1,0:T(1,128)} %param.7) | copy-start | bytes 52
  92.7 13.9 %collective-permute-start.20 = (f32[2,64,1024]{2,1,0:T(8,128)}, f32[2,64,1024]{2,1,0:T(8,128)S(1)}, u32[]{:S(2)}, u32[]{:S(2)}) collective-permute-start(f32[2,64,1024]{2,1,0:T(8,128)} %collective-permute-done.11.refs_2_), channel_id=1, source_target_pairs={{0,3},{1,2},{2,1},{3,0},{4,7},{5,6},{6,5},{7,4},{8,11},{9,10},{10,... | collective-permute-start | bytes 1572872 | tf_op jit(solution)/shard_map/ppermute | solution.py:525
  96.9 9.6 %collective-permute-start.21 = (f32[2,64,1024]{2,1,0:T(8,128)S(1)}, f32[2,64,1024]{2,1,0:T(8,128)S(1)}, u32[]{:S(2)}, u32[]{:S(2)}) collective-permute-start(f32[2,64,1024]{2,1,0:T(8,128)S(1)} %collective-permute-done.10.refs_2_), channel_id=1, source_target_pairs={{0,1},{1,0},{2,3},{3,2},{4,5},{5,4},{6,7},{7,6},{8,9},{9,8},{10,11... | collective-permute-start | bytes 1572872 | tf_op jit(solution)/shard_map/ppermute | solution.py:525
  96.9 9.6 %collective-permute-start.22 = (f32[2,64,1024]{2,1,0:T(8,128)S(1)}, f32[2,64,1024]{2,1,0:T(8,128)S(1)}, u32[]{:S(2)}, u32[]{:S(2)}) collective-permute-start(f32[2,64,1024]{2,1,0:T(8,128)S(1)} %collective-permute-done.12.refs_3_), channel_id=1, source_target_pairs={{0,1},{1,0},{2,3},{3,2},{4,5},{5,4},{6,7},{7,6},{8,9},{9,8},{10,11... | collective-permute-start | bytes 1572872 | tf_op jit(solution)/shard_map/ppermute | solution.py:525
  97.4 21.1 %collective-permute-start.17 = (f32[2,64,1024]{2,1,0:T(8,128)S(1)}, f32[2,64,1024]{2,1,0:T(8,128)S(1)}, u32[]{:S(2)}, u32[]{:S(2)}) collective-permute-start(f32[2,64,1024]{2,1,0:T(8,128)S(1)} %collective-permute-done.12.refs_3_), channel_id=1, source_target_pairs={{0,3},{1,2},{2,1},{3,0},{4,7},{5,6},{6,5},{7,4},{8,11},{9,10},{10,... | collective-permute-start | bytes 1572872 | tf_op jit(solution)/shard_map/ppermute | solution.py:525
  97.4 21.1 %collective-permute-start.16 = (f32[2,64,1024]{2,1,0:T(8,128)S(1)}, f32[2,64,1024]{2,1,0:T(8,128)S(1)}, u32[]{:S(2)}, u32[]{:S(2)}) collective-permute-start(f32[2,64,1024]{2,1,0:T(8,128)S(1)} %collective-permute-done.13.refs_4_), channel_id=1, source_target_pairs={{0,8},{1,9},{2,10},{3,11},{4,28},{5,29},{6,30},{7,31},{8,16},{9,17... | collective-permute-start | bytes 1572872 | tf_op jit(solution)/shard_map/ppermute | solution.py:525
  125.2 30.6 %collective-permute-start.29 = (f32[4,64,1024]{2,1,0:T(8,128)S(1)}, f32[4,64,1024]{2,1,0:T(8,128)S(1)}, u32[]{:S(2)}, u32[]{:S(2)}) collective-permute-start(f32[4,64,1024]{2,1,0:T(8,128)S(1)} %get-tuple-element.79), channel_id=1, source_target_pairs={{0,1},{1,0},{2,3},{3,2},{4,5},{5,4},{6,7},{7,6},{8,9},{9,8},{10,11... | collective-permute-start | bytes 3145736 | tf_op jit(solution)/shard_map/ppermute | solution.py:525
  126.6 16.2 %collective-permute-start.23 = (f32[2,64,1024]{2,1,0:T(8,128)S(1)}, f32[2,64,1024]{2,1,0:T(8,128)S(1)}, u32[]{:S(2)}, u32[]{:S(2)}) collective-permute-start(f32[2,64,1024]{2,1,0:T(8,128)S(1)} %get-tuple-element.74), channel_id=1, source_target_pairs={{0,4},{1,5},{2,6},{3,7},{4,0},{5,1},{6,2},{7,3},{8,12},{9,13},{10,... | collective-permute-start | bytes 1572872 | tf_op jit(solution)/shard_map/ppermute | solution.py:525
  130.1 14.2 %collective-permute-start.24 = (f32[2,64,1024]{2,1,0:T(8,128)S(1)}, f32[2,64,1024]{2,1,0:T(8,128)S(1)}, u32[]{:S(2)}, u32[]{:S(2)}) collective-permute-start(f32[2,64,1024]{2,1,0:T(8,128)S(1)} %get-tuple-element.74), channel_id=1, source_target_pairs={{0,3},{1,2},{2,1},{3,0},{4,7},{5,6},{6,5},{7,4},{8,11},{9,10},{10,... | collective-permute-start | bytes 1572872 | tf_op jit(solution)/shard_map/ppermute | solution.py:525
  130.1 23.4 %collective-permute-start.26 = (f32[2,64,1024]{2,1,0:T(8,128)S(1)}, f32[2,64,1024]{2,1,0:T(8,128)S(1)}, u32[]{:S(2)}, u32[]{:S(2)}) collective-permute-start(f32[2,64,1024]{2,1,0:T(8,128)S(1)} %get-tuple-element.77), channel_id=1, source_target_pairs={{0,4},{1,5},{2,6},{3,7},{4,0},{5,1},{6,2},{7,3},{8,12},{9,13},{10,... | collective-permute-start | bytes 1572872 | tf_op jit(solution)/shard_map/ppermute | solution.py:525
  130.2 25.4 %collective-permute-start.30 = (f32[2,64,1024]{2,1,0:T(8,128)S(1)}, f32[2,64,1024]{2,1,0:T(8,128)S(1)}, u32[]{:S(2)}, u32[]{:S(2)}) collective-permute-start(f32[2,64,1024]{2,1,0:T(8,128)S(1)} %get-tuple-element.77), channel_id=1, source_target_pairs={{0,3},{1,2},{2,1},{3,0},{4,7},{5,6},{6,5},{7,4},{8,11},{9,10},{10,... | collective-permute-start | bytes 1572872 | tf_op jit(solution)/shard_map/ppermute | solution.py:525
  144.3 22.5 %collective-permute-start.25 = (f32[2,64,1024]{2,1,0:T(8,128)S(1)}, f32[2,64,1024]{2,1,0:T(8,128)S(1)}, u32[]{:S(2)}, u32[]{:S(2)}) collective-permute-start(f32[2,64,1024]{2,1,0:T(8,128)S(1)} %collective-permute-done.23.refs_1_), channel_id=1, source_target_pairs={{0,8},{1,9},{2,10},{3,11},{4,28},{5,29},{6,30},{7,31},{8,16},{9,17... | collective-permute-start | bytes 1572872 | tf_op jit(solution)/shard_map/ppermute | solution.py:525
  144.6 27.2 %collective-permute-start.33 = (f32[2,64,1024]{2,1,0:T(8,128)S(1)}, f32[2,64,1024]{2,1,0:T(8,128)S(1)}, u32[]{:S(2)}, u32[]{:S(2)}) collective-permute-start(f32[2,64,1024]{2,1,0:T(8,128)S(1)} %collective-permute-done.23.refs_1_), channel_id=1, source_target_pairs={{0,1},{1,0},{2,3},{3,2},{4,5},{5,4},{6,7},{7,6},{8,9},{9,8},{10,11... | collective-permute-start | bytes 1572872 | tf_op jit(solution)/shard_map/ppermute | solution.py:525
  153.5 13.4 %collective-permute-start.28 = (f32[2,64,1024]{2,1,0:T(8,128)S(1)}, f32[2,64,1024]{2,1,0:T(8,128)S(1)}, u32[]{:S(2)}, u32[]{:S(2)}) collective-permute-start(f32[2,64,1024]{2,1,0:T(8,128)S(1)} %collective-permute-done.24.refs_3_), channel_id=1, source_target_pairs={{0,4},{1,5},{2,6},{3,7},{4,0},{5,1},{6,2},{7,3},{8,12},{9,13},{10,... | collective-permute-start | bytes 1572872 | tf_op jit(solution)/shard_map/ppermute | solution.py:525
  155.6 15.7 %collective-permute-start.27 = (f32[2,64,1024]{2,1,0:T(8,128)S(1)}, f32[2,64,1024]{2,1,0:T(8,128)S(1)}, u32[]{:S(2)}, u32[]{:S(2)}) collective-permute-start(f32[2,64,1024]{2,1,0:T(8,128)S(1)} %collective-permute-done.26.refs_2_), channel_id=1, source_target_pairs={{0,8},{1,9},{2,10},{3,11},{4,28},{5,29},{6,30},{7,31},{8,16},{9,17... | collective-permute-start | bytes 1572872 | tf_op jit(solution)/shard_map/ppermute | solution.py:525
  155.8 16.2 %collective-permute-start.34 = (f32[2,64,1024]{2,1,0:T(8,128)S(1)}, f32[2,64,1024]{2,1,0:T(8,128)S(1)}, u32[]{:S(2)}, u32[]{:S(2)}) collective-permute-start(f32[2,64,1024]{2,1,0:T(8,128)S(1)} %collective-permute-done.26.refs_2_), channel_id=1, source_target_pairs={{0,1},{1,0},{2,3},{3,2},{4,5},{5,4},{6,7},{7,6},{8,9},{9,8},{10,11... | collective-permute-start | bytes 1572872 | tf_op jit(solution)/shard_map/ppermute | solution.py:525
  166.8 13.6 %collective-permute-start.35 = (f32[2,64,1024]{2,1,0:T(8,128)S(1)}, f32[2,64,1024]{2,1,0:T(8,128)S(1)}, u32[]{:S(2)}, u32[]{:S(2)}) collective-permute-start(f32[2,64,1024]{2,1,0:T(8,128)S(1)} %collective-permute-done.26.refs_2_), channel_id=1, source_target_pairs={{0,3},{1,2},{2,1},{3,0},{4,7},{5,6},{6,5},{7,4},{8,11},{9,10},{10,... | collective-permute-start | bytes 1572872 | tf_op jit(solution)/shard_map/ppermute | solution.py:525
  171.3 9.2 %collective-permute-start.36 = (f32[2,64,1024]{2,1,0:T(8,128)S(1)}, f32[2,64,1024]{2,1,0:T(8,128)S(1)}, u32[]{:S(2)}, u32[]{:S(2)}) collective-permute-start(f32[2,64,1024]{2,1,0:T(8,128)S(1)} %collective-permute-done.25.refs_2_), channel_id=1, source_target_pairs={{0,1},{1,0},{2,3},{3,2},{4,5},{5,4},{6,7},{7,6},{8,9},{9,8},{10,11... | collective-permute-start | bytes 1572872 | tf_op jit(solution)/shard_map/ppermute | solution.py:525
  171.3 9.2 %collective-permute-start.37 = (f32[2,64,1024]{2,1,0:T(8,128)S(1)}, f32[2,64,1024]{2,1,0:T(8,128)S(1)}, u32[]{:S(2)}, u32[]{:S(2)}) collective-permute-start(f32[2,64,1024]{2,1,0:T(8,128)S(1)} %collective-permute-done.27.refs_3_), channel_id=1, source_target_pairs={{0,1},{1,0},{2,3},{3,2},{4,5},{5,4},{6,7},{7,6},{8,9},{9,8},{10,11... | collective-permute-start | bytes 1572872 | tf_op jit(solution)/shard_map/ppermute | solution.py:525
  171.8 20.7 %collective-permute-start.32 = (f32[2,64,1024]{2,1,0:T(8,128)S(1)}, f32[2,64,1024]{2,1,0:T(8,128)S(1)}, u32[]{:S(2)}, u32[]{:S(2)}) collective-permute-start(f32[2,64,1024]{2,1,0:T(8,128)S(1)} %collective-permute-done.27.refs_3_), channel_id=1, source_target_pairs={{0,3},{1,2},{2,1},{3,0},{4,7},{5,6},{6,5},{7,4},{8,11},{9,10},{10,... | collective-permute-start | bytes 1572872 | tf_op jit(solution)/shard_map/ppermute | solution.py:525
  172.0 20.5 %collective-permute-start.31 = (f32[2,64,1024]{2,1,0:T(8,128)S(1)}, f32[2,64,1024]{2,1,0:T(8,128)S(1)}, u32[]{:S(2)}, u32[]{:S(2)}) collective-permute-start(f32[2,64,1024]{2,1,0:T(8,128)S(1)} %collective-permute-done.28.refs_4_), channel_id=1, source_target_pairs={{0,8},{1,9},{2,10},{3,11},{4,28},{5,29},{6,30},{7,31},{8,16},{9,17... | collective-permute-start | bytes 1572872 | tf_op jit(solution)/shard_map/ppermute | solution.py:525
  200.0 2.9 %collective-permute-start.38 = (f32[3]{0:T(128)S(1)}, f32[3]{0:T(128)S(1)}, u32[]{:S(2)}, u32[]{:S(2)}) collective-permute-start(f32[3]{0:T(128)S(1)} %get-tuple-element.87), channel_id=1, source_target_pairs={{0,1},{1,0},{2,3},{3,2},{4,5},{5,4},{6,7},{7,6},{8,9},{9,8},{10,11... | collective-permute-start | bytes 44 | tf_op jit(solution)/shard_map/ppermute | solution.py:484
  201.4 3.5 %collective-permute-start.39 = (f32[3]{0:T(128)S(1)}, f32[3]{0:T(128)S(1)}, u32[]{:S(2)}, u32[]{:S(2)}) collective-permute-start(f32[3]{0:T(128)S(1)} %get-tuple-element.87), channel_id=1, source_target_pairs={{0,2},{1,3},{2,0},{3,1},{4,6},{5,7},{6,4},{7,5},{8,10},{9,11},{10,... | collective-permute-start | bytes 44 | tf_op jit(solution)/shard_map/ppermute | solution.py:484
  201.5 3.5 %collective-permute-start.40 = (f32[3]{0:T(128)S(1)}, f32[3]{0:T(128)S(1)}, u32[]{:S(2)}, u32[]{:S(2)}) collective-permute-start(f32[3]{0:T(128)S(1)} %get-tuple-element.87), channel_id=1, source_target_pairs={{0,3},{1,2},{2,1},{3,0},{4,7},{5,6},{6,5},{7,4},{8,11},{9,10},{10,... | collective-permute-start | bytes 44 | tf_op jit(solution)/shard_map/ppermute | solution.py:484
  205.0 3.6 %collective-permute-start.41 = (f32[3]{0:T(128)S(1)}, f32[3]{0:T(128)S(1)}, u32[]{:S(2)}, u32[]{:S(2)}) collective-permute-start(f32[3]{0:T(128)S(1)} %add_add_fusion.1), channel_id=1, source_target_pairs={{0,4},{1,5},{2,6},{3,7},{4,0},{5,1},{6,2},{7,3},{8,12},{9,13},{10,... | collective-permute-start | bytes 44 | tf_op jit(solution)/shard_map/ppermute | solution.py:484
  207.1 3.5 %collective-permute-start.42 = (f32[3]{0:T(128)S(1)}, f32[3]{0:T(128)S(1)}, u32[]{:S(2)}, u32[]{:S(2)}) collective-permute-start(f32[3]{0:T(128)S(1)} %add_add_fusion.1), channel_id=1, source_target_pairs={{0,8},{1,9},{2,10},{3,11},{4,12},{5,13},{6,14},{7,15},{8,0},{9,1},... | collective-permute-start | bytes 44 | tf_op jit(solution)/shard_map/ppermute | solution.py:484
  207.1 4.4 %collective-permute-start.43 = (f32[3]{0:T(128)S(1)}, f32[3]{0:T(128)S(1)}, u32[]{:S(2)}, u32[]{:S(2)}) collective-permute-start(f32[3]{0:T(128)S(1)} %add_add_fusion.1), channel_id=1, source_target_pairs={{0,12},{1,13},{2,14},{3,15},{4,8},{5,9},{6,10},{7,11},{8,4},{9,5},... | collective-permute-start | bytes 44 | tf_op jit(solution)/shard_map/ppermute | solution.py:484
  211.6 4.4 %collective-permute-start.44 = (f32[3]{0:T(128)S(1)}, f32[3]{0:T(128)S(1)}, u32[]{:S(2)}, u32[]{:S(2)}) collective-permute-start(f32[3]{0:T(128)S(1)} %add_add_fusion), channel_id=1, source_target_pairs={{0,16},{1,17},{2,18},{3,19},{4,20},{5,21},{6,22},{7,23},{8,24},{9,... | collective-permute-start | bytes 44 | tf_op jit(solution)/shard_map/ppermute | solution.py:484

commit v3 on v2

v3 whole, which is shorter than its diff:
```python
import functools

import jax
import jax.numpy as jnp
import numpy as np
from jax import lax
from jax.experimental import pallas as pl
from jax.experimental.pallas import tpu as pltpu
from jax.sharding import PartitionSpec as P

STEPS = 2
AXES = ("gx", "gy")
LANES = 128
TILE = 256

step_x = np.array([0, 0, -1, 1, -1, 1, -1, 1])
step_y = np.array([-1, 1, -1, 1, 1, -1, 0, 0])

FRAME = {
    "C": (0, 1),
    "A": (1, 0),
    "Y": (0, -1),
    "CA": (1, 1),
    "B": (-1, 0),
    "YA": (1, -1),
    "CB": (-1, 1),
    "YB": (-1, -1),
}


OWN_TILES = 2
TILES = (
    (("C", 0, 4),),
    (("A", 2, 2), ("Y", 0, 2)),
    (("A", 0, 2), ("Y", 2, 2)),
    (("B", 2, 2), ("YA", 2, 2)),
    (("B", 0, 2), ("YA", 0, 2)),
    (("CA", 0, 4),),
    (("CB", 0, 4),),
    (("YB", 0, 4),),
)


def pool_places(rows):
    places = {}
    for t, members in enumerate(TILES):
        at = rows + 4 * t
        for name, begin, count in members:
            places.setdefault(name, [0, 0])
            if begin == 0:
                places[name][0] = at
            if begin + count == 4:
                places[name][1] = at + count - 2
            at += count
    return places


def reach(t):
    def frames(n):
        return [(0, 0)] if n < OWN_TILES else [FRAME[m[0]] for m in TILES[n - OWN_TILES]]

    near = lambda p, q: abs(p[0] - q[0]) <= 1 and abs(p[1] - q[1]) <= 1
    count = OWN_TILES + len(TILES)
    found = [n for n in range(count) if any(near(p, q) for p in frames(t) for q in frames(n))]
    if len(found) % 2:
        found.append(next(n for n in range(count) if n not in found))
    return found


def flat_perm(count_x, count_y, move):
    pairs = []
    for i in range(count_x):
        for j in range(count_y):
            x, y = move(i, j)
            pairs.append((i * count_y + j, (x % count_x) * count_y + y % count_y))
    return pairs


def toward_a(i, j):
    return i ^ 1, j


def along_b(i, j):
    return (i + 2 if i % 2 == 0 else i - 2), j


def toward_c(i, j):
    return i, j ^ 1


def toward_y(i, j):
    return i, (j - 1 if j % 2 == 0 else j + 1)


def split(value):
    high = value.astype(jnp.bfloat16)
    low = (value - high.astype(jnp.float32)).astype(jnp.bfloat16)
    return high, low


def trace_of(block):
    row = lax.broadcasted_iota(jnp.int32, block.shape, 0)
    lane = lax.broadcasted_iota(jnp.int32, block.shape, 1)
    return jnp.sum(jnp.where(row == lane, block, 0.0))


def quotient(value, by, most):
    total = jnp.zeros_like(value)
    for k in range(1, most + 1):
        total += (value >= by * k).astype(jnp.int32)
    return total


VMEM = pl.BlockSpec(memory_space=pltpu.VMEM)
SMEM = pl.BlockSpec(memory_space=pltpu.SMEM)


def pack(moves, rims, cols, rows, count_x, count_y):
    row_count, block, strip = rows.shape
    slots = cols.shape[1]
    rim_count = rims.shape[0]
    tiles = strip // LANES
    ways = len(step_x)

    def kernel(moves_in, rims_in, cols_in, rows_in, *refs):
        outs, refs = refs[:ways], refs[ways:]
        small_ref, cols_ref, moves_ref, rims_ref, rows_ref, codes_ref, tail_ref, sems = refs
        copies = [
            pltpu.make_async_copy(source, target, sems.at[k])
            for k, (source, target) in enumerate(
                (
                    (moves_in, moves_ref),
                    (rims_in, rims_ref),
                    (cols_in, cols_ref),
                    (rows_in, rows_ref),
                )
            )
        ]
        for copy in copies:
            copy.start()
        index_x = lax.axis_index("gx")
        index_y = lax.axis_index("gy")
        for copy in copies[:3]:
            copy.wait()
        cols = cols_ref[...]
        inner = jnp.full(cols.shape, -1, jnp.int32)
        for m in range(rim_count):
            small_ref[ways + m] = rims_ref[m]
            inner = jnp.where(cols == rims_ref[m], 4 * rim_count + m, inner)
        away = cols - row_count
        direction = quotient(away, rim_count, ways - 1)
        place = direction + (direction >= 4).astype(jnp.int32)
        code = jnp.where(
            cols < row_count, inner, place * rim_count + away - direction * rim_count
        )
        codes_ref[...] = jnp.zeros(codes_ref.shape, jnp.float32)
        tail_ref[...] = jnp.zeros(tail_ref.shape, jnp.float32)
        codes_ref[:, :slots] = code.astype(jnp.float32)
        for m in range(rim_count):
            tail_ref[pl.ds(m, 1), :] = codes_ref[pl.ds(rims_ref[m], 1), :]
        leaving = []
        for d in range(ways):
            x = lax.rem(index_x + int(step_x[d]) + count_x, count_x)
            y = lax.rem(index_y + int(step_y[d]) + count_y, count_y)
            first = (x * count_y + y) * row_count
            slot = jnp.int32(0)
            for r in range(1, row_count):
                target = moves_ref[r]
                slot = jnp.where((target >= first) & (target < first + row_count), r, slot)
            small_ref[d] = slot
            leaving.append(slot)
        copies[3].wait()
        for d in range(ways):
            for k in range(tiles):
                outs[d][k * block : (k + 1) * block, :] = rows_ref[
                    leaving[d], :, k * LANES : (k + 1) * LANES
                ]
            outs[d][tiles * block :, :] = tail_ref[...]

    message = jax.ShapeDtypeStruct((tiles * block + 8, LANES), jnp.float32)
    return pl.pallas_call(
        kernel,
        out_shape=(message,) * ways
        + (
            jax.ShapeDtypeStruct((ways + rim_count,), jnp.int32),
            jax.ShapeDtypeStruct(cols.shape, jnp.int32),
        ),
        in_specs=[pl.BlockSpec(memory_space=pltpu.HBM)] * 4,
        out_specs=(VMEM,) * ways + (SMEM, VMEM),
        scratch_shapes=[
            pltpu.SMEM((row_count,), jnp.int32),
            pltpu.SMEM((rim_count,), jnp.int32),
            pltpu.VMEM(rows.shape, jnp.float32),
            pltpu.VMEM((row_count, LANES), jnp.float32),
            pltpu.VMEM((8, LANES), jnp.float32),
            pltpu.SemaphoreType.DMA((4,)),
        ],
        compiler_params=pltpu.CompilerParams(vmem_limit_bytes=16 * 2**20),
        name="pack_rows",
    )(moves, rims, cols, rows)


def share(rows_ref, small_ref, rim_refs):
    rim_ref, a_1, y_0, a_0, y_1 = rim_refs
    count = rim_ref.shape[0]
    for m in range(count):
        row = rows_ref[small_ref[len(step_x) + m]]
        rim_ref[m] = row
        for ref in (a_0, y_0) if m < count // 2 else (a_1, y_1):
            ref[m % (count // 2)] = row


def place(small, arrived, strip):
    rows = len(arrived)
    tiles = strip // LANES
    block = (arrived[0].shape[0] - 8) // tiles
    count = small.shape[0] - rows
    half = count // 2

    def kernel(small_ref, *refs):
        ins, outs = refs[:rows], refs[rows:]
        current_ref, *rim_refs, trace_ref = outs
        total = jnp.float32(0.0)
        for d in range(rows):
            for k in range(tiles):
                current_ref[small_ref[d], :, k * LANES : (k + 1) * LANES] = ins[d][
                    k * block : (k + 1) * block, :
                ]
            total += trace_of(ins[d][:block, :])
        trace_ref[0] = total
        share(current_ref, small_ref, rim_refs)

    rim = lambda n: jax.ShapeDtypeStruct((n, block, strip), jnp.float32)
    return pl.pallas_call(
        kernel,
        out_shape=(rim(rows), rim(count), rim(half), rim(half), rim(half), rim(half))
        + (jax.ShapeDtypeStruct((1,), jnp.float32),),
        in_specs=[SMEM] + [VMEM] * rows,
        out_specs=(VMEM,) * 6 + (SMEM,),
        compiler_params=pltpu.CompilerParams(vmem_limit_bytes=16 * 2**20),
        name="place_rows",
    )(small, *arrived)


def tables(small, cols, arrived):
    rows, slots = cols.shape
    rim_count = small.shape[0] - len(arrived)
    half = rim_count // 2
    pool = rows + len(TILES) * rim_count
    tail = arrived[0].shape[0] // 8 - 1
    base_of = [[0, 0]] * 9
    for name, (one, two) in pool_places(rows).items():
        x, y = FRAME[name]
        base_of[3 * (x + 1) + y + 1] = [one, two - half]

    def kernel(small_ref, cols_ref, *refs):
        tails, (spots_ref, table_ref, all_ref) = refs[: len(arrived)], refs[len(arrived) :]
        sign_x = 1 - 2 * lax.rem(lax.axis_index("gx"), 2)
        sign_y = 1 - 2 * lax.rem(lax.axis_index("gy"), 2)

        def locate(place, index, shift_x, shift_y):
            third = quotient(place, 3, 2)
            x = (third - 1) * sign_x + shift_x
            y = (place - 3 * third - 1) * sign_y + shift_y
            inside = (x >= -1) & (x <= 1) & (y >= -1) & (y <= 1)
            at = 3 * (x + 1) + y + 1
            one = two = jnp.zeros_like(index)
            for k in range(9):
                one = jnp.where(at == k, base_of[k][0], one)
                two = jnp.where(at == k, base_of[k][1], two)
            spot = index + jnp.where(index < half, one, two)
            for m in range(rim_count):
                spot = jnp.where((at == 4) & (index == m), small_ref[len(arrived) + m], spot)
            return jnp.where(inside, spot, -1)

        cols = cols_ref[...]
        away = cols - rows
        direction = quotient(away, rim_count, 7)
        place = direction + (direction >= 4).astype(jnp.int32)
        spots = locate(place, away - direction * rim_count, 0, 0)
        spots = jnp.where(cols < rows, cols, spots)
        spots_ref[...] = spots
        all_ref[...] = jnp.full(all_ref.shape, -1, jnp.int32)
        all_ref[:rows, :slots] = spots
        for d in range(len(arrived)):
            x = -int(step_x[d]) * sign_x
            y = -int(step_y[d]) * sign_y
            at = 3 * (x + 1) + y + 1
            bases = []
            for part in range(2):
                base = jnp.int32(0)
                for k in range(9):
                    base = jnp.where(at == k, base_of[k][part], base)
                bases.append(base)
            near = tails[d][...].astype(jnp.int32)
            place = quotient(near, rim_count, 8)
            spots = locate(place, near - place * rim_count, x, y)
            spots = jnp.where(near < 0, -1, spots)
            for m in range(rim_count):
                all_ref[pl.ds(bases[m // half] + m, 1), :] = spots[m : m + 1, :]
        lane = lax.broadcasted_iota(jnp.int32, (pool, LANES), 1)
        found = jnp.full((pool, LANES), -1, jnp.int32)
        for u in range(slots):
            found = jnp.where(all_ref[:, u : u + 1] == lane, u, found)
        entry = (found >> 1) + 16 * ((found ^ lane) & 1)
        table_ref[...] = jnp.where(found < 0, slots // 2, entry)

    last = pl.BlockSpec((8, LANES), lambda n: (tail, 0))
    full = lambda shape: pl.BlockSpec(shape, lambda n: (0, 0))
    return pl.pallas_call(
        kernel,
        grid=(1,),
        out_shape=(
            jax.ShapeDtypeStruct((rows, slots), jnp.int32),
            jax.ShapeDtypeStruct((pool, LANES), jnp.int32),
        ),
        in_specs=[SMEM, full((rows, slots))] + [last] * len(arrived),
        out_specs=(full((rows, slots)), full((pool, LANES))),
        scratch_shapes=[pltpu.VMEM((pool, LANES), jnp.int32)],
        name="make_tables",
    )(small, cols, *arrived)


def spread(parts, high_ref, low_ref):
    base = 0
    strip = parts[0].shape[2]
    for ref in parts:

        def one(c, carry, ref=ref, base=base):
            at = pl.ds(pl.multiple_of((base + c) * 64, 64), 64)
            for k in range(strip // LANES):
                to = pl.ds(k * LANES, LANES)
                value = ref[c, :, to]
                for turn in range(2):
                    high, low = split(pltpu.roll(value, 64, 1) if turn else value)
                    high_ref[turn, at, to] = high
                    low_ref[turn, at, to] = low
            zeros = jnp.zeros((64, LANES), jnp.bfloat16)
            high_ref[0, at, pl.ds(strip, LANES)] = zeros
            low_ref[0, at, pl.ds(strip, LANES)] = zeros
            return carry

        lax.fori_loop(0, ref.shape[0], one, 0)
        base += ref.shape[0]


def fill(table_ref, first, member, members, tile, source, targets):
    left_half = lax.broadcasted_iota(jnp.int32, (64, LANES), 1) < 64
    spot = tile * (TILE // 64)
    for c in range(members):
        at = pl.ds(pl.multiple_of((member + c) * 64, 64), 64)
        for q in range(TILE // LANES):
            left = table_ref[first + member + c, spot + 2 * q]
            right = table_ref[first + member + c, spot + 2 * q + 1]
            from_left = pl.ds(pl.multiple_of((left & 15) * LANES, LANES), LANES)
            from_right = pl.ds(pl.multiple_of((right & 15) * LANES, LANES), LANES)
            for k in range(2):
                value = jnp.where(
                    left_half,
                    source[k][left >> 4, at, from_left],
                    source[k][right >> 4, at, from_right],
                )
                for refs, lane in targets:
                    to = pl.ds(pl.multiple_of(lane + q * LANES, LANES), LANES)
                    refs[k][pl.ds(c * 64, 64), to] = value


def three_products(a_high, a_low, d_high, d_low):
    left = jnp.concatenate([a_high, a_high, a_low], axis=1)
    right = jnp.concatenate([d_high, d_low, d_high], axis=0)
    return jnp.dot(left, right, preferred_element_type=jnp.float32)


def wide_scratch(members, strip):
    return [pltpu.VMEM((2, members * 64, strip + LANES), jnp.bfloat16)] * 2


def pipelined(units, fill_one, multiply, buffers):
    even, odd = buffers
    fill_one(jnp.int32(0), even)

    def two(j, carry):
        fill_one(2 * j + 1, odd)
        multiply(2 * j, even)
        fill_one(jnp.minimum(2 * j + 2, units - 1), even)
        multiply(2 * j + 1, odd)
        return carry

    lax.fori_loop(0, units // 2, two, 0)
    if units % 2:
        multiply(units - 1, even)


def lane(tile):
    return pl.multiple_of(tile * TILE, TILE)


def cost(units):
    return pl.CostEstimate(flops=units * 2**27, bytes_accessed=2**16, transcendentals=0)


def spread_own(current):
    rows, block, strip = current.shape

    def kernel(current_ref, high_ref, low_ref):
        spread([current_ref], high_ref, low_ref)

    wide = jax.ShapeDtypeStruct((2, rows * block, strip + LANES), jnp.bfloat16)
    return pl.pallas_call(
        kernel,
        out_shape=(wide, wide),
        in_specs=[VMEM],
        out_specs=(VMEM, VMEM),
        compiler_params=pltpu.CompilerParams(vmem_limit_bytes=16 * 2**20),
        cost_estimate=cost(1),
        name="spread_own",
    )(current)


def own_product(table, wide, rows, block):
    width = table.shape[0] * block
    depth = rows * block
    tiles = width // TILE

    def kernel(table_ref, wide_high, wide_low, high_ref, low_ref, total_ref, *scratch):
        wide = wide_high, wide_low
        own, even, odd = scratch[0:2], scratch[2:4], scratch[4:6]
        for n in range(depth // TILE):
            fill(table_ref, 0, 0, rows, n, wide, [(own, n * TILE)])

        def fill_one(i, buffers):
            for k in range(2):
                fill(
                    table_ref, 0, 0, rows, 2 * i + k, wide,
                    [(buffers, k * TILE), ((high_ref, low_ref), (2 * i + k) * TILE)],
                )

        def multiply(i, buffers):
            to = pl.ds(pl.multiple_of(2 * i * TILE, 2 * TILE), 2 * TILE)
            total_ref[:, to] = three_products(
                own[0][...], own[1][...], buffers[0][...], buffers[1][...]
            )

        pipelined(tiles // 2, fill_one, multiply, (even, odd))

    dense = lambda t: jax.ShapeDtypeStruct((depth, width), t)
    return pl.pallas_call(
        kernel,
        out_shape=(dense(jnp.bfloat16), dense(jnp.bfloat16), dense(jnp.float32)),
        in_specs=[SMEM, VMEM, VMEM],
        out_specs=(VMEM, VMEM, VMEM),
        scratch_shapes=[pltpu.VMEM((depth, depth), jnp.bfloat16)] * 2
        + [pltpu.VMEM((depth, 2 * TILE), jnp.bfloat16)] * 4,
        compiler_params=pltpu.CompilerParams(vmem_limit_bytes=24 * 2**20),
        cost_estimate=cost(2 * tiles),
        name="own_product",
    )(table, *wide)


def extract(spots_ref, total_ref, current_ref, out_ref, blend):
    left_half = lax.broadcasted_iota(jnp.int32, (64, LANES), 1) < 64

    def one_row(g, carry):
        at = pl.ds(pl.multiple_of(g * 64, 64), 64)
        for k in range(out_ref.shape[2] // LANES):
            sides = []
            for side in range(2):
                spot = spots_ref[g, 2 * k + side]
                tile = pl.ds(pl.multiple_of((spot >> 1) * LANES, LANES), LANES)
                sides.append(pltpu.roll(total_ref[at, tile], ((spot ^ side) & 1) * 64, 1))
            value = jnp.where(left_half, *sides)
            to = pl.ds(k * LANES, LANES)
            if blend:
                value = 2.0 * current_ref[g, :, to] - value
            out_ref[g, :, to] = value
        return carry

    lax.fori_loop(0, out_ref.shape[0], one_row, 0)


def add_traces(traces_ref, total_ref, trace_ref):
    known = traces_ref.shape[0]
    for k in range(known):
        trace_ref[k] = traces_ref[k]
    row = lax.broadcasted_iota(jnp.int32, (64, LANES), 0)
    spot = lax.broadcasted_iota(jnp.int32, (64, LANES), 1)
    found = jnp.zeros((64, LANES), jnp.float32)
    for g in range(total_ref.shape[0] // 64):
        block = total_ref[g * 64 : (g + 1) * 64, (g // 2) * LANES : (g // 2 + 1) * LANES]
        found += jnp.where(spot - row == 64 * (g % 2), block, 0.0)
    trace_ref[known] = jnp.sum(found)


def finish(spots, total, current):
    def kernel(spots_ref, total_ref, current_ref, out_ref):
        extract(spots_ref, total_ref, current_ref, out_ref, True)

    return pl.pallas_call(
        kernel,
        out_shape=jax.ShapeDtypeStruct(current.shape, jnp.float32),
        in_specs=[SMEM, VMEM, VMEM],
        out_specs=VMEM,
        compiler_params=pltpu.CompilerParams(vmem_limit_bytes=16 * 2**20),
        cost_estimate=cost(4),
        name="finish",
    )(spots, total, current)


def add_product(begin, count, table, high, low, parts, total, label, lists=None, traces=None, square=None):
    depth_own, width = total.shape
    _, block, strip = parts[0].shape
    rows = depth_own // block
    each = TILE // block
    first = begin * each
    lists = lists or [reach(begin + k) for k in range(count)]
    starts = [sum(len(t) for t in lists[:k]) // 2 for k in range(count + 1)]
    codes = [
        [sum(t << (4 * k) for k, t in enumerate(tiles[side::2])) for side in range(2)]
        for tiles in lists
    ]

    def unit(i):
        group, start = jnp.int32(0), jnp.int32(0)
        code = [jnp.int32(c) for c in codes[0]]
        for k in range(1, count):
            after = i >= starts[k]
            group = jnp.where(after, k, group)
            start = jnp.where(after, starts[k], start)
            code = [jnp.where(after, new, old) for new, old in zip(codes[k], code)]
        return group, [(c >> (4 * (i - start))) & 15 for c in code]

    def kernel(table_ref, high_ref, low_ref, *refs):
        refs = list(refs)
        part_refs = [refs.pop(0) for _ in parts]
        refs.pop(0)
        if traces is not None:
            traces_ref = refs.pop(0)
        if square is not None:
            spots_ref, small_ref = refs.pop(0), refs.pop(0)
        total_ref = refs.pop(0)
        if traces is not None:
            trace_ref = refs.pop(0)
        if square is not None:
            out_ref, *rim_refs = (refs.pop(0) for _ in range(6))
        wide, even, odd = refs[0:2], refs[2:4], refs[4:6]
        spread(part_refs, *wide)

        def fill_one(i, buffers):
            group, tiles = unit(i)
            for k in range(2):
                fill(table_ref, first, group * each, each, tiles[k], wide, [(buffers, k * TILE)])

        def multiply(i, buffers):
            group, tiles = unit(i)
            at = pl.ds(lane(begin + group), TILE)
            value = three_products(
                high_ref[:, at], low_ref[:, at], buffers[0][...], buffers[1][...]
            )
            for k in range(2):
                to = pl.ds(lane(tiles[k]), TILE)
                total_ref[:, to] += value[:, k * TILE : (k + 1) * TILE]

        pipelined(starts[-1], fill_one, multiply, (even, odd))
        if traces is not None:
            add_traces(traces_ref, total_ref, trace_ref)
        if square is not None:
            extract(spots_ref, total_ref, None, out_ref, False)
            share(out_ref, small_ref, rim_refs)

    ins = [table, high, low, *parts, total]
    in_specs = [SMEM] + [VMEM] * (3 + len(parts))
    out_shape = [jax.ShapeDtypeStruct((depth_own, width), jnp.float32)]
    out_specs = [VMEM]
    if traces is not None:
        ins.append(traces)
        in_specs.append(SMEM)
        out_shape.append(jax.ShapeDtypeStruct((traces.shape[0] + 1,), jnp.float32))
        out_specs.append(SMEM)
    if square is not None:
        ins += square
        in_specs += [SMEM, SMEM]
        shape = lambda n: jax.ShapeDtypeStruct((n, block, strip), jnp.float32)
        out_shape += [shape(rows), shape(each)] + [shape(each // 2)] * 4
        out_specs += [VMEM] * 6
    scratch = wide_scratch(count * each, strip)
    scratch += [pltpu.VMEM((TILE, 2 * TILE), jnp.bfloat16)] * 4
    return pl.pallas_call(
        kernel,
        out_shape=out_shape,
        in_specs=in_specs,
        out_specs=out_specs,
        scratch_shapes=scratch,
        input_output_aliases={3 + len(parts): 0},
        compiler_params=pltpu.CompilerParams(vmem_limit_bytes=24 * 2**20),
        cost_estimate=cost(2 * starts[-1]),
        name=label,
    )(*ins)


def sum_rounds(count_x, count_y):
    rounds = []
    for count, at in ((count_y, 1), (count_x, 0)):
        bit = 1
        while bit < count:
            bits = [bit, 2 * bit, 3 * bit] if 2 * bit < count else [bit]
            rounds.append(
                [
                    flat_perm(count_x, count_y, lambda i, j: (i, j ^ b) if at else (i ^ b, j))
                    for b in bits
                ]
            )
            bit *= 4
    return rounds


def sum_round(value, perms):
    others = [lax.ppermute(value, AXES, perm) for perm in perms]
    if len(others) == 1:
        return value + others[0]
    return (value + others[0]) + (others[1] + others[2])


def shards(density, moves, cols, halo_rows):
    row_count, block, strip = density.shape[2:]
    rim_count = halo_rows.shape[2]
    count_x = lax.axis_size("gx")
    count_y = lax.axis_size("gy")
    rows = density.reshape(row_count, block, strip)
    rims = halo_rows.reshape(rim_count)
    own_cols = cols.reshape(row_count, -1)

    *leaving, small, own_cols = pack(
        moves.reshape(row_count), rims, own_cols, rows, count_x, count_y
    )
    arrived = [None] * len(step_x)
    for d in range(len(step_x)):
        dx, dy = int(step_x[d]), int(step_y[d])
        perm = flat_perm(count_x, count_y, lambda i, j: (i + dx, j + dy))
        arrived[d] = lax.ppermute(leaving[d], AXES, perm)

    current, *shared, traces = place(small, arrived, strip)
    spots, table = tables(small, own_cols, arrived)
    swap = {
        "A": flat_perm(count_x, count_y, toward_a),
        "B": flat_perm(count_x, count_y, along_b),
        "C": flat_perm(count_x, count_y, toward_c),
        "Y": flat_perm(count_x, count_y, toward_y),
    }
    go = lambda value, way: lax.ppermute(value, AXES, swap[way])
    rounds = sum_rounds(count_x, count_y)
    tie = lax.optimization_barrier
    for step in range(STEPS):
        c, a_1, y_0 = (go(rim, way) for rim, way in zip(shared[:3], "CAY"))
        wide_high, wide_low = spread_own(current)
        wide_high, *shared = tie((wide_high, *shared[3:]))
        a_0, y_1 = (go(rim, way) for rim, way in zip(shared, "AY"))
        high, low, total = own_product(table, (wide_high, wide_low), row_count, block)
        add = functools.partial(add_product, table=table, high=high, low=low)
        a_1, y_0, c, total = tie((a_1, y_0, c, total))
        b_1, ya_1, ya_0 = go(a_1, "B"), go(a_1, "Y"), go(y_0, "A")
        (total,) = add(2, 2, parts=[c, a_1, y_0], total=total, label="first_product")
        a_0, y_1, total = tie((a_0, y_1, total))
        b_0 = go(a_0, "B")
        (total,) = add(4, 1, parts=[a_0, y_1], total=total, label="second_product")
        a_0, b_1, ya_0, total = tie((a_0, b_1, ya_0, total))
        yb_1, yb_0 = go(b_1, "Y"), go(ya_0, "B")
        ca = go(jnp.concatenate([a_0, a_1]), "C")
        (total,) = add(5, 1, parts=[b_1, ya_1], total=total, label="third_product")
        b_0, total = tie((b_0, total))
        cb = go(jnp.concatenate([b_0, b_1]), "C")
        (total,) = add(6, 2, parts=[b_0, ya_0, ca], total=total, label="fourth_product")
        (total,) = add(8, 1, parts=[cb], total=total, label="fifth_product")
        last = functools.partial(add, 9, 1, parts=[yb_0, yb_1])
        if step % 2 == 0:
            total, traces, current, *shared = last(
                total=total, label="last_product", traces=traces, square=(spots, small)
            )
        else:
            others = [t for t in reach(9) if t >= OWN_TILES]
            total, traces = last(
                total=total, label="trace_product", lists=[list(range(OWN_TILES))], traces=traces
            )
            sums = sum_round(traces, rounds[0])
            (total,) = last(total=total, label="other_product", lists=[others])
            sums, total = tie((sums, total))
            sums = sum_round(sums, rounds[1])
            current = finish(spots, total, current)
    for perms in rounds[2:]:
        sums, current = tie((sums, current))
        sums = sum_round(sums, perms)
    sums = sums * (1.0 / (count_x * count_y * row_count * block))
    occupation = jnp.stack([sums[0], sums[1], sums[1], sums[2]])
    return (current.reshape(density.shape), occupation)


def solution(mesh):
    in_specs = (
        P("gx", "gy", None, None, None),
        P("gx", "gy", None),
        P("gx", "gy", None, None),
        P("gx", "gy", None),
    )
    out_specs = (P("gx", "gy", None, None, None), P())
    return jax.shard_map(shards, mesh=mesh, in_specs=in_specs, out_specs=out_specs, check_vma=False)
```

time: 217 us -> 203 us (0.935)
  waiting for transfers between devices: 91.1 us -> 48.7 us
  Pallas kernels: 84 us -> 97.4 us
  starting transfers between devices: 34.2 us -> 43.8 us
  local copies, waits for them, and re-layouts: 5.78 us -> 10.6 us
    ppermute x30 -> x26, waiting for transfers between devices: 49.1 us -> 25 us  [shards(): go = lambda value, way: lax.ppermute(value, AXES, swap[way])]
    pallas_call x6 -> x16, Pallas kernels: 61.1 us -> 77.3 us  [the longest x13 71.5 us: add_product(): pl.pallas_call(kernel, out_shape=out_shape, in_specs=in_specs, out_specs=...]
    ppermute x8, waiting for transfers between devices: 34.7 us -> 19.9 us  [shards(): arrived[d] = lax.ppermute(leaving[d], AXES, perm)]
    ppermute x8, starting transfers between devices: 10.6 us -> 19.9 us  [shards(): arrived[d] = lax.ppermute(leaving[d], AXES, perm)]
    unnamed x34 -> x44, local copies, waits for them, and re-layouts: 5.71 us -> 10.5 us
    ppermute x7, waiting for transfers between devices: 7.27 us -> 3.74 us  [sum_round(): others = [lax.ppermute(value, AXES, perm) for perm in perms]]
    pallas_call x2, Pallas kernels: 17.8 us -> 14.6 us  [own_product(): pl.pallas_call(kernel, out_shape=(dense(jnp.bfloat16), dense(jnp.bfloat16...]
    ppermute x30 -> x26, starting transfers between devices: 14.9 us -> 17.6 us  [shards(): go = lambda value, way: lax.ppermute(value, AXES, swap[way])]
  transfers between devices with their start and end apart: 45 -> 41, of which waited for: 19 -> 15; matrix products, arithmetic and copies ran while one was open for 0% -> 0% of each run, Pallas kernels for 31% -> 41%
where the time goes in v3:
time: 203 us; the launch traced here: 202 us
  Pallas kernels  97.4 us (48%)
  waiting for transfers between devices  48.7 us (24%)
  starting transfers between devices  43.8 us (22%)
  local copies, waits for them, and re-layouts  10.6 us (5%)
    pallas_call x13, Pallas kernels, add_product(): pl.pallas_call(kernel, out_shape=out_shape, in_specs=in_specs, out_specs=...  71.5 us
    ppermute x26, waiting for transfers between devices, shards(): go = lambda value, way: lax.ppermute(value, AXES, swap[way])  25 us
    ppermute x8, waiting for transfers between devices, shards(): arrived[d] = lax.ppermute(leaving[d], AXES, perm)  19.9 us
    ppermute x8, starting transfers between devices, shards(): arrived[d] = lax.ppermute(leaving[d], AXES, perm)  19.9 us
    ppermute x26, starting transfers between devices, shards(): go = lambda value, way: lax.ppermute(value, AXES, swap[way])  17.6 us
    pallas_call x2, Pallas kernels, own_product(): pl.pallas_call(kernel, out_shape=(dense(jnp.bfloat16), dense(jnp.bfloat16...  14.6 us
    unnamed x44, local copies, waits for them, and re-layouts  10.5 us
    ppermute x7, starting transfers between devices, sum_round(): others = [lax.ppermute(value, AXES, perm) for perm in perms]  6.26 us
  transfers between devices with their start and end apart: 41, of which 15 were waited for; matrix products, arithmetic and copies ran while one was open for 0% of the time, Pallas kernels for 41%

profile of v3, /device:TPU:0, one launch (start us, length us, event | category | flops | bytes accessed | tf_op | source)
XLA Modules:
  0.0 202.5 jit_solution(17209944903696765073)
XLA Ops:
  0.6 1.6 copy-done.2
  2.2 0.7 copy-done.14
  2.9 0.7 copy-done.16
  3.6 0.7 copy-done.17
  4.2 1.3 pack_rows.1
  5.5 2.5 %collective-permute-start = (f32[520,128]{1,0:T(8,128)S(1)}, f32[520,128]{1,0:T(8,128)S(1)}, u32[]{:S(2)}, u32[]{:S(2)}) collective-permute-start(f32[520,128]{1,0:T(8,128)S(1)} %get-tuple-element.78), channel_id=1, source_target_pairs={{0,3},{1,0},{2,1},{3,2},{4,7},{5,4},{6,5},{7,6},{8,11},{9,8},{10,9... | collective-permute-start | bytes 798728 | tf_op jit(solution)/shard_map/ppermute | solution.py:639
  8.0 5.7 %collective-permute-start.2 = (f32[520,128]{1,0:T(8,128)S(1)}, f32[520,128]{1,0:T(8,128)S(1)}, u32[]{:S(2)}, u32[]{:S(2)}) collective-permute-start(f32[520,128]{1,0:T(8,128)S(1)} %get-tuple-element.80), channel_id=1, source_target_pairs={{0,31},{1,28},{2,29},{3,30},{4,3},{5,0},{6,1},{7,2},{8,7},{9,4},{1... | collective-permute-start | bytes 798728 | tf_op jit(solution)/shard_map/ppermute | solution.py:639
  13.7 4.5 %collective-permute-start.4 = (f32[520,128]{1,0:T(8,128)S(1)}, f32[520,128]{1,0:T(8,128)S(1)}, u32[]{:S(2)}, u32[]{:S(2)}) collective-permute-start(f32[520,128]{1,0:T(8,128)S(1)} %get-tuple-element.82), channel_id=1, source_target_pairs={{0,29},{1,30},{2,31},{3,28},{4,1},{5,2},{6,3},{7,0},{8,5},{9,6},{1... | collective-permute-start | bytes 798728 | tf_op jit(solution)/shard_map/ppermute | solution.py:639
  18.5 5.2 %collective-permute-start.5 = (f32[520,128]{1,0:T(8,128)S(1)}, f32[520,128]{1,0:T(8,128)S(1)}, u32[]{:S(2)}, u32[]{:S(2)}) collective-permute-start(f32[520,128]{1,0:T(8,128)S(1)} %get-tuple-element.83), channel_id=1, source_target_pairs={{0,7},{1,4},{2,5},{3,6},{4,11},{5,8},{6,9},{7,10},{8,15},{9,12},{1... | collective-permute-start | bytes 798728 | tf_op jit(solution)/shard_map/ppermute | solution.py:639
  23.6 1.2 collective-permute-start.6
  24.8 0.8 collective-permute-start.7
  25.7 8.1 %collective-permute-done.3.refs_3_ = f32[520,128]{1,0:T(8,128)S(1)} collective-permute-done((f32[520,128]{1,0:T(8,128)S(1)}, f32[520,128]{1,0:T(8,128)S(1)}, u32[]{:S(2)}, u32[]{:S(2)}) %collective-permute-start.3) | collective-permute-done | bytes 266272 | tf_op jit(solution)/shard_map/ppermute | solution.py:639
  33.8 6.7 %collective-permute-done.4.refs_4_ = f32[520,128]{1,0:T(8,128)S(1)} collective-permute-done((f32[520,128]{1,0:T(8,128)S(1)}, f32[520,128]{1,0:T(8,128)S(1)}, u32[]{:S(2)}, u32[]{:S(2)}) %collective-permute-start.4) | collective-permute-done | bytes 266272 | tf_op jit(solution)/shard_map/ppermute | solution.py:639
  40.5 4.9 %collective-permute-done.6.refs_6_ = f32[520,128]{1,0:T(8,128)S(1)} collective-permute-done((f32[520,128]{1,0:T(8,128)S(1)}, f32[520,128]{1,0:T(8,128)S(1)}, u32[]{:S(2)}, u32[]{:S(2)}) %collective-permute-start.6) | collective-permute-done | bytes 266272 | tf_op jit(solution)/shard_map/ppermute | solution.py:639
  45.4 2.5 %place_rows.1 = (f32[8,64,1024]{2,1,0:T(8,128)S(1)}, f32[4,64,1024]{2,1,0:T(8,128)}, f32[2,64,1024]{2,1,0:T(8,128)}, f32[2,64,1024]{2,1,0:T(8,128)}, f32[2,64,10...) custom-call(s32[12]{0:T(128)S(1)} %get-tuple-element.76.small_ref.refs_5_, ...), custom_call_target="tpu_custom_call" | custom-call | tf_op jit(solution)/shard_map/place_rows/pallas_call | solution.py:234
  48.0 2.2 %collective-permute-start.10 = (f32[2,64,1024]{2,1,0:T(8,128)}, f32[2,64,1024]{2,1,0:T(8,128)S(1)}, u32[]{:S(2)}, u32[]{:S(2)}) collective-permute-start(f32[2,64,1024]{2,1,0:T(8,128)} %get-tuple-element.97), channel_id=1, source_target_pairs={{0,4},{1,5},{2,6},{3,7},{4,0},{5,1},{6,2},{7,3},{8,12},{9,13},{10,... | collective-permute-start | bytes 1572872 | tf_op jit(solution)/shard_map/ppermute | solution.py:649
  50.2 0.8 collective-permute-start.11
  51.1 1.1 spread_own.2
  52.2 1.4 copy-done.18
  53.6 1.4 copy-done.20
  55.3 0.6 collective-permute-start.9
  56.0 1.7 make_tables.1
  57.7 0.7 copy-done
  58.5 1.7 copy-done.19
  60.1 1.7 copy-done.21
  61.8 7.3 %own_product.2 = (bf16[512,2560]{1,0:T(8,128)(2,1)S(1)}, bf16[512,2560]{1,0:T(8,128)(2,1)S(1)}, f32[512,2560]{1,0:T(8,128)S(1)}) custom-call(s32[40,128]{1,0:T(8,128)S(1)} %copy-done, bf16[2,512,1152]{2,1,0:T(8,128)(2,1)S(1)} %copy-done.19, bf16[2,512,1152]{2,1,0:T(8,128)(2,1)S(1)} %copy-done.21), custom_call_target="tpu_custom_call" | custom-call | flops 2684354560 | bytes 65536 | tf_op jit(solution)/shard_map/own_product/pallas_call | solution.py:447
  69.2 1.8 collective-permute-start.14
  71.0 1.7 collective-permute-start.13
  73.0 9.3 %first_product.2.refs_2_ = f32[512,2560]{1,0:T(8,128)S(1)} custom-call(s32[40,128]{1,0:T(8,128)S(1)} %copy-done, bf16[512,2560]{1,0:T(8,128)(2,1)S(1)} %get-tuple-element.93.high_ref, bf16[512,2560]{1,0:T(8,128)(2,1)S(1)} %get-tuple-element.94.low_ref, f32[4,64,1024]{2,1,0:T(8,128)} %collective-permute-done.12.refs_0_, ...), custom_call_target="tpu_custom_call", output_to_operand_aliasing={{}: (6, {})} | custom-call | flops 2684354560 | bytes 65536 | tf_op jit(solution)/shard_map/first_product/pallas_call | solution.py:587
  82.3 1.6 collective-permute-start.17
  84.0 4.9 %second_product.2.refs_2_ = f32[512,2560]{1,0:T(8,128)S(1)} custom-call(s32[40,128]{1,0:T(8,128)S(1)} %copy-done, bf16[512,2560]{1,0:T(8,128)(2,1)S(1)} %get-tuple-element.93.high_ref, bf16[512,2560]{1,0:T(8,128)(2,1)S(1)} %get-tuple-element.94.low_ref, f32[2,64,1024]{2,1,0:T(8,128)S(1)} %collective-permute-done.8.refs_0_, ...), custom_call_target="tpu_custom_call", output_to_operand_aliasing={{}: (5, {})} | custom-call | flops 1342177280 | bytes 65536 | tf_op jit(solution)/shard_map/second_product/pallas_call | solution.py:587
  89.5 4.7 %third_product.2.refs_3_ = f32[512,2560]{1,0:T(8,128)S(1)} custom-call(s32[40,128]{1,0:T(8,128)S(1)} %copy-done, bf16[512,2560]{1,0:T(8,128)(2,1)S(1)} %get-tuple-element.93.high_ref, bf16[512,2560]{1,0:T(8,128)(2,1)S(1)} %get-tuple-element.94.low_ref, f32[2,64,1024]{2,1,0:T(8,128)S(1)} %collective-permute-done.13.refs_0_, ...), custom_call_target="tpu_custom_call", output_to_operand_aliasing={{}: (5, {})} | custom-call | flops 1342177280 | bytes 65536 | tf_op jit(solution)/shard_map/third_product/pallas_call | solution.py:587
  94.2 4.5 %collective-permute-done.17.refs_0_ = f32[2,64,1024]{2,1,0:T(8,128)S(1)} collective-permute-done((f32[2,64,1024]{2,1,0:T(8,128)S(1)}, f32[2,64,1024]{2,1,0:T(8,128)S(1)}, u32[]{:S(2)}, u32[]{:S(2)}) %collective-permute-start.17) | collective-permute-done | bytes 524320 | tf_op jit(solution)/shard_map/ppermute | solution.py:649
  99.1 0.9 collective-permute-start.16
  100.1 7.5 %fourth_product.2.refs_1_ = f32[512,2560]{1,0:T(8,128)S(1)} custom-call(s32[40,128]{1,0:T(8,128)S(1)} %copy-done, bf16[512,2560]{1,0:T(8,128)(2,1)S(1)} %get-tuple-element.93.high_ref, bf16[512,2560]{1,0:T(8,128)(2,1)S(1)} %get-tuple-element.94.low_ref, f32[2,64,1024]{2,1,0:T(8,128)S(1)} %collective-permute-done.17.refs_0_, ...), custom_call_target="tpu_custom_call", output_to_operand_aliasing={{}: (6, {})} | custom-call | flops 2147483648 | bytes 65536 | tf_op jit(solution)/shard_map/fourth_product/pallas_call | solution.py:587
  107.6 3.2 %fifth_product.2.refs_2_ = f32[512,2560]{1,0:T(8,128)S(1)} custom-call(s32[40,128]{1,0:T(8,128)S(1)} %copy-done, bf16[512,2560]{1,0:T(8,128)(2,1)S(1)} %get-tuple-element.93.high_ref, bf16[512,2560]{1,0:T(8,128)(2,1)S(1)} %get-tuple-element.94.low_ref, f32[4,64,1024]{2,1,0:T(8,128)S(1)} %collective-permute-done.19.refs_0_, ...), custom_call_target="tpu_custom_call", output_to_operand_aliasing={{}: (4, {})} | custom-call | flops 805306368 | bytes 65536 | tf_op jit(solution)/shard_map/fifth_product/pallas_call | solution.py:587
  110.8 4.2 %collective-permute-done.15.refs_0_ = f32[2,64,1024]{2,1,0:T(8,128)S(1)} collective-permute-done((f32[2,64,1024]{2,1,0:T(8,128)S(1)}, f32[2,64,1024]{2,1,0:T(8,128)S(1)}, u32[]{:S(2)}, u32[]{:S(2)}) %collective-permute-start.15) | collective-permute-done | bytes 524320 | tf_op jit(solution)/shard_map/ppermute | solution.py:649
  115.0 7.1 %last_product.1 = (f32[512,2560]{1,0:T(8,128)S(1)}, f32[2]{0:T(128)S(1)}, f32[8,64,1024]{2,1,0:T(8,128)S(1)}, f32[4,64,1024]{2,1,0:T(8,128)S(1)}, f32[2,64,1024]...) custom-call(s32[40,128]{1,0:T(8,128)S(1)} %copy-done.1, ...), custom_call_target="tpu_custom_call", output_to_operand_aliasing={{0}: (5, {})} | custom-call | flops 1073741824 | bytes 65536 | tf_op jit(solution)/shard_map/last_product/pallas_call | solution.py:587
  122.2 2.0 %collective-permute-start.23 = (f32[2,64,1024]{2,1,0:T(8,128)S(1)}, f32[2,64,1024]{2,1,0:T(8,128)S(1)}, u32[]{:S(2)}, u32[]{:S(2)}) collective-permute-start(f32[2,64,1024]{2,1,0:T(8,128)S(1)} %get-tuple-element.126), channel_id=1, source_target_pairs={{0,4},{1,5},{2,6},{3,7},{4,0},{5,1},{6,2},{7,3},{8,12},{9,13},{10,... | collective-permute-start | bytes 1572872 | tf_op jit(solution)/shard_map/ppermute | solution.py:649
  124.4 1.1 spread_own.3
  125.5 0.8 collective-permute-start.21
  126.3 1.0 collective-permute-start.22
  127.2 7.2 %own_product.3 = (bf16[512,2560]{1,0:T(8,128)(2,1)S(1)}, bf16[512,2560]{1,0:T(8,128)(2,1)S(1)}, f32[512,2560]{1,0:T(8,128)S(1)}) custom-call(s32[40,128]{1,0:T(8,128)S(1)} %copy-done.1, bf16[2,512,1152]{2,1,0:T(8,128)(2,1)S(1)} %get-tuple-element.120.wide_high, bf16[2,512,1152]{2,1,0:T(8,128)(2,1)S(1)} %get-tuple-element.121.wide_low), custom_call_target="tpu_custom_call" | custom-call | flops 2684354560 | bytes 65536 | tf_op jit(solution)/shard_map/own_product/pallas_call | solution.py:447
  134.5 2.6 %collective-permute-done.23.refs_1_ = f32[2,64,1024]{2,1,0:T(8,128)S(1)} collective-permute-done((f32[2,64,1024]{2,1,0:T(8,128)S(1)}, f32[2,64,1024]{2,1,0:T(8,128)S(1)}, u32[]{:S(2)}, u32[]{:S(2)}) %collective-permute-start.23) | collective-permute-done | bytes 524320 | tf_op jit(solution)/shard_map/ppermute | solution.py:649
  137.1 1.1 collective-permute-done.24.refs_2_
  138.1 0.8 collective-permute-start.27
  139.3 8.8 %first_product.3.refs_2_ = f32[512,2560]{1,0:T(8,128)S(1)} custom-call(s32[40,128]{1,0:T(8,128)S(1)} %copy-done.1, bf16[512,2560]{1,0:T(8,128)(2,1)S(1)} %get-tuple-element.122.high_ref, bf16[512,2560]{1,0:T(8,128)(2,1)S(1)} %get-tuple-element.123.low_ref, f32[4,64,1024]{2,1,0:T(8,128)S(1)} %collective-permute-done.25.refs_0_, ...), custom_call_target="tpu_custom_call", output_to_operand_aliasing={{}: (6, {})} | custom-call | flops 2684354560 | bytes 65536 | tf_op jit(solution)/shard_map/first_product/pallas_call | solution.py:587
  148.3 1.1 collective-permute-done.22.refs_1_
  149.4 4.7 %second_product.3.refs_2_ = f32[512,2560]{1,0:T(8,128)S(1)} custom-call(s32[40,128]{1,0:T(8,128)S(1)} %copy-done.1, bf16[512,2560]{1,0:T(8,128)(2,1)S(1)} %get-tuple-element.122.high_ref, bf16[512,2560]{1,0:T(8,128)(2,1)S(1)} %get-tuple-element.123.low_ref, f32[2,64,1024]{2,1,0:T(8,128)S(1)} %collective-permute-done.21.refs_0_, ...), custom_call_target="tpu_custom_call", output_to_operand_aliasing={{}: (5, {})} | custom-call | flops 1342177280 | bytes 65536 | tf_op jit(solution)/shard_map/second_product/pallas_call | solution.py:587
  154.1 5.1 %collective-permute-done.27.refs_1_ = f32[2,64,1024]{2,1,0:T(8,128)S(1)} collective-permute-done((f32[2,64,1024]{2,1,0:T(8,128)S(1)}, f32[2,64,1024]{2,1,0:T(8,128)S(1)}, u32[]{:S(2)}, u32[]{:S(2)}) %collective-permute-start.27) | collective-permute-done | bytes 524320 | tf_op jit(solution)/shard_map/ppermute | solution.py:649
  159.3 1.2 collective-permute-done.31.refs_1_
  160.6 4.7 %third_product.3.refs_3_ = f32[512,2560]{1,0:T(8,128)S(1)} custom-call(s32[40,128]{1,0:T(8,128)S(1)} %copy-done.1, bf16[512,2560]{1,0:T(8,128)(2,1)S(1)} %get-tuple-element.122.high_ref, bf16[512,2560]{1,0:T(8,128)(2,1)S(1)} %get-tuple-element.123.low_ref, f32[2,64,1024]{2,1,0:T(8,128)S(1)} %collective-permute-done.26.refs_0_, ...), custom_call_target="tpu_custom_call", output_to_operand_aliasing={{}: (5, {})} | custom-call | flops 1342177280 | bytes 65536 | tf_op jit(solution)/shard_map/third_product/pallas_call | solution.py:587
  166.0 0.9 collective-permute-start.29
  166.9 7.5 %fourth_product.3.refs_1_ = f32[512,2560]{1,0:T(8,128)S(1)} custom-call(s32[40,128]{1,0:T(8,128)S(1)} %copy-done.1, bf16[512,2560]{1,0:T(8,128)(2,1)S(1)} %get-tuple-element.122.high_ref, bf16[512,2560]{1,0:T(8,128)(2,1)S(1)} %get-tuple-element.123.low_ref, f32[2,64,1024]{2,1,0:T(8,128)S(1)} %collective-permute-done.30.refs_0_, ...), custom_call_target="tpu_custom_call", output_to_operand_aliasing={{}: (6, {})} | custom-call | flops 2147483648 | bytes 65536 | tf_op jit(solution)/shard_map/fourth_product/pallas_call | solution.py:587
  174.3 3.2 %fifth_product.3.refs_2_ = f32[512,2560]{1,0:T(8,128)S(1)} custom-call(s32[40,128]{1,0:T(8,128)S(1)} %copy-done.1, bf16[512,2560]{1,0:T(8,128)(2,1)S(1)} %get-tuple-element.122.high_ref, bf16[512,2560]{1,0:T(8,128)(2,1)S(1)} %get-tuple-element.123.low_ref, f32[4,64,1024]{2,1,0:T(8,128)S(1)} %collective-permute-done.32.refs_0_, ...), custom_call_target="tpu_custom_call", output_to_operand_aliasing={{}: (4, {})} | custom-call | flops 805306368 | bytes 65536 | tf_op jit(solution)/shard_map/fifth_product/pallas_call | solution.py:587
  177.6 4.5 %collective-permute-done.28.refs_0_ = f32[2,64,1024]{2,1,0:T(8,128)S(1)} collective-permute-done((f32[2,64,1024]{2,1,0:T(8,128)S(1)}, f32[2,64,1024]{2,1,0:T(8,128)S(1)}, u32[]{:S(2)}, u32[]{:S(2)}) %collective-permute-start.28) | collective-permute-done | bytes 524320 | tf_op jit(solution)/shard_map/ppermute | solution.py:649
  182.1 2.8 %trace_product.1 = (f32[512,2560]{1,0:T(8,128)S(1)}, f32[3]{0:T(128)S(1)}) custom-call(s32[40,128]{1,0:T(8,128)S(1)} %copy-done.1, bf16[512,2560]{1,0:T(8,128)(2,1)S(1)} %get-tuple-element.122.high_ref, bf16[512,2560]{1,0:T(8,128)(2,1)S(1)} %get-tuple-element.123.low_ref, ...), custom_call_target="tpu_custom_call", output_to_operand_aliasing={{0}: (5, {})} | custom-call | flops 268435456 | bytes 65536 | tf_op jit(solution)/shard_map/trace_product/pallas_call | solution.py:587
  185.1 1.2 collective-permute-start.35
  186.9 3.2 %other_product.1.total_ref = f32[512,2560]{1,0:T(8,128)S(1)} custom-call(s32[40,128]{1,0:T(8,128)S(1)} %copy-done.1, bf16[512,2560]{1,0:T(8,128)(2,1)S(1)} %get-tuple-element.122.high_ref, bf16[512,2560]{1,0:T(8,128)(2,1)S(1)} %get-tuple-element.123.low_ref, f32[2,64,1024]{2,1,0:T(8,128)S(1)} %collective-permute-done.28.refs_0_, ...), custom_call_target="tpu_custom_call", output_to_operand_aliasing={{}: (5, {})} | custom-call | flops 805306368 | bytes 65536 | tf_op jit(solution)/shard_map/other_product/pallas_call | solution.py:587
  190.3 2.8 %collective-permute-start.38 = (f32[3]{0:T(128)S(1)}, f32[3]{0:T(128)S(1)}, u32[]{:S(2)}, u32[]{:S(2)}) collective-permute-start(f32[3]{0:T(128)S(1)} %add_add_fusion.1), channel_id=1, source_target_pairs={{0,8},{1,9},{2,10},{3,11},{4,12},{5,13},{6,14},{7,15},{8,0},{9,1},... | collective-permute-start | bytes 44 | tf_op jit(solution)/shard_map/ppermute | solution.py:617
  193.0 0.6 collective-permute-start.37
  193.7 3.6 %finish.1 = f32[8,64,1024]{2,1,0:T(8,128)} custom-call(s32[8,16]{1,0:T(8,128)S(1)} %copy-done.11, f32[512,2560]{1,0:T(8,128)S(1)} %other_product.1.total_ref, f32[8,64,1024]{2,1,0:T(8,128)S(1)} %get-tuple-element.116.current_ref), custom_call_target="tpu_custom_call" | custom-call | flops 536870912 | bytes 65536 | tf_op jit(solution)/shard_map/finish/pallas_call | solution.py:498
  197.3 0.8 collective-permute-start.40
  198.1 3.7 %collective-permute-done.40 = f32[3]{0:T(128)S(1)} collective-permute-done((f32[3]{0:T(128)S(1)}, f32[3]{0:T(128)S(1)}, u32[]{:S(2)}, u32[]{:S(2)}) %collective-permute-start.40) | collective-permute-done | bytes 44 | tf_op jit(solution)/shard_map/ppermute | solution.py:617
  (92 shorter events, 5.4 us)
Async XLA Ops:
  0.6 1.6 copy-start.2
  2.2 0.7 copy-start.14
  2.9 0.7 copy-start.16
  3.6 0.7 copy-start.17
  5.5 39.9 %copy-start.15 = (s32[8,16]{1,0:T(8,128)}, s32[8,16]{1,0:T(8,128)S(1)}, u32[]{:S(2)}) copy-start(s32[8,16]{1,0:T(8,128)S(1)} %get-tuple-element.77.cols_ref) | copy-start | bytes 1540
  5.5 50.4 %copy-start.12 = (s32[12]{0:T(128)}, s32[12]{0:T(128)S(1)}, u32[]{:S(2)}) copy-start(s32[12]{0:T(128)S(1)} %get-tuple-element.76.small_ref.refs_5_) | copy-start | bytes 148
  5.5 12.9 %collective-permute-start = (f32[520,128]{1,0:T(8,128)S(1)}, f32[520,128]{1,0:T(8,128)S(1)}, u32[]{:S(2)}, u32[]{:S(2)}) collective-permute-start(f32[520,128]{1,0:T(8,128)S(1)} %get-tuple-element.78), channel_id=1, source_target_pairs={{0,3},{1,0},{2,1},{3,2},{4,7},{5,4},{6,5},{7,6},{8,11},{9,8},{10,9... | collective-permute-start | bytes 798728 | tf_op jit(solution)/shard_map/ppermute | solution.py:639
  8.0 15.6 %collective-permute-start.1 = (f32[520,128]{1,0:T(8,128)S(1)}, f32[520,128]{1,0:T(8,128)S(1)}, u32[]{:S(2)}, u32[]{:S(2)}) collective-permute-start(f32[520,128]{1,0:T(8,128)S(1)} %get-tuple-element.79), channel_id=1, source_target_pairs={{0,1},{1,2},{2,3},{3,0},{4,5},{5,6},{6,7},{7,4},{8,9},{9,10},{10,1... | collective-permute-start | bytes 798728 | tf_op jit(solution)/shard_map/ppermute | solution.py:639
  8.0 16.8 %collective-permute-start.2 = (f32[520,128]{1,0:T(8,128)S(1)}, f32[520,128]{1,0:T(8,128)S(1)}, u32[]{:S(2)}, u32[]{:S(2)}) collective-permute-start(f32[520,128]{1,0:T(8,128)S(1)} %get-tuple-element.80), channel_id=1, source_target_pairs={{0,31},{1,28},{2,29},{3,30},{4,3},{5,0},{6,1},{7,2},{8,7},{9,4},{1... | collective-permute-start | bytes 798728 | tf_op jit(solution)/shard_map/ppermute | solution.py:639
  13.7 20.1 %collective-permute-start.3 = (f32[520,128]{1,0:T(8,128)S(1)}, f32[520,128]{1,0:T(8,128)S(1)}, u32[]{:S(2)}, u32[]{:S(2)}) collective-permute-start(f32[520,128]{1,0:T(8,128)S(1)} %get-tuple-element.81), channel_id=1, source_target_pairs={{0,5},{1,6},{2,7},{3,4},{4,9},{5,10},{6,11},{7,8},{8,13},{9,14},{1... | collective-permute-start | bytes 798728 | tf_op jit(solution)/shard_map/ppermute | solution.py:639
  13.7 26.8 %collective-permute-start.4 = (f32[520,128]{1,0:T(8,128)S(1)}, f32[520,128]{1,0:T(8,128)S(1)}, u32[]{:S(2)}, u32[]{:S(2)}) collective-permute-start(f32[520,128]{1,0:T(8,128)S(1)} %get-tuple-element.82), channel_id=1, source_target_pairs={{0,29},{1,30},{2,31},{3,28},{4,1},{5,2},{6,3},{7,0},{8,5},{9,6},{1... | collective-permute-start | bytes 798728 | tf_op jit(solution)/shard_map/ppermute | solution.py:639
  18.5 37.5 %copy-start.3 = (f32[520,128]{1,0:T(8,128)}, f32[520,128]{1,0:T(8,128)S(1)}, u32[]{:S(2)}) copy-start(f32[520,128]{1,0:T(8,128)S(1)} %collective-permute-done.refs_0_) | copy-start | bytes 798724
  18.5 22.0 %collective-permute-start.5 = (f32[520,128]{1,0:T(8,128)S(1)}, f32[520,128]{1,0:T(8,128)S(1)}, u32[]{:S(2)}, u32[]{:S(2)}) collective-permute-start(f32[520,128]{1,0:T(8,128)S(1)} %get-tuple-element.83), channel_id=1, source_target_pairs={{0,7},{1,4},{2,5},{3,6},{4,11},{5,8},{6,9},{7,10},{8,15},{9,12},{1... | collective-permute-start | bytes 798728 | tf_op jit(solution)/shard_map/ppermute | solution.py:639
  23.6 32.3 %copy-start.4 = (f32[520,128]{1,0:T(8,128)}, f32[520,128]{1,0:T(8,128)S(1)}, u32[]{:S(2)}) copy-start(f32[520,128]{1,0:T(8,128)S(1)} %collective-permute-done.1.refs_1_) | copy-start | bytes 798724
  23.6 21.7 %collective-permute-start.6 = (f32[520,128]{1,0:T(8,128)S(1)}, f32[520,128]{1,0:T(8,128)S(1)}, u32[]{:S(2)}, u32[]{:S(2)}) collective-permute-start(f32[520,128]{1,0:T(8,128)S(1)} %get-tuple-element.84), channel_id=1, source_target_pairs={{0,28},{1,29},{2,30},{3,31},{4,0},{5,1},{6,2},{7,3},{8,4},{9,5},{1... | collective-permute-start | bytes 798728 | tf_op jit(solution)/shard_map/ppermute | solution.py:639
  24.8 31.1 %copy-start.5 = (f32[520,128]{1,0:T(8,128)}, f32[520,128]{1,0:T(8,128)S(1)}, u32[]{:S(2)}) copy-start(f32[520,128]{1,0:T(8,128)S(1)} %collective-permute-done.2.refs_2_) | copy-start | bytes 798724
  24.8 20.5 %collective-permute-start.7 = (f32[520,128]{1,0:T(8,128)S(1)}, f32[520,128]{1,0:T(8,128)S(1)}, u32[]{:S(2)}, u32[]{:S(2)}) collective-permute-start(f32[520,128]{1,0:T(8,128)S(1)} %get-tuple-element.85), channel_id=1, source_target_pairs={{0,4},{1,5},{2,6},{3,7},{4,8},{5,9},{6,10},{7,11},{8,12},{9,13},{1... | collective-permute-start | bytes 798728 | tf_op jit(solution)/shard_map/ppermute | solution.py:639
  33.8 22.1 %copy-start.6 = (f32[520,128]{1,0:T(8,128)}, f32[520,128]{1,0:T(8,128)S(1)}, u32[]{:S(2)}) copy-start(f32[520,128]{1,0:T(8,128)S(1)} %collective-permute-done.3.refs_3_) | copy-start | bytes 798724
  40.5 15.5 %copy-start.7 = (f32[520,128]{1,0:T(8,128)}, f32[520,128]{1,0:T(8,128)S(1)}, u32[]{:S(2)}) copy-start(f32[520,128]{1,0:T(8,128)S(1)} %collective-permute-done.4.refs_4_) | copy-start | bytes 798724
  40.5 15.5 %copy-start.8 = (f32[520,128]{1,0:T(8,128)}, f32[520,128]{1,0:T(8,128)S(1)}, u32[]{:S(2)}) copy-start(f32[520,128]{1,0:T(8,128)S(1)} %collective-permute-done.5.refs_5_) | copy-start | bytes 798724
  45.4 10.6 %copy-start.9 = (f32[520,128]{1,0:T(8,128)}, f32[520,128]{1,0:T(8,128)S(1)}, u32[]{:S(2)}) copy-start(f32[520,128]{1,0:T(8,128)S(1)} %collective-permute-done.6.refs_6_) | copy-start | bytes 798724
  45.4 10.6 %copy-start.10 = (f32[520,128]{1,0:T(8,128)}, f32[520,128]{1,0:T(8,128)S(1)}, u32[]{:S(2)}) copy-start(f32[520,128]{1,0:T(8,128)S(1)} %collective-permute-done.7.refs_7_) | copy-start | bytes 798724
  47.9 21.3 %collective-permute-start.12 = (f32[4,64,1024]{2,1,0:T(8,128)}, f32[4,64,1024]{2,1,0:T(8,128)}, u32[]{:S(2)}, u32[]{:S(2)}) collective-permute-start(f32[4,64,1024]{2,1,0:T(8,128)} %get-tuple-element.99), channel_id=1, source_target_pairs={{0,1},{1,0},{2,3},{3,2},{4,5},{5,4},{6,7},{7,6},{8,9},{9,8},{10,11... | collective-permute-start | bytes 3145736 | tf_op jit(solution)/shard_map/ppermute | solution.py:649
  48.0 21.1 %collective-permute-start.10 = (f32[2,64,1024]{2,1,0:T(8,128)}, f32[2,64,1024]{2,1,0:T(8,128)S(1)}, u32[]{:S(2)}, u32[]{:S(2)}) collective-permute-start(f32[2,64,1024]{2,1,0:T(8,128)} %get-tuple-element.97), channel_id=1, source_target_pairs={{0,4},{1,5},{2,6},{3,7},{4,0},{5,1},{6,2},{7,3},{8,12},{9,13},{10,... | collective-permute-start | bytes 1572872 | tf_op jit(solution)/shard_map/ppermute | solution.py:649
  50.2 18.9 %collective-permute-start.11 = (f32[2,64,1024]{2,1,0:T(8,128)}, f32[2,64,1024]{2,1,0:T(8,128)}, u32[]{:S(2)}, u32[]{:S(2)}) collective-permute-start(f32[2,64,1024]{2,1,0:T(8,128)} %get-tuple-element.98), channel_id=1, source_target_pairs={{0,3},{1,2},{2,1},{3,0},{4,7},{5,6},{6,5},{7,4},{8,11},{9,10},{10,... | collective-permute-start | bytes 1572872 | tf_op jit(solution)/shard_map/ppermute | solution.py:649
  52.2 1.4 copy-start.18
  53.6 1.4 copy-start.20
  55.0 27.3 %collective-permute-start.8 = (f32[2,64,1024]{2,1,0:T(8,128)}, f32[2,64,1024]{2,1,0:T(8,128)S(1)}, u32[]{:S(2)}, u32[]{:S(2)}) collective-permute-start(f32[2,64,1024]{2,1,0:T(8,128)} %get-tuple-element.95), channel_id=1, source_target_pairs={{0,4},{1,5},{2,6},{3,7},{4,0},{5,1},{6,2},{7,3},{8,12},{9,13},{10,... | collective-permute-start | bytes 1572872 | tf_op jit(solution)/shard_map/ppermute | solution.py:649
  55.3 27.0 %collective-permute-start.9 = (f32[2,64,1024]{2,1,0:T(8,128)}, f32[2,64,1024]{2,1,0:T(8,128)}, u32[]{:S(2)}, u32[]{:S(2)}) collective-permute-start(f32[2,64,1024]{2,1,0:T(8,128)} %get-tuple-element.96), channel_id=1, source_target_pairs={{0,3},{1,2},{2,1},{3,0},{4,7},{5,6},{6,5},{7,4},{8,11},{9,10},{10,... | collective-permute-start | bytes 1572872 | tf_op jit(solution)/shard_map/ppermute | solution.py:649
  57.7 0.7 copy-start
  58.5 1.7 copy-start.19
  60.1 1.7 copy-start.21
  69.2 19.7 %collective-permute-start.14 = (f32[2,64,1024]{2,1,0:T(8,128)}, f32[2,64,1024]{2,1,0:T(8,128)S(1)}, u32[]{:S(2)}, u32[]{:S(2)}) collective-permute-start(f32[2,64,1024]{2,1,0:T(8,128)} %collective-permute-done.11.refs_2_), channel_id=1, source_target_pairs={{0,4},{1,5},{2,6},{3,7},{4,0},{5,1},{6,2},{7,3},{8,12},{9,13},{10,... | collective-permute-start | bytes 1572872 | tf_op jit(solution)/shard_map/ppermute | solution.py:649
  71.0 17.9 %collective-permute-start.13 = (f32[2,64,1024]{2,1,0:T(8,128)S(1)}, f32[2,64,1024]{2,1,0:T(8,128)S(1)}, u32[]{:S(2)}, u32[]{:S(2)}) collective-permute-start(f32[2,64,1024]{2,1,0:T(8,128)S(1)} %collective-permute-done.10.refs_1_), channel_id=1, source_target_pairs={{0,8},{1,9},{2,10},{3,11},{4,28},{5,29},{6,30},{7,31},{8,16},{9,17... | collective-permute-start | bytes 1572872 | tf_op jit(solution)/shard_map/ppermute | solution.py:649
  72.7 16.8 %collective-permute-start.18 = (f32[2,64,1024]{2,1,0:T(8,128)S(1)}, f32[2,64,1024]{2,1,0:T(8,128)S(1)}, u32[]{:S(2)}, u32[]{:S(2)}) collective-permute-start(f32[2,64,1024]{2,1,0:T(8,128)S(1)} %collective-permute-done.10.refs_1_), channel_id=1, source_target_pairs={{0,3},{1,2},{2,1},{3,0},{4,7},{5,6},{6,5},{7,4},{8,11},{9,10},{10,... | collective-permute-start | bytes 1572872 | tf_op jit(solution)/shard_map/ppermute | solution.py:649
  82.3 16.4 %collective-permute-start.17 = (f32[2,64,1024]{2,1,0:T(8,128)S(1)}, f32[2,64,1024]{2,1,0:T(8,128)S(1)}, u32[]{:S(2)}, u32[]{:S(2)}) collective-permute-start(f32[2,64,1024]{2,1,0:T(8,128)S(1)} %collective-permute-done.8.refs_0_), channel_id=1, source_target_pairs={{0,8},{1,9},{2,10},{3,11},{4,28},{5,29},{6,30},{7,31},{8,16},{9,17... | collective-permute-start | bytes 1572872 | tf_op jit(solution)/shard_map/ppermute | solution.py:649
  89.0 11.1 %collective-permute-start.20 = (f32[4,64,1024]{2,1,0:T(8,128)S(1)}, f32[4,64,1024]{2,1,0:T(8,128)S(1)}, u32[]{:S(2)}, u32[]{:S(2)}) collective-permute-start(f32[4,64,1024]{2,1,0:T(8,128)S(1)} %pad_maximum_fusion.1), channel_id=1, source_target_pairs={{0,1},{1,0},{2,3},{3,2},{4,5},{5,4},{6,7},{7,6},{8,9},{9,8},{10,11... | collective-permute-start | bytes 3145736 | tf_op jit(solution)/shard_map/ppermute | solution.py:649
  98.8 8.7 %collective-permute-start.19 = (f32[4,64,1024]{2,1,0:T(8,128)S(1)}, f32[4,64,1024]{2,1,0:T(8,128)S(1)}, u32[]{:S(2)}, u32[]{:S(2)}) collective-permute-start(f32[4,64,1024]{2,1,0:T(8,128)S(1)} %pad_maximum_fusion), channel_id=1, source_target_pairs={{0,1},{1,0},{2,3},{3,2},{4,5},{5,4},{6,7},{7,6},{8,9},{9,8},{10,11... | collective-permute-start | bytes 3145736 | tf_op jit(solution)/shard_map/ppermute | solution.py:649
  98.9 16.1 %collective-permute-start.15 = (f32[2,64,1024]{2,1,0:T(8,128)S(1)}, f32[2,64,1024]{2,1,0:T(8,128)S(1)}, u32[]{:S(2)}, u32[]{:S(2)}) collective-permute-start(f32[2,64,1024]{2,1,0:T(8,128)S(1)} %collective-permute-done.14.refs_1_), channel_id=1, source_target_pairs={{0,8},{1,9},{2,10},{3,11},{4,28},{5,29},{6,30},{7,31},{8,16},{9,17... | collective-permute-start | bytes 1572872 | tf_op jit(solution)/shard_map/ppermute | solution.py:649
  99.1 15.9 %collective-permute-start.16 = (f32[2,64,1024]{2,1,0:T(8,128)S(1)}, f32[2,64,1024]{2,1,0:T(8,128)S(1)}, u32[]{:S(2)}, u32[]{:S(2)}) collective-permute-start(f32[2,64,1024]{2,1,0:T(8,128)S(1)} %collective-permute-done.13.refs_0_), channel_id=1, source_target_pairs={{0,3},{1,2},{2,1},{3,0},{4,7},{5,6},{6,5},{7,4},{8,11},{9,10},{10,... | collective-permute-start | bytes 1572872 | tf_op jit(solution)/shard_map/ppermute | solution.py:649
  107.5 7.5 %copy-start.1 = (s32[40,128]{1,0:T(8,128)S(1)}, s32[40,128]{1,0:T(8,128)}, u32[]{:S(2)}) copy-start(s32[40,128]{1,0:T(8,128)} %get-tuple-element.86.table_ref) | copy-start | bytes 61444
  107.5 7.5 %copy-start.11 = (s32[8,16]{1,0:T(8,128)S(1)}, s32[8,16]{1,0:T(8,128)}, u32[]{:S(2)}) copy-start(s32[8,16]{1,0:T(8,128)} %get-tuple-element.115.refs_4_.spots_ref) | copy-start | bytes 1540
  107.5 7.5 %copy-start.13 = (s32[12]{0:T(128)S(1)}, s32[12]{0:T(128)}, u32[]{:S(2)}) copy-start(s32[12]{0:T(128)} %copy-done.12) | copy-start | bytes 148
  122.1 16.0 %collective-permute-start.25 = (f32[4,64,1024]{2,1,0:T(8,128)S(1)}, f32[4,64,1024]{2,1,0:T(8,128)S(1)}, u32[]{:S(2)}, u32[]{:S(2)}) collective-permute-start(f32[4,64,1024]{2,1,0:T(8,128)S(1)} %get-tuple-element.128), channel_id=1, source_target_pairs={{0,1},{1,0},{2,3},{3,2},{4,5},{5,4},{6,7},{7,6},{8,9},{9,8},{10,11... | collective-permute-start | bytes 3145736 | tf_op jit(solution)/shard_map/ppermute | solution.py:649
  122.2 14.9 %collective-permute-start.23 = (f32[2,64,1024]{2,1,0:T(8,128)S(1)}, f32[2,64,1024]{2,1,0:T(8,128)S(1)}, u32[]{:S(2)}, u32[]{:S(2)}) collective-permute-start(f32[2,64,1024]{2,1,0:T(8,128)S(1)} %get-tuple-element.126), channel_id=1, source_target_pairs={{0,4},{1,5},{2,6},{3,7},{4,0},{5,1},{6,2},{7,3},{8,12},{9,13},{10,... | collective-permute-start | bytes 1572872 | tf_op jit(solution)/shard_map/ppermute | solution.py:649
  124.2 13.9 %collective-permute-start.24 = (f32[2,64,1024]{2,1,0:T(8,128)S(1)}, f32[2,64,1024]{2,1,0:T(8,128)S(1)}, u32[]{:S(2)}, u32[]{:S(2)}) collective-permute-start(f32[2,64,1024]{2,1,0:T(8,128)S(1)} %get-tuple-element.127), channel_id=1, source_target_pairs={{0,3},{1,2},{2,1},{3,0},{4,7},{5,6},{6,5},{7,4},{8,11},{9,10},{10,... | collective-permute-start | bytes 1572872 | tf_op jit(solution)/shard_map/ppermute | solution.py:649
  125.5 22.8 %collective-permute-start.21 = (f32[2,64,1024]{2,1,0:T(8,128)S(1)}, f32[2,64,1024]{2,1,0:T(8,128)S(1)}, u32[]{:S(2)}, u32[]{:S(2)}) collective-permute-start(f32[2,64,1024]{2,1,0:T(8,128)S(1)} %get-tuple-element.124), channel_id=1, source_target_pairs={{0,4},{1,5},{2,6},{3,7},{4,0},{5,1},{6,2},{7,3},{8,12},{9,13},{10,... | collective-permute-start | bytes 1572872 | tf_op jit(solution)/shard_map/ppermute | solution.py:649
  126.3 23.1 %collective-permute-start.22 = (f32[2,64,1024]{2,1,0:T(8,128)S(1)}, f32[2,64,1024]{2,1,0:T(8,128)S(1)}, u32[]{:S(2)}, u32[]{:S(2)}) collective-permute-start(f32[2,64,1024]{2,1,0:T(8,128)S(1)} %get-tuple-element.125), channel_id=1, source_target_pairs={{0,3},{1,2},{2,1},{3,0},{4,7},{5,6},{6,5},{7,4},{8,11},{9,10},{10,... | collective-permute-start | bytes 1572872 | tf_op jit(solution)/shard_map/ppermute | solution.py:649
  138.1 21.1 %collective-permute-start.27 = (f32[2,64,1024]{2,1,0:T(8,128)S(1)}, f32[2,64,1024]{2,1,0:T(8,128)S(1)}, u32[]{:S(2)}, u32[]{:S(2)}) collective-permute-start(f32[2,64,1024]{2,1,0:T(8,128)S(1)} %collective-permute-done.24.refs_2_), channel_id=1, source_target_pairs={{0,4},{1,5},{2,6},{3,7},{4,0},{5,1},{6,2},{7,3},{8,12},{9,13},{10,... | collective-permute-start | bytes 1572872 | tf_op jit(solution)/shard_map/ppermute | solution.py:649
  139.0 20.2 %collective-permute-start.26 = (f32[2,64,1024]{2,1,0:T(8,128)S(1)}, f32[2,64,1024]{2,1,0:T(8,128)S(1)}, u32[]{:S(2)}, u32[]{:S(2)}) collective-permute-start(f32[2,64,1024]{2,1,0:T(8,128)S(1)} %collective-permute-done.23.refs_1_), channel_id=1, source_target_pairs={{0,8},{1,9},{2,10},{3,11},{4,28},{5,29},{6,30},{7,31},{8,16},{9,17... | collective-permute-start | bytes 1572872 | tf_op jit(solution)/shard_map/ppermute | solution.py:649
  139.0 21.6 %collective-permute-start.31 = (f32[2,64,1024]{2,1,0:T(8,128)S(1)}, f32[2,64,1024]{2,1,0:T(8,128)S(1)}, u32[]{:S(2)}, u32[]{:S(2)}) collective-permute-start(f32[2,64,1024]{2,1,0:T(8,128)S(1)} %collective-permute-done.23.refs_1_), channel_id=1, source_target_pairs={{0,3},{1,2},{2,1},{3,0},{4,7},{5,6},{6,5},{7,4},{8,11},{9,10},{10,... | collective-permute-start | bytes 1572872 | tf_op jit(solution)/shard_map/ppermute | solution.py:649
  149.4 16.4 %collective-permute-start.30 = (f32[2,64,1024]{2,1,0:T(8,128)S(1)}, f32[2,64,1024]{2,1,0:T(8,128)S(1)}, u32[]{:S(2)}, u32[]{:S(2)}) collective-permute-start(f32[2,64,1024]{2,1,0:T(8,128)S(1)} %collective-permute-done.21.refs_0_), channel_id=1, source_target_pairs={{0,8},{1,9},{2,10},{3,11},{4,28},{5,29},{6,30},{7,31},{8,16},{9,17... | collective-permute-start | bytes 1572872 | tf_op jit(solution)/shard_map/ppermute | solution.py:649
  159.3 7.6 %collective-permute-start.33 = (f32[4,64,1024]{2,1,0:T(8,128)S(1)}, f32[4,64,1024]{2,1,0:T(8,128)S(1)}, u32[]{:S(2)}, u32[]{:S(2)}) collective-permute-start(f32[4,64,1024]{2,1,0:T(8,128)S(1)} %pad_maximum_fusion.3), channel_id=1, source_target_pairs={{0,1},{1,0},{2,3},{3,2},{4,5},{5,4},{6,7},{7,6},{8,9},{9,8},{10,11... | collective-permute-start | bytes 3145736 | tf_op jit(solution)/shard_map/ppermute | solution.py:649
  165.9 8.5 %collective-permute-start.32 = (f32[4,64,1024]{2,1,0:T(8,128)S(1)}, f32[4,64,1024]{2,1,0:T(8,128)S(1)}, u32[]{:S(2)}, u32[]{:S(2)}) collective-permute-start(f32[4,64,1024]{2,1,0:T(8,128)S(1)} %pad_maximum_fusion.2), channel_id=1, source_target_pairs={{0,1},{1,0},{2,3},{3,2},{4,5},{5,4},{6,7},{7,6},{8,9},{9,8},{10,11... | collective-permute-start | bytes 3145736 | tf_op jit(solution)/shard_map/ppermute | solution.py:649
  165.9 16.1 %collective-permute-start.28 = (f32[2,64,1024]{2,1,0:T(8,128)S(1)}, f32[2,64,1024]{2,1,0:T(8,128)S(1)}, u32[]{:S(2)}, u32[]{:S(2)}) collective-permute-start(f32[2,64,1024]{2,1,0:T(8,128)S(1)} %collective-permute-done.27.refs_1_), channel_id=1, source_target_pairs={{0,8},{1,9},{2,10},{3,11},{4,28},{5,29},{6,30},{7,31},{8,16},{9,17... | collective-permute-start | bytes 1572872 | tf_op jit(solution)/shard_map/ppermute | solution.py:649
  166.0 16.1 %collective-permute-start.29 = (f32[2,64,1024]{2,1,0:T(8,128)S(1)}, f32[2,64,1024]{2,1,0:T(8,128)S(1)}, u32[]{:S(2)}, u32[]{:S(2)}) collective-permute-start(f32[2,64,1024]{2,1,0:T(8,128)S(1)} %collective-permute-done.26.refs_0_), channel_id=1, source_target_pairs={{0,3},{1,2},{2,1},{3,0},{4,7},{5,6},{6,5},{7,4},{8,11},{9,10},{10,... | collective-permute-start | bytes 1572872 | tf_op jit(solution)/shard_map/ppermute | solution.py:649
  184.9 5.1 %collective-permute-start.36 = (f32[3]{0:T(128)S(1)}, f32[3]{0:T(128)S(1)}, u32[]{:S(2)}, u32[]{:S(2)}) collective-permute-start(f32[3]{0:T(128)S(1)} %get-tuple-element.144), channel_id=1, source_target_pairs={{0,3},{1,2},{2,1},{3,0},{4,7},{5,6},{6,5},{7,4},{8,11},{9,10},{10,... | collective-permute-start | bytes 44 | tf_op jit(solution)/shard_map/ppermute | solution.py:617
  185.1 5.0 %collective-permute-start.35 = (f32[3]{0:T(128)S(1)}, f32[3]{0:T(128)S(1)}, u32[]{:S(2)}, u32[]{:S(2)}) collective-permute-start(f32[3]{0:T(128)S(1)} %get-tuple-element.144), channel_id=1, source_target_pairs={{0,2},{1,3},{2,0},{3,1},{4,6},{5,7},{6,4},{7,5},{8,10},{9,11},{10,... | collective-permute-start | bytes 44 | tf_op jit(solution)/shard_map/ppermute | solution.py:617
  186.3 3.8 %collective-permute-start.34 = (f32[3]{0:T(128)S(1)}, f32[3]{0:T(128)S(1)}, u32[]{:S(2)}, u32[]{:S(2)}) collective-permute-start(f32[3]{0:T(128)S(1)} %get-tuple-element.144), channel_id=1, source_target_pairs={{0,1},{1,0},{2,3},{3,2},{4,5},{5,4},{6,7},{7,6},{8,9},{9,8},{10,11... | collective-permute-start | bytes 44 | tf_op jit(solution)/shard_map/ppermute | solution.py:617
  190.1 7.1 %collective-permute-start.39 = (f32[3]{0:T(128)S(1)}, f32[3]{0:T(128)S(1)}, u32[]{:S(2)}, u32[]{:S(2)}) collective-permute-start(f32[3]{0:T(128)S(1)} %add_add_fusion.1), channel_id=1, source_target_pairs={{0,12},{1,13},{2,14},{3,15},{4,8},{5,9},{6,10},{7,11},{8,4},{9,5},... | collective-permute-start | bytes 44 | tf_op jit(solution)/shard_map/ppermute | solution.py:617
  190.3 7.0 %collective-permute-start.38 = (f32[3]{0:T(128)S(1)}, f32[3]{0:T(128)S(1)}, u32[]{:S(2)}, u32[]{:S(2)}) collective-permute-start(f32[3]{0:T(128)S(1)} %add_add_fusion.1), channel_id=1, source_target_pairs={{0,8},{1,9},{2,10},{3,11},{4,12},{5,13},{6,14},{7,15},{8,0},{9,1},... | collective-permute-start | bytes 44 | tf_op jit(solution)/shard_map/ppermute | solution.py:617
  193.0 4.2 %collective-permute-start.37 = (f32[3]{0:T(128)S(1)}, f32[3]{0:T(128)S(1)}, u32[]{:S(2)}, u32[]{:S(2)}) collective-permute-start(f32[3]{0:T(128)S(1)} %add_add_fusion.1), channel_id=1, source_target_pairs={{0,4},{1,5},{2,6},{3,7},{4,0},{5,1},{6,2},{7,3},{8,12},{9,13},{10,... | collective-permute-start | bytes 44 | tf_op jit(solution)/shard_map/ppermute | solution.py:617
  197.3 4.5 %collective-permute-start.40 = (f32[3]{0:T(128)S(1)}, f32[3]{0:T(128)S(1)}, u32[]{:S(2)}, u32[]{:S(2)}) collective-permute-start(f32[3]{0:T(128)S(1)} %add_add_fusion), channel_id=1, source_target_pairs={{0,16},{1,17},{2,18},{3,19},{4,20},{5,21},{6,22},{7,23},{8,24},{9,... | collective-permute-start | bytes 44 | tf_op jit(solution)/shard_map/ppermute | solution.py:617

commit v4 on v3

--- a/solution.py
+++ b/solution.py
@@ -317,6 +317,7 @@
         in_specs=[SMEM, full((rows, slots))] + [last] * len(arrived),
         out_specs=(full((rows, slots)), full((pool, LANES))),
         scratch_shapes=[pltpu.VMEM((pool, LANES), jnp.int32)],
+        compiler_params=pltpu.CompilerParams(vmem_limit_bytes=4 * 2**20),
         name="make_tables",
     )(small, cols, *arrived)
 
@@ -344,25 +345,28 @@
         base += ref.shape[0]
 
 
+def fill_pair(table_ref, position, spot, source, member, targets):
+    left_half = lax.broadcasted_iota(jnp.int32, (64, LANES), 1) < 64
+    at = pl.ds(pl.multiple_of(member * 64, 64), 64)
+    left = table_ref[position, spot]
+    right = table_ref[position, spot + 1]
+    from_left = pl.ds(pl.multiple_of((left & 15) * LANES, LANES), LANES)
+    from_right = pl.ds(pl.multiple_of((right & 15) * LANES, LANES), LANES)
+    for k in range(2):
+        value = jnp.where(
+            left_half, source[k][left >> 4, at, from_left], source[k][right >> 4, at, from_right]
+        )
+        for refs, row, first in targets:
+            refs[k][pl.ds(row, 64), pl.ds(pl.multiple_of(first, LANES), LANES)] = value
+
+
 def fill(table_ref, first, member, members, tile, source, targets):
-    left_half = lax.broadcasted_iota(jnp.int32, (64, LANES), 1) < 64
-    spot = tile * (TILE // 64)
     for c in range(members):
-        at = pl.ds(pl.multiple_of((member + c) * 64, 64), 64)
         for q in range(TILE // LANES):
-            left = table_ref[first + member + c, spot + 2 * q]
-            right = table_ref[first + member + c, spot + 2 * q + 1]
-            from_left = pl.ds(pl.multiple_of((left & 15) * LANES, LANES), LANES)
-            from_right = pl.ds(pl.multiple_of((right & 15) * LANES, LANES), LANES)
-            for k in range(2):
-                value = jnp.where(
-                    left_half,
-                    source[k][left >> 4, at, from_left],
-                    source[k][right >> 4, at, from_right],
-                )
-                for refs, lane in targets:
-                    to = pl.ds(pl.multiple_of(lane + q * LANES, LANES), LANES)
-                    refs[k][pl.ds(c * 64, 64), to] = value
+            fill_pair(
+                table_ref, first + member + c, tile * (TILE // 64) + 2 * q, source, member + c,
+                [(refs, c * 64, to + q * LANES) for refs, to in targets],
+            )
 
 
 def three_products(a_high, a_low, d_high, d_low):
@@ -478,7 +482,7 @@
     lax.fori_loop(0, out_ref.shape[0], one_row, 0)
 
 
-def add_traces(traces_ref, total_ref, trace_ref):
+def add_traces(traces_ref, extra_ref, total_ref, trace_ref):
     known = traces_ref.shape[0]
     for k in range(known):
         trace_ref[k] = traces_ref[k]
@@ -488,31 +492,56 @@
     for g in range(total_ref.shape[0] // 64):
         block = total_ref[g * 64 : (g + 1) * 64, (g // 2) * LANES : (g // 2 + 1) * LANES]
         found += jnp.where(spot - row == 64 * (g % 2), block, 0.0)
-    trace_ref[known] = jnp.sum(found)
-
-
-def finish(spots, total, current):
-    def kernel(spots_ref, total_ref, current_ref, out_ref):
-        extract(spots_ref, total_ref, current_ref, out_ref, True)
+    trace_ref[known] = jnp.sum(found) + (0.0 if extra_ref is None else extra_ref[0])
+
+
+def far_trace(table, c, y_0, y_1, b_0, b_1):
+    parts = [c, y_0, y_1, b_0, b_1]
+    _, block, strip = c.shape
+    places = pool_places(8)
+    members = {"C": 0, "Y": 4, "B": 8}
+
+    def kernel(table_ref, *refs):
+        part_refs, trace_ref, wide, one, two = refs[:5], refs[5], refs[6:8], refs[8:10], refs[10:12]
+        spread(part_refs, *wide)
+        for k, name in enumerate("CY"):
+            for m in range(4):
+                for q in range(2):
+                    fill_pair(
+                        table_ref, places["B"][m // 2] + m % 2, places[name][q], wide,
+                        members["B"] + m, [(one, m * 64, k * TILE + q * LANES)],
+                    )
+                    fill_pair(
+                        table_ref, places[name][m // 2] + m % 2, places["B"][q], wide,
+                        members[name] + m, [(two, k * TILE + m * 64, q * LANES)],
+                    )
+        product = three_products(one[0][...], one[1][...], two[0][...], two[1][...])
+        row = lax.broadcasted_iota(jnp.int32, product.shape, 0)
+        spot = lax.broadcasted_iota(jnp.int32, product.shape, 1)
+        trace_ref[0] = jnp.sum(jnp.where(row == spot, product, 0.0))
 
     return pl.pallas_call(
         kernel,
-        out_shape=jax.ShapeDtypeStruct(current.shape, jnp.float32),
-        in_specs=[SMEM, VMEM, VMEM],
-        out_specs=VMEM,
-        compiler_params=pltpu.CompilerParams(vmem_limit_bytes=16 * 2**20),
+        out_shape=jax.ShapeDtypeStruct((1,), jnp.float32),
+        in_specs=[SMEM] + [VMEM] * 5,
+        out_specs=SMEM,
+        scratch_shapes=wide_scratch(12, strip)
+        + [pltpu.VMEM((TILE, 2 * TILE), jnp.bfloat16)] * 2
+        + [pltpu.VMEM((2 * TILE, TILE), jnp.bfloat16)] * 2,
+        compiler_params=pltpu.CompilerParams(vmem_limit_bytes=24 * 2**20),
         cost_estimate=cost(4),
-        name="finish",
-    )(spots, total, current)
-
-
-def add_product(begin, count, table, high, low, parts, total, label, lists=None, traces=None, square=None):
+        name="far_trace",
+    )(table, *parts)
+
+
+def add_product(begin, count, table, high, low, parts, total, label, traces=None, extra=None, square=None):
     depth_own, width = total.shape
     _, block, strip = parts[0].shape
     rows = depth_own // block
     each = TILE // block
     first = begin * each
-    lists = lists or [reach(begin + k) for k in range(count)]
+    lists = [reach(begin + k) for k in range(count)]
+    blend = square is not None and len(square) == 3
     starts = [sum(len(t) for t in lists[:k]) // 2 for k in range(count + 1)]
     codes = [
         [sum(t << (4 * k) for k, t in enumerate(tiles[side::2])) for side in range(2)]
@@ -535,13 +564,15 @@
         refs.pop(0)
         if traces is not None:
             traces_ref = refs.pop(0)
+        extra_ref = refs.pop(0) if extra is not None else None
         if square is not None:
             spots_ref, small_ref = refs.pop(0), refs.pop(0)
+        current_ref = refs.pop(0) if blend else None
         total_ref = refs.pop(0)
         if traces is not None:
             trace_ref = refs.pop(0)
         if square is not None:
-            out_ref, *rim_refs = (refs.pop(0) for _ in range(6))
+            out_ref, *rim_refs = (refs.pop(0) for _ in range(1 if blend else 6))
         wide, even, odd = refs[0:2], refs[2:4], refs[4:6]
         spread(part_refs, *wide)
 
@@ -562,10 +593,11 @@
 
         pipelined(starts[-1], fill_one, multiply, (even, odd))
         if traces is not None:
-            add_traces(traces_ref, total_ref, trace_ref)
+            add_traces(traces_ref, extra_ref, total_ref, trace_ref)
         if square is not None:
-            extract(spots_ref, total_ref, None, out_ref, False)
-            share(out_ref, small_ref, rim_refs)
+            extract(spots_ref, total_ref, current_ref, out_ref, blend)
+            if not blend:
+                share(out_ref, small_ref, rim_refs)
 
     ins = [table, high, low, *parts, total]
     in_specs = [SMEM] + [VMEM] * (3 + len(parts))
@@ -576,12 +608,17 @@
         in_specs.append(SMEM)
         out_shape.append(jax.ShapeDtypeStruct((traces.shape[0] + 1,), jnp.float32))
         out_specs.append(SMEM)
+    if extra is not None:
+        ins.append(extra)
+        in_specs.append(SMEM)
     if square is not None:
         ins += square
-        in_specs += [SMEM, SMEM]
+        in_specs += [SMEM, SMEM] + [VMEM] * blend
         shape = lambda n: jax.ShapeDtypeStruct((n, block, strip), jnp.float32)
-        out_shape += [shape(rows), shape(each)] + [shape(each // 2)] * 4
-        out_specs += [VMEM] * 6
+        out_shape.append(shape(rows))
+        if not blend:
+            out_shape += [shape(each)] + [shape(each // 2)] * 4
+        out_specs += [VMEM] * (len(out_shape) - len(out_specs))
     scratch = wide_scratch(count * each, strip)
     scratch += [pltpu.VMEM((TILE, 2 * TILE), jnp.bfloat16)] * 4
     return pl.pallas_call(
@@ -668,26 +705,26 @@
         (total,) = add(5, 1, parts=[b_1, ya_1], total=total, label="third_product")
         b_0, total = tie((b_0, total))
         cb = go(jnp.concatenate([b_0, b_1]), "C")
-        (total,) = add(6, 2, parts=[b_0, ya_0, ca], total=total, label="fourth_product")
-        (total,) = add(8, 1, parts=[cb], total=total, label="fifth_product")
-        last = functools.partial(add, 9, 1, parts=[yb_0, yb_1])
+        last = functools.partial(add, 9, 1, parts=[yb_0, yb_1], label="last_product")
+        fourth = functools.partial(add, 6, 2, parts=[b_0, ya_0, ca], label="fourth_product")
+        fifth = functools.partial(add, 8, 1, parts=[cb], label="fifth_product")
         if step % 2 == 0:
+            (total,) = fourth(total=total)
+            (total,) = fifth(total=total)
             total, traces, current, *shared = last(
-                total=total, label="last_product", traces=traces, square=(spots, small)
+                total=total, traces=traces, square=(spots, small)
             )
         else:
-            others = [t for t in reach(9) if t >= OWN_TILES]
-            total, traces = last(
-                total=total, label="trace_product", lists=[list(range(OWN_TILES))], traces=traces
-            )
-            sums = sum_round(traces, rounds[0])
-            (total,) = last(total=total, label="other_product", lists=[others])
+            extra = far_trace(table, c, y_0, y_1, b_0, b_1)
+            total, sums = fourth(total=total, traces=traces, extra=extra)
+            sums = sum_round(sums, rounds[0])
+            (total,) = fifth(total=total)
             sums, total = tie((sums, total))
-            sums = sum_round(sums, rounds[1])
-            current = finish(spots, total, current)
-    for perms in rounds[2:]:
-        sums, current = tie((sums, current))
-        sums = sum_round(sums, perms)
+            for perms in rounds[1:-1]:
+                sums = sum_round(sums, perms)
+            sums, total = tie((sums, total))
+            sums = sum_round(sums, rounds[-1])
+            _, current = last(total=total, square=(spots, small, current))
     sums = sums * (1.0 / (count_x * count_y * row_count * block))
     occupation = jnp.stack([sums[0], sums[1], sums[1], sums[2]])
     return (current.reshape(density.shape), occupation)

time: 203 us -> 197 us (0.970)
  local copies, waits for them, and re-layouts: 10.6 us -> 3.65 us
  starting transfers between devices: 43.8 us -> 48.4 us
  waiting for transfers between devices: 48.7 us -> 45.3 us
    unnamed x44 -> x8, local copies, waits for them, and re-layouts: 10.5 us -> 3.58 us
    ppermute x26, starting transfers between devices: 17.6 us -> 20.5 us  [shards(): go = lambda value, way: lax.ppermute(value, AXES, swap[way])]
    ppermute x26, waiting for transfers between devices: 25 us -> 22.5 us  [shards(): go = lambda value, way: lax.ppermute(value, AXES, swap[way])]
    pallas_call x13 -> x12, Pallas kernels: 71.5 us -> 73.3 us  [add_product(): pl.pallas_call(kernel, out_shape=out_shape, in_specs=in_specs, out_specs=...]
  transfers between devices with their start and end apart: 41 -> 41, of which waited for: 15 -> 15; matrix products, arithmetic and copies ran while one was open for 0% -> 0% of each run, Pallas kernels for 41% -> 45%
where the time goes in v4:
time: 197 us
  Pallas kernels  97.3 us (49%)
  starting transfers between devices  48.4 us (25%)
  waiting for transfers between devices  45.3 us (23%)
  local copies, waits for them, and re-layouts  3.65 us (2%)
    pallas_call x12, Pallas kernels, add_product(): pl.pallas_call(kernel, out_shape=out_shape, in_specs=in_specs, out_specs=...  73.3 us
    ppermute x26, waiting for transfers between devices, shards(): go = lambda value, way: lax.ppermute(value, AXES, swap[way])  22.5 us
    ppermute x26, starting transfers between devices, shards(): go = lambda value, way: lax.ppermute(value, AXES, swap[way])  20.5 us
    ppermute x8, waiting for transfers between devices, shards(): arrived[d] = lax.ppermute(leaving[d], AXES, perm)  20 us
    ppermute x8, starting transfers between devices, shards(): arrived[d] = lax.ppermute(leaving[d], AXES, perm)  19.9 us
    pallas_call x2, Pallas kernels, own_product(): pl.pallas_call(kernel, out_shape=(dense(jnp.bfloat16), dense(jnp.bfloat16...  14.6 us
    ppermute x7, starting transfers between devices, sum_round(): others = [lax.ppermute(value, AXES, perm) for perm in perms]  8.03 us
  transfers between devices with their start and end apart: 41, of which 15 were waited for; matrix products, arithmetic and copies ran while one was open for 0% of the time, Pallas kernels for 45%

profile of v4, /device:TPU:0, one launch (start us, length us, event | category | flops | bytes accessed | tf_op | source)
XLA Modules:
  0.0 196.6 jit_solution(9433099646554003710)
XLA Ops:
  0.6 1.6 copy-done
  2.2 0.7 copy-done.1
  2.9 0.7 copy-done.2
  3.6 0.7 copy-done.3
  4.2 1.3 pack_rows.1
  5.5 2.5 %collective-permute-start = (f32[520,128]{1,0:T(8,128)S(1)}, f32[520,128]{1,0:T(8,128)S(1)}, u32[]{:S(2)}, u32[]{:S(2)}) collective-permute-start(f32[520,128]{1,0:T(8,128)S(1)} %get-tuple-element.79), channel_id=1, source_target_pairs={{0,3},{1,0},{2,1},{3,2},{4,7},{5,4},{6,5},{7,6},{8,11},{9,8},{10,9... | collective-permute-start | bytes 798728 | tf_op jit(solution)/shard_map/ppermute | solution.py:676
  8.0 5.7 %collective-permute-start.2 = (f32[520,128]{1,0:T(8,128)S(1)}, f32[520,128]{1,0:T(8,128)S(1)}, u32[]{:S(2)}, u32[]{:S(2)}) collective-permute-start(f32[520,128]{1,0:T(8,128)S(1)} %get-tuple-element.81), channel_id=1, source_target_pairs={{0,31},{1,28},{2,29},{3,30},{4,3},{5,0},{6,1},{7,2},{8,7},{9,4},{1... | collective-permute-start | bytes 798728 | tf_op jit(solution)/shard_map/ppermute | solution.py:676
  13.7 4.5 %collective-permute-start.4 = (f32[520,128]{1,0:T(8,128)S(1)}, f32[520,128]{1,0:T(8,128)S(1)}, u32[]{:S(2)}, u32[]{:S(2)}) collective-permute-start(f32[520,128]{1,0:T(8,128)S(1)} %get-tuple-element.83), channel_id=1, source_target_pairs={{0,29},{1,30},{2,31},{3,28},{4,1},{5,2},{6,3},{7,0},{8,5},{9,6},{1... | collective-permute-start | bytes 798728 | tf_op jit(solution)/shard_map/ppermute | solution.py:676
  18.4 5.2 %collective-permute-start.5 = (f32[520,128]{1,0:T(8,128)S(1)}, f32[520,128]{1,0:T(8,128)S(1)}, u32[]{:S(2)}, u32[]{:S(2)}) collective-permute-start(f32[520,128]{1,0:T(8,128)S(1)} %get-tuple-element.84), channel_id=1, source_target_pairs={{0,7},{1,4},{2,5},{3,6},{4,11},{5,8},{6,9},{7,10},{8,15},{9,12},{1... | collective-permute-start | bytes 798728 | tf_op jit(solution)/shard_map/ppermute | solution.py:676
  23.6 1.2 collective-permute-start.6
  24.8 0.8 collective-permute-start.7
  25.6 8.1 %collective-permute-done.3.refs_3_ = f32[520,128]{1,0:T(8,128)S(1)} collective-permute-done((f32[520,128]{1,0:T(8,128)S(1)}, f32[520,128]{1,0:T(8,128)S(1)}, u32[]{:S(2)}, u32[]{:S(2)}) %collective-permute-start.3) | collective-permute-done | bytes 266272 | tf_op jit(solution)/shard_map/ppermute | solution.py:676
  33.8 6.7 %collective-permute-done.4.refs_4_ = f32[520,128]{1,0:T(8,128)S(1)} collective-permute-done((f32[520,128]{1,0:T(8,128)S(1)}, f32[520,128]{1,0:T(8,128)S(1)}, u32[]{:S(2)}, u32[]{:S(2)}) %collective-permute-start.4) | collective-permute-done | bytes 266272 | tf_op jit(solution)/shard_map/ppermute | solution.py:676
  40.5 4.9 %collective-permute-done.6.refs_6_ = f32[520,128]{1,0:T(8,128)S(1)} collective-permute-done((f32[520,128]{1,0:T(8,128)S(1)}, f32[520,128]{1,0:T(8,128)S(1)}, u32[]{:S(2)}, u32[]{:S(2)}) %collective-permute-start.6) | collective-permute-done | bytes 266272 | tf_op jit(solution)/shard_map/ppermute | solution.py:676
  45.3 1.2 place_rows.1
  46.8 2.2 %collective-permute-start.10 = (f32[2,64,1024]{2,1,0:T(8,128)S(1)}, f32[2,64,1024]{2,1,0:T(8,128)S(1)}, u32[]{:S(2)}, u32[]{:S(2)}) collective-permute-start(f32[2,64,1024]{2,1,0:T(8,128)S(1)} %get-tuple-element.98), channel_id=1, source_target_pairs={{0,4},{1,5},{2,6},{3,7},{4,0},{5,1},{6,2},{7,3},{8,12},{9,13},{10,... | collective-permute-start | bytes 1572872 | tf_op jit(solution)/shard_map/ppermute | solution.py:686
  49.0 0.8 collective-permute-start.11
  49.8 1.1 spread_own.2
  50.9 0.3 collective-permute-start.8
  51.3 0.7 collective-permute-start.9
  52.0 0.8 make_tables.1
  52.8 7.3 %own_product.2 = (bf16[512,2560]{1,0:T(8,128)(2,1)S(1)}, bf16[512,2560]{1,0:T(8,128)(2,1)S(1)}, f32[512,2560]{1,0:T(8,128)S(1)}) custom-call(s32[40,128]{1,0:T(8,128)S(1)} %get-tuple-element.87.table_ref, bf16[2,512,1152]{2,1,0:T(8,128)(2,1)S(1)} %get-tuple-element.92.wide_high, bf16[2,512,1152]{2,1,0:T(8,128)(2,1)S(1)} %get-tuple-element.93.wide_low), custom_call_target="tpu_custom_call" | custom-call | flops 2684354560 | bytes 65536 | tf_op jit(solution)/shard_map/own_product/pallas_call | solution.py:451
  60.1 1.6 collective-permute-done.10.refs_1_
  61.7 1.1 collective-permute-done.11.refs_2_
  62.9 1.8 collective-permute-start.13
  64.6 3.4 %collective-permute-start.14 = (f32[2,64,1024]{2,1,0:T(8,128)S(1)}, f32[2,64,1024]{2,1,0:T(8,128)S(1)}, u32[]{:S(2)}, u32[]{:S(2)}) collective-permute-start(f32[2,64,1024]{2,1,0:T(8,128)S(1)} %collective-permute-done.11.refs_2_), channel_id=1, source_target_pairs={{0,4},{1,5},{2,6},{3,7},{4,0},{5,1},{6,2},{7,3},{8,12},{9,13},{10,... | collective-permute-start | bytes 1572872 | tf_op jit(solution)/shard_map/ppermute | solution.py:686
  68.0 8.8 %first_product.2.refs_2_ = f32[512,2560]{1,0:T(8,128)S(1)} custom-call(s32[40,128]{1,0:T(8,128)S(1)} %get-tuple-element.87.table_ref, bf16[512,2560]{1,0:T(8,128)(2,1)S(1)} %get-tuple-element.94.high_ref, bf16[512,2560]{1,0:T(8,128)(2,1)S(1)} %get-tuple-element.95.low_ref, ...), custom_call_target="tpu_custom_call", output_to_operand_aliasing={{}: (6, {})} | custom-call | flops 2684354560 | bytes 65536 | tf_op jit(solution)/shard_map/first_product/pallas_call | solution.py:624
  76.9 4.7 %second_product.2.refs_2_ = f32[512,2560]{1,0:T(8,128)S(1)} custom-call(s32[40,128]{1,0:T(8,128)S(1)} %get-tuple-element.87.table_ref, bf16[512,2560]{1,0:T(8,128)(2,1)S(1)} %get-tuple-element.94.high_ref, bf16[512,2560]{1,0:T(8,128)(2,1)S(1)} %get-tuple-element.95.low_ref, ...), custom_call_target="tpu_custom_call", output_to_operand_aliasing={{}: (5, {})} | custom-call | flops 1342177280 | bytes 65536 | tf_op jit(solution)/shard_map/second_product/pallas_call | solution.py:624
  81.6 2.4 %collective-permute-done.14.refs_1_ = f32[2,64,1024]{2,1,0:T(8,128)S(1)} collective-permute-done((f32[2,64,1024]{2,1,0:T(8,128)S(1)}, f32[2,64,1024]{2,1,0:T(8,128)S(1)}, u32[]{:S(2)}, u32[]{:S(2)}) %collective-permute-start.14) | collective-permute-done | bytes 524320 | tf_op jit(solution)/shard_map/ppermute | solution.py:686
  84.1 1.2 collective-permute-done.18.refs_1_
  85.3 4.7 %third_product.2.refs_3_ = f32[512,2560]{1,0:T(8,128)S(1)} custom-call(s32[40,128]{1,0:T(8,128)S(1)} %get-tuple-element.87.table_ref, bf16[512,2560]{1,0:T(8,128)(2,1)S(1)} %get-tuple-element.94.high_ref, bf16[512,2560]{1,0:T(8,128)(2,1)S(1)} %get-tuple-element.95.low_ref, ...), custom_call_target="tpu_custom_call", output_to_operand_aliasing={{}: (5, {})} | custom-call | flops 1342177280 | bytes 65536 | tf_op jit(solution)/shard_map/third_product/pallas_call | solution.py:624
  90.0 3.1 %collective-permute-done.17.refs_0_ = f32[2,64,1024]{2,1,0:T(8,128)S(1)} collective-permute-done((f32[2,64,1024]{2,1,0:T(8,128)S(1)}, f32[2,64,1024]{2,1,0:T(8,128)S(1)}, u32[]{:S(2)}, u32[]{:S(2)}) %collective-permute-start.17) | collective-permute-done | bytes 524320 | tf_op jit(solution)/shard_map/ppermute | solution.py:686
  93.5 1.3 collective-permute-start.16
  94.8 7.4 %fourth_product.2.refs_1_ = f32[512,2560]{1,0:T(8,128)S(1)} custom-call(s32[40,128]{1,0:T(8,128)S(1)} %get-tuple-element.87.table_ref, bf16[512,2560]{1,0:T(8,128)(2,1)S(1)} %get-tuple-element.94.high_ref, bf16[512,2560]{1,0:T(8,128)(2,1)S(1)} %get-tuple-element.95.low_ref, ...), custom_call_target="tpu_custom_call", output_to_operand_aliasing={{}: (6, {})} | custom-call | flops 2147483648 | bytes 65536 | tf_op jit(solution)/shard_map/fourth_product/pallas_call | solution.py:624
  102.2 3.2 %fifth_product.2.refs_2_ = f32[512,2560]{1,0:T(8,128)S(1)} custom-call(s32[40,128]{1,0:T(8,128)S(1)} %get-tuple-element.87.table_ref, bf16[512,2560]{1,0:T(8,128)(2,1)S(1)} %get-tuple-element.94.high_ref, bf16[512,2560]{1,0:T(8,128)(2,1)S(1)} %get-tuple-element.95.low_ref, ...), custom_call_target="tpu_custom_call", output_to_operand_aliasing={{}: (4, {})} | custom-call | flops 805306368 | bytes 65536 | tf_op jit(solution)/shard_map/fifth_product/pallas_call | solution.py:624
  105.5 3.9 %collective-permute-done.15.refs_0_ = f32[2,64,1024]{2,1,0:T(8,128)S(1)} collective-permute-done((f32[2,64,1024]{2,1,0:T(8,128)S(1)}, f32[2,64,1024]{2,1,0:T(8,128)S(1)}, u32[]{:S(2)}, u32[]{:S(2)}) %collective-permute-start.15) | collective-permute-done | bytes 524320 | tf_op jit(solution)/shard_map/ppermute | solution.py:686
  109.4 7.1 %last_product.2 = (f32[512,2560]{1,0:T(8,128)S(1)}, f32[2]{0:T(128)S(1)}, f32[8,64,1024]{2,1,0:T(8,128)S(1)}, f32[4,64,1024]{2,1,0:T(8,128)S(1)}, f32[2,64,1024]...) custom-call(s32[40,128]{1,0:T(8,128)S(1)} %get-tuple-element.87.tabl, ...), custom_call_target="tpu_custom_call", output_to_operand_aliasing={{0}: (5, {})} | custom-call | flops 1073741824 | bytes 65536 | tf_op jit(solution)/shard_map/last_product/pallas_call | solution.py:624
  116.6 0.3 collective-permute-start.23
  116.9 1.3 collective-permute-start.24
  118.1 1.1 spread_own.3
  119.3 1.8 collective-permute-start.21
  121.4 7.3 %own_product.3 = (bf16[512,2560]{1,0:T(8,128)(2,1)S(1)}, bf16[512,2560]{1,0:T(8,128)(2,1)S(1)}, f32[512,2560]{1,0:T(8,128)S(1)}) custom-call(s32[40,128]{1,0:T(8,128)S(1)} %get-tuple-element.87.table_ref, bf16[2,512,1152]{2,1,0:T(8,128)(2,1)S(1)} %get-tuple-element.121.wide_high, bf16[2,512,1152]{2,1,0:T(8,128)(2,1)S(1)} %get-tuple-element.122.wide_low), custom_call_target="tpu_custom_call" | custom-call | flops 2684354560 | bytes 65536 | tf_op jit(solution)/shard_map/own_product/pallas_call | solution.py:451
  128.7 2.7 %collective-permute-done.23.refs_1_ = f32[2,64,1024]{2,1,0:T(8,128)S(1)} collective-permute-done((f32[2,64,1024]{2,1,0:T(8,128)S(1)}, f32[2,64,1024]{2,1,0:T(8,128)S(1)}, u32[]{:S(2)}, u32[]{:S(2)}) %collective-permute-start.23) | collective-permute-done | bytes 524320 | tf_op jit(solution)/shard_map/ppermute | solution.py:686
  131.4 3.3 %collective-permute-start.27 = (f32[2,64,1024]{2,1,0:T(8,128)S(1)}, f32[2,64,1024]{2,1,0:T(8,128)S(1)}, u32[]{:S(2)}, u32[]{:S(2)}) collective-permute-start(f32[2,64,1024]{2,1,0:T(8,128)S(1)} %collective-permute-done.24.refs_2_.refs_1_), channel_id=1, source_target_pairs={{0,4},{1,5},{2,6},{3,7},{4,0},{5,1},{6,2},{7,3},{8,12},{9,13},{10,... | collective-permute-start | bytes 1572872 | tf_op jit(solution)/shard_map/ppermute | solution.py:686
  134.7 1.1 collective-permute-start.31
  135.8 8.8 %first_product.3.refs_2_ = f32[512,2560]{1,0:T(8,128)S(1)} custom-call(s32[40,128]{1,0:T(8,128)S(1)} %get-tuple-element.87.table_ref, bf16[512,2560]{1,0:T(8,128)(2,1)S(1)} %get-tuple-element.123.high_ref, bf16[512,2560]{1,0:T(8,128)(2,1)S(1)} %get-tuple-element.124.low_ref, ...), custom_call_target="tpu_custom_call", output_to_operand_aliasing={{}: (6, {})} | custom-call | flops 2684354560 | bytes 65536 | tf_op jit(solution)/shard_map/first_product/pallas_call | solution.py:624
  144.6 0.3 collective-permute-start.30
  145.0 4.7 %second_product.3.refs_2_ = f32[512,2560]{1,0:T(8,128)S(1)} custom-call(s32[40,128]{1,0:T(8,128)S(1)} %get-tuple-element.87.table_ref, bf16[512,2560]{1,0:T(8,128)(2,1)S(1)} %get-tuple-element.123.high_ref, bf16[512,2560]{1,0:T(8,128)(2,1)S(1)} %get-tuple-element.124.low_ref, ...), custom_call_target="tpu_custom_call", output_to_operand_aliasing={{}: (5, {})} | custom-call | flops 1342177280 | bytes 65536 | tf_op jit(solution)/shard_map/second_product/pallas_call | solution.py:624
  149.7 3.8 %collective-permute-done.27.refs_1_ = f32[2,64,1024]{2,1,0:T(8,128)S(1)} collective-permute-done((f32[2,64,1024]{2,1,0:T(8,128)S(1)}, f32[2,64,1024]{2,1,0:T(8,128)S(1)}, u32[]{:S(2)}, u32[]{:S(2)}) %collective-permute-start.27) | collective-permute-done | bytes 524320 | tf_op jit(solution)/shard_map/ppermute | solution.py:686
  153.6 4.7 %third_product.3.refs_3_ = f32[512,2560]{1,0:T(8,128)S(1)} custom-call(s32[40,128]{1,0:T(8,128)S(1)} %get-tuple-element.87.table_ref, bf16[512,2560]{1,0:T(8,128)(2,1)S(1)} %get-tuple-element.123.high_ref, bf16[512,2560]{1,0:T(8,128)(2,1)S(1)} %get-tuple-element.124.low_ref, ...), custom_call_target="tpu_custom_call", output_to_operand_aliasing={{}: (5, {})} | custom-call | flops 1342177280 | bytes 65536 | tf_op jit(solution)/shard_map/third_product/pallas_call | solution.py:624
  158.3 2.7 %collective-permute-done.30.refs_3_.refs_0_ = f32[2,64,1024]{2,1,0:T(8,128)S(1)} collective-permute-done((f32[2,64,1024]{2,1,0:T(8,128)S(1)}, f32[2,64,1024]{2,1,0:T(8,128)S(1)}, u32[]{:S(2)}, u32[]{:S(2)}) %collective-permute-start.30) | collective-permute-done | bytes 524320 | tf_op jit(solution)/shard_map/ppermute | solution.py:686
  161.1 0.7 collective-permute-start.29
  161.9 3.8 %far_trace.1.refs_5_ = f32[1]{0:T(128)} custom-call(s32[40,128]{1,0:T(8,128)S(1)} %get-tuple-element.87.table_ref, f32[4,64,1024]{2,1,0:T(8,128)S(1)} %collective-permute-done.25.refs_0_, f32[2,64,1024]{2,1,0:T(8,128)S(1)} %collective-permute-done.24.refs_2_.refs_1_, f32[2,64,1024]{2,1,0:T(8,128)S(1)} %collective-permute-done.22.refs_1_.refs_2_, ...), custom_call_target="tpu_custom_call" | custom-call | flops 536870912 | bytes 65536 | tf_op jit(solution)/shard_map/far_trace/pallas_call | solution.py:523
  165.7 8.8 %fourth_product.3 = (f32[512,2560]{1,0:T(8,128)S(1)}, f32[3]{0:T(128)S(1)}) custom-call(s32[40,128]{1,0:T(8,128)S(1)} %get-tuple-element.87.table_ref, bf16[512,2560]{1,0:T(8,128)(2,1)S(1)} %get-tuple-element.123.high_ref, bf16[512,2560]{1,0:T(8,128)(2,1)S(1)} %get-tuple-element.124.low_ref, ...), custom_call_target="tpu_custom_call", output_to_operand_aliasing={{0}: (6, {})} | custom-call | flops 2147483648 | bytes 65536 | tf_op jit(solution)/shard_map/fourth_product/pallas_call | solution.py:624
  174.7 1.4 collective-permute-start.34
  176.1 0.4 collective-permute-start.35
  176.5 3.2 %fifth_product.3.refs_2_ = f32[512,2560]{1,0:T(8,128)S(1)} custom-call(s32[40,128]{1,0:T(8,128)S(1)} %get-tuple-element.87.table_ref, bf16[512,2560]{1,0:T(8,128)(2,1)S(1)} %get-tuple-element.123.high_ref, bf16[512,2560]{1,0:T(8,128)(2,1)S(1)} %get-tuple-element.124.low_ref, ...), custom_call_target="tpu_custom_call", output_to_operand_aliasing={{}: (4, {})} | custom-call | flops 805306368 | bytes 65536 | tf_op jit(solution)/shard_map/fifth_product/pallas_call | solution.py:624
  179.8 2.6 %collective-permute-start.37 = (f32[3]{0:T(128)S(1)}, f32[3]{0:T(128)S(1)}, u32[]{:S(2)}, u32[]{:S(2)}) collective-permute-start(f32[3]{0:T(128)S(1)} %add_add_fusion.1), channel_id=1, source_target_pairs={{0,4},{1,5},{2,6},{3,7},{4,0},{5,1},{6,2},{7,3},{8,12},{9,13},{10,... | collective-permute-start | bytes 44 | tf_op jit(solution)/shard_map/ppermute | solution.py:654
  182.3 1.5 collective-permute-start.39
  183.9 2.0 %collective-permute-done.38 = f32[3]{0:T(128)S(1)} collective-permute-done((f32[3]{0:T(128)S(1)}, f32[3]{0:T(128)S(1)}, u32[]{:S(2)}, u32[]{:S(2)}) %collective-permute-start.38) | collective-permute-done | bytes 44 | tf_op jit(solution)/shard_map/ppermute | solution.py:654
  185.9 0.9 collective-permute-done.39
  186.8 2.0 %collective-permute-start.40 = (f32[3]{0:T(128)S(1)}, f32[3]{0:T(128)S(1)}, u32[]{:S(2)}, u32[]{:S(2)}) collective-permute-start(f32[3]{0:T(128)S(1)} %add_add_fusion), channel_id=1, source_target_pairs={{0,16},{1,17},{2,18},{3,19},{4,20},{5,21},{6,22},{7,23},{8,24},{9,... | collective-permute-start | bytes 44 | tf_op jit(solution)/shard_map/ppermute | solution.py:654
  188.8 7.2 %last_product.3 = (f32[512,2560]{1,0:T(8,128)S(1)}, f32[8,64,1024]{2,1,0:T(8,128)}) custom-call(s32[40,128]{1,0:T(8,128)S(1)} %get-tuple-element.87.table_ref, bf16[512,2560]{1,0:T(8,128)(2,1)S(1)} %get-tuple-element.123.high_ref, bf16[512,2560]{1,0:T(8,128)(2,1)S(1)} %get-tuple-element.124.low_ref, ...), custom_call_target="tpu_custom_call", output_to_operand_aliasing={{0}: (5, {})} | custom-call | flops 1073741824 | bytes 65536 | tf_op jit(solution)/shard_map/last_product/pallas_call | solution.py:624
  196.0 0.6 pad_maximum_fusion.4
  (55 shorter events, 2.0 us)
Async XLA Ops:
  0.6 1.6 copy-start
  2.2 0.7 copy-start.1
  2.9 0.7 copy-start.2
  3.6 0.7 copy-start.3
  5.5 12.9 %collective-permute-start = (f32[520,128]{1,0:T(8,128)S(1)}, f32[520,128]{1,0:T(8,128)S(1)}, u32[]{:S(2)}, u32[]{:S(2)}) collective-permute-start(f32[520,128]{1,0:T(8,128)S(1)} %get-tuple-element.79), channel_id=1, source_target_pairs={{0,3},{1,0},{2,1},{3,2},{4,7},{5,4},{6,5},{7,6},{8,11},{9,8},{10,9... | collective-permute-start | bytes 798728 | tf_op jit(solution)/shard_map/ppermute | solution.py:676
  8.0 15.6 %collective-permute-start.1 = (f32[520,128]{1,0:T(8,128)S(1)}, f32[520,128]{1,0:T(8,128)S(1)}, u32[]{:S(2)}, u32[]{:S(2)}) collective-permute-start(f32[520,128]{1,0:T(8,128)S(1)} %get-tuple-element.80), channel_id=1, source_target_pairs={{0,1},{1,2},{2,3},{3,0},{4,5},{5,6},{6,7},{7,4},{8,9},{9,10},{10,1... | collective-permute-start | bytes 798728 | tf_op jit(solution)/shard_map/ppermute | solution.py:676
  8.0 16.8 %collective-permute-start.2 = (f32[520,128]{1,0:T(8,128)S(1)}, f32[520,128]{1,0:T(8,128)S(1)}, u32[]{:S(2)}, u32[]{:S(2)}) collective-permute-start(f32[520,128]{1,0:T(8,128)S(1)} %get-tuple-element.81), channel_id=1, source_target_pairs={{0,31},{1,28},{2,29},{3,30},{4,3},{5,0},{6,1},{7,2},{8,7},{9,4},{1... | collective-permute-start | bytes 798728 | tf_op jit(solution)/shard_map/ppermute | solution.py:676
  13.7 20.1 %collective-permute-start.3 = (f32[520,128]{1,0:T(8,128)S(1)}, f32[520,128]{1,0:T(8,128)S(1)}, u32[]{:S(2)}, u32[]{:S(2)}) collective-permute-start(f32[520,128]{1,0:T(8,128)S(1)} %get-tuple-element.82), channel_id=1, source_target_pairs={{0,5},{1,6},{2,7},{3,4},{4,9},{5,10},{6,11},{7,8},{8,13},{9,14},{1... | collective-permute-start | bytes 798728 | tf_op jit(solution)/shard_map/ppermute | solution.py:676
  13.7 26.8 %collective-permute-start.4 = (f32[520,128]{1,0:T(8,128)S(1)}, f32[520,128]{1,0:T(8,128)S(1)}, u32[]{:S(2)}, u32[]{:S(2)}) collective-permute-start(f32[520,128]{1,0:T(8,128)S(1)} %get-tuple-element.83), channel_id=1, source_target_pairs={{0,29},{1,30},{2,31},{3,28},{4,1},{5,2},{6,3},{7,0},{8,5},{9,6},{1... | collective-permute-start | bytes 798728 | tf_op jit(solution)/shard_map/ppermute | solution.py:676
  18.4 22.0 %collective-permute-start.5 = (f32[520,128]{1,0:T(8,128)S(1)}, f32[520,128]{1,0:T(8,128)S(1)}, u32[]{:S(2)}, u32[]{:S(2)}) collective-permute-start(f32[520,128]{1,0:T(8,128)S(1)} %get-tuple-element.84), channel_id=1, source_target_pairs={{0,7},{1,4},{2,5},{3,6},{4,11},{5,8},{6,9},{7,10},{8,15},{9,12},{1... | collective-permute-start | bytes 798728 | tf_op jit(solution)/shard_map/ppermute | solution.py:676
  23.6 21.7 %collective-permute-start.6 = (f32[520,128]{1,0:T(8,128)S(1)}, f32[520,128]{1,0:T(8,128)S(1)}, u32[]{:S(2)}, u32[]{:S(2)}) collective-permute-start(f32[520,128]{1,0:T(8,128)S(1)} %get-tuple-element.85), channel_id=1, source_target_pairs={{0,28},{1,29},{2,30},{3,31},{4,0},{5,1},{6,2},{7,3},{8,4},{9,5},{1... | collective-permute-start | bytes 798728 | tf_op jit(solution)/shard_map/ppermute | solution.py:676
  24.8 20.5 %collective-permute-start.7 = (f32[520,128]{1,0:T(8,128)S(1)}, f32[520,128]{1,0:T(8,128)S(1)}, u32[]{:S(2)}, u32[]{:S(2)}) collective-permute-start(f32[520,128]{1,0:T(8,128)S(1)} %get-tuple-element.86), channel_id=1, source_target_pairs={{0,4},{1,5},{2,6},{3,7},{4,8},{5,9},{6,10},{7,11},{8,12},{9,13},{1... | collective-permute-start | bytes 798728 | tf_op jit(solution)/shard_map/ppermute | solution.py:676
  46.6 16.3 %collective-permute-start.12 = (f32[4,64,1024]{2,1,0:T(8,128)S(1)}, f32[4,64,1024]{2,1,0:T(8,128)S(1)}, u32[]{:S(2)}, u32[]{:S(2)}) collective-permute-start(f32[4,64,1024]{2,1,0:T(8,128)S(1)} %get-tuple-element.100), channel_id=1, source_target_pairs={{0,1},{1,0},{2,3},{3,2},{4,5},{5,4},{6,7},{7,6},{8,9},{9,8},{10,11... | collective-permute-start | bytes 3145736 | tf_op jit(solution)/shard_map/ppermute | solution.py:686
  46.8 15.0 %collective-permute-start.10 = (f32[2,64,1024]{2,1,0:T(8,128)S(1)}, f32[2,64,1024]{2,1,0:T(8,128)S(1)}, u32[]{:S(2)}, u32[]{:S(2)}) collective-permute-start(f32[2,64,1024]{2,1,0:T(8,128)S(1)} %get-tuple-element.98), channel_id=1, source_target_pairs={{0,4},{1,5},{2,6},{3,7},{4,0},{5,1},{6,2},{7,3},{8,12},{9,13},{10,... | collective-permute-start | bytes 1572872 | tf_op jit(solution)/shard_map/ppermute | solution.py:686
  49.0 13.9 %collective-permute-start.11 = (f32[2,64,1024]{2,1,0:T(8,128)S(1)}, f32[2,64,1024]{2,1,0:T(8,128)S(1)}, u32[]{:S(2)}, u32[]{:S(2)}) collective-permute-start(f32[2,64,1024]{2,1,0:T(8,128)S(1)} %get-tuple-element.99), channel_id=1, source_target_pairs={{0,3},{1,2},{2,1},{3,0},{4,7},{5,6},{6,5},{7,4},{8,11},{9,10},{10,... | collective-permute-start | bytes 1572872 | tf_op jit(solution)/shard_map/ppermute | solution.py:686
  50.9 25.8 %collective-permute-start.8 = (f32[2,64,1024]{2,1,0:T(8,128)S(1)}, f32[2,64,1024]{2,1,0:T(8,128)S(1)}, u32[]{:S(2)}, u32[]{:S(2)}) collective-permute-start(f32[2,64,1024]{2,1,0:T(8,128)S(1)} %get-tuple-element.96), channel_id=1, source_target_pairs={{0,4},{1,5},{2,6},{3,7},{4,0},{5,1},{6,2},{7,3},{8,12},{9,13},{10,... | collective-permute-start | bytes 1572872 | tf_op jit(solution)/shard_map/ppermute | solution.py:686
  51.3 25.5 %collective-permute-start.9 = (f32[2,64,1024]{2,1,0:T(8,128)S(1)}, f32[2,64,1024]{2,1,0:T(8,128)S(1)}, u32[]{:S(2)}, u32[]{:S(2)}) collective-permute-start(f32[2,64,1024]{2,1,0:T(8,128)S(1)} %get-tuple-element.97), channel_id=1, source_target_pairs={{0,3},{1,2},{2,1},{3,0},{4,7},{5,6},{6,5},{7,4},{8,11},{9,10},{10,... | collective-permute-start | bytes 1572872 | tf_op jit(solution)/shard_map/ppermute | solution.py:686
  62.9 18.7 %collective-permute-start.13 = (f32[2,64,1024]{2,1,0:T(8,128)S(1)}, f32[2,64,1024]{2,1,0:T(8,128)S(1)}, u32[]{:S(2)}, u32[]{:S(2)}) collective-permute-start(f32[2,64,1024]{2,1,0:T(8,128)S(1)} %collective-permute-done.10.refs_1_), channel_id=1, source_target_pairs={{0,8},{1,9},{2,10},{3,11},{4,28},{5,29},{6,30},{7,31},{8,16},{9,17... | collective-permute-start | bytes 1572872 | tf_op jit(solution)/shard_map/ppermute | solution.py:686
  64.6 19.3 %collective-permute-start.14 = (f32[2,64,1024]{2,1,0:T(8,128)S(1)}, f32[2,64,1024]{2,1,0:T(8,128)S(1)}, u32[]{:S(2)}, u32[]{:S(2)}) collective-permute-start(f32[2,64,1024]{2,1,0:T(8,128)S(1)} %collective-permute-done.11.refs_2_), channel_id=1, source_target_pairs={{0,4},{1,5},{2,6},{3,7},{4,0},{5,1},{6,2},{7,3},{8,12},{9,13},{10,... | collective-permute-start | bytes 1572872 | tf_op jit(solution)/shard_map/ppermute | solution.py:686
  68.0 17.3 %collective-permute-start.18 = (f32[2,64,1024]{2,1,0:T(8,128)S(1)}, f32[2,64,1024]{2,1,0:T(8,128)S(1)}, u32[]{:S(2)}, u32[]{:S(2)}) collective-permute-start(f32[2,64,1024]{2,1,0:T(8,128)S(1)} %collective-permute-done.10.refs_1_), channel_id=1, source_target_pairs={{0,3},{1,2},{2,1},{3,0},{4,7},{5,6},{6,5},{7,4},{8,11},{9,10},{10,... | collective-permute-start | bytes 1572872 | tf_op jit(solution)/shard_map/ppermute | solution.py:686
  76.8 16.3 %collective-permute-start.17 = (f32[2,64,1024]{2,1,0:T(8,128)S(1)}, f32[2,64,1024]{2,1,0:T(8,128)S(1)}, u32[]{:S(2)}, u32[]{:S(2)}) collective-permute-start(f32[2,64,1024]{2,1,0:T(8,128)S(1)} %collective-permute-done.8.refs_0_), channel_id=1, source_target_pairs={{0,8},{1,9},{2,10},{3,11},{4,28},{5,29},{6,30},{7,31},{8,16},{9,17... | collective-permute-start | bytes 1572872 | tf_op jit(solution)/shard_map/ppermute | solution.py:686
  84.1 10.7 %collective-permute-start.20 = (f32[4,64,1024]{2,1,0:T(8,128)S(1)}, f32[4,64,1024]{2,1,0:T(8,128)S(1)}, u32[]{:S(2)}, u32[]{:S(2)}) collective-permute-start(f32[4,64,1024]{2,1,0:T(8,128)S(1)} %pad_maximum_fusion.1), channel_id=1, source_target_pairs={{0,1},{1,0},{2,3},{3,2},{4,5},{5,4},{6,7},{7,6},{8,9},{9,8},{10,11... | collective-permute-start | bytes 3145736 | tf_op jit(solution)/shard_map/ppermute | solution.py:686
  93.2 9.1 %collective-permute-start.19 = (f32[4,64,1024]{2,1,0:T(8,128)S(1)}, f32[4,64,1024]{2,1,0:T(8,128)S(1)}, u32[]{:S(2)}, u32[]{:S(2)}) collective-permute-start(f32[4,64,1024]{2,1,0:T(8,128)S(1)} %pad_maximum_fusion), channel_id=1, source_target_pairs={{0,1},{1,0},{2,3},{3,2},{4,5},{5,4},{6,7},{7,6},{8,9},{9,8},{10,11... | collective-permute-start | bytes 3145736 | tf_op jit(solution)/shard_map/ppermute | solution.py:686
  93.3 16.1 %collective-permute-start.15 = (f32[2,64,1024]{2,1,0:T(8,128)S(1)}, f32[2,64,1024]{2,1,0:T(8,128)S(1)}, u32[]{:S(2)}, u32[]{:S(2)}) collective-permute-start(f32[2,64,1024]{2,1,0:T(8,128)S(1)} %collective-permute-done.14.refs_1_), channel_id=1, source_target_pairs={{0,8},{1,9},{2,10},{3,11},{4,28},{5,29},{6,30},{7,31},{8,16},{9,17... | collective-permute-start | bytes 1572872 | tf_op jit(solution)/shard_map/ppermute | solution.py:686
  93.5 15.9 %collective-permute-start.16 = (f32[2,64,1024]{2,1,0:T(8,128)S(1)}, f32[2,64,1024]{2,1,0:T(8,128)S(1)}, u32[]{:S(2)}, u32[]{:S(2)}) collective-permute-start(f32[2,64,1024]{2,1,0:T(8,128)S(1)} %collective-permute-done.13.refs_0_), channel_id=1, source_target_pairs={{0,3},{1,2},{2,1},{3,0},{4,7},{5,6},{6,5},{7,4},{8,11},{9,10},{10,... | collective-permute-start | bytes 1572872 | tf_op jit(solution)/shard_map/ppermute | solution.py:686
  116.5 14.9 %collective-permute-start.25 = (f32[4,64,1024]{2,1,0:T(8,128)S(1)}, f32[4,64,1024]{2,1,0:T(8,128)S(1)}, u32[]{:S(2)}, u32[]{:S(2)}) collective-permute-start(f32[4,64,1024]{2,1,0:T(8,128)S(1)} %get-tuple-element.129), channel_id=1, source_target_pairs={{0,1},{1,0},{2,3},{3,2},{4,5},{5,4},{6,7},{7,6},{8,9},{9,8},{10,11... | collective-permute-start | bytes 3145736 | tf_op jit(solution)/shard_map/ppermute | solution.py:686
  116.6 14.8 %collective-permute-start.23 = (f32[2,64,1024]{2,1,0:T(8,128)S(1)}, f32[2,64,1024]{2,1,0:T(8,128)S(1)}, u32[]{:S(2)}, u32[]{:S(2)}) collective-permute-start(f32[2,64,1024]{2,1,0:T(8,128)S(1)} %get-tuple-element.127), channel_id=1, source_target_pairs={{0,4},{1,5},{2,6},{3,7},{4,0},{5,1},{6,2},{7,3},{8,12},{9,13},{10,... | collective-permute-start | bytes 1572872 | tf_op jit(solution)/shard_map/ppermute | solution.py:686
  116.9 14.5 %collective-permute-start.24 = (f32[2,64,1024]{2,1,0:T(8,128)S(1)}, f32[2,64,1024]{2,1,0:T(8,128)S(1)}, u32[]{:S(2)}, u32[]{:S(2)}) collective-permute-start(f32[2,64,1024]{2,1,0:T(8,128)S(1)} %get-tuple-element.128), channel_id=1, source_target_pairs={{0,3},{1,2},{2,1},{3,0},{4,7},{5,6},{6,5},{7,4},{8,11},{9,10},{10,... | collective-permute-start | bytes 1572872 | tf_op jit(solution)/shard_map/ppermute | solution.py:686
  119.3 25.4 %collective-permute-start.21 = (f32[2,64,1024]{2,1,0:T(8,128)S(1)}, f32[2,64,1024]{2,1,0:T(8,128)S(1)}, u32[]{:S(2)}, u32[]{:S(2)}) collective-permute-start(f32[2,64,1024]{2,1,0:T(8,128)S(1)} %get-tuple-element.125), channel_id=1, source_target_pairs={{0,4},{1,5},{2,6},{3,7},{4,0},{5,1},{6,2},{7,3},{8,12},{9,13},{10,... | collective-permute-start | bytes 1572872 | tf_op jit(solution)/shard_map/ppermute | solution.py:686
  121.1 23.5 %collective-permute-start.22 = (f32[2,64,1024]{2,1,0:T(8,128)S(1)}, f32[2,64,1024]{2,1,0:T(8,128)S(1)}, u32[]{:S(2)}, u32[]{:S(2)}) collective-permute-start(f32[2,64,1024]{2,1,0:T(8,128)S(1)} %get-tuple-element.126), channel_id=1, source_target_pairs={{0,3},{1,2},{2,1},{3,0},{4,7},{5,6},{6,5},{7,4},{8,11},{9,10},{10,... | collective-permute-start | bytes 1572872 | tf_op jit(solution)/shard_map/ppermute | solution.py:686
  131.4 18.3 %collective-permute-start.26 = (f32[2,64,1024]{2,1,0:T(8,128)S(1)}, f32[2,64,1024]{2,1,0:T(8,128)S(1)}, u32[]{:S(2)}, u32[]{:S(2)}) collective-permute-start(f32[2,64,1024]{2,1,0:T(8,128)S(1)} %collective-permute-done.23.refs_1_), channel_id=1, source_target_pairs={{0,8},{1,9},{2,10},{3,11},{4,28},{5,29},{6,30},{7,31},{8,16},{9,17... | collective-permute-start | bytes 1572872 | tf_op jit(solution)/shard_map/ppermute | solution.py:686
  131.4 22.0 %collective-permute-start.27 = (f32[2,64,1024]{2,1,0:T(8,128)S(1)}, f32[2,64,1024]{2,1,0:T(8,128)S(1)}, u32[]{:S(2)}, u32[]{:S(2)}) collective-permute-start(f32[2,64,1024]{2,1,0:T(8,128)S(1)} %collective-permute-done.24.refs_2_.refs_1_), channel_id=1, source_target_pairs={{0,4},{1,5},{2,6},{3,7},{4,0},{5,1},{6,2},{7,3},{8,12},{9,13},{10,... | collective-permute-start | bytes 1572872 | tf_op jit(solution)/shard_map/ppermute | solution.py:686
  134.7 18.8 %collective-permute-start.31 = (f32[2,64,1024]{2,1,0:T(8,128)S(1)}, f32[2,64,1024]{2,1,0:T(8,128)S(1)}, u32[]{:S(2)}, u32[]{:S(2)}) collective-permute-start(f32[2,64,1024]{2,1,0:T(8,128)S(1)} %collective-permute-done.23.refs_1_), channel_id=1, source_target_pairs={{0,3},{1,2},{2,1},{3,0},{4,7},{5,6},{6,5},{7,4},{8,11},{9,10},{10,... | collective-permute-start | bytes 1572872 | tf_op jit(solution)/shard_map/ppermute | solution.py:686
  144.6 16.3 %collective-permute-start.30 = (f32[2,64,1024]{2,1,0:T(8,128)S(1)}, f32[2,64,1024]{2,1,0:T(8,128)S(1)}, u32[]{:S(2)}, u32[]{:S(2)}) collective-permute-start(f32[2,64,1024]{2,1,0:T(8,128)S(1)} %collective-permute-done.21.refs_0_), channel_id=1, source_target_pairs={{0,8},{1,9},{2,10},{3,11},{4,28},{5,29},{6,30},{7,31},{8,16},{9,17... | collective-permute-start | bytes 1572872 | tf_op jit(solution)/shard_map/ppermute | solution.py:686
  153.5 12.2 %collective-permute-start.32 = (f32[4,64,1024]{2,1,0:T(8,128)S(1)}, f32[4,64,1024]{2,1,0:T(8,128)S(1)}, u32[]{:S(2)}, u32[]{:S(2)}) collective-permute-start(f32[4,64,1024]{2,1,0:T(8,128)S(1)} %pad_maximum_fusion.2), channel_id=1, source_target_pairs={{0,1},{1,0},{2,3},{3,2},{4,5},{5,4},{6,7},{7,6},{8,9},{9,8},{10,11... | collective-permute-start | bytes 3145736 | tf_op jit(solution)/shard_map/ppermute | solution.py:686
  161.1 15.0 %collective-permute-start.36 = (f32[4,64,1024]{2,1,0:T(8,128)S(1)}, f32[4,64,1024]{2,1,0:T(8,128)S(1)}, u32[]{:S(2)}, u32[]{:S(2)}) collective-permute-start(f32[4,64,1024]{2,1,0:T(8,128)S(1)} %pad_maximum_fusion.3), channel_id=1, source_target_pairs={{0,1},{1,0},{2,3},{3,2},{4,5},{5,4},{6,7},{7,6},{8,9},{9,8},{10,11... | collective-permute-start | bytes 3145736 | tf_op jit(solution)/shard_map/ppermute | solution.py:686
  161.1 27.6 %collective-permute-start.29 = (f32[2,64,1024]{2,1,0:T(8,128)S(1)}, f32[2,64,1024]{2,1,0:T(8,128)S(1)}, u32[]{:S(2)}, u32[]{:S(2)}) collective-permute-start(f32[2,64,1024]{2,1,0:T(8,128)S(1)} %collective-permute-done.26.refs_0_.refs_4_), channel_id=1, source_target_pairs={{0,3},{1,2},{2,1},{3,0},{4,7},{5,6},{6,5},{7,4},{8,11},{9,10},{10,... | collective-permute-start | bytes 1572872 | tf_op jit(solution)/shard_map/ppermute | solution.py:686
  161.9 26.9 %collective-permute-start.28 = (f32[2,64,1024]{2,1,0:T(8,128)S(1)}, f32[2,64,1024]{2,1,0:T(8,128)S(1)}, u32[]{:S(2)}, u32[]{:S(2)}) collective-permute-start(f32[2,64,1024]{2,1,0:T(8,128)S(1)} %collective-permute-done.27.refs_1_), channel_id=1, source_target_pairs={{0,8},{1,9},{2,10},{3,11},{4,28},{5,29},{6,30},{7,31},{8,16},{9,17... | collective-permute-start | bytes 1572872 | tf_op jit(solution)/shard_map/ppermute | solution.py:686
  174.5 5.2 %collective-permute-start.33 = (f32[3]{0:T(128)S(1)}, f32[3]{0:T(128)S(1)}, u32[]{:S(2)}, u32[]{:S(2)}) collective-permute-start(f32[3]{0:T(128)S(1)} %get-tuple-element.145), channel_id=1, source_target_pairs={{0,1},{1,0},{2,3},{3,2},{4,5},{5,4},{6,7},{7,6},{8,9},{9,8},{10,11... | collective-permute-start | bytes 44 | tf_op jit(solution)/shard_map/ppermute | solution.py:654
  174.7 5.1 %collective-permute-start.34 = (f32[3]{0:T(128)S(1)}, f32[3]{0:T(128)S(1)}, u32[]{:S(2)}, u32[]{:S(2)}) collective-permute-start(f32[3]{0:T(128)S(1)} %get-tuple-element.145), channel_id=1, source_target_pairs={{0,2},{1,3},{2,0},{3,1},{4,6},{5,7},{6,4},{7,5},{8,10},{9,11},{10,... | collective-permute-start | bytes 44 | tf_op jit(solution)/shard_map/ppermute | solution.py:654
  176.1 3.6 %collective-permute-start.35 = (f32[3]{0:T(128)S(1)}, f32[3]{0:T(128)S(1)}, u32[]{:S(2)}, u32[]{:S(2)}) collective-permute-start(f32[3]{0:T(128)S(1)} %get-tuple-element.145), channel_id=1, source_target_pairs={{0,3},{1,2},{2,1},{3,0},{4,7},{5,6},{6,5},{7,4},{8,11},{9,10},{10,... | collective-permute-start | bytes 44 | tf_op jit(solution)/shard_map/ppermute | solution.py:654
  179.8 4.1 %collective-permute-start.37 = (f32[3]{0:T(128)S(1)}, f32[3]{0:T(128)S(1)}, u32[]{:S(2)}, u32[]{:S(2)}) collective-permute-start(f32[3]{0:T(128)S(1)} %add_add_fusion.1), channel_id=1, source_target_pairs={{0,4},{1,5},{2,6},{3,7},{4,0},{5,1},{6,2},{7,3},{8,12},{9,13},{10,... | collective-permute-start | bytes 44 | tf_op jit(solution)/shard_map/ppermute | solution.py:654
  182.3 3.5 %collective-permute-start.38 = (f32[3]{0:T(128)S(1)}, f32[3]{0:T(128)S(1)}, u32[]{:S(2)}, u32[]{:S(2)}) collective-permute-start(f32[3]{0:T(128)S(1)} %add_add_fusion.1), channel_id=1, source_target_pairs={{0,8},{1,9},{2,10},{3,11},{4,12},{5,13},{6,14},{7,15},{8,0},{9,1},... | collective-permute-start | bytes 44 | tf_op jit(solution)/shard_map/ppermute | solution.py:654
  182.3 4.4 %collective-permute-start.39 = (f32[3]{0:T(128)S(1)}, f32[3]{0:T(128)S(1)}, u32[]{:S(2)}, u32[]{:S(2)}) collective-permute-start(f32[3]{0:T(128)S(1)} %add_add_fusion.1), channel_id=1, source_target_pairs={{0,12},{1,13},{2,14},{3,15},{4,8},{5,9},{6,10},{7,11},{8,4},{9,5},... | collective-permute-start | bytes 44 | tf_op jit(solution)/shard_map/ppermute | solution.py:654
  186.8 9.2 %collective-permute-start.40 = (f32[3]{0:T(128)S(1)}, f32[3]{0:T(128)S(1)}, u32[]{:S(2)}, u32[]{:S(2)}) collective-permute-start(f32[3]{0:T(128)S(1)} %add_add_fusion), channel_id=1, source_target_pairs={{0,16},{1,17},{2,18},{3,19},{4,20},{5,21},{6,22},{7,23},{8,24},{9,... | collective-permute-start | bytes 44 | tf_op jit(solution)/shard_map/ppermute | solution.py:654

commit v5 on v4

--- a/solution.py
+++ b/solution.py
@@ -12,6 +12,7 @@
 AXES = ("gx", "gy")
 LANES = 128
 TILE = 256
+STEP_FLOPS = 6000 * 10**6
 
 step_x = np.array([0, 0, -1, 1, -1, 1, -1, 1])
 step_y = np.array([-1, 1, -1, 1, 1, -1, 0, 0])
@@ -36,8 +37,8 @@
     (("B", 2, 2), ("YA", 2, 2)),
     (("B", 0, 2), ("YA", 0, 2)),
     (("CA", 0, 4),),
+    (("YB", 0, 4),),
     (("CB", 0, 4),),
-    (("YB", 0, 4),),
 )
 
 
@@ -399,8 +400,8 @@
     return pl.multiple_of(tile * TILE, TILE)
 
 
-def cost(units):
-    return pl.CostEstimate(flops=units * 2**27, bytes_accessed=2**16, transcendentals=0)
+def cost(flops=STEP_FLOPS):
+    return pl.CostEstimate(flops=flops, bytes_accessed=2**16, transcendentals=0)
 
 
 def spread_own(current):
@@ -416,7 +417,7 @@
         in_specs=[VMEM],
         out_specs=(VMEM, VMEM),
         compiler_params=pltpu.CompilerParams(vmem_limit_bytes=16 * 2**20),
-        cost_estimate=cost(1),
+        cost_estimate=cost(2**28),
         name="spread_own",
     )(current)
 
@@ -456,7 +457,7 @@
         scratch_shapes=[pltpu.VMEM((depth, depth), jnp.bfloat16)] * 2
         + [pltpu.VMEM((depth, 2 * TILE), jnp.bfloat16)] * 4,
         compiler_params=pltpu.CompilerParams(vmem_limit_bytes=24 * 2**20),
-        cost_estimate=cost(2 * tiles),
+        cost_estimate=cost(),
         name="own_product",
     )(table, *wide)
 
@@ -529,12 +530,12 @@
         + [pltpu.VMEM((TILE, 2 * TILE), jnp.bfloat16)] * 2
         + [pltpu.VMEM((2 * TILE, TILE), jnp.bfloat16)] * 2,
         compiler_params=pltpu.CompilerParams(vmem_limit_bytes=24 * 2**20),
-        cost_estimate=cost(4),
+        cost_estimate=cost(2**20),
         name="far_trace",
     )(table, *parts)
 
 
-def add_product(begin, count, table, high, low, parts, total, label, traces=None, extra=None, square=None):
+def add_product(begin, count, table, high, low, parts, total, label, traces=None, extra=None, square=None, flops=STEP_FLOPS):
     depth_own, width = total.shape
     _, block, strip = parts[0].shape
     rows = depth_own // block
@@ -629,7 +630,7 @@
         scratch_shapes=scratch,
         input_output_aliases={3 + len(parts): 0},
         compiler_params=pltpu.CompilerParams(vmem_limit_bytes=24 * 2**20),
-        cost_estimate=cost(2 * starts[-1]),
+        cost_estimate=cost(flops),
         name=label,
     )(*ins)
 
@@ -639,22 +640,24 @@
     for count, at in ((count_y, 1), (count_x, 0)):
         bit = 1
         while bit < count:
-            bits = [bit, 2 * bit, 3 * bit] if 2 * bit < count else [bit]
+            reached = min(8, count // bit)
             rounds.append(
                 [
                     flat_perm(count_x, count_y, lambda i, j: (i, j ^ b) if at else (i ^ b, j))
-                    for b in bits
+                    for b in range(bit, reached * bit, bit)
                 ]
             )
-            bit *= 4
+            bit *= reached
     return rounds
 
 
-def sum_round(value, perms):
-    others = [lax.ppermute(value, AXES, perm) for perm in perms]
-    if len(others) == 1:
-        return value + others[0]
-    return (value + others[0]) + (others[1] + others[2])
+def sum_round(value, perms, beside=None):
+    values = [value] + [lax.ppermute(value, AXES, perm) for perm in perms]
+    if beside is not None:
+        *values, _ = lax.optimization_barrier((*values, beside))
+    while len(values) > 1:
+        values = [one + two for one, two in zip(values[::2], values[1::2])]
+    return values[0]
 
 
 def shards(density, moves, cols, halo_rows):
@@ -699,15 +702,15 @@
         a_0, y_1, total = tie((a_0, y_1, total))
         b_0 = go(a_0, "B")
         (total,) = add(4, 1, parts=[a_0, y_1], total=total, label="second_product")
-        a_0, b_1, ya_0, total = tie((a_0, b_1, ya_0, total))
+        b_1, ya_0, total = tie((b_1, ya_0, total))
         yb_1, yb_0 = go(b_1, "Y"), go(ya_0, "B")
         ca = go(jnp.concatenate([a_0, a_1]), "C")
         (total,) = add(5, 1, parts=[b_1, ya_1], total=total, label="third_product")
         b_0, total = tie((b_0, total))
         cb = go(jnp.concatenate([b_0, b_1]), "C")
-        last = functools.partial(add, 9, 1, parts=[yb_0, yb_1], label="last_product")
-        fourth = functools.partial(add, 6, 2, parts=[b_0, ya_0, ca], label="fourth_product")
-        fifth = functools.partial(add, 8, 1, parts=[cb], label="fifth_product")
+        last = functools.partial(add, 9, 1, parts=[cb], label="last_product")
+        fourth = functools.partial(add, 6, 2, parts=[b_0, ya_0, ca], label="fourth_product", flops=2**20)
+        fifth = functools.partial(add, 8, 1, parts=[yb_0, yb_1], label="fifth_product", flops=2**37)
         if step % 2 == 0:
             (total,) = fourth(total=total)
             (total,) = fifth(total=total)
@@ -722,9 +725,9 @@
             sums, total = tie((sums, total))
             for perms in rounds[1:-1]:
                 sums = sum_round(sums, perms)
-            sums, total = tie((sums, total))
-            sums = sum_round(sums, rounds[-1])
+                sums, total = tie((sums, total))
             _, current = last(total=total, square=(spots, small, current))
+            sums = sum_round(sums, rounds[-1], current)
     sums = sums * (1.0 / (count_x * count_y * row_count * block))
     occupation = jnp.stack([sums[0], sums[1], sums[1], sums[2]])
     return (current.reshape(density.shape), occupation)

time: 197 us -> 202 us (1.025)
  starting transfers between devices: 48.4 us -> 54.3 us
    ppermute x7 -> x10, starting transfers between devices: 8.03 us -> 13.2 us  [sum_round(): values = [value] + [lax.ppermute(value, AXES, perm) for perm in perms]]
    ppermute x26, waiting for transfers between devices: 22.5 us -> 20.1 us  [shards(): go = lambda value, way: lax.ppermute(value, AXES, swap[way])]
    ppermute x7 -> x10, waiting for transfers between devices: 2.91 us -> 4.96 us  [sum_round(): values = [value] + [lax.ppermute(value, AXES, perm) for perm in perms]]
  transfers between devices with their start and end apart: 41 -> 44, of which waited for: 15 -> 14; matrix products, arithmetic and copies ran while one was open for 0% -> 0% of each run, Pallas kernels for 45% -> 44%
where the time goes in v5:
time: 202 us
  Pallas kernels  97.2 us (48%)
  starting transfers between devices  54.3 us (27%)
  waiting for transfers between devices  45 us (22%)
  local copies, waits for them, and re-layouts  3.67 us (2%)
    pallas_call x12, Pallas kernels, add_product(): pl.pallas_call(kernel, out_shape=out_shape, in_specs=in_specs, out_specs=...  73.2 us
    ppermute x26, starting transfers between devices, shards(): go = lambda value, way: lax.ppermute(value, AXES, swap[way])  21.3 us
    ppermute x26, waiting for transfers between devices, shards(): go = lambda value, way: lax.ppermute(value, AXES, swap[way])  20.1 us
    ppermute x8, waiting for transfers between devices, shards(): arrived[d] = lax.ppermute(leaving[d], AXES, perm)  20 us
    ppermute x8, starting transfers between devices, shards(): arrived[d] = lax.ppermute(leaving[d], AXES, perm)  19.9 us
    pallas_call x2, Pallas kernels, own_product(): pl.pallas_call(kernel, out_shape=(dense(jnp.bfloat16), dense(jnp.bfloat16...  14.6 us
    ppermute x10, starting transfers between devices, sum_round(): values = [value] + [lax.ppermute(value, AXES, perm) for perm in perms]  13.2 us
    ppermute x10, waiting for transfers between devices, sum_round(): values = [value] + [lax.ppermute(value, AXES, perm) for perm in perms]  4.96 us
  transfers between devices with their start and end apart: 44, of which 14 were waited for; matrix products, arithmetic and copies ran while one was open for 0% of the time, Pallas kernels for 44%

profile of v5, /device:TPU:0, one launch (start us, length us, event | category | flops | bytes accessed | tf_op | source)
XLA Modules:
  0.0 202.1 jit_solution(5634437160335275029)
XLA Ops:
  0.6 1.6 copy-done
  2.2 0.7 copy-done.3
  2.9 0.7 copy-done.4
  3.6 0.7 copy-done.5
  4.2 1.3 pack_rows.1
  5.5 2.5 %collective-permute-start = (f32[520,128]{1,0:T(8,128)S(1)}, f32[520,128]{1,0:T(8,128)S(1)}, u32[]{:S(2)}, u32[]{:S(2)}) collective-permute-start(f32[520,128]{1,0:T(8,128)S(1)} %get-tuple-element.83), channel_id=1, source_target_pairs={{0,3},{1,0},{2,1},{3,2},{4,7},{5,4},{6,5},{7,6},{8,11},{9,8},{10,9... | collective-permute-start | bytes 798728 | tf_op jit(solution)/shard_map/ppermute | solution.py:679
  8.0 5.7 %collective-permute-start.2 = (f32[520,128]{1,0:T(8,128)S(1)}, f32[520,128]{1,0:T(8,128)S(1)}, u32[]{:S(2)}, u32[]{:S(2)}) collective-permute-start(f32[520,128]{1,0:T(8,128)S(1)} %get-tuple-element.85), channel_id=1, source_target_pairs={{0,31},{1,28},{2,29},{3,30},{4,3},{5,0},{6,1},{7,2},{8,7},{9,4},{1... | collective-permute-start | bytes 798728 | tf_op jit(solution)/shard_map/ppermute | solution.py:679
  13.7 4.5 %collective-permute-start.4 = (f32[520,128]{1,0:T(8,128)S(1)}, f32[520,128]{1,0:T(8,128)S(1)}, u32[]{:S(2)}, u32[]{:S(2)}) collective-permute-start(f32[520,128]{1,0:T(8,128)S(1)} %get-tuple-element.87), channel_id=1, source_target_pairs={{0,29},{1,30},{2,31},{3,28},{4,1},{5,2},{6,3},{7,0},{8,5},{9,6},{1... | collective-permute-start | bytes 798728 | tf_op jit(solution)/shard_map/ppermute | solution.py:679
  18.4 5.2 %collective-permute-start.5 = (f32[520,128]{1,0:T(8,128)S(1)}, f32[520,128]{1,0:T(8,128)S(1)}, u32[]{:S(2)}, u32[]{:S(2)}) collective-permute-start(f32[520,128]{1,0:T(8,128)S(1)} %get-tuple-element.88), channel_id=1, source_target_pairs={{0,7},{1,4},{2,5},{3,6},{4,11},{5,8},{6,9},{7,10},{8,15},{9,12},{1... | collective-permute-start | bytes 798728 | tf_op jit(solution)/shard_map/ppermute | solution.py:679
  23.6 1.2 collective-permute-start.6
  24.8 0.8 collective-permute-start.7
  25.6 8.1 %collective-permute-done.3.refs_3_ = f32[520,128]{1,0:T(8,128)S(1)} collective-permute-done((f32[520,128]{1,0:T(8,128)S(1)}, f32[520,128]{1,0:T(8,128)S(1)}, u32[]{:S(2)}, u32[]{:S(2)}) %collective-permute-start.3) | collective-permute-done | bytes 266272 | tf_op jit(solution)/shard_map/ppermute | solution.py:679
  33.8 6.7 %collective-permute-done.4.refs_4_ = f32[520,128]{1,0:T(8,128)S(1)} collective-permute-done((f32[520,128]{1,0:T(8,128)S(1)}, f32[520,128]{1,0:T(8,128)S(1)}, u32[]{:S(2)}, u32[]{:S(2)}) %collective-permute-start.4) | collective-permute-done | bytes 266272 | tf_op jit(solution)/shard_map/ppermute | solution.py:679
  40.5 4.9 %collective-permute-done.6.refs_6_ = f32[520,128]{1,0:T(8,128)S(1)} collective-permute-done((f32[520,128]{1,0:T(8,128)S(1)}, f32[520,128]{1,0:T(8,128)S(1)}, u32[]{:S(2)}, u32[]{:S(2)}) %collective-permute-start.6) | collective-permute-done | bytes 266272 | tf_op jit(solution)/shard_map/ppermute | solution.py:679
  45.3 1.2 place_rows.1
  46.8 1.1 spread_own.2
  47.9 2.2 %collective-permute-start.10 = (f32[2,64,1024]{2,1,0:T(8,128)S(1)}, f32[2,64,1024]{2,1,0:T(8,128)S(1)}, u32[]{:S(2)}, u32[]{:S(2)}) collective-permute-start(f32[2,64,1024]{2,1,0:T(8,128)S(1)} %get-tuple-element.102), channel_id=1, source_target_pairs={{0,4},{1,5},{2,6},{3,7},{4,0},{5,1},{6,2},{7,3},{8,12},{9,13},{10,... | collective-permute-start | bytes 1572872 | tf_op jit(solution)/shard_map/ppermute | solution.py:689
  50.1 0.9 collective-permute-start.11
  51.9 0.8 make_tables.1
  52.7 7.3 %own_product.2 = (bf16[512,2560]{1,0:T(8,128)(2,1)S(1)}, bf16[512,2560]{1,0:T(8,128)(2,1)S(1)}, f32[512,2560]{1,0:T(8,128)S(1)}) custom-call(s32[40,128]{1,0:T(8,128)S(1)} %get-tuple-element.91.table_ref, bf16[2,512,1152]{2,1,0:T(8,128)(2,1)S(1)} %get-tuple-element.96.wide_high, bf16[2,512,1152]{2,1,0:T(8,128)(2,1)S(1)} %get-tuple-element.97.wide_low), custom_call_target="tpu_custom_call" | custom-call | flops 6000000000 | bytes 65536 | tf_op jit(solution)/shard_map/own_product/pallas_call | solution.py:452
  60.0 2.8 %collective-permute-done.10.refs_1_ = f32[2,64,1024]{2,1,0:T(8,128)S(1)} collective-permute-done((f32[2,64,1024]{2,1,0:T(8,128)S(1)}, f32[2,64,1024]{2,1,0:T(8,128)S(1)}, u32[]{:S(2)}, u32[]{:S(2)}) %collective-permute-start.10) | collective-permute-done | bytes 524320 | tf_op jit(solution)/shard_map/ppermute | solution.py:689
  62.9 1.1 collective-permute-done.11.refs_2_
  64.0 1.8 collective-permute-start.14
  65.8 1.0 collective-permute-start.16
  66.8 2.4 %collective-permute-start.15 = (f32[2,64,1024]{2,1,0:T(8,128)S(1)}, f32[2,64,1024]{2,1,0:T(8,128)S(1)}, u32[]{:S(2)}, u32[]{:S(2)}) collective-permute-start(f32[2,64,1024]{2,1,0:T(8,128)S(1)} %collective-permute-done.11.refs_2_), channel_id=1, source_target_pairs={{0,4},{1,5},{2,6},{3,7},{4,0},{5,1},{6,2},{7,3},{8,12},{9,13},{10,... | collective-permute-start | bytes 1572872 | tf_op jit(solution)/shard_map/ppermute | solution.py:689
  69.2 8.8 %first_product.2.refs_2_ = f32[512,2560]{1,0:T(8,128)S(1)} custom-call(s32[40,128]{1,0:T(8,128)S(1)} %get-tuple-element.91.table_ref, bf16[512,2560]{1,0:T(8,128)(2,1)S(1)} %get-tuple-element.98.high_ref, bf16[512,2560]{1,0:T(8,128)(2,1)S(1)} %get-tuple-element.99.low_ref, ...), custom_call_target="tpu_custom_call", output_to_operand_aliasing={{}: (6, {})} | custom-call | flops 6000000000 | bytes 65536 | tf_op jit(solution)/shard_map/first_product/pallas_call | solution.py:625
  78.6 4.7 %second_product.2.refs_2_ = f32[512,2560]{1,0:T(8,128)S(1)} custom-call(s32[40,128]{1,0:T(8,128)S(1)} %get-tuple-element.91.table_ref, bf16[512,2560]{1,0:T(8,128)(2,1)S(1)} %get-tuple-element.98.high_ref, bf16[512,2560]{1,0:T(8,128)(2,1)S(1)} %get-tuple-element.99.low_ref, ...), custom_call_target="tpu_custom_call", output_to_operand_aliasing={{}: (5, {})} | custom-call | flops 6000000000 | bytes 65536 | tf_op jit(solution)/shard_map/second_product/pallas_call | solution.py:625
  83.3 1.9 collective-permute-done.15.refs_1_
  85.2 1.6 collective-permute-start.18
  86.9 4.7 %third_product.2.refs_3_ = f32[512,2560]{1,0:T(8,128)S(1)} custom-call(s32[40,128]{1,0:T(8,128)S(1)} %get-tuple-element.91.table_ref, bf16[512,2560]{1,0:T(8,128)(2,1)S(1)} %get-tuple-element.98.high_ref, bf16[512,2560]{1,0:T(8,128)(2,1)S(1)} %get-tuple-element.99.low_ref, ...), custom_call_target="tpu_custom_call", output_to_operand_aliasing={{}: (5, {})} | custom-call | flops 6000000000 | bytes 65536 | tf_op jit(solution)/shard_map/third_product/pallas_call | solution.py:625
  91.6 3.1 %collective-permute-done.13.refs_0_ = f32[2,64,1024]{2,1,0:T(8,128)S(1)} collective-permute-done((f32[2,64,1024]{2,1,0:T(8,128)S(1)}, f32[2,64,1024]{2,1,0:T(8,128)S(1)}, u32[]{:S(2)}, u32[]{:S(2)}) %collective-permute-start.13) | collective-permute-done | bytes 524320 | tf_op jit(solution)/shard_map/ppermute | solution.py:689
  94.8 7.4 %fourth_product.2.refs_2_ = f32[512,2560]{1,0:T(8,128)S(1)} custom-call(s32[40,128]{1,0:T(8,128)S(1)} %get-tuple-element.91.table_ref, bf16[512,2560]{1,0:T(8,128)(2,1)S(1)} %get-tuple-element.98.high_ref, bf16[512,2560]{1,0:T(8,128)(2,1)S(1)} %get-tuple-element.99.low_ref, ...), custom_call_target="tpu_custom_call", output_to_operand_aliasing={{}: (6, {})} | custom-call | flops 1048576 | bytes 65536 | tf_op jit(solution)/shard_map/fourth_product/pallas_call | solution.py:625
  102.3 3.1 %collective-permute-done.18.refs_0_ = f32[2,64,1024]{2,1,0:T(8,128)S(1)} collective-permute-done((f32[2,64,1024]{2,1,0:T(8,128)S(1)}, f32[2,64,1024]{2,1,0:T(8,128)S(1)}, u32[]{:S(2)}, u32[]{:S(2)}) %collective-permute-start.18) | collective-permute-done | bytes 524320 | tf_op jit(solution)/shard_map/ppermute | solution.py:689
  105.4 4.1 %fifth_product.2.refs_1_ = f32[512,2560]{1,0:T(8,128)S(1)} custom-call(s32[40,128]{1,0:T(8,128)S(1)} %get-tuple-element.91.table_ref, bf16[512,2560]{1,0:T(8,128)(2,1)S(1)} %get-tuple-element.98.high_ref, bf16[512,2560]{1,0:T(8,128)(2,1)S(1)} %get-tuple-element.99.low_ref, ...), custom_call_target="tpu_custom_call", output_to_operand_aliasing={{}: (5, {})} | custom-call | flops 137438953472 | bytes 65536 | tf_op jit(solution)/shard_map/fifth_product/pallas_call | solution.py:625
  109.5 6.1 %last_product.2 = (f32[512,2560]{1,0:T(8,128)S(1)}, f32[2]{0:T(128)S(1)}, f32[8,64,1024]{2,1,0:T(8,128)S(1)}, f32[4,64,1024]{2,1,0:T(8,128)S(1)}, f32[2,64,1024]...) custom-call(s32[40,128]{1,0:T(8,128)S(1)} %get-tuple-element.91.tabl, ...), custom_call_target="tpu_custom_call", output_to_operand_aliasing={{0}: (4, {})} | custom-call | flops 6000000000 | bytes 65536 | tf_op jit(solution)/shard_map/last_product/pallas_call | solution.py:625
  115.7 1.1 spread_own.3
  116.9 1.7 collective-permute-start.24
  118.5 1.7 collective-permute-start.21
  120.4 7.3 %own_product.3 = (bf16[512,2560]{1,0:T(8,128)(2,1)S(1)}, bf16[512,2560]{1,0:T(8,128)(2,1)S(1)}, f32[512,2560]{1,0:T(8,128)S(1)}) custom-call(s32[40,128]{1,0:T(8,128)S(1)} %get-tuple-element.91.table_ref, bf16[2,512,1152]{2,1,0:T(8,128)(2,1)S(1)} %get-tuple-element.124.wide_high, bf16[2,512,1152]{2,1,0:T(8,128)(2,1)S(1)} %get-tuple-element.125.wide_low), custom_call_target="tpu_custom_call" | custom-call | flops 6000000000 | bytes 65536 | tf_op jit(solution)/shard_map/own_product/pallas_call | solution.py:452
  127.7 3.9 %collective-permute-done.23.refs_1_ = f32[2,64,1024]{2,1,0:T(8,128)S(1)} collective-permute-done((f32[2,64,1024]{2,1,0:T(8,128)S(1)}, f32[2,64,1024]{2,1,0:T(8,128)S(1)}, u32[]{:S(2)}, u32[]{:S(2)}) %collective-permute-start.23) | collective-permute-done | bytes 524320 | tf_op jit(solution)/shard_map/ppermute | solution.py:689
  131.6 1.4 collective-permute-start.29
  133.0 1.6 collective-permute-start.28
  134.6 8.8 %first_product.3.refs_2_ = f32[512,2560]{1,0:T(8,128)S(1)} custom-call(s32[40,128]{1,0:T(8,128)S(1)} %get-tuple-element.91.table_ref, bf16[512,2560]{1,0:T(8,128)(2,1)S(1)} %get-tuple-element.126.high_ref, bf16[512,2560]{1,0:T(8,128)(2,1)S(1)} %get-tuple-element.127.low_ref, ...), custom_call_target="tpu_custom_call", output_to_operand_aliasing={{}: (6, {})} | custom-call | flops 6000000000 | bytes 65536 | tf_op jit(solution)/shard_map/first_product/pallas_call | solution.py:625
  143.4 1.8 collective-permute-start.26
  145.4 4.7 %second_product.3.refs_2_ = f32[512,2560]{1,0:T(8,128)S(1)} custom-call(s32[40,128]{1,0:T(8,128)S(1)} %get-tuple-element.91.table_ref, bf16[512,2560]{1,0:T(8,128)(2,1)S(1)} %get-tuple-element.126.high_ref, bf16[512,2560]{1,0:T(8,128)(2,1)S(1)} %get-tuple-element.127.low_ref, ...), custom_call_target="tpu_custom_call", output_to_operand_aliasing={{}: (5, {})} | custom-call | flops 6000000000 | bytes 65536 | tf_op jit(solution)/shard_map/second_product/pallas_call | solution.py:625
  150.1 3.6 %collective-permute-done.28.refs_1_ = f32[2,64,1024]{2,1,0:T(8,128)S(1)} collective-permute-done((f32[2,64,1024]{2,1,0:T(8,128)S(1)}, f32[2,64,1024]{2,1,0:T(8,128)S(1)}, u32[]{:S(2)}, u32[]{:S(2)}) %collective-permute-start.28) | collective-permute-done | bytes 524320 | tf_op jit(solution)/shard_map/ppermute | solution.py:689
  153.7 0.8 collective-permute-start.36
  154.5 4.7 %third_product.3.refs_3_ = f32[512,2560]{1,0:T(8,128)S(1)} custom-call(s32[40,128]{1,0:T(8,128)S(1)} %get-tuple-element.91.table_ref, bf16[512,2560]{1,0:T(8,128)(2,1)S(1)} %get-tuple-element.126.high_ref, bf16[512,2560]{1,0:T(8,128)(2,1)S(1)} %get-tuple-element.127.low_ref, ...), custom_call_target="tpu_custom_call", output_to_operand_aliasing={{}: (5, {})} | custom-call | flops 6000000000 | bytes 65536 | tf_op jit(solution)/shard_map/third_product/pallas_call | solution.py:625
  159.2 0.5 collective-permute-done.26.refs_3_.refs_0_
  160.1 3.8 %far_trace.1.refs_5_ = f32[1]{0:T(128)} custom-call(s32[40,128]{1,0:T(8,128)S(1)} %get-tuple-element.91.table_ref, f32[4,64,1024]{2,1,0:T(8,128)S(1)} %collective-permute-done.25.refs_0_, f32[2,64,1024]{2,1,0:T(8,128)S(1)} %collective-permute-done.24.refs_2_.refs_1_, f32[2,64,1024]{2,1,0:T(8,128)S(1)} %collective-permute-done.22.refs_1_.refs_2_, ...), custom_call_target="tpu_custom_call" | custom-call | flops 1048576 | bytes 65536 | tf_op jit(solution)/shard_map/far_trace/pallas_call | solution.py:524
  164.0 8.9 %fourth_product.3 = (f32[512,2560]{1,0:T(8,128)S(1)}, f32[3]{0:T(128)S(1)}) custom-call(s32[40,128]{1,0:T(8,128)S(1)} %get-tuple-element.91.table_ref, bf16[512,2560]{1,0:T(8,128)(2,1)S(1)} %get-tuple-element.126.high_ref, bf16[512,2560]{1,0:T(8,128)(2,1)S(1)} %get-tuple-element.127.low_ref, ...), custom_call_target="tpu_custom_call", output_to_operand_aliasing={{0}: (6, {})} | custom-call | flops 1048576 | bytes 65536 | tf_op jit(solution)/shard_map/fourth_product/pallas_call | solution.py:625
  173.1 1.2 collective-permute-start.33
  174.8 4.1 %fifth_product.3.refs_1_ = f32[512,2560]{1,0:T(8,128)S(1)} custom-call(s32[40,128]{1,0:T(8,128)S(1)} %get-tuple-element.91.table_ref, bf16[512,2560]{1,0:T(8,128)(2,1)S(1)} %get-tuple-element.126.high_ref, bf16[512,2560]{1,0:T(8,128)(2,1)S(1)} %get-tuple-element.127.low_ref, ...), custom_call_target="tpu_custom_call", output_to_operand_aliasing={{}: (5, {})} | custom-call | flops 137438953472 | bytes 65536 | tf_op jit(solution)/shard_map/fifth_product/pallas_call | solution.py:625
  178.9 1.3 collective-permute-start.37
  180.3 1.1 collective-permute-start.38
  181.3 1.2 collective-permute-start.39
  182.5 2.3 %collective-permute-start.40 = (f32[3]{0:T(128)S(1)}, f32[3]{0:T(128)S(1)}, u32[]{:S(2)}, u32[]{:S(2)}) collective-permute-start(f32[3]{0:T(128)S(1)} %add_add_fusion), channel_id=1, source_target_pairs={{0,16},{1,17},{2,18},{3,19},{4,20},{5,21},{6,22},{7,23},{8,24},{9,... | collective-permute-start | bytes 44 | tf_op jit(solution)/shard_map/ppermute | solution.py:655
  184.9 1.3 collective-permute-start.41
  186.1 6.3 %last_product.3 = (f32[512,2560]{1,0:T(8,128)S(1)}, f32[8,64,1024]{2,1,0:T(8,128)}) custom-call(s32[40,128]{1,0:T(8,128)S(1)} %get-tuple-element.91.table_ref, bf16[512,2560]{1,0:T(8,128)(2,1)S(1)} %get-tuple-element.126.high_ref, bf16[512,2560]{1,0:T(8,128)(2,1)S(1)} %get-tuple-element.127.low_ref, ...), custom_call_target="tpu_custom_call", output_to_operand_aliasing={{0}: (4, {})} | custom-call | flops 6000000000 | bytes 65536 | tf_op jit(solution)/shard_map/last_product/pallas_call | solution.py:625
  192.4 2.8 %collective-permute-start.42 = (f32[3]{0:T(128)S(1)}, f32[3]{0:T(128)S(1)}, u32[]{:S(2)}, u32[]{:S(2)}) collective-permute-start(f32[3]{0:T(128)S(1)} %add_add_fusion), channel_id=1, source_target_pairs={{0,24},{1,25},{2,26},{3,27},{4,28},{5,29},{6,30},{7,31},{8,16},{9,... | collective-permute-start | bytes 44 | tf_op jit(solution)/shard_map/ppermute | solution.py:655
  195.2 1.3 collective-permute-start.43
  196.5 1.2 collective-permute-done.42
  197.7 3.7 %collective-permute-done.43 = f32[3]{0:T(128)S(1)} collective-permute-done((f32[3]{0:T(128)S(1)}, f32[3]{0:T(128)S(1)}, u32[]{:S(2)}, u32[]{:S(2)}) %collective-permute-start.43) | collective-permute-done | bytes 44 | tf_op jit(solution)/shard_map/ppermute | solution.py:655
  201.5 0.6 pad_maximum_fusion.4
  (68 shorter events, 4.0 us)
Async XLA Ops:
  0.6 1.6 copy-start
  2.2 0.7 copy-start.3
  2.9 0.7 copy-start.4
  3.6 0.7 copy-start.5
  5.5 12.9 %collective-permute-start = (f32[520,128]{1,0:T(8,128)S(1)}, f32[520,128]{1,0:T(8,128)S(1)}, u32[]{:S(2)}, u32[]{:S(2)}) collective-permute-start(f32[520,128]{1,0:T(8,128)S(1)} %get-tuple-element.83), channel_id=1, source_target_pairs={{0,3},{1,0},{2,1},{3,2},{4,7},{5,4},{6,5},{7,6},{8,11},{9,8},{10,9... | collective-permute-start | bytes 798728 | tf_op jit(solution)/shard_map/ppermute | solution.py:679
  8.0 15.6 %collective-permute-start.1 = (f32[520,128]{1,0:T(8,128)S(1)}, f32[520,128]{1,0:T(8,128)S(1)}, u32[]{:S(2)}, u32[]{:S(2)}) collective-permute-start(f32[520,128]{1,0:T(8,128)S(1)} %get-tuple-element.84), channel_id=1, source_target_pairs={{0,1},{1,2},{2,3},{3,0},{4,5},{5,6},{6,7},{7,4},{8,9},{9,10},{10,1... | collective-permute-start | bytes 798728 | tf_op jit(solution)/shard_map/ppermute | solution.py:679
  8.0 16.8 %collective-permute-start.2 = (f32[520,128]{1,0:T(8,128)S(1)}, f32[520,128]{1,0:T(8,128)S(1)}, u32[]{:S(2)}, u32[]{:S(2)}) collective-permute-start(f32[520,128]{1,0:T(8,128)S(1)} %get-tuple-element.85), channel_id=1, source_target_pairs={{0,31},{1,28},{2,29},{3,30},{4,3},{5,0},{6,1},{7,2},{8,7},{9,4},{1... | collective-permute-start | bytes 798728 | tf_op jit(solution)/shard_map/ppermute | solution.py:679
  13.7 20.1 %collective-permute-start.3 = (f32[520,128]{1,0:T(8,128)S(1)}, f32[520,128]{1,0:T(8,128)S(1)}, u32[]{:S(2)}, u32[]{:S(2)}) collective-permute-start(f32[520,128]{1,0:T(8,128)S(1)} %get-tuple-element.86), channel_id=1, source_target_pairs={{0,5},{1,6},{2,7},{3,4},{4,9},{5,10},{6,11},{7,8},{8,13},{9,14},{1... | collective-permute-start | bytes 798728 | tf_op jit(solution)/shard_map/ppermute | solution.py:679
  13.7 26.8 %collective-permute-start.4 = (f32[520,128]{1,0:T(8,128)S(1)}, f32[520,128]{1,0:T(8,128)S(1)}, u32[]{:S(2)}, u32[]{:S(2)}) collective-permute-start(f32[520,128]{1,0:T(8,128)S(1)} %get-tuple-element.87), channel_id=1, source_target_pairs={{0,29},{1,30},{2,31},{3,28},{4,1},{5,2},{6,3},{7,0},{8,5},{9,6},{1... | collective-permute-start | bytes 798728 | tf_op jit(solution)/shard_map/ppermute | solution.py:679
  18.4 22.0 %collective-permute-start.5 = (f32[520,128]{1,0:T(8,128)S(1)}, f32[520,128]{1,0:T(8,128)S(1)}, u32[]{:S(2)}, u32[]{:S(2)}) collective-permute-start(f32[520,128]{1,0:T(8,128)S(1)} %get-tuple-element.88), channel_id=1, source_target_pairs={{0,7},{1,4},{2,5},{3,6},{4,11},{5,8},{6,9},{7,10},{8,15},{9,12},{1... | collective-permute-start | bytes 798728 | tf_op jit(solution)/shard_map/ppermute | solution.py:679
  23.6 21.7 %collective-permute-start.6 = (f32[520,128]{1,0:T(8,128)S(1)}, f32[520,128]{1,0:T(8,128)S(1)}, u32[]{:S(2)}, u32[]{:S(2)}) collective-permute-start(f32[520,128]{1,0:T(8,128)S(1)} %get-tuple-element.89), channel_id=1, source_target_pairs={{0,28},{1,29},{2,30},{3,31},{4,0},{5,1},{6,2},{7,3},{8,4},{9,5},{1... | collective-permute-start | bytes 798728 | tf_op jit(solution)/shard_map/ppermute | solution.py:679
  24.8 20.5 %collective-permute-start.7 = (f32[520,128]{1,0:T(8,128)S(1)}, f32[520,128]{1,0:T(8,128)S(1)}, u32[]{:S(2)}, u32[]{:S(2)}) collective-permute-start(f32[520,128]{1,0:T(8,128)S(1)} %get-tuple-element.90), channel_id=1, source_target_pairs={{0,4},{1,5},{2,6},{3,7},{4,8},{5,9},{6,10},{7,11},{8,12},{9,13},{1... | collective-permute-start | bytes 798728 | tf_op jit(solution)/shard_map/ppermute | solution.py:679
  46.6 17.4 %collective-permute-start.12 = (f32[4,64,1024]{2,1,0:T(8,128)S(1)}, f32[4,64,1024]{2,1,0:T(8,128)S(1)}, u32[]{:S(2)}, u32[]{:S(2)}) collective-permute-start(f32[4,64,1024]{2,1,0:T(8,128)S(1)} %get-tuple-element.104), channel_id=1, source_target_pairs={{0,1},{1,0},{2,3},{3,2},{4,5},{5,4},{6,7},{7,6},{8,9},{9,8},{10,11... | collective-permute-start | bytes 3145736 | tf_op jit(solution)/shard_map/ppermute | solution.py:689
  47.9 15.0 %collective-permute-start.10 = (f32[2,64,1024]{2,1,0:T(8,128)S(1)}, f32[2,64,1024]{2,1,0:T(8,128)S(1)}, u32[]{:S(2)}, u32[]{:S(2)}) collective-permute-start(f32[2,64,1024]{2,1,0:T(8,128)S(1)} %get-tuple-element.102), channel_id=1, source_target_pairs={{0,4},{1,5},{2,6},{3,7},{4,0},{5,1},{6,2},{7,3},{8,12},{9,13},{10,... | collective-permute-start | bytes 1572872 | tf_op jit(solution)/shard_map/ppermute | solution.py:689
  50.1 13.9 %collective-permute-start.11 = (f32[2,64,1024]{2,1,0:T(8,128)S(1)}, f32[2,64,1024]{2,1,0:T(8,128)S(1)}, u32[]{:S(2)}, u32[]{:S(2)}) collective-permute-start(f32[2,64,1024]{2,1,0:T(8,128)S(1)} %get-tuple-element.103), channel_id=1, source_target_pairs={{0,3},{1,2},{2,1},{3,0},{4,7},{5,6},{6,5},{7,4},{8,11},{9,10},{10,... | collective-permute-start | bytes 1572872 | tf_op jit(solution)/shard_map/ppermute | solution.py:689
  51.0 27.0 %collective-permute-start.8 = (f32[2,64,1024]{2,1,0:T(8,128)S(1)}, f32[2,64,1024]{2,1,0:T(8,128)S(1)}, u32[]{:S(2)}, u32[]{:S(2)}) collective-permute-start(f32[2,64,1024]{2,1,0:T(8,128)S(1)} %get-tuple-element.100), channel_id=1, source_target_pairs={{0,4},{1,5},{2,6},{3,7},{4,0},{5,1},{6,2},{7,3},{8,12},{9,13},{10,... | collective-permute-start | bytes 1572872 | tf_op jit(solution)/shard_map/ppermute | solution.py:689
  51.4 26.6 %collective-permute-start.9 = (f32[2,64,1024]{2,1,0:T(8,128)S(1)}, f32[2,64,1024]{2,1,0:T(8,128)S(1)}, u32[]{:S(2)}, u32[]{:S(2)}) collective-permute-start(f32[2,64,1024]{2,1,0:T(8,128)S(1)} %get-tuple-element.101), channel_id=1, source_target_pairs={{0,3},{1,2},{2,1},{3,0},{4,7},{5,6},{6,5},{7,4},{8,11},{9,10},{10,... | collective-permute-start | bytes 1572872 | tf_op jit(solution)/shard_map/ppermute | solution.py:689
  52.7 56.8 %copy-start.6 = (s32[8,16]{1,0:T(8,128)}, s32[8,16]{1,0:T(8,128)S(1)}, u32[]{:S(2)}) copy-start(s32[8,16]{1,0:T(8,128)S(1)} %get-tuple-element.119.refs_3_.refs_2_) | copy-start | bytes 1540
  64.0 19.2 %collective-permute-start.14 = (f32[2,64,1024]{2,1,0:T(8,128)S(1)}, f32[2,64,1024]{2,1,0:T(8,128)S(1)}, u32[]{:S(2)}, u32[]{:S(2)}) collective-permute-start(f32[2,64,1024]{2,1,0:T(8,128)S(1)} %collective-permute-done.10.refs_1_), channel_id=1, source_target_pairs={{0,8},{1,9},{2,10},{3,11},{4,28},{5,29},{6,30},{7,31},{8,16},{9,17... | collective-permute-start | bytes 1572872 | tf_op jit(solution)/shard_map/ppermute | solution.py:689
  65.8 21.1 %collective-permute-start.16 = (f32[2,64,1024]{2,1,0:T(8,128)S(1)}, f32[2,64,1024]{2,1,0:T(8,128)S(1)}, u32[]{:S(2)}, u32[]{:S(2)}) collective-permute-start(f32[2,64,1024]{2,1,0:T(8,128)S(1)} %collective-permute-done.10.refs_1_), channel_id=1, source_target_pairs={{0,3},{1,2},{2,1},{3,0},{4,7},{5,6},{6,5},{7,4},{8,11},{9,10},{10,... | collective-permute-start | bytes 1572872 | tf_op jit(solution)/shard_map/ppermute | solution.py:689
  66.8 18.4 %collective-permute-start.15 = (f32[2,64,1024]{2,1,0:T(8,128)S(1)}, f32[2,64,1024]{2,1,0:T(8,128)S(1)}, u32[]{:S(2)}, u32[]{:S(2)}) collective-permute-start(f32[2,64,1024]{2,1,0:T(8,128)S(1)} %collective-permute-done.11.refs_2_), channel_id=1, source_target_pairs={{0,4},{1,5},{2,6},{3,7},{4,0},{5,1},{6,2},{7,3},{8,12},{9,13},{10,... | collective-permute-start | bytes 1572872 | tf_op jit(solution)/shard_map/ppermute | solution.py:689
  78.1 16.6 %collective-permute-start.13 = (f32[2,64,1024]{2,1,0:T(8,128)S(1)}, f32[2,64,1024]{2,1,0:T(8,128)S(1)}, u32[]{:S(2)}, u32[]{:S(2)}) collective-permute-start(f32[2,64,1024]{2,1,0:T(8,128)S(1)} %collective-permute-done.8.refs_0_), channel_id=1, source_target_pairs={{0,8},{1,9},{2,10},{3,11},{4,28},{5,29},{6,30},{7,31},{8,16},{9,17... | collective-permute-start | bytes 1572872 | tf_op jit(solution)/shard_map/ppermute | solution.py:689
  78.1 16.7 %collective-permute-start.20 = (f32[4,64,1024]{2,1,0:T(8,128)S(1)}, f32[4,64,1024]{2,1,0:T(8,128)S(1)}, u32[]{:S(2)}, u32[]{:S(2)}) collective-permute-start(f32[4,64,1024]{2,1,0:T(8,128)S(1)} %pad_maximum_fusion.1), channel_id=1, source_target_pairs={{0,1},{1,0},{2,3},{3,2},{4,5},{5,4},{6,7},{7,6},{8,9},{9,8},{10,11... | collective-permute-start | bytes 3145736 | tf_op jit(solution)/shard_map/ppermute | solution.py:689
  85.2 20.2 %collective-permute-start.18 = (f32[2,64,1024]{2,1,0:T(8,128)S(1)}, f32[2,64,1024]{2,1,0:T(8,128)S(1)}, u32[]{:S(2)}, u32[]{:S(2)}) collective-permute-start(f32[2,64,1024]{2,1,0:T(8,128)S(1)} %collective-permute-done.15.refs_1_), channel_id=1, source_target_pairs={{0,8},{1,9},{2,10},{3,11},{4,28},{5,29},{6,30},{7,31},{8,16},{9,17... | collective-permute-start | bytes 1572872 | tf_op jit(solution)/shard_map/ppermute | solution.py:689
  86.8 18.6 %collective-permute-start.19 = (f32[2,64,1024]{2,1,0:T(8,128)S(1)}, f32[2,64,1024]{2,1,0:T(8,128)S(1)}, u32[]{:S(2)}, u32[]{:S(2)}) collective-permute-start(f32[2,64,1024]{2,1,0:T(8,128)S(1)} %collective-permute-done.14.refs_0_), channel_id=1, source_target_pairs={{0,3},{1,2},{2,1},{3,0},{4,7},{5,6},{6,5},{7,4},{8,11},{9,10},{10,... | collective-permute-start | bytes 1572872 | tf_op jit(solution)/shard_map/ppermute | solution.py:689
  94.8 14.7 %collective-permute-start.17 = (f32[4,64,1024]{2,1,0:T(8,128)S(1)}, f32[4,64,1024]{2,1,0:T(8,128)S(1)}, u32[]{:S(2)}, u32[]{:S(2)}) collective-permute-start(f32[4,64,1024]{2,1,0:T(8,128)S(1)} %pad_maximum_fusion), channel_id=1, source_target_pairs={{0,1},{1,0},{2,3},{3,2},{4,5},{5,4},{6,7},{7,6},{8,9},{9,8},{10,11... | collective-permute-start | bytes 3145736 | tf_op jit(solution)/shard_map/ppermute | solution.py:689
  115.6 4.8 %copy-start.1 = (f32[8,64,1024]{2,1,0:T(8,128)}, f32[8,64,1024]{2,1,0:T(8,128)S(1)}, u32[]{:S(2)}) copy-start(f32[8,64,1024]{2,1,0:T(8,128)S(1)} %get-tuple-element.120.current_ref.refs_4_) | copy-start | bytes 6291460
  115.6 16.0 %collective-permute-start.25 = (f32[4,64,1024]{2,1,0:T(8,128)S(1)}, f32[4,64,1024]{2,1,0:T(8,128)S(1)}, u32[]{:S(2)}, u32[]{:S(2)}) collective-permute-start(f32[4,64,1024]{2,1,0:T(8,128)S(1)} %get-tuple-element.132), channel_id=1, source_target_pairs={{0,1},{1,0},{2,3},{3,2},{4,5},{5,4},{6,7},{7,6},{8,9},{9,8},{10,11... | collective-permute-start | bytes 3145736 | tf_op jit(solution)/shard_map/ppermute | solution.py:689
  116.8 14.8 %collective-permute-start.23 = (f32[2,64,1024]{2,1,0:T(8,128)S(1)}, f32[2,64,1024]{2,1,0:T(8,128)S(1)}, u32[]{:S(2)}, u32[]{:S(2)}) collective-permute-start(f32[2,64,1024]{2,1,0:T(8,128)S(1)} %get-tuple-element.130), channel_id=1, source_target_pairs={{0,4},{1,5},{2,6},{3,7},{4,0},{5,1},{6,2},{7,3},{8,12},{9,13},{10,... | collective-permute-start | bytes 1572872 | tf_op jit(solution)/shard_map/ppermute | solution.py:689
  116.9 14.7 %collective-permute-start.24 = (f32[2,64,1024]{2,1,0:T(8,128)S(1)}, f32[2,64,1024]{2,1,0:T(8,128)S(1)}, u32[]{:S(2)}, u32[]{:S(2)}) collective-permute-start(f32[2,64,1024]{2,1,0:T(8,128)S(1)} %get-tuple-element.131), channel_id=1, source_target_pairs={{0,3},{1,2},{2,1},{3,0},{4,7},{5,6},{6,5},{7,4},{8,11},{9,10},{10,... | collective-permute-start | bytes 1572872 | tf_op jit(solution)/shard_map/ppermute | solution.py:689
  118.5 24.9 %collective-permute-start.21 = (f32[2,64,1024]{2,1,0:T(8,128)S(1)}, f32[2,64,1024]{2,1,0:T(8,128)S(1)}, u32[]{:S(2)}, u32[]{:S(2)}) collective-permute-start(f32[2,64,1024]{2,1,0:T(8,128)S(1)} %get-tuple-element.128), channel_id=1, source_target_pairs={{0,4},{1,5},{2,6},{3,7},{4,0},{5,1},{6,2},{7,3},{8,12},{9,13},{10,... | collective-permute-start | bytes 1572872 | tf_op jit(solution)/shard_map/ppermute | solution.py:689
  120.2 23.2 %collective-permute-start.22 = (f32[2,64,1024]{2,1,0:T(8,128)S(1)}, f32[2,64,1024]{2,1,0:T(8,128)S(1)}, u32[]{:S(2)}, u32[]{:S(2)}) collective-permute-start(f32[2,64,1024]{2,1,0:T(8,128)S(1)} %get-tuple-element.129), channel_id=1, source_target_pairs={{0,3},{1,2},{2,1},{3,0},{4,7},{5,6},{6,5},{7,4},{8,11},{9,10},{10,... | collective-permute-start | bytes 1572872 | tf_op jit(solution)/shard_map/ppermute | solution.py:689
  131.6 18.5 %collective-permute-start.27 = (f32[2,64,1024]{2,1,0:T(8,128)S(1)}, f32[2,64,1024]{2,1,0:T(8,128)S(1)}, u32[]{:S(2)}, u32[]{:S(2)}) collective-permute-start(f32[2,64,1024]{2,1,0:T(8,128)S(1)} %collective-permute-done.23.refs_1_), channel_id=1, source_target_pairs={{0,8},{1,9},{2,10},{3,11},{4,28},{5,29},{6,30},{7,31},{8,16},{9,17... | collective-permute-start | bytes 1572872 | tf_op jit(solution)/shard_map/ppermute | solution.py:689
  131.6 22.9 %collective-permute-start.29 = (f32[2,64,1024]{2,1,0:T(8,128)S(1)}, f32[2,64,1024]{2,1,0:T(8,128)S(1)}, u32[]{:S(2)}, u32[]{:S(2)}) collective-permute-start(f32[2,64,1024]{2,1,0:T(8,128)S(1)} %collective-permute-done.23.refs_1_), channel_id=1, source_target_pairs={{0,3},{1,2},{2,1},{3,0},{4,7},{5,6},{6,5},{7,4},{8,11},{9,10},{10,... | collective-permute-start | bytes 1572872 | tf_op jit(solution)/shard_map/ppermute | solution.py:689
  133.0 20.7 %collective-permute-start.28 = (f32[2,64,1024]{2,1,0:T(8,128)S(1)}, f32[2,64,1024]{2,1,0:T(8,128)S(1)}, u32[]{:S(2)}, u32[]{:S(2)}) collective-permute-start(f32[2,64,1024]{2,1,0:T(8,128)S(1)} %collective-permute-done.24.refs_2_.refs_1_), channel_id=1, source_target_pairs={{0,4},{1,5},{2,6},{3,7},{4,0},{5,1},{6,2},{7,3},{8,12},{9,13},{10,... | collective-permute-start | bytes 1572872 | tf_op jit(solution)/shard_map/ppermute | solution.py:689
  143.4 16.3 %collective-permute-start.26 = (f32[2,64,1024]{2,1,0:T(8,128)S(1)}, f32[2,64,1024]{2,1,0:T(8,128)S(1)}, u32[]{:S(2)}, u32[]{:S(2)}) collective-permute-start(f32[2,64,1024]{2,1,0:T(8,128)S(1)} %collective-permute-done.21.refs_0_), channel_id=1, source_target_pairs={{0,8},{1,9},{2,10},{3,11},{4,28},{5,29},{6,30},{7,31},{8,16},{9,17... | collective-permute-start | bytes 1572872 | tf_op jit(solution)/shard_map/ppermute | solution.py:689
  145.3 18.7 %collective-permute-start.31 = (f32[4,64,1024]{2,1,0:T(8,128)S(1)}, f32[4,64,1024]{2,1,0:T(8,128)S(1)}, u32[]{:S(2)}, u32[]{:S(2)}) collective-permute-start(f32[4,64,1024]{2,1,0:T(8,128)S(1)} %pad_maximum_fusion.3), channel_id=1, source_target_pairs={{0,1},{1,0},{2,3},{3,2},{4,5},{5,4},{6,7},{7,6},{8,9},{9,8},{10,11... | collective-permute-start | bytes 3145736 | tf_op jit(solution)/shard_map/ppermute | solution.py:689
  153.7 20.6 %collective-permute-start.35 = (f32[2,64,1024]{2,1,0:T(8,128)S(1)}, f32[2,64,1024]{2,1,0:T(8,128)S(1)}, u32[]{:S(2)}, u32[]{:S(2)}) collective-permute-start(f32[2,64,1024]{2,1,0:T(8,128)S(1)} %collective-permute-done.28.refs_1_), channel_id=1, source_target_pairs={{0,8},{1,9},{2,10},{3,11},{4,28},{5,29},{6,30},{7,31},{8,16},{9,17... | collective-permute-start | bytes 1572872 | tf_op jit(solution)/shard_map/ppermute | solution.py:689
  153.7 21.1 %collective-permute-start.36 = (f32[2,64,1024]{2,1,0:T(8,128)S(1)}, f32[2,64,1024]{2,1,0:T(8,128)S(1)}, u32[]{:S(2)}, u32[]{:S(2)}) collective-permute-start(f32[2,64,1024]{2,1,0:T(8,128)S(1)} %collective-permute-done.27.refs_0_.refs_4_), channel_id=1, source_target_pairs={{0,3},{1,2},{2,1},{3,0},{4,7},{5,6},{6,5},{7,4},{8,11},{9,10},{10,... | collective-permute-start | bytes 1572872 | tf_op jit(solution)/shard_map/ppermute | solution.py:689
  159.8 25.0 %collective-permute-start.30 = (f32[4,64,1024]{2,1,0:T(8,128)S(1)}, f32[4,64,1024]{2,1,0:T(8,128)S(1)}, u32[]{:S(2)}, u32[]{:S(2)}) collective-permute-start(f32[4,64,1024]{2,1,0:T(8,128)S(1)} %pad_maximum_fusion.2), channel_id=1, source_target_pairs={{0,1},{1,0},{2,3},{3,2},{4,5},{5,4},{6,7},{7,6},{8,9},{9,8},{10,11... | collective-permute-start | bytes 3145736 | tf_op jit(solution)/shard_map/ppermute | solution.py:689
  172.8 6.1 %collective-permute-start.32 = (f32[3]{0:T(128)S(1)}, f32[3]{0:T(128)S(1)}, u32[]{:S(2)}, u32[]{:S(2)}) collective-permute-start(f32[3]{0:T(128)S(1)} %get-tuple-element.147), channel_id=1, source_target_pairs={{0,1},{1,0},{2,3},{3,2},{4,5},{5,4},{6,7},{7,6},{8,9},{9,8},{10,11... | collective-permute-start | bytes 44 | tf_op jit(solution)/shard_map/ppermute | solution.py:655
  173.1 5.8 %collective-permute-start.33 = (f32[3]{0:T(128)S(1)}, f32[3]{0:T(128)S(1)}, u32[]{:S(2)}, u32[]{:S(2)}) collective-permute-start(f32[3]{0:T(128)S(1)} %get-tuple-element.147), channel_id=1, source_target_pairs={{0,2},{1,3},{2,0},{3,1},{4,6},{5,7},{6,4},{7,5},{8,10},{9,11},{10,... | collective-permute-start | bytes 44 | tf_op jit(solution)/shard_map/ppermute | solution.py:655
  174.3 4.7 %collective-permute-start.34 = (f32[3]{0:T(128)S(1)}, f32[3]{0:T(128)S(1)}, u32[]{:S(2)}, u32[]{:S(2)}) collective-permute-start(f32[3]{0:T(128)S(1)} %get-tuple-element.147), channel_id=1, source_target_pairs={{0,3},{1,2},{2,1},{3,0},{4,7},{5,6},{6,5},{7,4},{8,11},{9,10},{10,... | collective-permute-start | bytes 44 | tf_op jit(solution)/shard_map/ppermute | solution.py:655
  174.8 11.3 %copy-start.2 = (f32[8,64,1024]{2,1,0:T(8,128)S(1)}, f32[8,64,1024]{2,1,0:T(8,128)}, u32[]{:S(2)}) copy-start(f32[8,64,1024]{2,1,0:T(8,128)} %copy-done.1) | copy-start | bytes 6291460
  174.8 11.3 %copy-start.7 = (s32[8,16]{1,0:T(8,128)S(1)}, s32[8,16]{1,0:T(8,128)}, u32[]{:S(2)}) copy-start(s32[8,16]{1,0:T(8,128)} %copy-done.6) | copy-start | bytes 1540
  178.9 13.4 %collective-permute-start.37 = (f32[3]{0:T(128)S(1)}, f32[3]{0:T(128)S(1)}, u32[]{:S(2)}, u32[]{:S(2)}) collective-permute-start(f32[3]{0:T(128)S(1)} %add_add_fusion), channel_id=1, source_target_pairs={{0,4},{1,5},{2,6},{3,7},{4,0},{5,1},{6,2},{7,3},{8,12},{9,13},{10,... | collective-permute-start | bytes 44 | tf_op jit(solution)/shard_map/ppermute | solution.py:655
  180.3 14.9 %collective-permute-start.38 = (f32[3]{0:T(128)S(1)}, f32[3]{0:T(128)S(1)}, u32[]{:S(2)}, u32[]{:S(2)}) collective-permute-start(f32[3]{0:T(128)S(1)} %add_add_fusion), channel_id=1, source_target_pairs={{0,8},{1,9},{2,10},{3,11},{4,12},{5,13},{6,14},{7,15},{8,0},{9,1},... | collective-permute-start | bytes 44 | tf_op jit(solution)/shard_map/ppermute | solution.py:655
  181.3 15.2 %collective-permute-start.39 = (f32[3]{0:T(128)S(1)}, f32[3]{0:T(128)S(1)}, u32[]{:S(2)}, u32[]{:S(2)}) collective-permute-start(f32[3]{0:T(128)S(1)} %add_add_fusion), channel_id=1, source_target_pairs={{0,12},{1,13},{2,14},{3,15},{4,8},{5,9},{6,10},{7,11},{8,4},{9,5},... | collective-permute-start | bytes 44 | tf_op jit(solution)/shard_map/ppermute | solution.py:655
  182.5 14.0 %collective-permute-start.40 = (f32[3]{0:T(128)S(1)}, f32[3]{0:T(128)S(1)}, u32[]{:S(2)}, u32[]{:S(2)}) collective-permute-start(f32[3]{0:T(128)S(1)} %add_add_fusion), channel_id=1, source_target_pairs={{0,16},{1,17},{2,18},{3,19},{4,20},{5,21},{6,22},{7,23},{8,24},{9,... | collective-permute-start | bytes 44 | tf_op jit(solution)/shard_map/ppermute | solution.py:655
  184.9 11.6 %collective-permute-start.41 = (f32[3]{0:T(128)S(1)}, f32[3]{0:T(128)S(1)}, u32[]{:S(2)}, u32[]{:S(2)}) collective-permute-start(f32[3]{0:T(128)S(1)} %add_add_fusion), channel_id=1, source_target_pairs={{0,20},{1,21},{2,22},{3,23},{4,16},{5,17},{6,18},{7,19},{8,28},{9,... | collective-permute-start | bytes 44 | tf_op jit(solution)/shard_map/ppermute | solution.py:655
  192.4 5.3 %collective-permute-start.42 = (f32[3]{0:T(128)S(1)}, f32[3]{0:T(128)S(1)}, u32[]{:S(2)}, u32[]{:S(2)}) collective-permute-start(f32[3]{0:T(128)S(1)} %add_add_fusion), channel_id=1, source_target_pairs={{0,24},{1,25},{2,26},{3,27},{4,28},{5,29},{6,30},{7,31},{8,16},{9,... | collective-permute-start | bytes 44 | tf_op jit(solution)/shard_map/ppermute | solution.py:655
  195.2 6.2 %collective-permute-start.43 = (f32[3]{0:T(128)S(1)}, f32[3]{0:T(128)S(1)}, u32[]{:S(2)}, u32[]{:S(2)}) collective-permute-start(f32[3]{0:T(128)S(1)} %add_add_fusion), channel_id=1, source_target_pairs={{0,28},{1,29},{2,30},{3,31},{4,24},{5,25},{6,26},{7,27},{8,20},{9,... | collective-permute-start | bytes 44 | tf_op jit(solution)/shard_map/ppermute | solution.py:655

commit v6 on v4

--- a/solution.py
+++ b/solution.py
@@ -30,9 +30,9 @@
 
 OWN_TILES = 2
 TILES = (
-    (("C", 0, 4),),
     (("A", 2, 2), ("Y", 0, 2)),
     (("A", 0, 2), ("Y", 2, 2)),
+    (("C", 0, 4),),
     (("B", 2, 2), ("YA", 2, 2)),
     (("B", 0, 2), ("YA", 0, 2)),
     (("CA", 0, 4),),
@@ -695,10 +695,10 @@
         add = functools.partial(add_product, table=table, high=high, low=low)
         a_1, y_0, c, total = tie((a_1, y_0, c, total))
         b_1, ya_1, ya_0 = go(a_1, "B"), go(a_1, "Y"), go(y_0, "A")
-        (total,) = add(2, 2, parts=[c, a_1, y_0], total=total, label="first_product")
+        (total,) = add(2, 1, parts=[a_1, y_0], total=total, label="first_product")
         a_0, y_1, total = tie((a_0, y_1, total))
         b_0 = go(a_0, "B")
-        (total,) = add(4, 1, parts=[a_0, y_1], total=total, label="second_product")
+        (total,) = add(3, 2, parts=[a_0, y_1, c], total=total, label="second_product")
         a_0, b_1, ya_0, total = tie((a_0, b_1, ya_0, total))
         yb_1, yb_0 = go(b_1, "Y"), go(ya_0, "B")
         ca = go(jnp.concatenate([a_0, a_1]), "C")

time: 197 us -> 194 us (0.985)
  waiting for transfers between devices: 45.3 us -> 42.5 us
    ppermute x26, waiting for transfers between devices: 22.5 us -> 19.6 us  [shards(): go = lambda value, way: lax.ppermute(value, AXES, swap[way])]
  transfers between devices with their start and end apart: 41 -> 41, of which waited for: 15 -> 20; matrix products, arithmetic and copies ran while one was open for 0% -> 0% of each run, Pallas kernels for 45% -> 45%
where the time goes in v6:
time: 194 us
  Pallas kernels  97.4 us (50%)
  starting transfers between devices  48.2 us (25%)
  waiting for transfers between devices  42.5 us (22%)
  local copies, waits for them, and re-layouts  3.65 us (2%)
    pallas_call x12, Pallas kernels, add_product(): pl.pallas_call(kernel, out_shape=out_shape, in_specs=in_specs, out_specs=...  73.3 us
    ppermute x26, starting transfers between devices, shards(): go = lambda value, way: lax.ppermute(value, AXES, swap[way])  20.4 us
    ppermute x8, waiting for transfers between devices, shards(): arrived[d] = lax.ppermute(leaving[d], AXES, perm)  20 us
    ppermute x8, starting transfers between devices, shards(): arrived[d] = lax.ppermute(leaving[d], AXES, perm)  19.9 us
    ppermute x26, waiting for transfers between devices, shards(): go = lambda value, way: lax.ppermute(value, AXES, swap[way])  19.6 us
    pallas_call x2, Pallas kernels, own_product(): pl.pallas_call(kernel, out_shape=(dense(jnp.bfloat16), dense(jnp.bfloat16...  14.7 us
    ppermute x7, starting transfers between devices, sum_round(): others = [lax.ppermute(value, AXES, perm) for perm in perms]  7.92 us
  transfers between devices with their start and end apart: 41, of which 20 were waited for; matrix products, arithmetic and copies ran while one was open for 0% of the time, Pallas kernels for 45%

profile of v6, /device:TPU:0, one launch (start us, length us, event | category | flops | bytes accessed | tf_op | source)
XLA Modules:
  0.0 193.6 jit_solution(17876830658243109749)
XLA Ops:
  0.6 1.6 copy-done
  2.2 0.7 copy-done.1
  2.9 0.7 copy-done.2
  3.6 0.7 copy-done.3
  4.2 1.3 pack_rows.1
  5.5 2.5 %collective-permute-start = (f32[520,128]{1,0:T(8,128)S(1)}, f32[520,128]{1,0:T(8,128)S(1)}, u32[]{:S(2)}, u32[]{:S(2)}) collective-permute-start(f32[520,128]{1,0:T(8,128)S(1)} %get-tuple-element.79), channel_id=1, source_target_pairs={{0,3},{1,0},{2,1},{3,2},{4,7},{5,4},{6,5},{7,6},{8,11},{9,8},{10,9... | collective-permute-start | bytes 798728 | tf_op jit(solution)/shard_map/ppermute | solution.py:676
  8.0 5.7 %collective-permute-start.2 = (f32[520,128]{1,0:T(8,128)S(1)}, f32[520,128]{1,0:T(8,128)S(1)}, u32[]{:S(2)}, u32[]{:S(2)}) collective-permute-start(f32[520,128]{1,0:T(8,128)S(1)} %get-tuple-element.81), channel_id=1, source_target_pairs={{0,31},{1,28},{2,29},{3,30},{4,3},{5,0},{6,1},{7,2},{8,7},{9,4},{1... | collective-permute-start | bytes 798728 | tf_op jit(solution)/shard_map/ppermute | solution.py:676
  13.7 4.5 %collective-permute-start.4 = (f32[520,128]{1,0:T(8,128)S(1)}, f32[520,128]{1,0:T(8,128)S(1)}, u32[]{:S(2)}, u32[]{:S(2)}) collective-permute-start(f32[520,128]{1,0:T(8,128)S(1)} %get-tuple-element.83), channel_id=1, source_target_pairs={{0,29},{1,30},{2,31},{3,28},{4,1},{5,2},{6,3},{7,0},{8,5},{9,6},{1... | collective-permute-start | bytes 798728 | tf_op jit(solution)/shard_map/ppermute | solution.py:676
  18.4 5.2 %collective-permute-start.5 = (f32[520,128]{1,0:T(8,128)S(1)}, f32[520,128]{1,0:T(8,128)S(1)}, u32[]{:S(2)}, u32[]{:S(2)}) collective-permute-start(f32[520,128]{1,0:T(8,128)S(1)} %get-tuple-element.84), channel_id=1, source_target_pairs={{0,7},{1,4},{2,5},{3,6},{4,11},{5,8},{6,9},{7,10},{8,15},{9,12},{1... | collective-permute-start | bytes 798728 | tf_op jit(solution)/shard_map/ppermute | solution.py:676
  23.6 1.2 collective-permute-start.6
  24.8 0.8 collective-permute-start.7
  25.6 8.1 %collective-permute-done.3.refs_3_ = f32[520,128]{1,0:T(8,128)S(1)} collective-permute-done((f32[520,128]{1,0:T(8,128)S(1)}, f32[520,128]{1,0:T(8,128)S(1)}, u32[]{:S(2)}, u32[]{:S(2)}) %collective-permute-start.3) | collective-permute-done | bytes 266272 | tf_op jit(solution)/shard_map/ppermute | solution.py:676
  33.8 6.7 %collective-permute-done.4.refs_4_ = f32[520,128]{1,0:T(8,128)S(1)} collective-permute-done((f32[520,128]{1,0:T(8,128)S(1)}, f32[520,128]{1,0:T(8,128)S(1)}, u32[]{:S(2)}, u32[]{:S(2)}) %collective-permute-start.4) | collective-permute-done | bytes 266272 | tf_op jit(solution)/shard_map/ppermute | solution.py:676
  40.5 4.9 %collective-permute-done.6.refs_6_ = f32[520,128]{1,0:T(8,128)S(1)} collective-permute-done((f32[520,128]{1,0:T(8,128)S(1)}, f32[520,128]{1,0:T(8,128)S(1)}, u32[]{:S(2)}, u32[]{:S(2)}) %collective-permute-start.6) | collective-permute-done | bytes 266272 | tf_op jit(solution)/shard_map/ppermute | solution.py:676
  45.3 1.2 place_rows.1
  46.8 2.2 %collective-permute-start.10 = (f32[2,64,1024]{2,1,0:T(8,128)S(1)}, f32[2,64,1024]{2,1,0:T(8,128)S(1)}, u32[]{:S(2)}, u32[]{:S(2)}) collective-permute-start(f32[2,64,1024]{2,1,0:T(8,128)S(1)} %get-tuple-element.98), channel_id=1, source_target_pairs={{0,4},{1,5},{2,6},{3,7},{4,0},{5,1},{6,2},{7,3},{8,12},{9,13},{10,... | collective-permute-start | bytes 1572872 | tf_op jit(solution)/shard_map/ppermute | solution.py:686
  49.0 0.8 collective-permute-start.11
  49.8 1.1 spread_own.2
  50.9 0.3 collective-permute-start.8
  51.3 0.7 collective-permute-start.9
  52.0 0.8 make_tables.1
  52.8 7.3 %own_product.2 = (bf16[512,2560]{1,0:T(8,128)(2,1)S(1)}, bf16[512,2560]{1,0:T(8,128)(2,1)S(1)}, f32[512,2560]{1,0:T(8,128)S(1)}) custom-call(s32[40,128]{1,0:T(8,128)S(1)} %get-tuple-element.87.table_ref, bf16[2,512,1152]{2,1,0:T(8,128)(2,1)S(1)} %get-tuple-element.92.wide_high, bf16[2,512,1152]{2,1,0:T(8,128)(2,1)S(1)} %get-tuple-element.93.wide_low), custom_call_target="tpu_custom_call" | custom-call | flops 2684354560 | bytes 65536 | tf_op jit(solution)/shard_map/own_product/pallas_call | solution.py:451
  60.2 1.6 collective-permute-done.10.refs_0_
  61.7 1.1 collective-permute-done.11.refs_1_
  62.9 1.8 collective-permute-start.13
  64.6 3.4 %collective-permute-start.14 = (f32[2,64,1024]{2,1,0:T(8,128)S(1)}, f32[2,64,1024]{2,1,0:T(8,128)S(1)}, u32[]{:S(2)}, u32[]{:S(2)}) collective-permute-start(f32[2,64,1024]{2,1,0:T(8,128)S(1)} %collective-permute-done.11.refs_1_), channel_id=1, source_target_pairs={{0,4},{1,5},{2,6},{3,7},{4,0},{5,1},{6,2},{7,3},{8,12},{9,13},{10,... | collective-permute-start | bytes 1572872 | tf_op jit(solution)/shard_map/ppermute | solution.py:686
  68.0 4.7 %first_product.2.refs_3_ = f32[512,2560]{1,0:T(8,128)S(1)} custom-call(s32[40,128]{1,0:T(8,128)S(1)} %get-tuple-element.87.table_ref, bf16[512,2560]{1,0:T(8,128)(2,1)S(1)} %get-tuple-element.94.high_ref, bf16[512,2560]{1,0:T(8,128)(2,1)S(1)} %get-tuple-element.95.low_ref, ...), custom_call_target="tpu_custom_call", output_to_operand_aliasing={{}: (5, {})} | custom-call | flops 1342177280 | bytes 65536 | tf_op jit(solution)/shard_map/first_product/pallas_call | solution.py:624
  73.0 1.1 collective-permute-done.9.refs_1_
  74.1 1.8 collective-permute-start.17
  75.9 8.8 %second_product.2.refs_2_ = f32[512,2560]{1,0:T(8,128)S(1)} custom-call(s32[40,128]{1,0:T(8,128)S(1)} %get-tuple-element.87.table_ref, bf16[512,2560]{1,0:T(8,128)(2,1)S(1)} %get-tuple-element.94.high_ref, bf16[512,2560]{1,0:T(8,128)(2,1)S(1)} %get-tuple-element.95.low_ref, ...), custom_call_target="tpu_custom_call", output_to_operand_aliasing={{}: (6, {})} | custom-call | flops 2684354560 | bytes 65536 | tf_op jit(solution)/shard_map/second_product/pallas_call | solution.py:624
  84.7 0.4 collective-permute-start.20
  85.3 4.7 %third_product.2.refs_3_ = f32[512,2560]{1,0:T(8,128)S(1)} custom-call(s32[40,128]{1,0:T(8,128)S(1)} %get-tuple-element.87.table_ref, bf16[512,2560]{1,0:T(8,128)(2,1)S(1)} %get-tuple-element.94.high_ref, bf16[512,2560]{1,0:T(8,128)(2,1)S(1)} %get-tuple-element.95.low_ref, ...), custom_call_target="tpu_custom_call", output_to_operand_aliasing={{}: (5, {})} | custom-call | flops 1342177280 | bytes 65536 | tf_op jit(solution)/shard_map/third_product/pallas_call | solution.py:624
  90.0 1.2 collective-permute-done.17.refs_0_
  91.4 0.9 collective-permute-start.15
  92.3 0.6 collective-permute-start.16
  92.9 7.4 %fourth_product.2.refs_1_ = f32[512,2560]{1,0:T(8,128)S(1)} custom-call(s32[40,128]{1,0:T(8,128)S(1)} %get-tuple-element.87.table_ref, bf16[512,2560]{1,0:T(8,128)(2,1)S(1)} %get-tuple-element.94.high_ref, bf16[512,2560]{1,0:T(8,128)(2,1)S(1)} %get-tuple-element.95.low_ref, ...), custom_call_target="tpu_custom_call", output_to_operand_aliasing={{}: (6, {})} | custom-call | flops 2147483648 | bytes 65536 | tf_op jit(solution)/shard_map/fourth_product/pallas_call | solution.py:624
  100.3 3.2 %fifth_product.2.refs_2_ = f32[512,2560]{1,0:T(8,128)S(1)} custom-call(s32[40,128]{1,0:T(8,128)S(1)} %get-tuple-element.87.table_ref, bf16[512,2560]{1,0:T(8,128)(2,1)S(1)} %get-tuple-element.94.high_ref, bf16[512,2560]{1,0:T(8,128)(2,1)S(1)} %get-tuple-element.95.low_ref, ...), custom_call_target="tpu_custom_call", output_to_operand_aliasing={{}: (4, {})} | custom-call | flops 805306368 | bytes 65536 | tf_op jit(solution)/shard_map/fifth_product/pallas_call | solution.py:624
  103.6 3.9 %collective-permute-done.15.refs_0_ = f32[2,64,1024]{2,1,0:T(8,128)S(1)} collective-permute-done((f32[2,64,1024]{2,1,0:T(8,128)S(1)}, f32[2,64,1024]{2,1,0:T(8,128)S(1)}, u32[]{:S(2)}, u32[]{:S(2)}) %collective-permute-start.15) | collective-permute-done | bytes 524320 | tf_op jit(solution)/shard_map/ppermute | solution.py:686
  107.5 7.1 %last_product.2 = (f32[512,2560]{1,0:T(8,128)S(1)}, f32[2]{0:T(128)S(1)}, f32[8,64,1024]{2,1,0:T(8,128)S(1)}, f32[4,64,1024]{2,1,0:T(8,128)S(1)}, f32[2,64,1024]...) custom-call(s32[40,128]{1,0:T(8,128)S(1)} %get-tuple-element.87.tabl, ...), custom_call_target="tpu_custom_call", output_to_operand_aliasing={{0}: (5, {})} | custom-call | flops 1073741824 | bytes 65536 | tf_op jit(solution)/shard_map/last_product/pallas_call | solution.py:624
  114.7 2.2 %collective-permute-start.23 = (f32[2,64,1024]{2,1,0:T(8,128)S(1)}, f32[2,64,1024]{2,1,0:T(8,128)S(1)}, u32[]{:S(2)}, u32[]{:S(2)}) collective-permute-start(f32[2,64,1024]{2,1,0:T(8,128)S(1)} %get-tuple-element.127), channel_id=1, source_target_pairs={{0,4},{1,5},{2,6},{3,7},{4,0},{5,1},{6,2},{7,3},{8,12},{9,13},{10,... | collective-permute-start | bytes 1572872 | tf_op jit(solution)/shard_map/ppermute | solution.py:686
  116.9 1.1 spread_own.3
  118.2 1.7 collective-permute-start.22
  119.9 7.4 %own_product.3 = (bf16[512,2560]{1,0:T(8,128)(2,1)S(1)}, bf16[512,2560]{1,0:T(8,128)(2,1)S(1)}, f32[512,2560]{1,0:T(8,128)S(1)}) custom-call(s32[40,128]{1,0:T(8,128)S(1)} %get-tuple-element.87.table_ref, bf16[2,512,1152]{2,1,0:T(8,128)(2,1)S(1)} %get-tuple-element.121.wide_high, bf16[2,512,1152]{2,1,0:T(8,128)(2,1)S(1)} %get-tuple-element.122.wide_low), custom_call_target="tpu_custom_call" | custom-call | flops 2684354560 | bytes 65536 | tf_op jit(solution)/shard_map/own_product/pallas_call | solution.py:451
  127.2 2.4 %collective-permute-done.23.refs_0_ = f32[2,64,1024]{2,1,0:T(8,128)S(1)} collective-permute-done((f32[2,64,1024]{2,1,0:T(8,128)S(1)}, f32[2,64,1024]{2,1,0:T(8,128)S(1)}, u32[]{:S(2)}, u32[]{:S(2)}) %collective-permute-start.23) | collective-permute-done | bytes 524320 | tf_op jit(solution)/shard_map/ppermute | solution.py:686
  129.6 1.2 collective-permute-done.24.refs_1_
  130.9 2.5 %collective-permute-start.27 = (f32[2,64,1024]{2,1,0:T(8,128)S(1)}, f32[2,64,1024]{2,1,0:T(8,128)S(1)}, u32[]{:S(2)}, u32[]{:S(2)}) collective-permute-start(f32[2,64,1024]{2,1,0:T(8,128)S(1)} %collective-permute-done.24.refs_1_), channel_id=1, source_target_pairs={{0,4},{1,5},{2,6},{3,7},{4,0},{5,1},{6,2},{7,3},{8,12},{9,13},{10,... | collective-permute-start | bytes 1572872 | tf_op jit(solution)/shard_map/ppermute | solution.py:686
  133.3 4.7 %first_product.3.refs_3_ = f32[512,2560]{1,0:T(8,128)S(1)} custom-call(s32[40,128]{1,0:T(8,128)S(1)} %get-tuple-element.87.table_ref, bf16[512,2560]{1,0:T(8,128)(2,1)S(1)} %get-tuple-element.123.high_ref, bf16[512,2560]{1,0:T(8,128)(2,1)S(1)} %get-tuple-element.124.low_ref, ...), custom_call_target="tpu_custom_call", output_to_operand_aliasing={{}: (5, {})} | custom-call | flops 1342177280 | bytes 65536 | tf_op jit(solution)/shard_map/first_product/pallas_call | solution.py:624
  138.0 2.8 %collective-permute-done.21.refs_0_ = f32[2,64,1024]{2,1,0:T(8,128)S(1)} collective-permute-done((f32[2,64,1024]{2,1,0:T(8,128)S(1)}, f32[2,64,1024]{2,1,0:T(8,128)S(1)}, u32[]{:S(2)}, u32[]{:S(2)}) %collective-permute-start.21) | collective-permute-done | bytes 524320 | tf_op jit(solution)/shard_map/ppermute | solution.py:686
  140.8 1.2 collective-permute-done.22.refs_1_.refs_2_
  142.1 8.8 %second_product.3.refs_2_ = f32[512,2560]{1,0:T(8,128)S(1)} custom-call(s32[40,128]{1,0:T(8,128)S(1)} %get-tuple-element.87.table_ref, bf16[512,2560]{1,0:T(8,128)(2,1)S(1)} %get-tuple-element.123.high_ref, bf16[512,2560]{1,0:T(8,128)(2,1)S(1)} %get-tuple-element.124.low_ref, ...), custom_call_target="tpu_custom_call", output_to_operand_aliasing={{}: (6, {})} | custom-call | flops 2684354560 | bytes 65536 | tf_op jit(solution)/shard_map/second_product/pallas_call | solution.py:624
  150.9 0.9 collective-permute-done.27.refs_1_
  151.9 1.4 collective-permute-done.31.refs_1_
  153.3 4.7 %third_product.3.refs_3_ = f32[512,2560]{1,0:T(8,128)S(1)} custom-call(s32[40,128]{1,0:T(8,128)S(1)} %get-tuple-element.87.table_ref, bf16[512,2560]{1,0:T(8,128)(2,1)S(1)} %get-tuple-element.123.high_ref, bf16[512,2560]{1,0:T(8,128)(2,1)S(1)} %get-tuple-element.124.low_ref, ...), custom_call_target="tpu_custom_call", output_to_operand_aliasing={{}: (5, {})} | custom-call | flops 1342177280 | bytes 65536 | tf_op jit(solution)/shard_map/third_product/pallas_call | solution.py:624
  158.8 3.8 %far_trace.1.refs_5_ = f32[1]{0:T(128)} custom-call(s32[40,128]{1,0:T(8,128)S(1)} %get-tuple-element.87.table_ref, f32[4,64,1024]{2,1,0:T(8,128)S(1)} %collective-permute-done.25.refs_2_.refs_0_, f32[2,64,1024]{2,1,0:T(8,128)S(1)} %collective-permute-done.24.refs_1_, f32[2,64,1024]{2,1,0:T(8,128)S(1)} %collective-permute-done.22.refs_1_.refs_2_, ...), custom_call_target="tpu_custom_call" | custom-call | flops 536870912 | bytes 65536 | tf_op jit(solution)/shard_map/far_trace/pallas_call | solution.py:523
  162.7 8.8 %fourth_product.3 = (f32[512,2560]{1,0:T(8,128)S(1)}, f32[3]{0:T(128)S(1)}) custom-call(s32[40,128]{1,0:T(8,128)S(1)} %get-tuple-element.87.table_ref, bf16[512,2560]{1,0:T(8,128)(2,1)S(1)} %get-tuple-element.123.high_ref, bf16[512,2560]{1,0:T(8,128)(2,1)S(1)} %get-tuple-element.124.low_ref, ...), custom_call_target="tpu_custom_call", output_to_operand_aliasing={{0}: (6, {})} | custom-call | flops 2147483648 | bytes 65536 | tf_op jit(solution)/shard_map/fourth_product/pallas_call | solution.py:624
  171.7 1.7 collective-permute-start.34
  173.5 3.2 %fifth_product.3.refs_2_ = f32[512,2560]{1,0:T(8,128)S(1)} custom-call(s32[40,128]{1,0:T(8,128)S(1)} %get-tuple-element.87.table_ref, bf16[512,2560]{1,0:T(8,128)(2,1)S(1)} %get-tuple-element.123.high_ref, bf16[512,2560]{1,0:T(8,128)(2,1)S(1)} %get-tuple-element.124.low_ref, ...), custom_call_target="tpu_custom_call", output_to_operand_aliasing={{}: (4, {})} | custom-call | flops 805306368 | bytes 65536 | tf_op jit(solution)/shard_map/fifth_product/pallas_call | solution.py:624
  176.8 2.1 %collective-permute-start.37 = (f32[3]{0:T(128)S(1)}, f32[3]{0:T(128)S(1)}, u32[]{:S(2)}, u32[]{:S(2)}) collective-permute-start(f32[3]{0:T(128)S(1)} %add_add_fusion.1), channel_id=1, source_target_pairs={{0,4},{1,5},{2,6},{3,7},{4,0},{5,1},{6,2},{7,3},{8,12},{9,13},{10,... | collective-permute-start | bytes 44 | tf_op jit(solution)/shard_map/ppermute | solution.py:654
  179.0 1.4 collective-permute-start.39
  180.5 2.0 %collective-permute-done.38 = f32[3]{0:T(128)S(1)} collective-permute-done((f32[3]{0:T(128)S(1)}, f32[3]{0:T(128)S(1)}, u32[]{:S(2)}, u32[]{:S(2)}) %collective-permute-start.38) | collective-permute-done | bytes 44 | tf_op jit(solution)/shard_map/ppermute | solution.py:654
  182.5 1.0 collective-permute-done.39
  183.5 2.3 %collective-permute-start.40 = (f32[3]{0:T(128)S(1)}, f32[3]{0:T(128)S(1)}, u32[]{:S(2)}, u32[]{:S(2)}) collective-permute-start(f32[3]{0:T(128)S(1)} %add_add_fusion), channel_id=1, source_target_pairs={{0,16},{1,17},{2,18},{3,19},{4,20},{5,21},{6,22},{7,23},{8,24},{9,... | collective-permute-start | bytes 44 | tf_op jit(solution)/shard_map/ppermute | solution.py:654
  185.8 7.2 %last_product.3 = (f32[512,2560]{1,0:T(8,128)S(1)}, f32[8,64,1024]{2,1,0:T(8,128)}) custom-call(s32[40,128]{1,0:T(8,128)S(1)} %get-tuple-element.87.table_ref, bf16[512,2560]{1,0:T(8,128)(2,1)S(1)} %get-tuple-element.123.high_ref, bf16[512,2560]{1,0:T(8,128)(2,1)S(1)} %get-tuple-element.124.low_ref, ...), custom_call_target="tpu_custom_call", output_to_operand_aliasing={{0}: (5, {})} | custom-call | flops 1073741824 | bytes 65536 | tf_op jit(solution)/shard_map/last_product/pallas_call | solution.py:624
  193.0 0.6 pad_maximum_fusion.4
  (55 shorter events, 3.0 us)
Async XLA Ops:
  0.6 1.6 copy-start
  2.2 0.7 copy-start.1
  2.9 0.7 copy-start.2
  3.6 0.7 copy-start.3
  5.5 12.9 %collective-permute-start = (f32[520,128]{1,0:T(8,128)S(1)}, f32[520,128]{1,0:T(8,128)S(1)}, u32[]{:S(2)}, u32[]{:S(2)}) collective-permute-start(f32[520,128]{1,0:T(8,128)S(1)} %get-tuple-element.79), channel_id=1, source_target_pairs={{0,3},{1,0},{2,1},{3,2},{4,7},{5,4},{6,5},{7,6},{8,11},{9,8},{10,9... | collective-permute-start | bytes 798728 | tf_op jit(solution)/shard_map/ppermute | solution.py:676
  8.0 15.6 %collective-permute-start.1 = (f32[520,128]{1,0:T(8,128)S(1)}, f32[520,128]{1,0:T(8,128)S(1)}, u32[]{:S(2)}, u32[]{:S(2)}) collective-permute-start(f32[520,128]{1,0:T(8,128)S(1)} %get-tuple-element.80), channel_id=1, source_target_pairs={{0,1},{1,2},{2,3},{3,0},{4,5},{5,6},{6,7},{7,4},{8,9},{9,10},{10,1... | collective-permute-start | bytes 798728 | tf_op jit(solution)/shard_map/ppermute | solution.py:676
  8.0 16.8 %collective-permute-start.2 = (f32[520,128]{1,0:T(8,128)S(1)}, f32[520,128]{1,0:T(8,128)S(1)}, u32[]{:S(2)}, u32[]{:S(2)}) collective-permute-start(f32[520,128]{1,0:T(8,128)S(1)} %get-tuple-element.81), channel_id=1, source_target_pairs={{0,31},{1,28},{2,29},{3,30},{4,3},{5,0},{6,1},{7,2},{8,7},{9,4},{1... | collective-permute-start | bytes 798728 | tf_op jit(solution)/shard_map/ppermute | solution.py:676
  13.7 20.1 %collective-permute-start.3 = (f32[520,128]{1,0:T(8,128)S(1)}, f32[520,128]{1,0:T(8,128)S(1)}, u32[]{:S(2)}, u32[]{:S(2)}) collective-permute-start(f32[520,128]{1,0:T(8,128)S(1)} %get-tuple-element.82), channel_id=1, source_target_pairs={{0,5},{1,6},{2,7},{3,4},{4,9},{5,10},{6,11},{7,8},{8,13},{9,14},{1... | collective-permute-start | bytes 798728 | tf_op jit(solution)/shard_map/ppermute | solution.py:676
  13.7 26.8 %collective-permute-start.4 = (f32[520,128]{1,0:T(8,128)S(1)}, f32[520,128]{1,0:T(8,128)S(1)}, u32[]{:S(2)}, u32[]{:S(2)}) collective-permute-start(f32[520,128]{1,0:T(8,128)S(1)} %get-tuple-element.83), channel_id=1, source_target_pairs={{0,29},{1,30},{2,31},{3,28},{4,1},{5,2},{6,3},{7,0},{8,5},{9,6},{1... | collective-permute-start | bytes 798728 | tf_op jit(solution)/shard_map/ppermute | solution.py:676
  18.4 22.0 %collective-permute-start.5 = (f32[520,128]{1,0:T(8,128)S(1)}, f32[520,128]{1,0:T(8,128)S(1)}, u32[]{:S(2)}, u32[]{:S(2)}) collective-permute-start(f32[520,128]{1,0:T(8,128)S(1)} %get-tuple-element.84), channel_id=1, source_target_pairs={{0,7},{1,4},{2,5},{3,6},{4,11},{5,8},{6,9},{7,10},{8,15},{9,12},{1... | collective-permute-start | bytes 798728 | tf_op jit(solution)/shard_map/ppermute | solution.py:676
  23.6 21.7 %collective-permute-start.6 = (f32[520,128]{1,0:T(8,128)S(1)}, f32[520,128]{1,0:T(8,128)S(1)}, u32[]{:S(2)}, u32[]{:S(2)}) collective-permute-start(f32[520,128]{1,0:T(8,128)S(1)} %get-tuple-element.85), channel_id=1, source_target_pairs={{0,28},{1,29},{2,30},{3,31},{4,0},{5,1},{6,2},{7,3},{8,4},{9,5},{1... | collective-permute-start | bytes 798728 | tf_op jit(solution)/shard_map/ppermute | solution.py:676
  24.8 20.5 %collective-permute-start.7 = (f32[520,128]{1,0:T(8,128)S(1)}, f32[520,128]{1,0:T(8,128)S(1)}, u32[]{:S(2)}, u32[]{:S(2)}) collective-permute-start(f32[520,128]{1,0:T(8,128)S(1)} %get-tuple-element.86), channel_id=1, source_target_pairs={{0,4},{1,5},{2,6},{3,7},{4,8},{5,9},{6,10},{7,11},{8,12},{9,13},{1... | collective-permute-start | bytes 798728 | tf_op jit(solution)/shard_map/ppermute | solution.py:676
  46.6 16.3 %collective-permute-start.12 = (f32[4,64,1024]{2,1,0:T(8,128)S(1)}, f32[4,64,1024]{2,1,0:T(8,128)S(1)}, u32[]{:S(2)}, u32[]{:S(2)}) collective-permute-start(f32[4,64,1024]{2,1,0:T(8,128)S(1)} %get-tuple-element.100), channel_id=1, source_target_pairs={{0,1},{1,0},{2,3},{3,2},{4,5},{5,4},{6,7},{7,6},{8,9},{9,8},{10,11... | collective-permute-start | bytes 3145736 | tf_op jit(solution)/shard_map/ppermute | solution.py:686
  46.8 15.0 %collective-permute-start.10 = (f32[2,64,1024]{2,1,0:T(8,128)S(1)}, f32[2,64,1024]{2,1,0:T(8,128)S(1)}, u32[]{:S(2)}, u32[]{:S(2)}) collective-permute-start(f32[2,64,1024]{2,1,0:T(8,128)S(1)} %get-tuple-element.98), channel_id=1, source_target_pairs={{0,4},{1,5},{2,6},{3,7},{4,0},{5,1},{6,2},{7,3},{8,12},{9,13},{10,... | collective-permute-start | bytes 1572872 | tf_op jit(solution)/shard_map/ppermute | solution.py:686
  49.0 13.9 %collective-permute-start.11 = (f32[2,64,1024]{2,1,0:T(8,128)S(1)}, f32[2,64,1024]{2,1,0:T(8,128)S(1)}, u32[]{:S(2)}, u32[]{:S(2)}) collective-permute-start(f32[2,64,1024]{2,1,0:T(8,128)S(1)} %get-tuple-element.99), channel_id=1, source_target_pairs={{0,3},{1,2},{2,1},{3,0},{4,7},{5,6},{6,5},{7,4},{8,11},{9,10},{10,... | collective-permute-start | bytes 1572872 | tf_op jit(solution)/shard_map/ppermute | solution.py:686
  50.9 22.0 %collective-permute-start.8 = (f32[2,64,1024]{2,1,0:T(8,128)S(1)}, f32[2,64,1024]{2,1,0:T(8,128)S(1)}, u32[]{:S(2)}, u32[]{:S(2)}) collective-permute-start(f32[2,64,1024]{2,1,0:T(8,128)S(1)} %get-tuple-element.96), channel_id=1, source_target_pairs={{0,4},{1,5},{2,6},{3,7},{4,0},{5,1},{6,2},{7,3},{8,12},{9,13},{10,... | collective-permute-start | bytes 1572872 | tf_op jit(solution)/shard_map/ppermute | solution.py:686
  51.3 22.8 %collective-permute-start.9 = (f32[2,64,1024]{2,1,0:T(8,128)S(1)}, f32[2,64,1024]{2,1,0:T(8,128)S(1)}, u32[]{:S(2)}, u32[]{:S(2)}) collective-permute-start(f32[2,64,1024]{2,1,0:T(8,128)S(1)} %get-tuple-element.97), channel_id=1, source_target_pairs={{0,3},{1,2},{2,1},{3,0},{4,7},{5,6},{6,5},{7,4},{8,11},{9,10},{10,... | collective-permute-start | bytes 1572872 | tf_op jit(solution)/shard_map/ppermute | solution.py:686
  62.9 21.8 %collective-permute-start.13 = (f32[2,64,1024]{2,1,0:T(8,128)S(1)}, f32[2,64,1024]{2,1,0:T(8,128)S(1)}, u32[]{:S(2)}, u32[]{:S(2)}) collective-permute-start(f32[2,64,1024]{2,1,0:T(8,128)S(1)} %collective-permute-done.10.refs_0_), channel_id=1, source_target_pairs={{0,8},{1,9},{2,10},{3,11},{4,28},{5,29},{6,30},{7,31},{8,16},{9,17... | collective-permute-start | bytes 1572872 | tf_op jit(solution)/shard_map/ppermute | solution.py:686
  64.6 20.0 %collective-permute-start.14 = (f32[2,64,1024]{2,1,0:T(8,128)S(1)}, f32[2,64,1024]{2,1,0:T(8,128)S(1)}, u32[]{:S(2)}, u32[]{:S(2)}) collective-permute-start(f32[2,64,1024]{2,1,0:T(8,128)S(1)} %collective-permute-done.11.refs_1_), channel_id=1, source_target_pairs={{0,4},{1,5},{2,6},{3,7},{4,0},{5,1},{6,2},{7,3},{8,12},{9,13},{10,... | collective-permute-start | bytes 1572872 | tf_op jit(solution)/shard_map/ppermute | solution.py:686
  68.0 17.3 %collective-permute-start.18 = (f32[2,64,1024]{2,1,0:T(8,128)S(1)}, f32[2,64,1024]{2,1,0:T(8,128)S(1)}, u32[]{:S(2)}, u32[]{:S(2)}) collective-permute-start(f32[2,64,1024]{2,1,0:T(8,128)S(1)} %collective-permute-done.10.refs_0_), channel_id=1, source_target_pairs={{0,3},{1,2},{2,1},{3,0},{4,7},{5,6},{6,5},{7,4},{8,11},{9,10},{10,... | collective-permute-start | bytes 1572872 | tf_op jit(solution)/shard_map/ppermute | solution.py:686
  74.1 17.1 %collective-permute-start.17 = (f32[2,64,1024]{2,1,0:T(8,128)S(1)}, f32[2,64,1024]{2,1,0:T(8,128)S(1)}, u32[]{:S(2)}, u32[]{:S(2)}) collective-permute-start(f32[2,64,1024]{2,1,0:T(8,128)S(1)} %collective-permute-done.8.refs_0_), channel_id=1, source_target_pairs={{0,8},{1,9},{2,10},{3,11},{4,28},{5,29},{6,30},{7,31},{8,16},{9,17... | collective-permute-start | bytes 1572872 | tf_op jit(solution)/shard_map/ppermute | solution.py:686
  84.7 8.1 %collective-permute-start.20 = (f32[4,64,1024]{2,1,0:T(8,128)S(1)}, f32[4,64,1024]{2,1,0:T(8,128)S(1)}, u32[]{:S(2)}, u32[]{:S(2)}) collective-permute-start(f32[4,64,1024]{2,1,0:T(8,128)S(1)} %pad_maximum_fusion.1), channel_id=1, source_target_pairs={{0,1},{1,0},{2,3},{3,2},{4,5},{5,4},{6,7},{7,6},{8,9},{9,8},{10,11... | collective-permute-start | bytes 3145736 | tf_op jit(solution)/shard_map/ppermute | solution.py:686
  91.3 9.1 %collective-permute-start.19 = (f32[4,64,1024]{2,1,0:T(8,128)S(1)}, f32[4,64,1024]{2,1,0:T(8,128)S(1)}, u32[]{:S(2)}, u32[]{:S(2)}) collective-permute-start(f32[4,64,1024]{2,1,0:T(8,128)S(1)} %pad_maximum_fusion), channel_id=1, source_target_pairs={{0,1},{1,0},{2,3},{3,2},{4,5},{5,4},{6,7},{7,6},{8,9},{9,8},{10,11... | collective-permute-start | bytes 3145736 | tf_op jit(solution)/shard_map/ppermute | solution.py:686
  91.4 16.1 %collective-permute-start.15 = (f32[2,64,1024]{2,1,0:T(8,128)S(1)}, f32[2,64,1024]{2,1,0:T(8,128)S(1)}, u32[]{:S(2)}, u32[]{:S(2)}) collective-permute-start(f32[2,64,1024]{2,1,0:T(8,128)S(1)} %collective-permute-done.14.refs_1_), channel_id=1, source_target_pairs={{0,8},{1,9},{2,10},{3,11},{4,28},{5,29},{6,30},{7,31},{8,16},{9,17... | collective-permute-start | bytes 1572872 | tf_op jit(solution)/shard_map/ppermute | solution.py:686
  92.3 15.1 %collective-permute-start.16 = (f32[2,64,1024]{2,1,0:T(8,128)S(1)}, f32[2,64,1024]{2,1,0:T(8,128)S(1)}, u32[]{:S(2)}, u32[]{:S(2)}) collective-permute-start(f32[2,64,1024]{2,1,0:T(8,128)S(1)} %collective-permute-done.13.refs_0_), channel_id=1, source_target_pairs={{0,3},{1,2},{2,1},{3,0},{4,7},{5,6},{6,5},{7,4},{8,11},{9,10},{10,... | collective-permute-start | bytes 1572872 | tf_op jit(solution)/shard_map/ppermute | solution.py:686
  114.6 16.2 %collective-permute-start.25 = (f32[4,64,1024]{2,1,0:T(8,128)S(1)}, f32[4,64,1024]{2,1,0:T(8,128)S(1)}, u32[]{:S(2)}, u32[]{:S(2)}) collective-permute-start(f32[4,64,1024]{2,1,0:T(8,128)S(1)} %get-tuple-element.129), channel_id=1, source_target_pairs={{0,1},{1,0},{2,3},{3,2},{4,5},{5,4},{6,7},{7,6},{8,9},{9,8},{10,11... | collective-permute-start | bytes 3145736 | tf_op jit(solution)/shard_map/ppermute | solution.py:686
  114.7 14.9 %collective-permute-start.23 = (f32[2,64,1024]{2,1,0:T(8,128)S(1)}, f32[2,64,1024]{2,1,0:T(8,128)S(1)}, u32[]{:S(2)}, u32[]{:S(2)}) collective-permute-start(f32[2,64,1024]{2,1,0:T(8,128)S(1)} %get-tuple-element.127), channel_id=1, source_target_pairs={{0,4},{1,5},{2,6},{3,7},{4,0},{5,1},{6,2},{7,3},{8,12},{9,13},{10,... | collective-permute-start | bytes 1572872 | tf_op jit(solution)/shard_map/ppermute | solution.py:686
  116.9 14.0 %collective-permute-start.24 = (f32[2,64,1024]{2,1,0:T(8,128)S(1)}, f32[2,64,1024]{2,1,0:T(8,128)S(1)}, u32[]{:S(2)}, u32[]{:S(2)}) collective-permute-start(f32[2,64,1024]{2,1,0:T(8,128)S(1)} %get-tuple-element.128), channel_id=1, source_target_pairs={{0,3},{1,2},{2,1},{3,0},{4,7},{5,6},{6,5},{7,4},{8,11},{9,10},{10,... | collective-permute-start | bytes 1572872 | tf_op jit(solution)/shard_map/ppermute | solution.py:686
  118.0 22.9 %collective-permute-start.21 = (f32[2,64,1024]{2,1,0:T(8,128)S(1)}, f32[2,64,1024]{2,1,0:T(8,128)S(1)}, u32[]{:S(2)}, u32[]{:S(2)}) collective-permute-start(f32[2,64,1024]{2,1,0:T(8,128)S(1)} %get-tuple-element.125), channel_id=1, source_target_pairs={{0,4},{1,5},{2,6},{3,7},{4,0},{5,1},{6,2},{7,3},{8,12},{9,13},{10,... | collective-permute-start | bytes 1572872 | tf_op jit(solution)/shard_map/ppermute | solution.py:686
  118.2 23.9 %collective-permute-start.22 = (f32[2,64,1024]{2,1,0:T(8,128)S(1)}, f32[2,64,1024]{2,1,0:T(8,128)S(1)}, u32[]{:S(2)}, u32[]{:S(2)}) collective-permute-start(f32[2,64,1024]{2,1,0:T(8,128)S(1)} %get-tuple-element.126), channel_id=1, source_target_pairs={{0,3},{1,2},{2,1},{3,0},{4,7},{5,6},{6,5},{7,4},{8,11},{9,10},{10,... | collective-permute-start | bytes 1572872 | tf_op jit(solution)/shard_map/ppermute | solution.py:686
  130.8 20.0 %collective-permute-start.26 = (f32[2,64,1024]{2,1,0:T(8,128)S(1)}, f32[2,64,1024]{2,1,0:T(8,128)S(1)}, u32[]{:S(2)}, u32[]{:S(2)}) collective-permute-start(f32[2,64,1024]{2,1,0:T(8,128)S(1)} %collective-permute-done.23.refs_0_), channel_id=1, source_target_pairs={{0,8},{1,9},{2,10},{3,11},{4,28},{5,29},{6,30},{7,31},{8,16},{9,17... | collective-permute-start | bytes 1572872 | tf_op jit(solution)/shard_map/ppermute | solution.py:686
  130.9 20.9 %collective-permute-start.27 = (f32[2,64,1024]{2,1,0:T(8,128)S(1)}, f32[2,64,1024]{2,1,0:T(8,128)S(1)}, u32[]{:S(2)}, u32[]{:S(2)}) collective-permute-start(f32[2,64,1024]{2,1,0:T(8,128)S(1)} %collective-permute-done.24.refs_1_), channel_id=1, source_target_pairs={{0,4},{1,5},{2,6},{3,7},{4,0},{5,1},{6,2},{7,3},{8,12},{9,13},{10,... | collective-permute-start | bytes 1572872 | tf_op jit(solution)/shard_map/ppermute | solution.py:686
  133.3 20.0 %collective-permute-start.31 = (f32[2,64,1024]{2,1,0:T(8,128)S(1)}, f32[2,64,1024]{2,1,0:T(8,128)S(1)}, u32[]{:S(2)}, u32[]{:S(2)}) collective-permute-start(f32[2,64,1024]{2,1,0:T(8,128)S(1)} %collective-permute-done.23.refs_0_), channel_id=1, source_target_pairs={{0,3},{1,2},{2,1},{3,0},{4,7},{5,6},{6,5},{7,4},{8,11},{9,10},{10,... | collective-permute-start | bytes 1572872 | tf_op jit(solution)/shard_map/ppermute | solution.py:686
  142.1 16.3 %collective-permute-start.30 = (f32[2,64,1024]{2,1,0:T(8,128)S(1)}, f32[2,64,1024]{2,1,0:T(8,128)S(1)}, u32[]{:S(2)}, u32[]{:S(2)}) collective-permute-start(f32[2,64,1024]{2,1,0:T(8,128)S(1)} %collective-permute-done.21.refs_0_), channel_id=1, source_target_pairs={{0,8},{1,9},{2,10},{3,11},{4,28},{5,29},{6,30},{7,31},{8,16},{9,17... | collective-permute-start | bytes 1572872 | tf_op jit(solution)/shard_map/ppermute | solution.py:686
  151.8 10.8 %collective-permute-start.32 = (f32[4,64,1024]{2,1,0:T(8,128)S(1)}, f32[4,64,1024]{2,1,0:T(8,128)S(1)}, u32[]{:S(2)}, u32[]{:S(2)}) collective-permute-start(f32[4,64,1024]{2,1,0:T(8,128)S(1)} %pad_maximum_fusion.2), channel_id=1, source_target_pairs={{0,1},{1,0},{2,3},{3,2},{4,5},{5,4},{6,7},{7,6},{8,9},{9,8},{10,11... | collective-permute-start | bytes 3145736 | tf_op jit(solution)/shard_map/ppermute | solution.py:686
  158.4 15.1 %collective-permute-start.36 = (f32[4,64,1024]{2,1,0:T(8,128)S(1)}, f32[4,64,1024]{2,1,0:T(8,128)S(1)}, u32[]{:S(2)}, u32[]{:S(2)}) collective-permute-start(f32[4,64,1024]{2,1,0:T(8,128)S(1)} %pad_maximum_fusion.3), channel_id=1, source_target_pairs={{0,1},{1,0},{2,3},{3,2},{4,5},{5,4},{6,7},{7,6},{8,9},{9,8},{10,11... | collective-permute-start | bytes 3145736 | tf_op jit(solution)/shard_map/ppermute | solution.py:686
  158.5 27.2 %collective-permute-start.29 = (f32[2,64,1024]{2,1,0:T(8,128)S(1)}, f32[2,64,1024]{2,1,0:T(8,128)S(1)}, u32[]{:S(2)}, u32[]{:S(2)}) collective-permute-start(f32[2,64,1024]{2,1,0:T(8,128)S(1)} %collective-permute-done.26.refs_0_.refs_4_), channel_id=1, source_target_pairs={{0,3},{1,2},{2,1},{3,0},{4,7},{5,6},{6,5},{7,4},{8,11},{9,10},{10,... | collective-permute-start | bytes 1572872 | tf_op jit(solution)/shard_map/ppermute | solution.py:686
  158.8 26.9 %collective-permute-start.28 = (f32[2,64,1024]{2,1,0:T(8,128)S(1)}, f32[2,64,1024]{2,1,0:T(8,128)S(1)}, u32[]{:S(2)}, u32[]{:S(2)}) collective-permute-start(f32[2,64,1024]{2,1,0:T(8,128)S(1)} %collective-permute-done.27.refs_1_), channel_id=1, source_target_pairs={{0,8},{1,9},{2,10},{3,11},{4,28},{5,29},{6,30},{7,31},{8,16},{9,17... | collective-permute-start | bytes 1572872 | tf_op jit(solution)/shard_map/ppermute | solution.py:686
  171.5 5.2 %collective-permute-start.33 = (f32[3]{0:T(128)S(1)}, f32[3]{0:T(128)S(1)}, u32[]{:S(2)}, u32[]{:S(2)}) collective-permute-start(f32[3]{0:T(128)S(1)} %get-tuple-element.145), channel_id=1, source_target_pairs={{0,1},{1,0},{2,3},{3,2},{4,5},{5,4},{6,7},{7,6},{8,9},{9,8},{10,11... | collective-permute-start | bytes 44 | tf_op jit(solution)/shard_map/ppermute | solution.py:654
  171.7 5.0 %collective-permute-start.34 = (f32[3]{0:T(128)S(1)}, f32[3]{0:T(128)S(1)}, u32[]{:S(2)}, u32[]{:S(2)}) collective-permute-start(f32[3]{0:T(128)S(1)} %get-tuple-element.145), channel_id=1, source_target_pairs={{0,2},{1,3},{2,0},{3,1},{4,6},{5,7},{6,4},{7,5},{8,10},{9,11},{10,... | collective-permute-start | bytes 44 | tf_op jit(solution)/shard_map/ppermute | solution.py:654
  173.4 3.3 %collective-permute-start.35 = (f32[3]{0:T(128)S(1)}, f32[3]{0:T(128)S(1)}, u32[]{:S(2)}, u32[]{:S(2)}) collective-permute-start(f32[3]{0:T(128)S(1)} %get-tuple-element.145), channel_id=1, source_target_pairs={{0,3},{1,2},{2,1},{3,0},{4,7},{5,6},{6,5},{7,4},{8,11},{9,10},{10,... | collective-permute-start | bytes 44 | tf_op jit(solution)/shard_map/ppermute | solution.py:654
  176.8 3.7 %collective-permute-start.37 = (f32[3]{0:T(128)S(1)}, f32[3]{0:T(128)S(1)}, u32[]{:S(2)}, u32[]{:S(2)}) collective-permute-start(f32[3]{0:T(128)S(1)} %add_add_fusion.1), channel_id=1, source_target_pairs={{0,4},{1,5},{2,6},{3,7},{4,0},{5,1},{6,2},{7,3},{8,12},{9,13},{10,... | collective-permute-start | bytes 44 | tf_op jit(solution)/shard_map/ppermute | solution.py:654
  178.9 3.5 %collective-permute-start.38 = (f32[3]{0:T(128)S(1)}, f32[3]{0:T(128)S(1)}, u32[]{:S(2)}, u32[]{:S(2)}) collective-permute-start(f32[3]{0:T(128)S(1)} %add_add_fusion.1), channel_id=1, source_target_pairs={{0,8},{1,9},{2,10},{3,11},{4,12},{5,13},{6,14},{7,15},{8,0},{9,1},... | collective-permute-start | bytes 44 | tf_op jit(solution)/shard_map/ppermute | solution.py:654
  179.0 4.4 %collective-permute-start.39 = (f32[3]{0:T(128)S(1)}, f32[3]{0:T(128)S(1)}, u32[]{:S(2)}, u32[]{:S(2)}) collective-permute-start(f32[3]{0:T(128)S(1)} %add_add_fusion.1), channel_id=1, source_target_pairs={{0,12},{1,13},{2,14},{3,15},{4,8},{5,9},{6,10},{7,11},{8,4},{9,5},... | collective-permute-start | bytes 44 | tf_op jit(solution)/shard_map/ppermute | solution.py:654
  183.5 9.5 %collective-permute-start.40 = (f32[3]{0:T(128)S(1)}, f32[3]{0:T(128)S(1)}, u32[]{:S(2)}, u32[]{:S(2)}) collective-permute-start(f32[3]{0:T(128)S(1)} %add_add_fusion), channel_id=1, source_target_pairs={{0,16},{1,17},{2,18},{3,19},{4,20},{5,21},{6,22},{7,23},{8,24},{9,... | collective-permute-start | bytes 44 | tf_op jit(solution)/shard_map/ppermute | solution.py:654

commit v7 on v6

--- a/solution.py
+++ b/solution.py
@@ -384,10 +384,10 @@
     fill_one(jnp.int32(0), even)
 
     def two(j, carry):
+        multiply(2 * j, even)
         fill_one(2 * j + 1, odd)
-        multiply(2 * j, even)
+        multiply(2 * j + 1, odd)
         fill_one(jnp.minimum(2 * j + 2, units - 1), even)
-        multiply(2 * j + 1, odd)
         return carry
 
     lax.fori_loop(0, units // 2, two, 0)

time: 194 us -> 194 us (level)
  no operation moved by 1% of the time
where the time goes in v7:
time: 194 us
  Pallas kernels  97.5 us (50%)
  starting transfers between devices  48.4 us (25%)
  waiting for transfers between devices  42.3 us (22%)
  local copies, waits for them, and re-layouts  3.65 us (2%)
    pallas_call x12, Pallas kernels, add_product(): pl.pallas_call(kernel, out_shape=out_shape, in_specs=in_specs, out_specs=...  73.4 us
    ppermute x26, starting transfers between devices, shards(): go = lambda value, way: lax.ppermute(value, AXES, swap[way])  20.7 us
    ppermute x8, waiting for transfers between devices, shards(): arrived[d] = lax.ppermute(leaving[d], AXES, perm)  20 us
    ppermute x8, starting transfers between devices, shards(): arrived[d] = lax.ppermute(leaving[d], AXES, perm)  19.9 us
    ppermute x26, waiting for transfers between devices, shards(): go = lambda value, way: lax.ppermute(value, AXES, swap[way])  19.3 us
    pallas_call x2, Pallas kernels, own_product(): pl.pallas_call(kernel, out_shape=(dense(jnp.bfloat16), dense(jnp.bfloat16...  14.7 us
    ppermute x7, starting transfers between devices, sum_round(): others = [lax.ppermute(value, AXES, perm) for perm in perms]  7.81 us
  transfers between devices with their start and end apart: 41, of which 20 were waited for; matrix products, arithmetic and copies ran while one was open for 0% of the time, Pallas kernels for 45%

profile of v7, /device:TPU:0, one launch (start us, length us, event | category | flops | bytes accessed | tf_op | source)
XLA Modules:
  0.0 193.7 jit_solution(3353081071066919516)
XLA Ops:
  0.6 1.6 copy-done
  2.2 0.7 copy-done.1
  2.9 0.7 copy-done.2
  3.6 0.7 copy-done.3
  4.2 1.3 pack_rows.1
  5.5 2.5 %collective-permute-start = (f32[520,128]{1,0:T(8,128)S(1)}, f32[520,128]{1,0:T(8,128)S(1)}, u32[]{:S(2)}, u32[]{:S(2)}) collective-permute-start(f32[520,128]{1,0:T(8,128)S(1)} %get-tuple-element.79), channel_id=1, source_target_pairs={{0,3},{1,0},{2,1},{3,2},{4,7},{5,4},{6,5},{7,6},{8,11},{9,8},{10,9... | collective-permute-start | bytes 798728 | tf_op jit(solution)/shard_map/ppermute | solution.py:676
  8.0 5.7 %collective-permute-start.2 = (f32[520,128]{1,0:T(8,128)S(1)}, f32[520,128]{1,0:T(8,128)S(1)}, u32[]{:S(2)}, u32[]{:S(2)}) collective-permute-start(f32[520,128]{1,0:T(8,128)S(1)} %get-tuple-element.81), channel_id=1, source_target_pairs={{0,31},{1,28},{2,29},{3,30},{4,3},{5,0},{6,1},{7,2},{8,7},{9,4},{1... | collective-permute-start | bytes 798728 | tf_op jit(solution)/shard_map/ppermute | solution.py:676
  13.7 4.5 %collective-permute-start.4 = (f32[520,128]{1,0:T(8,128)S(1)}, f32[520,128]{1,0:T(8,128)S(1)}, u32[]{:S(2)}, u32[]{:S(2)}) collective-permute-start(f32[520,128]{1,0:T(8,128)S(1)} %get-tuple-element.83), channel_id=1, source_target_pairs={{0,29},{1,30},{2,31},{3,28},{4,1},{5,2},{6,3},{7,0},{8,5},{9,6},{1... | collective-permute-start | bytes 798728 | tf_op jit(solution)/shard_map/ppermute | solution.py:676
  18.4 5.2 %collective-permute-start.5 = (f32[520,128]{1,0:T(8,128)S(1)}, f32[520,128]{1,0:T(8,128)S(1)}, u32[]{:S(2)}, u32[]{:S(2)}) collective-permute-start(f32[520,128]{1,0:T(8,128)S(1)} %get-tuple-element.84), channel_id=1, source_target_pairs={{0,7},{1,4},{2,5},{3,6},{4,11},{5,8},{6,9},{7,10},{8,15},{9,12},{1... | collective-permute-start | bytes 798728 | tf_op jit(solution)/shard_map/ppermute | solution.py:676
  23.6 1.2 collective-permute-start.6
  24.8 0.8 collective-permute-start.7
  25.6 8.1 %collective-permute-done.3.refs_3_ = f32[520,128]{1,0:T(8,128)S(1)} collective-permute-done((f32[520,128]{1,0:T(8,128)S(1)}, f32[520,128]{1,0:T(8,128)S(1)}, u32[]{:S(2)}, u32[]{:S(2)}) %collective-permute-start.3) | collective-permute-done | bytes 266272 | tf_op jit(solution)/shard_map/ppermute | solution.py:676
  33.8 6.7 %collective-permute-done.4.refs_4_ = f32[520,128]{1,0:T(8,128)S(1)} collective-permute-done((f32[520,128]{1,0:T(8,128)S(1)}, f32[520,128]{1,0:T(8,128)S(1)}, u32[]{:S(2)}, u32[]{:S(2)}) %collective-permute-start.4) | collective-permute-done | bytes 266272 | tf_op jit(solution)/shard_map/ppermute | solution.py:676
  40.5 4.9 %collective-permute-done.6.refs_6_ = f32[520,128]{1,0:T(8,128)S(1)} collective-permute-done((f32[520,128]{1,0:T(8,128)S(1)}, f32[520,128]{1,0:T(8,128)S(1)}, u32[]{:S(2)}, u32[]{:S(2)}) %collective-permute-start.6) | collective-permute-done | bytes 266272 | tf_op jit(solution)/shard_map/ppermute | solution.py:676
  45.3 1.2 place_rows.1
  46.8 2.2 %collective-permute-start.10 = (f32[2,64,1024]{2,1,0:T(8,128)S(1)}, f32[2,64,1024]{2,1,0:T(8,128)S(1)}, u32[]{:S(2)}, u32[]{:S(2)}) collective-permute-start(f32[2,64,1024]{2,1,0:T(8,128)S(1)} %get-tuple-element.98), channel_id=1, source_target_pairs={{0,4},{1,5},{2,6},{3,7},{4,0},{5,1},{6,2},{7,3},{8,12},{9,13},{10,... | collective-permute-start | bytes 1572872 | tf_op jit(solution)/shard_map/ppermute | solution.py:686
  49.0 0.8 collective-permute-start.11
  49.8 1.1 spread_own.2
  50.9 0.3 collective-permute-start.8
  51.3 0.7 collective-permute-start.9
  52.0 0.8 make_tables.1
  52.8 7.3 %own_product.2 = (bf16[512,2560]{1,0:T(8,128)(2,1)S(1)}, bf16[512,2560]{1,0:T(8,128)(2,1)S(1)}, f32[512,2560]{1,0:T(8,128)S(1)}) custom-call(s32[40,128]{1,0:T(8,128)S(1)} %get-tuple-element.87.table_ref, bf16[2,512,1152]{2,1,0:T(8,128)(2,1)S(1)} %get-tuple-element.92.wide_high, bf16[2,512,1152]{2,1,0:T(8,128)(2,1)S(1)} %get-tuple-element.93.wide_low), custom_call_target="tpu_custom_call" | custom-call | flops 2684354560 | bytes 65536 | tf_op jit(solution)/shard_map/own_product/pallas_call | solution.py:451
  60.2 1.5 collective-permute-done.10.refs_0_
  61.7 1.1 collective-permute-done.11.refs_1_
  62.9 1.8 collective-permute-start.13
  64.6 3.4 %collective-permute-start.14 = (f32[2,64,1024]{2,1,0:T(8,128)S(1)}, f32[2,64,1024]{2,1,0:T(8,128)S(1)}, u32[]{:S(2)}, u32[]{:S(2)}) collective-permute-start(f32[2,64,1024]{2,1,0:T(8,128)S(1)} %collective-permute-done.11.refs_1_), channel_id=1, source_target_pairs={{0,4},{1,5},{2,6},{3,7},{4,0},{5,1},{6,2},{7,3},{8,12},{9,13},{10,... | collective-permute-start | bytes 1572872 | tf_op jit(solution)/shard_map/ppermute | solution.py:686
  68.0 4.7 %first_product.2.refs_3_ = f32[512,2560]{1,0:T(8,128)S(1)} custom-call(s32[40,128]{1,0:T(8,128)S(1)} %get-tuple-element.87.table_ref, bf16[512,2560]{1,0:T(8,128)(2,1)S(1)} %get-tuple-element.94.high_ref, bf16[512,2560]{1,0:T(8,128)(2,1)S(1)} %get-tuple-element.95.low_ref, ...), custom_call_target="tpu_custom_call", output_to_operand_aliasing={{}: (5, {})} | custom-call | flops 1342177280 | bytes 65536 | tf_op jit(solution)/shard_map/first_product/pallas_call | solution.py:624
  73.0 1.1 collective-permute-done.9.refs_1_
  74.1 1.8 collective-permute-start.17
  75.9 8.8 %second_product.2.refs_2_ = f32[512,2560]{1,0:T(8,128)S(1)} custom-call(s32[40,128]{1,0:T(8,128)S(1)} %get-tuple-element.87.table_ref, bf16[512,2560]{1,0:T(8,128)(2,1)S(1)} %get-tuple-element.94.high_ref, bf16[512,2560]{1,0:T(8,128)(2,1)S(1)} %get-tuple-element.95.low_ref, ...), custom_call_target="tpu_custom_call", output_to_operand_aliasing={{}: (6, {})} | custom-call | flops 2684354560 | bytes 65536 | tf_op jit(solution)/shard_map/second_product/pallas_call | solution.py:624
  84.7 0.4 collective-permute-start.20
  85.3 4.7 %third_product.2.refs_3_ = f32[512,2560]{1,0:T(8,128)S(1)} custom-call(s32[40,128]{1,0:T(8,128)S(1)} %get-tuple-element.87.table_ref, bf16[512,2560]{1,0:T(8,128)(2,1)S(1)} %get-tuple-element.94.high_ref, bf16[512,2560]{1,0:T(8,128)(2,1)S(1)} %get-tuple-element.95.low_ref, ...), custom_call_target="tpu_custom_call", output_to_operand_aliasing={{}: (5, {})} | custom-call | flops 1342177280 | bytes 65536 | tf_op jit(solution)/shard_map/third_product/pallas_call | solution.py:624
  90.0 1.1 collective-permute-done.17.refs_0_
  91.4 1.0 collective-permute-start.15
  92.3 0.6 collective-permute-start.16
  92.9 7.4 %fourth_product.2.refs_1_ = f32[512,2560]{1,0:T(8,128)S(1)} custom-call(s32[40,128]{1,0:T(8,128)S(1)} %get-tuple-element.87.table_ref, bf16[512,2560]{1,0:T(8,128)(2,1)S(1)} %get-tuple-element.94.high_ref, bf16[512,2560]{1,0:T(8,128)(2,1)S(1)} %get-tuple-element.95.low_ref, ...), custom_call_target="tpu_custom_call", output_to_operand_aliasing={{}: (6, {})} | custom-call | flops 2147483648 | bytes 65536 | tf_op jit(solution)/shard_map/fourth_product/pallas_call | solution.py:624
  100.3 3.2 %fifth_product.2.refs_2_ = f32[512,2560]{1,0:T(8,128)S(1)} custom-call(s32[40,128]{1,0:T(8,128)S(1)} %get-tuple-element.87.table_ref, bf16[512,2560]{1,0:T(8,128)(2,1)S(1)} %get-tuple-element.94.high_ref, bf16[512,2560]{1,0:T(8,128)(2,1)S(1)} %get-tuple-element.95.low_ref, ...), custom_call_target="tpu_custom_call", output_to_operand_aliasing={{}: (4, {})} | custom-call | flops 805306368 | bytes 65536 | tf_op jit(solution)/shard_map/fifth_product/pallas_call | solution.py:624
  103.6 3.9 %collective-permute-done.15.refs_0_ = f32[2,64,1024]{2,1,0:T(8,128)S(1)} collective-permute-done((f32[2,64,1024]{2,1,0:T(8,128)S(1)}, f32[2,64,1024]{2,1,0:T(8,128)S(1)}, u32[]{:S(2)}, u32[]{:S(2)}) %collective-permute-start.15) | collective-permute-done | bytes 524320 | tf_op jit(solution)/shard_map/ppermute | solution.py:686
  107.5 7.1 %last_product.2 = (f32[512,2560]{1,0:T(8,128)S(1)}, f32[2]{0:T(128)S(1)}, f32[8,64,1024]{2,1,0:T(8,128)S(1)}, f32[4,64,1024]{2,1,0:T(8,128)S(1)}, f32[2,64,1024]...) custom-call(s32[40,128]{1,0:T(8,128)S(1)} %get-tuple-element.87.tabl, ...), custom_call_target="tpu_custom_call", output_to_operand_aliasing={{0}: (5, {})} | custom-call | flops 1073741824 | bytes 65536 | tf_op jit(solution)/shard_map/last_product/pallas_call | solution.py:624
  114.7 2.2 %collective-permute-start.23 = (f32[2,64,1024]{2,1,0:T(8,128)S(1)}, f32[2,64,1024]{2,1,0:T(8,128)S(1)}, u32[]{:S(2)}, u32[]{:S(2)}) collective-permute-start(f32[2,64,1024]{2,1,0:T(8,128)S(1)} %get-tuple-element.127), channel_id=1, source_target_pairs={{0,4},{1,5},{2,6},{3,7},{4,0},{5,1},{6,2},{7,3},{8,12},{9,13},{10,... | collective-permute-start | bytes 1572872 | tf_op jit(solution)/shard_map/ppermute | solution.py:686
  116.9 1.1 spread_own.3
  118.1 1.8 collective-permute-start.22
  119.9 7.3 %own_product.3 = (bf16[512,2560]{1,0:T(8,128)(2,1)S(1)}, bf16[512,2560]{1,0:T(8,128)(2,1)S(1)}, f32[512,2560]{1,0:T(8,128)S(1)}) custom-call(s32[40,128]{1,0:T(8,128)S(1)} %get-tuple-element.87.table_ref, bf16[2,512,1152]{2,1,0:T(8,128)(2,1)S(1)} %get-tuple-element.121.wide_high, bf16[2,512,1152]{2,1,0:T(8,128)(2,1)S(1)} %get-tuple-element.122.wide_low), custom_call_target="tpu_custom_call" | custom-call | flops 2684354560 | bytes 65536 | tf_op jit(solution)/shard_map/own_product/pallas_call | solution.py:451
  127.2 2.4 %collective-permute-done.23.refs_0_ = f32[2,64,1024]{2,1,0:T(8,128)S(1)} collective-permute-done((f32[2,64,1024]{2,1,0:T(8,128)S(1)}, f32[2,64,1024]{2,1,0:T(8,128)S(1)}, u32[]{:S(2)}, u32[]{:S(2)}) %collective-permute-start.23) | collective-permute-done | bytes 524320 | tf_op jit(solution)/shard_map/ppermute | solution.py:686
  129.6 1.2 collective-permute-done.24.refs_1_
  131.0 2.4 %collective-permute-start.27 = (f32[2,64,1024]{2,1,0:T(8,128)S(1)}, f32[2,64,1024]{2,1,0:T(8,128)S(1)}, u32[]{:S(2)}, u32[]{:S(2)}) collective-permute-start(f32[2,64,1024]{2,1,0:T(8,128)S(1)} %collective-permute-done.24.refs_1_), channel_id=1, source_target_pairs={{0,4},{1,5},{2,6},{3,7},{4,0},{5,1},{6,2},{7,3},{8,12},{9,13},{10,... | collective-permute-start | bytes 1572872 | tf_op jit(solution)/shard_map/ppermute | solution.py:686
  133.3 4.7 %first_product.3.refs_3_ = f32[512,2560]{1,0:T(8,128)S(1)} custom-call(s32[40,128]{1,0:T(8,128)S(1)} %get-tuple-element.87.table_ref, bf16[512,2560]{1,0:T(8,128)(2,1)S(1)} %get-tuple-element.123.high_ref, bf16[512,2560]{1,0:T(8,128)(2,1)S(1)} %get-tuple-element.124.low_ref, ...), custom_call_target="tpu_custom_call", output_to_operand_aliasing={{}: (5, {})} | custom-call | flops 1342177280 | bytes 65536 | tf_op jit(solution)/shard_map/first_product/pallas_call | solution.py:624
  138.1 2.8 %collective-permute-done.21.refs_0_ = f32[2,64,1024]{2,1,0:T(8,128)S(1)} collective-permute-done((f32[2,64,1024]{2,1,0:T(8,128)S(1)}, f32[2,64,1024]{2,1,0:T(8,128)S(1)}, u32[]{:S(2)}, u32[]{:S(2)}) %collective-permute-start.21) | collective-permute-done | bytes 524320 | tf_op jit(solution)/shard_map/ppermute | solution.py:686
  140.9 1.2 collective-permute-done.22.refs_1_.refs_2_
  142.2 8.8 %second_product.3.refs_2_ = f32[512,2560]{1,0:T(8,128)S(1)} custom-call(s32[40,128]{1,0:T(8,128)S(1)} %get-tuple-element.87.table_ref, bf16[512,2560]{1,0:T(8,128)(2,1)S(1)} %get-tuple-element.123.high_ref, bf16[512,2560]{1,0:T(8,128)(2,1)S(1)} %get-tuple-element.124.low_ref, ...), custom_call_target="tpu_custom_call", output_to_operand_aliasing={{}: (6, {})} | custom-call | flops 2684354560 | bytes 65536 | tf_op jit(solution)/shard_map/second_product/pallas_call | solution.py:624
  151.0 0.8 collective-permute-done.27.refs_1_
  151.9 1.4 collective-permute-done.31.refs_1_
  153.3 4.7 %third_product.3.refs_3_ = f32[512,2560]{1,0:T(8,128)S(1)} custom-call(s32[40,128]{1,0:T(8,128)S(1)} %get-tuple-element.87.table_ref, bf16[512,2560]{1,0:T(8,128)(2,1)S(1)} %get-tuple-element.123.high_ref, bf16[512,2560]{1,0:T(8,128)(2,1)S(1)} %get-tuple-element.124.low_ref, ...), custom_call_target="tpu_custom_call", output_to_operand_aliasing={{}: (5, {})} | custom-call | flops 1342177280 | bytes 65536 | tf_op jit(solution)/shard_map/third_product/pallas_call | solution.py:624
  159.0 3.8 %far_trace.1.refs_5_ = f32[1]{0:T(128)} custom-call(s32[40,128]{1,0:T(8,128)S(1)} %get-tuple-element.87.table_ref, f32[4,64,1024]{2,1,0:T(8,128)S(1)} %collective-permute-done.25.refs_2_.refs_0_, f32[2,64,1024]{2,1,0:T(8,128)S(1)} %collective-permute-done.24.refs_1_, f32[2,64,1024]{2,1,0:T(8,128)S(1)} %collective-permute-done.22.refs_1_.refs_2_, ...), custom_call_target="tpu_custom_call" | custom-call | flops 536870912 | bytes 65536 | tf_op jit(solution)/shard_map/far_trace/pallas_call | solution.py:523
  162.8 8.8 %fourth_product.3 = (f32[512,2560]{1,0:T(8,128)S(1)}, f32[3]{0:T(128)S(1)}) custom-call(s32[40,128]{1,0:T(8,128)S(1)} %get-tuple-element.87.table_ref, bf16[512,2560]{1,0:T(8,128)(2,1)S(1)} %get-tuple-element.123.high_ref, bf16[512,2560]{1,0:T(8,128)(2,1)S(1)} %get-tuple-element.124.low_ref, ...), custom_call_target="tpu_custom_call", output_to_operand_aliasing={{0}: (6, {})} | custom-call | flops 2147483648 | bytes 65536 | tf_op jit(solution)/shard_map/fourth_product/pallas_call | solution.py:624
  171.8 1.7 collective-permute-start.34
  173.6 3.2 %fifth_product.3.refs_2_ = f32[512,2560]{1,0:T(8,128)S(1)} custom-call(s32[40,128]{1,0:T(8,128)S(1)} %get-tuple-element.87.table_ref, bf16[512,2560]{1,0:T(8,128)(2,1)S(1)} %get-tuple-element.123.high_ref, bf16[512,2560]{1,0:T(8,128)(2,1)S(1)} %get-tuple-element.124.low_ref, ...), custom_call_target="tpu_custom_call", output_to_operand_aliasing={{}: (4, {})} | custom-call | flops 805306368 | bytes 65536 | tf_op jit(solution)/shard_map/fifth_product/pallas_call | solution.py:624
  176.9 2.1 %collective-permute-start.37 = (f32[3]{0:T(128)S(1)}, f32[3]{0:T(128)S(1)}, u32[]{:S(2)}, u32[]{:S(2)}) collective-permute-start(f32[3]{0:T(128)S(1)} %add_add_fusion.1), channel_id=1, source_target_pairs={{0,4},{1,5},{2,6},{3,7},{4,0},{5,1},{6,2},{7,3},{8,12},{9,13},{10,... | collective-permute-start | bytes 44 | tf_op jit(solution)/shard_map/ppermute | solution.py:654
  179.1 1.4 collective-permute-start.39
  180.5 2.0 %collective-permute-done.38 = f32[3]{0:T(128)S(1)} collective-permute-done((f32[3]{0:T(128)S(1)}, f32[3]{0:T(128)S(1)}, u32[]{:S(2)}, u32[]{:S(2)}) %collective-permute-start.38) | collective-permute-done | bytes 44 | tf_op jit(solution)/shard_map/ppermute | solution.py:654
  182.5 1.0 collective-permute-done.39
  183.6 2.2 %collective-permute-start.40 = (f32[3]{0:T(128)S(1)}, f32[3]{0:T(128)S(1)}, u32[]{:S(2)}, u32[]{:S(2)}) collective-permute-start(f32[3]{0:T(128)S(1)} %add_add_fusion), channel_id=1, source_target_pairs={{0,16},{1,17},{2,18},{3,19},{4,20},{5,21},{6,22},{7,23},{8,24},{9,... | collective-permute-start | bytes 44 | tf_op jit(solution)/shard_map/ppermute | solution.py:654
  185.8 7.2 %last_product.3 = (f32[512,2560]{1,0:T(8,128)S(1)}, f32[8,64,1024]{2,1,0:T(8,128)}) custom-call(s32[40,128]{1,0:T(8,128)S(1)} %get-tuple-element.87.table_ref, bf16[512,2560]{1,0:T(8,128)(2,1)S(1)} %get-tuple-element.123.high_ref, bf16[512,2560]{1,0:T(8,128)(2,1)S(1)} %get-tuple-element.124.low_ref, ...), custom_call_target="tpu_custom_call", output_to_operand_aliasing={{0}: (5, {})} | custom-call | flops 1073741824 | bytes 65536 | tf_op jit(solution)/shard_map/last_product/pallas_call | solution.py:624
  193.1 0.6 pad_maximum_fusion.4
  (55 shorter events, 3.2 us)
Async XLA Ops:
  0.6 1.6 copy-start
  2.2 0.7 copy-start.1
  2.9 0.7 copy-start.2
  3.6 0.7 copy-start.3
  5.5 12.9 %collective-permute-start = (f32[520,128]{1,0:T(8,128)S(1)}, f32[520,128]{1,0:T(8,128)S(1)}, u32[]{:S(2)}, u32[]{:S(2)}) collective-permute-start(f32[520,128]{1,0:T(8,128)S(1)} %get-tuple-element.79), channel_id=1, source_target_pairs={{0,3},{1,0},{2,1},{3,2},{4,7},{5,4},{6,5},{7,6},{8,11},{9,8},{10,9... | collective-permute-start | bytes 798728 | tf_op jit(solution)/shard_map/ppermute | solution.py:676
  8.0 15.6 %collective-permute-start.1 = (f32[520,128]{1,0:T(8,128)S(1)}, f32[520,128]{1,0:T(8,128)S(1)}, u32[]{:S(2)}, u32[]{:S(2)}) collective-permute-start(f32[520,128]{1,0:T(8,128)S(1)} %get-tuple-element.80), channel_id=1, source_target_pairs={{0,1},{1,2},{2,3},{3,0},{4,5},{5,6},{6,7},{7,4},{8,9},{9,10},{10,1... | collective-permute-start | bytes 798728 | tf_op jit(solution)/shard_map/ppermute | solution.py:676
  8.0 16.8 %collective-permute-start.2 = (f32[520,128]{1,0:T(8,128)S(1)}, f32[520,128]{1,0:T(8,128)S(1)}, u32[]{:S(2)}, u32[]{:S(2)}) collective-permute-start(f32[520,128]{1,0:T(8,128)S(1)} %get-tuple-element.81), channel_id=1, source_target_pairs={{0,31},{1,28},{2,29},{3,30},{4,3},{5,0},{6,1},{7,2},{8,7},{9,4},{1... | collective-permute-start | bytes 798728 | tf_op jit(solution)/shard_map/ppermute | solution.py:676
  13.7 20.1 %collective-permute-start.3 = (f32[520,128]{1,0:T(8,128)S(1)}, f32[520,128]{1,0:T(8,128)S(1)}, u32[]{:S(2)}, u32[]{:S(2)}) collective-permute-start(f32[520,128]{1,0:T(8,128)S(1)} %get-tuple-element.82), channel_id=1, source_target_pairs={{0,5},{1,6},{2,7},{3,4},{4,9},{5,10},{6,11},{7,8},{8,13},{9,14},{1... | collective-permute-start | bytes 798728 | tf_op jit(solution)/shard_map/ppermute | solution.py:676
  13.7 26.8 %collective-permute-start.4 = (f32[520,128]{1,0:T(8,128)S(1)}, f32[520,128]{1,0:T(8,128)S(1)}, u32[]{:S(2)}, u32[]{:S(2)}) collective-permute-start(f32[520,128]{1,0:T(8,128)S(1)} %get-tuple-element.83), channel_id=1, source_target_pairs={{0,29},{1,30},{2,31},{3,28},{4,1},{5,2},{6,3},{7,0},{8,5},{9,6},{1... | collective-permute-start | bytes 798728 | tf_op jit(solution)/shard_map/ppermute | solution.py:676
  18.4 22.0 %collective-permute-start.5 = (f32[520,128]{1,0:T(8,128)S(1)}, f32[520,128]{1,0:T(8,128)S(1)}, u32[]{:S(2)}, u32[]{:S(2)}) collective-permute-start(f32[520,128]{1,0:T(8,128)S(1)} %get-tuple-element.84), channel_id=1, source_target_pairs={{0,7},{1,4},{2,5},{3,6},{4,11},{5,8},{6,9},{7,10},{8,15},{9,12},{1... | collective-permute-start | bytes 798728 | tf_op jit(solution)/shard_map/ppermute | solution.py:676
  23.6 21.7 %collective-permute-start.6 = (f32[520,128]{1,0:T(8,128)S(1)}, f32[520,128]{1,0:T(8,128)S(1)}, u32[]{:S(2)}, u32[]{:S(2)}) collective-permute-start(f32[520,128]{1,0:T(8,128)S(1)} %get-tuple-element.85), channel_id=1, source_target_pairs={{0,28},{1,29},{2,30},{3,31},{4,0},{5,1},{6,2},{7,3},{8,4},{9,5},{1... | collective-permute-start | bytes 798728 | tf_op jit(solution)/shard_map/ppermute | solution.py:676
  24.8 20.5 %collective-permute-start.7 = (f32[520,128]{1,0:T(8,128)S(1)}, f32[520,128]{1,0:T(8,128)S(1)}, u32[]{:S(2)}, u32[]{:S(2)}) collective-permute-start(f32[520,128]{1,0:T(8,128)S(1)} %get-tuple-element.86), channel_id=1, source_target_pairs={{0,4},{1,5},{2,6},{3,7},{4,8},{5,9},{6,10},{7,11},{8,12},{9,13},{1... | collective-permute-start | bytes 798728 | tf_op jit(solution)/shard_map/ppermute | solution.py:676
  46.6 16.3 %collective-permute-start.12 = (f32[4,64,1024]{2,1,0:T(8,128)S(1)}, f32[4,64,1024]{2,1,0:T(8,128)S(1)}, u32[]{:S(2)}, u32[]{:S(2)}) collective-permute-start(f32[4,64,1024]{2,1,0:T(8,128)S(1)} %get-tuple-element.100), channel_id=1, source_target_pairs={{0,1},{1,0},{2,3},{3,2},{4,5},{5,4},{6,7},{7,6},{8,9},{9,8},{10,11... | collective-permute-start | bytes 3145736 | tf_op jit(solution)/shard_map/ppermute | solution.py:686
  46.8 15.0 %collective-permute-start.10 = (f32[2,64,1024]{2,1,0:T(8,128)S(1)}, f32[2,64,1024]{2,1,0:T(8,128)S(1)}, u32[]{:S(2)}, u32[]{:S(2)}) collective-permute-start(f32[2,64,1024]{2,1,0:T(8,128)S(1)} %get-tuple-element.98), channel_id=1, source_target_pairs={{0,4},{1,5},{2,6},{3,7},{4,0},{5,1},{6,2},{7,3},{8,12},{9,13},{10,... | collective-permute-start | bytes 1572872 | tf_op jit(solution)/shard_map/ppermute | solution.py:686
  49.0 13.9 %collective-permute-start.11 = (f32[2,64,1024]{2,1,0:T(8,128)S(1)}, f32[2,64,1024]{2,1,0:T(8,128)S(1)}, u32[]{:S(2)}, u32[]{:S(2)}) collective-permute-start(f32[2,64,1024]{2,1,0:T(8,128)S(1)} %get-tuple-element.99), channel_id=1, source_target_pairs={{0,3},{1,2},{2,1},{3,0},{4,7},{5,6},{6,5},{7,4},{8,11},{9,10},{10,... | collective-permute-start | bytes 1572872 | tf_op jit(solution)/shard_map/ppermute | solution.py:686
  50.9 22.0 %collective-permute-start.8 = (f32[2,64,1024]{2,1,0:T(8,128)S(1)}, f32[2,64,1024]{2,1,0:T(8,128)S(1)}, u32[]{:S(2)}, u32[]{:S(2)}) collective-permute-start(f32[2,64,1024]{2,1,0:T(8,128)S(1)} %get-tuple-element.96), channel_id=1, source_target_pairs={{0,4},{1,5},{2,6},{3,7},{4,0},{5,1},{6,2},{7,3},{8,12},{9,13},{10,... | collective-permute-start | bytes 1572872 | tf_op jit(solution)/shard_map/ppermute | solution.py:686
  51.3 22.8 %collective-permute-start.9 = (f32[2,64,1024]{2,1,0:T(8,128)S(1)}, f32[2,64,1024]{2,1,0:T(8,128)S(1)}, u32[]{:S(2)}, u32[]{:S(2)}) collective-permute-start(f32[2,64,1024]{2,1,0:T(8,128)S(1)} %get-tuple-element.97), channel_id=1, source_target_pairs={{0,3},{1,2},{2,1},{3,0},{4,7},{5,6},{6,5},{7,4},{8,11},{9,10},{10,... | collective-permute-start | bytes 1572872 | tf_op jit(solution)/shard_map/ppermute | solution.py:686
  62.9 21.8 %collective-permute-start.13 = (f32[2,64,1024]{2,1,0:T(8,128)S(1)}, f32[2,64,1024]{2,1,0:T(8,128)S(1)}, u32[]{:S(2)}, u32[]{:S(2)}) collective-permute-start(f32[2,64,1024]{2,1,0:T(8,128)S(1)} %collective-permute-done.10.refs_0_), channel_id=1, source_target_pairs={{0,8},{1,9},{2,10},{3,11},{4,28},{5,29},{6,30},{7,31},{8,16},{9,17... | collective-permute-start | bytes 1572872 | tf_op jit(solution)/shard_map/ppermute | solution.py:686
  64.6 20.0 %collective-permute-start.14 = (f32[2,64,1024]{2,1,0:T(8,128)S(1)}, f32[2,64,1024]{2,1,0:T(8,128)S(1)}, u32[]{:S(2)}, u32[]{:S(2)}) collective-permute-start(f32[2,64,1024]{2,1,0:T(8,128)S(1)} %collective-permute-done.11.refs_1_), channel_id=1, source_target_pairs={{0,4},{1,5},{2,6},{3,7},{4,0},{5,1},{6,2},{7,3},{8,12},{9,13},{10,... | collective-permute-start | bytes 1572872 | tf_op jit(solution)/shard_map/ppermute | solution.py:686
  68.0 17.3 %collective-permute-start.18 = (f32[2,64,1024]{2,1,0:T(8,128)S(1)}, f32[2,64,1024]{2,1,0:T(8,128)S(1)}, u32[]{:S(2)}, u32[]{:S(2)}) collective-permute-start(f32[2,64,1024]{2,1,0:T(8,128)S(1)} %collective-permute-done.10.refs_0_), channel_id=1, source_target_pairs={{0,3},{1,2},{2,1},{3,0},{4,7},{5,6},{6,5},{7,4},{8,11},{9,10},{10,... | collective-permute-start | bytes 1572872 | tf_op jit(solution)/shard_map/ppermute | solution.py:686
  74.1 17.1 %collective-permute-start.17 = (f32[2,64,1024]{2,1,0:T(8,128)S(1)}, f32[2,64,1024]{2,1,0:T(8,128)S(1)}, u32[]{:S(2)}, u32[]{:S(2)}) collective-permute-start(f32[2,64,1024]{2,1,0:T(8,128)S(1)} %collective-permute-done.8.refs_0_), channel_id=1, source_target_pairs={{0,8},{1,9},{2,10},{3,11},{4,28},{5,29},{6,30},{7,31},{8,16},{9,17... | collective-permute-start | bytes 1572872 | tf_op jit(solution)/shard_map/ppermute | solution.py:686
  84.7 8.2 %collective-permute-start.20 = (f32[4,64,1024]{2,1,0:T(8,128)S(1)}, f32[4,64,1024]{2,1,0:T(8,128)S(1)}, u32[]{:S(2)}, u32[]{:S(2)}) collective-permute-start(f32[4,64,1024]{2,1,0:T(8,128)S(1)} %pad_maximum_fusion.1), channel_id=1, source_target_pairs={{0,1},{1,0},{2,3},{3,2},{4,5},{5,4},{6,7},{7,6},{8,9},{9,8},{10,11... | collective-permute-start | bytes 3145736 | tf_op jit(solution)/shard_map/ppermute | solution.py:686
  91.3 9.1 %collective-permute-start.19 = (f32[4,64,1024]{2,1,0:T(8,128)S(1)}, f32[4,64,1024]{2,1,0:T(8,128)S(1)}, u32[]{:S(2)}, u32[]{:S(2)}) collective-permute-start(f32[4,64,1024]{2,1,0:T(8,128)S(1)} %pad_maximum_fusion), channel_id=1, source_target_pairs={{0,1},{1,0},{2,3},{3,2},{4,5},{5,4},{6,7},{7,6},{8,9},{9,8},{10,11... | collective-permute-start | bytes 3145736 | tf_op jit(solution)/shard_map/ppermute | solution.py:686
  91.4 16.1 %collective-permute-start.15 = (f32[2,64,1024]{2,1,0:T(8,128)S(1)}, f32[2,64,1024]{2,1,0:T(8,128)S(1)}, u32[]{:S(2)}, u32[]{:S(2)}) collective-permute-start(f32[2,64,1024]{2,1,0:T(8,128)S(1)} %collective-permute-done.14.refs_1_), channel_id=1, source_target_pairs={{0,8},{1,9},{2,10},{3,11},{4,28},{5,29},{6,30},{7,31},{8,16},{9,17... | collective-permute-start | bytes 1572872 | tf_op jit(solution)/shard_map/ppermute | solution.py:686
  92.3 15.1 %collective-permute-start.16 = (f32[2,64,1024]{2,1,0:T(8,128)S(1)}, f32[2,64,1024]{2,1,0:T(8,128)S(1)}, u32[]{:S(2)}, u32[]{:S(2)}) collective-permute-start(f32[2,64,1024]{2,1,0:T(8,128)S(1)} %collective-permute-done.13.refs_0_), channel_id=1, source_target_pairs={{0,3},{1,2},{2,1},{3,0},{4,7},{5,6},{6,5},{7,4},{8,11},{9,10},{10,... | collective-permute-start | bytes 1572872 | tf_op jit(solution)/shard_map/ppermute | solution.py:686
  114.6 16.2 %collective-permute-start.25 = (f32[4,64,1024]{2,1,0:T(8,128)S(1)}, f32[4,64,1024]{2,1,0:T(8,128)S(1)}, u32[]{:S(2)}, u32[]{:S(2)}) collective-permute-start(f32[4,64,1024]{2,1,0:T(8,128)S(1)} %get-tuple-element.129), channel_id=1, source_target_pairs={{0,1},{1,0},{2,3},{3,2},{4,5},{5,4},{6,7},{7,6},{8,9},{9,8},{10,11... | collective-permute-start | bytes 3145736 | tf_op jit(solution)/shard_map/ppermute | solution.py:686
  114.7 15.0 %collective-permute-start.23 = (f32[2,64,1024]{2,1,0:T(8,128)S(1)}, f32[2,64,1024]{2,1,0:T(8,128)S(1)}, u32[]{:S(2)}, u32[]{:S(2)}) collective-permute-start(f32[2,64,1024]{2,1,0:T(8,128)S(1)} %get-tuple-element.127), channel_id=1, source_target_pairs={{0,4},{1,5},{2,6},{3,7},{4,0},{5,1},{6,2},{7,3},{8,12},{9,13},{10,... | collective-permute-start | bytes 1572872 | tf_op jit(solution)/shard_map/ppermute | solution.py:686
  116.9 14.0 %collective-permute-start.24 = (f32[2,64,1024]{2,1,0:T(8,128)S(1)}, f32[2,64,1024]{2,1,0:T(8,128)S(1)}, u32[]{:S(2)}, u32[]{:S(2)}) collective-permute-start(f32[2,64,1024]{2,1,0:T(8,128)S(1)} %get-tuple-element.128), channel_id=1, source_target_pairs={{0,3},{1,2},{2,1},{3,0},{4,7},{5,6},{6,5},{7,4},{8,11},{9,10},{10,... | collective-permute-start | bytes 1572872 | tf_op jit(solution)/shard_map/ppermute | solution.py:686
  118.0 22.9 %collective-permute-start.21 = (f32[2,64,1024]{2,1,0:T(8,128)S(1)}, f32[2,64,1024]{2,1,0:T(8,128)S(1)}, u32[]{:S(2)}, u32[]{:S(2)}) collective-permute-start(f32[2,64,1024]{2,1,0:T(8,128)S(1)} %get-tuple-element.125), channel_id=1, source_target_pairs={{0,4},{1,5},{2,6},{3,7},{4,0},{5,1},{6,2},{7,3},{8,12},{9,13},{10,... | collective-permute-start | bytes 1572872 | tf_op jit(solution)/shard_map/ppermute | solution.py:686
  118.1 23.9 %collective-permute-start.22 = (f32[2,64,1024]{2,1,0:T(8,128)S(1)}, f32[2,64,1024]{2,1,0:T(8,128)S(1)}, u32[]{:S(2)}, u32[]{:S(2)}) collective-permute-start(f32[2,64,1024]{2,1,0:T(8,128)S(1)} %get-tuple-element.126), channel_id=1, source_target_pairs={{0,3},{1,2},{2,1},{3,0},{4,7},{5,6},{6,5},{7,4},{8,11},{9,10},{10,... | collective-permute-start | bytes 1572872 | tf_op jit(solution)/shard_map/ppermute | solution.py:686
  130.8 20.1 %collective-permute-start.26 = (f32[2,64,1024]{2,1,0:T(8,128)S(1)}, f32[2,64,1024]{2,1,0:T(8,128)S(1)}, u32[]{:S(2)}, u32[]{:S(2)}) collective-permute-start(f32[2,64,1024]{2,1,0:T(8,128)S(1)} %collective-permute-done.23.refs_0_), channel_id=1, source_target_pairs={{0,8},{1,9},{2,10},{3,11},{4,28},{5,29},{6,30},{7,31},{8,16},{9,17... | collective-permute-start | bytes 1572872 | tf_op jit(solution)/shard_map/ppermute | solution.py:686
  131.0 20.8 %collective-permute-start.27 = (f32[2,64,1024]{2,1,0:T(8,128)S(1)}, f32[2,64,1024]{2,1,0:T(8,128)S(1)}, u32[]{:S(2)}, u32[]{:S(2)}) collective-permute-start(f32[2,64,1024]{2,1,0:T(8,128)S(1)} %collective-permute-done.24.refs_1_), channel_id=1, source_target_pairs={{0,4},{1,5},{2,6},{3,7},{4,0},{5,1},{6,2},{7,3},{8,12},{9,13},{10,... | collective-permute-start | bytes 1572872 | tf_op jit(solution)/shard_map/ppermute | solution.py:686
  133.3 20.0 %collective-permute-start.31 = (f32[2,64,1024]{2,1,0:T(8,128)S(1)}, f32[2,64,1024]{2,1,0:T(8,128)S(1)}, u32[]{:S(2)}, u32[]{:S(2)}) collective-permute-start(f32[2,64,1024]{2,1,0:T(8,128)S(1)} %collective-permute-done.23.refs_0_), channel_id=1, source_target_pairs={{0,3},{1,2},{2,1},{3,0},{4,7},{5,6},{6,5},{7,4},{8,11},{9,10},{10,... | collective-permute-start | bytes 1572872 | tf_op jit(solution)/shard_map/ppermute | solution.py:686
  142.1 16.3 %collective-permute-start.30 = (f32[2,64,1024]{2,1,0:T(8,128)S(1)}, f32[2,64,1024]{2,1,0:T(8,128)S(1)}, u32[]{:S(2)}, u32[]{:S(2)}) collective-permute-start(f32[2,64,1024]{2,1,0:T(8,128)S(1)} %collective-permute-done.21.refs_0_), channel_id=1, source_target_pairs={{0,8},{1,9},{2,10},{3,11},{4,28},{5,29},{6,30},{7,31},{8,16},{9,17... | collective-permute-start | bytes 1572872 | tf_op jit(solution)/shard_map/ppermute | solution.py:686
  151.9 10.9 %collective-permute-start.32 = (f32[4,64,1024]{2,1,0:T(8,128)S(1)}, f32[4,64,1024]{2,1,0:T(8,128)S(1)}, u32[]{:S(2)}, u32[]{:S(2)}) collective-permute-start(f32[4,64,1024]{2,1,0:T(8,128)S(1)} %pad_maximum_fusion.2), channel_id=1, source_target_pairs={{0,1},{1,0},{2,3},{3,2},{4,5},{5,4},{6,7},{7,6},{8,9},{9,8},{10,11... | collective-permute-start | bytes 3145736 | tf_op jit(solution)/shard_map/ppermute | solution.py:686
  158.4 15.1 %collective-permute-start.36 = (f32[4,64,1024]{2,1,0:T(8,128)S(1)}, f32[4,64,1024]{2,1,0:T(8,128)S(1)}, u32[]{:S(2)}, u32[]{:S(2)}) collective-permute-start(f32[4,64,1024]{2,1,0:T(8,128)S(1)} %pad_maximum_fusion.3), channel_id=1, source_target_pairs={{0,1},{1,0},{2,3},{3,2},{4,5},{5,4},{6,7},{7,6},{8,9},{9,8},{10,11... | collective-permute-start | bytes 3145736 | tf_op jit(solution)/shard_map/ppermute | solution.py:686
  158.6 27.2 %collective-permute-start.29 = (f32[2,64,1024]{2,1,0:T(8,128)S(1)}, f32[2,64,1024]{2,1,0:T(8,128)S(1)}, u32[]{:S(2)}, u32[]{:S(2)}) collective-permute-start(f32[2,64,1024]{2,1,0:T(8,128)S(1)} %collective-permute-done.26.refs_0_.refs_4_), channel_id=1, source_target_pairs={{0,3},{1,2},{2,1},{3,0},{4,7},{5,6},{6,5},{7,4},{8,11},{9,10},{10,... | collective-permute-start | bytes 1572872 | tf_op jit(solution)/shard_map/ppermute | solution.py:686
  158.9 27.0 %collective-permute-start.28 = (f32[2,64,1024]{2,1,0:T(8,128)S(1)}, f32[2,64,1024]{2,1,0:T(8,128)S(1)}, u32[]{:S(2)}, u32[]{:S(2)}) collective-permute-start(f32[2,64,1024]{2,1,0:T(8,128)S(1)} %collective-permute-done.27.refs_1_), channel_id=1, source_target_pairs={{0,8},{1,9},{2,10},{3,11},{4,28},{5,29},{6,30},{7,31},{8,16},{9,17... | collective-permute-start | bytes 1572872 | tf_op jit(solution)/shard_map/ppermute | solution.py:686
  171.6 5.2 %collective-permute-start.33 = (f32[3]{0:T(128)S(1)}, f32[3]{0:T(128)S(1)}, u32[]{:S(2)}, u32[]{:S(2)}) collective-permute-start(f32[3]{0:T(128)S(1)} %get-tuple-element.145), channel_id=1, source_target_pairs={{0,1},{1,0},{2,3},{3,2},{4,5},{5,4},{6,7},{7,6},{8,9},{9,8},{10,11... | collective-permute-start | bytes 44 | tf_op jit(solution)/shard_map/ppermute | solution.py:654
  171.8 5.1 %collective-permute-start.34 = (f32[3]{0:T(128)S(1)}, f32[3]{0:T(128)S(1)}, u32[]{:S(2)}, u32[]{:S(2)}) collective-permute-start(f32[3]{0:T(128)S(1)} %get-tuple-element.145), channel_id=1, source_target_pairs={{0,2},{1,3},{2,0},{3,1},{4,6},{5,7},{6,4},{7,5},{8,10},{9,11},{10,... | collective-permute-start | bytes 44 | tf_op jit(solution)/shard_map/ppermute | solution.py:654
  173.5 3.4 %collective-permute-start.35 = (f32[3]{0:T(128)S(1)}, f32[3]{0:T(128)S(1)}, u32[]{:S(2)}, u32[]{:S(2)}) collective-permute-start(f32[3]{0:T(128)S(1)} %get-tuple-element.145), channel_id=1, source_target_pairs={{0,3},{1,2},{2,1},{3,0},{4,7},{5,6},{6,5},{7,4},{8,11},{9,10},{10,... | collective-permute-start | bytes 44 | tf_op jit(solution)/shard_map/ppermute | solution.py:654
  176.9 3.6 %collective-permute-start.37 = (f32[3]{0:T(128)S(1)}, f32[3]{0:T(128)S(1)}, u32[]{:S(2)}, u32[]{:S(2)}) collective-permute-start(f32[3]{0:T(128)S(1)} %add_add_fusion.1), channel_id=1, source_target_pairs={{0,4},{1,5},{2,6},{3,7},{4,0},{5,1},{6,2},{7,3},{8,12},{9,13},{10,... | collective-permute-start | bytes 44 | tf_op jit(solution)/shard_map/ppermute | solution.py:654
  179.0 3.5 %collective-permute-start.38 = (f32[3]{0:T(128)S(1)}, f32[3]{0:T(128)S(1)}, u32[]{:S(2)}, u32[]{:S(2)}) collective-permute-start(f32[3]{0:T(128)S(1)} %add_add_fusion.1), channel_id=1, source_target_pairs={{0,8},{1,9},{2,10},{3,11},{4,12},{5,13},{6,14},{7,15},{8,0},{9,1},... | collective-permute-start | bytes 44 | tf_op jit(solution)/shard_map/ppermute | solution.py:654
  179.1 4.4 %collective-permute-start.39 = (f32[3]{0:T(128)S(1)}, f32[3]{0:T(128)S(1)}, u32[]{:S(2)}, u32[]{:S(2)}) collective-permute-start(f32[3]{0:T(128)S(1)} %add_add_fusion.1), channel_id=1, source_target_pairs={{0,12},{1,13},{2,14},{3,15},{4,8},{5,9},{6,10},{7,11},{8,4},{9,5},... | collective-permute-start | bytes 44 | tf_op jit(solution)/shard_map/ppermute | solution.py:654
  183.6 9.5 %collective-permute-start.40 = (f32[3]{0:T(128)S(1)}, f32[3]{0:T(128)S(1)}, u32[]{:S(2)}, u32[]{:S(2)}) collective-permute-start(f32[3]{0:T(128)S(1)} %add_add_fusion), channel_id=1, source_target_pairs={{0,16},{1,17},{2,18},{3,19},{4,20},{5,21},{6,22},{7,23},{8,24},{9,... | collective-permute-start | bytes 44 | tf_op jit(solution)/shard_map/ppermute | solution.py:654

commit v8 on v6

--- a/solution.py
+++ b/solution.py
@@ -720,10 +720,8 @@
             sums = sum_round(sums, rounds[0])
             (total,) = fifth(total=total)
             sums, total = tie((sums, total))
-            for perms in rounds[1:-1]:
+            for perms in rounds[1:]:
                 sums = sum_round(sums, perms)
-            sums, total = tie((sums, total))
-            sums = sum_round(sums, rounds[-1])
             _, current = last(total=total, square=(spots, small, current))
     sums = sums * (1.0 / (count_x * count_y * row_count * block))
     occupation = jnp.stack([sums[0], sums[1], sums[1], sums[2]])

time: 194 us -> 193 us (level)
  transfers between devices with their start and end apart: 41 -> 41, of which waited for: 20 -> 19; matrix products, arithmetic and copies ran while one was open for 0% -> 0% of each run, Pallas kernels for 45% -> 46%
where the time goes in v8:
time: 193 us
  Pallas kernels  97.4 us (50%)
  starting transfers between devices  48.5 us (25%)
  waiting for transfers between devices  41.4 us (21%)
  local copies, waits for them, and re-layouts  3.65 us (2%)
    pallas_call x12, Pallas kernels, add_product(): pl.pallas_call(kernel, out_shape=out_shape, in_specs=in_specs, out_specs=...  73.4 us
    ppermute x26, starting transfers between devices, shards(): go = lambda value, way: lax.ppermute(value, AXES, swap[way])  20.7 us
    ppermute x8, waiting for transfers between devices, shards(): arrived[d] = lax.ppermute(leaving[d], AXES, perm)  20 us
    ppermute x8, starting transfers between devices, shards(): arrived[d] = lax.ppermute(leaving[d], AXES, perm)  19.9 us
    ppermute x26, waiting for transfers between devices, shards(): go = lambda value, way: lax.ppermute(value, AXES, swap[way])  19.3 us
    pallas_call x2, Pallas kernels, own_product(): pl.pallas_call(kernel, out_shape=(dense(jnp.bfloat16), dense(jnp.bfloat16...  14.6 us
    ppermute x7, starting transfers between devices, sum_round(): others = [lax.ppermute(value, AXES, perm) for perm in perms]  8 us
  transfers between devices with their start and end apart: 41, of which 19 were waited for; matrix products, arithmetic and copies ran while one was open for 0% of the time, Pallas kernels for 46%

profile of v8, /device:TPU:0, one launch (start us, length us, event | category | flops | bytes accessed | tf_op | source)
XLA Modules:
  0.0 192.8 jit_solution(11958296353430345018)
XLA Ops:
  0.6 1.6 copy-done
  2.2 0.7 copy-done.1
  2.9 0.7 copy-done.2
  3.6 0.7 copy-done.3
  4.2 1.3 pack_rows.1
  5.5 2.5 %collective-permute-start = (f32[520,128]{1,0:T(8,128)S(1)}, f32[520,128]{1,0:T(8,128)S(1)}, u32[]{:S(2)}, u32[]{:S(2)}) collective-permute-start(f32[520,128]{1,0:T(8,128)S(1)} %get-tuple-element.77), channel_id=1, source_target_pairs={{0,3},{1,0},{2,1},{3,2},{4,7},{5,4},{6,5},{7,6},{8,11},{9,8},{10,9... | collective-permute-start | bytes 798728 | tf_op jit(solution)/shard_map/ppermute | solution.py:676
  8.0 5.7 %collective-permute-start.2 = (f32[520,128]{1,0:T(8,128)S(1)}, f32[520,128]{1,0:T(8,128)S(1)}, u32[]{:S(2)}, u32[]{:S(2)}) collective-permute-start(f32[520,128]{1,0:T(8,128)S(1)} %get-tuple-element.79), channel_id=1, source_target_pairs={{0,31},{1,28},{2,29},{3,30},{4,3},{5,0},{6,1},{7,2},{8,7},{9,4},{1... | collective-permute-start | bytes 798728 | tf_op jit(solution)/shard_map/ppermute | solution.py:676
  13.7 4.5 %collective-permute-start.4 = (f32[520,128]{1,0:T(8,128)S(1)}, f32[520,128]{1,0:T(8,128)S(1)}, u32[]{:S(2)}, u32[]{:S(2)}) collective-permute-start(f32[520,128]{1,0:T(8,128)S(1)} %get-tuple-element.81), channel_id=1, source_target_pairs={{0,29},{1,30},{2,31},{3,28},{4,1},{5,2},{6,3},{7,0},{8,5},{9,6},{1... | collective-permute-start | bytes 798728 | tf_op jit(solution)/shard_map/ppermute | solution.py:676
  18.4 5.2 %collective-permute-start.5 = (f32[520,128]{1,0:T(8,128)S(1)}, f32[520,128]{1,0:T(8,128)S(1)}, u32[]{:S(2)}, u32[]{:S(2)}) collective-permute-start(f32[520,128]{1,0:T(8,128)S(1)} %get-tuple-element.82), channel_id=1, source_target_pairs={{0,7},{1,4},{2,5},{3,6},{4,11},{5,8},{6,9},{7,10},{8,15},{9,12},{1... | collective-permute-start | bytes 798728 | tf_op jit(solution)/shard_map/ppermute | solution.py:676
  23.6 1.2 collective-permute-start.6
  24.8 0.8 collective-permute-start.7
  25.6 8.1 %collective-permute-done.3.refs_3_ = f32[520,128]{1,0:T(8,128)S(1)} collective-permute-done((f32[520,128]{1,0:T(8,128)S(1)}, f32[520,128]{1,0:T(8,128)S(1)}, u32[]{:S(2)}, u32[]{:S(2)}) %collective-permute-start.3) | collective-permute-done | bytes 266272 | tf_op jit(solution)/shard_map/ppermute | solution.py:676
  33.8 6.7 %collective-permute-done.4.refs_4_ = f32[520,128]{1,0:T(8,128)S(1)} collective-permute-done((f32[520,128]{1,0:T(8,128)S(1)}, f32[520,128]{1,0:T(8,128)S(1)}, u32[]{:S(2)}, u32[]{:S(2)}) %collective-permute-start.4) | collective-permute-done | bytes 266272 | tf_op jit(solution)/shard_map/ppermute | solution.py:676
  40.5 4.9 %collective-permute-done.6.refs_6_ = f32[520,128]{1,0:T(8,128)S(1)} collective-permute-done((f32[520,128]{1,0:T(8,128)S(1)}, f32[520,128]{1,0:T(8,128)S(1)}, u32[]{:S(2)}, u32[]{:S(2)}) %collective-permute-start.6) | collective-permute-done | bytes 266272 | tf_op jit(solution)/shard_map/ppermute | solution.py:676
  45.3 1.2 place_rows.1
  46.8 2.2 %collective-permute-start.10 = (f32[2,64,1024]{2,1,0:T(8,128)S(1)}, f32[2,64,1024]{2,1,0:T(8,128)S(1)}, u32[]{:S(2)}, u32[]{:S(2)}) collective-permute-start(f32[2,64,1024]{2,1,0:T(8,128)S(1)} %get-tuple-element.96), channel_id=1, source_target_pairs={{0,4},{1,5},{2,6},{3,7},{4,0},{5,1},{6,2},{7,3},{8,12},{9,13},{10,... | collective-permute-start | bytes 1572872 | tf_op jit(solution)/shard_map/ppermute | solution.py:686
  49.0 0.8 collective-permute-start.11
  49.8 1.1 spread_own.2
  50.9 0.3 collective-permute-start.8
  51.3 0.7 collective-permute-start.9
  52.0 0.8 make_tables.1
  52.8 7.3 %own_product.2 = (bf16[512,2560]{1,0:T(8,128)(2,1)S(1)}, bf16[512,2560]{1,0:T(8,128)(2,1)S(1)}, f32[512,2560]{1,0:T(8,128)S(1)}) custom-call(s32[40,128]{1,0:T(8,128)S(1)} %get-tuple-element.85.table_ref, bf16[2,512,1152]{2,1,0:T(8,128)(2,1)S(1)} %get-tuple-element.90.wide_high, bf16[2,512,1152]{2,1,0:T(8,128)(2,1)S(1)} %get-tuple-element.91.wide_low), custom_call_target="tpu_custom_call" | custom-call | flops 2684354560 | bytes 65536 | tf_op jit(solution)/shard_map/own_product/pallas_call | solution.py:451
  60.2 1.6 collective-permute-done.10.refs_0_
  61.7 1.1 collective-permute-done.11.refs_1_
  62.9 1.8 collective-permute-start.13
  64.6 3.4 %collective-permute-start.14 = (f32[2,64,1024]{2,1,0:T(8,128)S(1)}, f32[2,64,1024]{2,1,0:T(8,128)S(1)}, u32[]{:S(2)}, u32[]{:S(2)}) collective-permute-start(f32[2,64,1024]{2,1,0:T(8,128)S(1)} %collective-permute-done.11.refs_1_), channel_id=1, source_target_pairs={{0,4},{1,5},{2,6},{3,7},{4,0},{5,1},{6,2},{7,3},{8,12},{9,13},{10,... | collective-permute-start | bytes 1572872 | tf_op jit(solution)/shard_map/ppermute | solution.py:686
  68.0 4.7 %first_product.2.refs_3_ = f32[512,2560]{1,0:T(8,128)S(1)} custom-call(s32[40,128]{1,0:T(8,128)S(1)} %get-tuple-element.85.table_ref, bf16[512,2560]{1,0:T(8,128)(2,1)S(1)} %get-tuple-element.92.high_ref, bf16[512,2560]{1,0:T(8,128)(2,1)S(1)} %get-tuple-element.93.low_ref, ...), custom_call_target="tpu_custom_call", output_to_operand_aliasing={{}: (5, {})} | custom-call | flops 1342177280 | bytes 65536 | tf_op jit(solution)/shard_map/first_product/pallas_call | solution.py:624
  73.0 1.1 collective-permute-done.9.refs_1_
  74.1 1.8 collective-permute-start.17
  75.9 8.8 %second_product.2.refs_2_ = f32[512,2560]{1,0:T(8,128)S(1)} custom-call(s32[40,128]{1,0:T(8,128)S(1)} %get-tuple-element.85.table_ref, bf16[512,2560]{1,0:T(8,128)(2,1)S(1)} %get-tuple-element.92.high_ref, bf16[512,2560]{1,0:T(8,128)(2,1)S(1)} %get-tuple-element.93.low_ref, ...), custom_call_target="tpu_custom_call", output_to_operand_aliasing={{}: (6, {})} | custom-call | flops 2684354560 | bytes 65536 | tf_op jit(solution)/shard_map/second_product/pallas_call | solution.py:624
  84.7 0.4 collective-permute-start.20
  85.3 4.7 %third_product.2.refs_3_ = f32[512,2560]{1,0:T(8,128)S(1)} custom-call(s32[40,128]{1,0:T(8,128)S(1)} %get-tuple-element.85.table_ref, bf16[512,2560]{1,0:T(8,128)(2,1)S(1)} %get-tuple-element.92.high_ref, bf16[512,2560]{1,0:T(8,128)(2,1)S(1)} %get-tuple-element.93.low_ref, ...), custom_call_target="tpu_custom_call", output_to_operand_aliasing={{}: (5, {})} | custom-call | flops 1342177280 | bytes 65536 | tf_op jit(solution)/shard_map/third_product/pallas_call | solution.py:624
  90.0 1.2 collective-permute-done.17.refs_0_
  91.4 0.9 collective-permute-start.15
  92.3 0.6 collective-permute-start.16
  92.9 7.4 %fourth_product.2.refs_1_ = f32[512,2560]{1,0:T(8,128)S(1)} custom-call(s32[40,128]{1,0:T(8,128)S(1)} %get-tuple-element.85.table_ref, bf16[512,2560]{1,0:T(8,128)(2,1)S(1)} %get-tuple-element.92.high_ref, bf16[512,2560]{1,0:T(8,128)(2,1)S(1)} %get-tuple-element.93.low_ref, ...), custom_call_target="tpu_custom_call", output_to_operand_aliasing={{}: (6, {})} | custom-call | flops 2147483648 | bytes 65536 | tf_op jit(solution)/shard_map/fourth_product/pallas_call | solution.py:624
  100.3 3.2 %fifth_product.2.refs_2_ = f32[512,2560]{1,0:T(8,128)S(1)} custom-call(s32[40,128]{1,0:T(8,128)S(1)} %get-tuple-element.85.table_ref, bf16[512,2560]{1,0:T(8,128)(2,1)S(1)} %get-tuple-element.92.high_ref, bf16[512,2560]{1,0:T(8,128)(2,1)S(1)} %get-tuple-element.93.low_ref, ...), custom_call_target="tpu_custom_call", output_to_operand_aliasing={{}: (4, {})} | custom-call | flops 805306368 | bytes 65536 | tf_op jit(solution)/shard_map/fifth_product/pallas_call | solution.py:624
  103.6 3.9 %collective-permute-done.15.refs_0_ = f32[2,64,1024]{2,1,0:T(8,128)S(1)} collective-permute-done((f32[2,64,1024]{2,1,0:T(8,128)S(1)}, f32[2,64,1024]{2,1,0:T(8,128)S(1)}, u32[]{:S(2)}, u32[]{:S(2)}) %collective-permute-start.15) | collective-permute-done | bytes 524320 | tf_op jit(solution)/shard_map/ppermute | solution.py:686
  107.5 7.1 %last_product.2 = (f32[512,2560]{1,0:T(8,128)S(1)}, f32[2]{0:T(128)S(1)}, f32[8,64,1024]{2,1,0:T(8,128)S(1)}, f32[4,64,1024]{2,1,0:T(8,128)S(1)}, f32[2,64,1024]...) custom-call(s32[40,128]{1,0:T(8,128)S(1)} %get-tuple-element.85.tabl, ...), custom_call_target="tpu_custom_call", output_to_operand_aliasing={{0}: (5, {})} | custom-call | flops 1073741824 | bytes 65536 | tf_op jit(solution)/shard_map/last_product/pallas_call | solution.py:624
  114.7 2.1 %collective-permute-start.23 = (f32[2,64,1024]{2,1,0:T(8,128)S(1)}, f32[2,64,1024]{2,1,0:T(8,128)S(1)}, u32[]{:S(2)}, u32[]{:S(2)}) collective-permute-start(f32[2,64,1024]{2,1,0:T(8,128)S(1)} %get-tuple-element.125), channel_id=1, source_target_pairs={{0,4},{1,5},{2,6},{3,7},{4,0},{5,1},{6,2},{7,3},{8,12},{9,13},{10,... | collective-permute-start | bytes 1572872 | tf_op jit(solution)/shard_map/ppermute | solution.py:686
  116.8 1.1 spread_own.3
  118.1 1.7 collective-permute-start.22
  119.8 7.3 %own_product.3 = (bf16[512,2560]{1,0:T(8,128)(2,1)S(1)}, bf16[512,2560]{1,0:T(8,128)(2,1)S(1)}, f32[512,2560]{1,0:T(8,128)S(1)}) custom-call(s32[40,128]{1,0:T(8,128)S(1)} %get-tuple-element.85.table_ref, bf16[2,512,1152]{2,1,0:T(8,128)(2,1)S(1)} %get-tuple-element.119.wide_high, bf16[2,512,1152]{2,1,0:T(8,128)(2,1)S(1)} %get-tuple-element.120.wide_low), custom_call_target="tpu_custom_call" | custom-call | flops 2684354560 | bytes 65536 | tf_op jit(solution)/shard_map/own_product/pallas_call | solution.py:451
  127.2 2.4 %collective-permute-done.23.refs_0_ = f32[2,64,1024]{2,1,0:T(8,128)S(1)} collective-permute-done((f32[2,64,1024]{2,1,0:T(8,128)S(1)}, f32[2,64,1024]{2,1,0:T(8,128)S(1)}, u32[]{:S(2)}, u32[]{:S(2)}) %collective-permute-start.23) | collective-permute-done | bytes 524320 | tf_op jit(solution)/shard_map/ppermute | solution.py:686
  129.6 1.1 collective-permute-done.24.refs_1_
  131.0 2.4 %collective-permute-start.27 = (f32[2,64,1024]{2,1,0:T(8,128)S(1)}, f32[2,64,1024]{2,1,0:T(8,128)S(1)}, u32[]{:S(2)}, u32[]{:S(2)}) collective-permute-start(f32[2,64,1024]{2,1,0:T(8,128)S(1)} %collective-permute-done.24.refs_1_), channel_id=1, source_target_pairs={{0,4},{1,5},{2,6},{3,7},{4,0},{5,1},{6,2},{7,3},{8,12},{9,13},{10,... | collective-permute-start | bytes 1572872 | tf_op jit(solution)/shard_map/ppermute | solution.py:686
  133.3 4.7 %first_product.3.refs_3_ = f32[512,2560]{1,0:T(8,128)S(1)} custom-call(s32[40,128]{1,0:T(8,128)S(1)} %get-tuple-element.85.table_ref, bf16[512,2560]{1,0:T(8,128)(2,1)S(1)} %get-tuple-element.121.high_ref, bf16[512,2560]{1,0:T(8,128)(2,1)S(1)} %get-tuple-element.122.low_ref, ...), custom_call_target="tpu_custom_call", output_to_operand_aliasing={{}: (5, {})} | custom-call | flops 1342177280 | bytes 65536 | tf_op jit(solution)/shard_map/first_product/pallas_call | solution.py:624
  138.0 2.8 %collective-permute-done.21.refs_0_ = f32[2,64,1024]{2,1,0:T(8,128)S(1)} collective-permute-done((f32[2,64,1024]{2,1,0:T(8,128)S(1)}, f32[2,64,1024]{2,1,0:T(8,128)S(1)}, u32[]{:S(2)}, u32[]{:S(2)}) %collective-permute-start.21) | collective-permute-done | bytes 524320 | tf_op jit(solution)/shard_map/ppermute | solution.py:686
  140.8 1.1 collective-permute-done.22.refs_1_.refs_2_
  142.2 8.8 %second_product.3.refs_2_ = f32[512,2560]{1,0:T(8,128)S(1)} custom-call(s32[40,128]{1,0:T(8,128)S(1)} %get-tuple-element.85.table_ref, bf16[512,2560]{1,0:T(8,128)(2,1)S(1)} %get-tuple-element.121.high_ref, bf16[512,2560]{1,0:T(8,128)(2,1)S(1)} %get-tuple-element.122.low_ref, ...), custom_call_target="tpu_custom_call", output_to_operand_aliasing={{}: (6, {})} | custom-call | flops 2684354560 | bytes 65536 | tf_op jit(solution)/shard_map/second_product/pallas_call | solution.py:624
  151.0 0.8 collective-permute-done.27.refs_1_
  151.9 1.3 collective-permute-done.31.refs_1_
  153.2 4.7 %third_product.3.refs_3_ = f32[512,2560]{1,0:T(8,128)S(1)} custom-call(s32[40,128]{1,0:T(8,128)S(1)} %get-tuple-element.85.table_ref, bf16[512,2560]{1,0:T(8,128)(2,1)S(1)} %get-tuple-element.121.high_ref, bf16[512,2560]{1,0:T(8,128)(2,1)S(1)} %get-tuple-element.122.low_ref, ...), custom_call_target="tpu_custom_call", output_to_operand_aliasing={{}: (5, {})} | custom-call | flops 1342177280 | bytes 65536 | tf_op jit(solution)/shard_map/third_product/pallas_call | solution.py:624
  157.9 0.5 collective-permute-done.30.refs_3_.refs_0_
  158.8 3.8 %far_trace.1.refs_5_ = f32[1]{0:T(128)} custom-call(s32[40,128]{1,0:T(8,128)S(1)} %get-tuple-element.85.table_ref, f32[4,64,1024]{2,1,0:T(8,128)S(1)} %collective-permute-done.25.refs_2_.refs_0_, f32[2,64,1024]{2,1,0:T(8,128)S(1)} %collective-permute-done.24.refs_1_, f32[2,64,1024]{2,1,0:T(8,128)S(1)} %collective-permute-done.22.refs_1_.refs_2_, ...), custom_call_target="tpu_custom_call" | custom-call | flops 536870912 | bytes 65536 | tf_op jit(solution)/shard_map/far_trace/pallas_call | solution.py:523
  162.7 8.8 %fourth_product.3 = (f32[512,2560]{1,0:T(8,128)S(1)}, f32[3]{0:T(128)S(1)}) custom-call(s32[40,128]{1,0:T(8,128)S(1)} %get-tuple-element.85.table_ref, bf16[512,2560]{1,0:T(8,128)(2,1)S(1)} %get-tuple-element.121.high_ref, bf16[512,2560]{1,0:T(8,128)(2,1)S(1)} %get-tuple-element.122.low_ref, ...), custom_call_target="tpu_custom_call", output_to_operand_aliasing={{0}: (6, {})} | custom-call | flops 2147483648 | bytes 65536 | tf_op jit(solution)/shard_map/fourth_product/pallas_call | solution.py:624
  171.8 1.7 collective-permute-start.34
  173.5 3.2 %fifth_product.3.refs_2_ = f32[512,2560]{1,0:T(8,128)S(1)} custom-call(s32[40,128]{1,0:T(8,128)S(1)} %get-tuple-element.85.table_ref, bf16[512,2560]{1,0:T(8,128)(2,1)S(1)} %get-tuple-element.121.high_ref, bf16[512,2560]{1,0:T(8,128)(2,1)S(1)} %get-tuple-element.122.low_ref, ...), custom_call_target="tpu_custom_call", output_to_operand_aliasing={{}: (4, {})} | custom-call | flops 805306368 | bytes 65536 | tf_op jit(solution)/shard_map/fifth_product/pallas_call | solution.py:624
  176.8 2.1 %collective-permute-start.37 = (f32[3]{0:T(128)S(1)}, f32[3]{0:T(128)S(1)}, u32[]{:S(2)}, u32[]{:S(2)}) collective-permute-start(f32[3]{0:T(128)S(1)} %add_add_fusion.1), channel_id=1, source_target_pairs={{0,4},{1,5},{2,6},{3,7},{4,0},{5,1},{6,2},{7,3},{8,12},{9,13},{10,... | collective-permute-start | bytes 44 | tf_op jit(solution)/shard_map/ppermute | solution.py:654
  179.1 1.4 collective-permute-start.39
  180.5 7.2 %last_product.3 = (f32[512,2560]{1,0:T(8,128)S(1)}, f32[8,64,1024]{2,1,0:T(8,128)}) custom-call(s32[40,128]{1,0:T(8,128)S(1)} %get-tuple-element.85.table_ref, bf16[512,2560]{1,0:T(8,128)(2,1)S(1)} %get-tuple-element.121.high_ref, bf16[512,2560]{1,0:T(8,128)(2,1)S(1)} %get-tuple-element.122.low_ref, ...), custom_call_target="tpu_custom_call", output_to_operand_aliasing={{0}: (5, {})} | custom-call | flops 1073741824 | bytes 65536 | tf_op jit(solution)/shard_map/last_product/pallas_call | solution.py:624
  187.7 2.3 %collective-permute-start.40 = (f32[3]{0:T(128)S(1)}, f32[3]{0:T(128)S(1)}, u32[]{:S(2)}, u32[]{:S(2)}) collective-permute-start(f32[3]{0:T(128)S(1)} %add_add_fusion), channel_id=1, source_target_pairs={{0,16},{1,17},{2,18},{3,19},{4,20},{5,21},{6,22},{7,23},{8,24},{9,... | collective-permute-start | bytes 44 | tf_op jit(solution)/shard_map/ppermute | solution.py:654
  190.0 2.2 %collective-permute-done.40 = f32[3]{0:T(128)S(1)} collective-permute-done((f32[3]{0:T(128)S(1)}, f32[3]{0:T(128)S(1)}, u32[]{:S(2)}, u32[]{:S(2)}) %collective-permute-start.40) | collective-permute-done | bytes 44 | tf_op jit(solution)/shard_map/ppermute | solution.py:654
  192.3 0.6 pad_maximum_fusion.4
  (55 shorter events, 3.2 us)
Async XLA Ops:
  0.6 1.6 copy-start
  2.2 0.7 copy-start.1
  2.9 0.7 copy-start.2
  3.6 0.7 copy-start.3
  5.5 12.9 %collective-permute-start = (f32[520,128]{1,0:T(8,128)S(1)}, f32[520,128]{1,0:T(8,128)S(1)}, u32[]{:S(2)}, u32[]{:S(2)}) collective-permute-start(f32[520,128]{1,0:T(8,128)S(1)} %get-tuple-element.77), channel_id=1, source_target_pairs={{0,3},{1,0},{2,1},{3,2},{4,7},{5,4},{6,5},{7,6},{8,11},{9,8},{10,9... | collective-permute-start | bytes 798728 | tf_op jit(solution)/shard_map/ppermute | solution.py:676
  8.0 15.6 %collective-permute-start.1 = (f32[520,128]{1,0:T(8,128)S(1)}, f32[520,128]{1,0:T(8,128)S(1)}, u32[]{:S(2)}, u32[]{:S(2)}) collective-permute-start(f32[520,128]{1,0:T(8,128)S(1)} %get-tuple-element.78), channel_id=1, source_target_pairs={{0,1},{1,2},{2,3},{3,0},{4,5},{5,6},{6,7},{7,4},{8,9},{9,10},{10,1... | collective-permute-start | bytes 798728 | tf_op jit(solution)/shard_map/ppermute | solution.py:676
  8.0 16.8 %collective-permute-start.2 = (f32[520,128]{1,0:T(8,128)S(1)}, f32[520,128]{1,0:T(8,128)S(1)}, u32[]{:S(2)}, u32[]{:S(2)}) collective-permute-start(f32[520,128]{1,0:T(8,128)S(1)} %get-tuple-element.79), channel_id=1, source_target_pairs={{0,31},{1,28},{2,29},{3,30},{4,3},{5,0},{6,1},{7,2},{8,7},{9,4},{1... | collective-permute-start | bytes 798728 | tf_op jit(solution)/shard_map/ppermute | solution.py:676
  13.7 20.1 %collective-permute-start.3 = (f32[520,128]{1,0:T(8,128)S(1)}, f32[520,128]{1,0:T(8,128)S(1)}, u32[]{:S(2)}, u32[]{:S(2)}) collective-permute-start(f32[520,128]{1,0:T(8,128)S(1)} %get-tuple-element.80), channel_id=1, source_target_pairs={{0,5},{1,6},{2,7},{3,4},{4,9},{5,10},{6,11},{7,8},{8,13},{9,14},{1... | collective-permute-start | bytes 798728 | tf_op jit(solution)/shard_map/ppermute | solution.py:676
  13.7 26.8 %collective-permute-start.4 = (f32[520,128]{1,0:T(8,128)S(1)}, f32[520,128]{1,0:T(8,128)S(1)}, u32[]{:S(2)}, u32[]{:S(2)}) collective-permute-start(f32[520,128]{1,0:T(8,128)S(1)} %get-tuple-element.81), channel_id=1, source_target_pairs={{0,29},{1,30},{2,31},{3,28},{4,1},{5,2},{6,3},{7,0},{8,5},{9,6},{1... | collective-permute-start | bytes 798728 | tf_op jit(solution)/shard_map/ppermute | solution.py:676
  18.4 22.0 %collective-permute-start.5 = (f32[520,128]{1,0:T(8,128)S(1)}, f32[520,128]{1,0:T(8,128)S(1)}, u32[]{:S(2)}, u32[]{:S(2)}) collective-permute-start(f32[520,128]{1,0:T(8,128)S(1)} %get-tuple-element.82), channel_id=1, source_target_pairs={{0,7},{1,4},{2,5},{3,6},{4,11},{5,8},{6,9},{7,10},{8,15},{9,12},{1... | collective-permute-start | bytes 798728 | tf_op jit(solution)/shard_map/ppermute | solution.py:676
  23.6 21.7 %collective-permute-start.6 = (f32[520,128]{1,0:T(8,128)S(1)}, f32[520,128]{1,0:T(8,128)S(1)}, u32[]{:S(2)}, u32[]{:S(2)}) collective-permute-start(f32[520,128]{1,0:T(8,128)S(1)} %get-tuple-element.83), channel_id=1, source_target_pairs={{0,28},{1,29},{2,30},{3,31},{4,0},{5,1},{6,2},{7,3},{8,4},{9,5},{1... | collective-permute-start | bytes 798728 | tf_op jit(solution)/shard_map/ppermute | solution.py:676
  24.8 20.5 %collective-permute-start.7 = (f32[520,128]{1,0:T(8,128)S(1)}, f32[520,128]{1,0:T(8,128)S(1)}, u32[]{:S(2)}, u32[]{:S(2)}) collective-permute-start(f32[520,128]{1,0:T(8,128)S(1)} %get-tuple-element.84), channel_id=1, source_target_pairs={{0,4},{1,5},{2,6},{3,7},{4,8},{5,9},{6,10},{7,11},{8,12},{9,13},{1... | collective-permute-start | bytes 798728 | tf_op jit(solution)/shard_map/ppermute | solution.py:676
  46.6 16.3 %collective-permute-start.12 = (f32[4,64,1024]{2,1,0:T(8,128)S(1)}, f32[4,64,1024]{2,1,0:T(8,128)S(1)}, u32[]{:S(2)}, u32[]{:S(2)}) collective-permute-start(f32[4,64,1024]{2,1,0:T(8,128)S(1)} %get-tuple-element.98), channel_id=1, source_target_pairs={{0,1},{1,0},{2,3},{3,2},{4,5},{5,4},{6,7},{7,6},{8,9},{9,8},{10,11... | collective-permute-start | bytes 3145736 | tf_op jit(solution)/shard_map/ppermute | solution.py:686
  46.8 15.0 %collective-permute-start.10 = (f32[2,64,1024]{2,1,0:T(8,128)S(1)}, f32[2,64,1024]{2,1,0:T(8,128)S(1)}, u32[]{:S(2)}, u32[]{:S(2)}) collective-permute-start(f32[2,64,1024]{2,1,0:T(8,128)S(1)} %get-tuple-element.96), channel_id=1, source_target_pairs={{0,4},{1,5},{2,6},{3,7},{4,0},{5,1},{6,2},{7,3},{8,12},{9,13},{10,... | collective-permute-start | bytes 1572872 | tf_op jit(solution)/shard_map/ppermute | solution.py:686
  49.0 13.9 %collective-permute-start.11 = (f32[2,64,1024]{2,1,0:T(8,128)S(1)}, f32[2,64,1024]{2,1,0:T(8,128)S(1)}, u32[]{:S(2)}, u32[]{:S(2)}) collective-permute-start(f32[2,64,1024]{2,1,0:T(8,128)S(1)} %get-tuple-element.97), channel_id=1, source_target_pairs={{0,3},{1,2},{2,1},{3,0},{4,7},{5,6},{6,5},{7,4},{8,11},{9,10},{10,... | collective-permute-start | bytes 1572872 | tf_op jit(solution)/shard_map/ppermute | solution.py:686
  50.9 22.0 %collective-permute-start.8 = (f32[2,64,1024]{2,1,0:T(8,128)S(1)}, f32[2,64,1024]{2,1,0:T(8,128)S(1)}, u32[]{:S(2)}, u32[]{:S(2)}) collective-permute-start(f32[2,64,1024]{2,1,0:T(8,128)S(1)} %get-tuple-element.94), channel_id=1, source_target_pairs={{0,4},{1,5},{2,6},{3,7},{4,0},{5,1},{6,2},{7,3},{8,12},{9,13},{10,... | collective-permute-start | bytes 1572872 | tf_op jit(solution)/shard_map/ppermute | solution.py:686
  51.3 22.8 %collective-permute-start.9 = (f32[2,64,1024]{2,1,0:T(8,128)S(1)}, f32[2,64,1024]{2,1,0:T(8,128)S(1)}, u32[]{:S(2)}, u32[]{:S(2)}) collective-permute-start(f32[2,64,1024]{2,1,0:T(8,128)S(1)} %get-tuple-element.95), channel_id=1, source_target_pairs={{0,3},{1,2},{2,1},{3,0},{4,7},{5,6},{6,5},{7,4},{8,11},{9,10},{10,... | collective-permute-start | bytes 1572872 | tf_op jit(solution)/shard_map/ppermute | solution.py:686
  62.9 21.8 %collective-permute-start.13 = (f32[2,64,1024]{2,1,0:T(8,128)S(1)}, f32[2,64,1024]{2,1,0:T(8,128)S(1)}, u32[]{:S(2)}, u32[]{:S(2)}) collective-permute-start(f32[2,64,1024]{2,1,0:T(8,128)S(1)} %collective-permute-done.10.refs_0_), channel_id=1, source_target_pairs={{0,8},{1,9},{2,10},{3,11},{4,28},{5,29},{6,30},{7,31},{8,16},{9,17... | collective-permute-start | bytes 1572872 | tf_op jit(solution)/shard_map/ppermute | solution.py:686
  64.6 20.0 %collective-permute-start.14 = (f32[2,64,1024]{2,1,0:T(8,128)S(1)}, f32[2,64,1024]{2,1,0:T(8,128)S(1)}, u32[]{:S(2)}, u32[]{:S(2)}) collective-permute-start(f32[2,64,1024]{2,1,0:T(8,128)S(1)} %collective-permute-done.11.refs_1_), channel_id=1, source_target_pairs={{0,4},{1,5},{2,6},{3,7},{4,0},{5,1},{6,2},{7,3},{8,12},{9,13},{10,... | collective-permute-start | bytes 1572872 | tf_op jit(solution)/shard_map/ppermute | solution.py:686
  68.0 17.3 %collective-permute-start.18 = (f32[2,64,1024]{2,1,0:T(8,128)S(1)}, f32[2,64,1024]{2,1,0:T(8,128)S(1)}, u32[]{:S(2)}, u32[]{:S(2)}) collective-permute-start(f32[2,64,1024]{2,1,0:T(8,128)S(1)} %collective-permute-done.10.refs_0_), channel_id=1, source_target_pairs={{0,3},{1,2},{2,1},{3,0},{4,7},{5,6},{6,5},{7,4},{8,11},{9,10},{10,... | collective-permute-start | bytes 1572872 | tf_op jit(solution)/shard_map/ppermute | solution.py:686
  74.1 17.1 %collective-permute-start.17 = (f32[2,64,1024]{2,1,0:T(8,128)S(1)}, f32[2,64,1024]{2,1,0:T(8,128)S(1)}, u32[]{:S(2)}, u32[]{:S(2)}) collective-permute-start(f32[2,64,1024]{2,1,0:T(8,128)S(1)} %collective-permute-done.8.refs_0_), channel_id=1, source_target_pairs={{0,8},{1,9},{2,10},{3,11},{4,28},{5,29},{6,30},{7,31},{8,16},{9,17... | collective-permute-start | bytes 1572872 | tf_op jit(solution)/shard_map/ppermute | solution.py:686
  84.7 8.2 %collective-permute-start.20 = (f32[4,64,1024]{2,1,0:T(8,128)S(1)}, f32[4,64,1024]{2,1,0:T(8,128)S(1)}, u32[]{:S(2)}, u32[]{:S(2)}) collective-permute-start(f32[4,64,1024]{2,1,0:T(8,128)S(1)} %pad_maximum_fusion.1), channel_id=1, source_target_pairs={{0,1},{1,0},{2,3},{3,2},{4,5},{5,4},{6,7},{7,6},{8,9},{9,8},{10,11... | collective-permute-start | bytes 3145736 | tf_op jit(solution)/shard_map/ppermute | solution.py:686
  91.3 9.1 %collective-permute-start.19 = (f32[4,64,1024]{2,1,0:T(8,128)S(1)}, f32[4,64,1024]{2,1,0:T(8,128)S(1)}, u32[]{:S(2)}, u32[]{:S(2)}) collective-permute-start(f32[4,64,1024]{2,1,0:T(8,128)S(1)} %pad_maximum_fusion), channel_id=1, source_target_pairs={{0,1},{1,0},{2,3},{3,2},{4,5},{5,4},{6,7},{7,6},{8,9},{9,8},{10,11... | collective-permute-start | bytes 3145736 | tf_op jit(solution)/shard_map/ppermute | solution.py:686
  91.4 16.1 %collective-permute-start.15 = (f32[2,64,1024]{2,1,0:T(8,128)S(1)}, f32[2,64,1024]{2,1,0:T(8,128)S(1)}, u32[]{:S(2)}, u32[]{:S(2)}) collective-permute-start(f32[2,64,1024]{2,1,0:T(8,128)S(1)} %collective-permute-done.14.refs_1_), channel_id=1, source_target_pairs={{0,8},{1,9},{2,10},{3,11},{4,28},{5,29},{6,30},{7,31},{8,16},{9,17... | collective-permute-start | bytes 1572872 | tf_op jit(solution)/shard_map/ppermute | solution.py:686
  92.3 15.1 %collective-permute-start.16 = (f32[2,64,1024]{2,1,0:T(8,128)S(1)}, f32[2,64,1024]{2,1,0:T(8,128)S(1)}, u32[]{:S(2)}, u32[]{:S(2)}) collective-permute-start(f32[2,64,1024]{2,1,0:T(8,128)S(1)} %collective-permute-done.13.refs_0_), channel_id=1, source_target_pairs={{0,3},{1,2},{2,1},{3,0},{4,7},{5,6},{6,5},{7,4},{8,11},{9,10},{10,... | collective-permute-start | bytes 1572872 | tf_op jit(solution)/shard_map/ppermute | solution.py:686
  114.6 16.1 %collective-permute-start.25 = (f32[4,64,1024]{2,1,0:T(8,128)S(1)}, f32[4,64,1024]{2,1,0:T(8,128)S(1)}, u32[]{:S(2)}, u32[]{:S(2)}) collective-permute-start(f32[4,64,1024]{2,1,0:T(8,128)S(1)} %get-tuple-element.127), channel_id=1, source_target_pairs={{0,1},{1,0},{2,3},{3,2},{4,5},{5,4},{6,7},{7,6},{8,9},{9,8},{10,11... | collective-permute-start | bytes 3145736 | tf_op jit(solution)/shard_map/ppermute | solution.py:686
  114.7 14.9 %collective-permute-start.23 = (f32[2,64,1024]{2,1,0:T(8,128)S(1)}, f32[2,64,1024]{2,1,0:T(8,128)S(1)}, u32[]{:S(2)}, u32[]{:S(2)}) collective-permute-start(f32[2,64,1024]{2,1,0:T(8,128)S(1)} %get-tuple-element.125), channel_id=1, source_target_pairs={{0,4},{1,5},{2,6},{3,7},{4,0},{5,1},{6,2},{7,3},{8,12},{9,13},{10,... | collective-permute-start | bytes 1572872 | tf_op jit(solution)/shard_map/ppermute | solution.py:686
  116.8 13.9 %collective-permute-start.24 = (f32[2,64,1024]{2,1,0:T(8,128)S(1)}, f32[2,64,1024]{2,1,0:T(8,128)S(1)}, u32[]{:S(2)}, u32[]{:S(2)}) collective-permute-start(f32[2,64,1024]{2,1,0:T(8,128)S(1)} %get-tuple-element.126), channel_id=1, source_target_pairs={{0,3},{1,2},{2,1},{3,0},{4,7},{5,6},{6,5},{7,4},{8,11},{9,10},{10,... | collective-permute-start | bytes 1572872 | tf_op jit(solution)/shard_map/ppermute | solution.py:686
  118.0 22.9 %collective-permute-start.21 = (f32[2,64,1024]{2,1,0:T(8,128)S(1)}, f32[2,64,1024]{2,1,0:T(8,128)S(1)}, u32[]{:S(2)}, u32[]{:S(2)}) collective-permute-start(f32[2,64,1024]{2,1,0:T(8,128)S(1)} %get-tuple-element.123), channel_id=1, source_target_pairs={{0,4},{1,5},{2,6},{3,7},{4,0},{5,1},{6,2},{7,3},{8,12},{9,13},{10,... | collective-permute-start | bytes 1572872 | tf_op jit(solution)/shard_map/ppermute | solution.py:686
  118.1 23.8 %collective-permute-start.22 = (f32[2,64,1024]{2,1,0:T(8,128)S(1)}, f32[2,64,1024]{2,1,0:T(8,128)S(1)}, u32[]{:S(2)}, u32[]{:S(2)}) collective-permute-start(f32[2,64,1024]{2,1,0:T(8,128)S(1)} %get-tuple-element.124), channel_id=1, source_target_pairs={{0,3},{1,2},{2,1},{3,0},{4,7},{5,6},{6,5},{7,4},{8,11},{9,10},{10,... | collective-permute-start | bytes 1572872 | tf_op jit(solution)/shard_map/ppermute | solution.py:686
  130.7 20.3 %collective-permute-start.26 = (f32[2,64,1024]{2,1,0:T(8,128)S(1)}, f32[2,64,1024]{2,1,0:T(8,128)S(1)}, u32[]{:S(2)}, u32[]{:S(2)}) collective-permute-start(f32[2,64,1024]{2,1,0:T(8,128)S(1)} %collective-permute-done.23.refs_0_), channel_id=1, source_target_pairs={{0,8},{1,9},{2,10},{3,11},{4,28},{5,29},{6,30},{7,31},{8,16},{9,17... | collective-permute-start | bytes 1572872 | tf_op jit(solution)/shard_map/ppermute | solution.py:686
  131.0 20.8 %collective-permute-start.27 = (f32[2,64,1024]{2,1,0:T(8,128)S(1)}, f32[2,64,1024]{2,1,0:T(8,128)S(1)}, u32[]{:S(2)}, u32[]{:S(2)}) collective-permute-start(f32[2,64,1024]{2,1,0:T(8,128)S(1)} %collective-permute-done.24.refs_1_), channel_id=1, source_target_pairs={{0,4},{1,5},{2,6},{3,7},{4,0},{5,1},{6,2},{7,3},{8,12},{9,13},{10,... | collective-permute-start | bytes 1572872 | tf_op jit(solution)/shard_map/ppermute | solution.py:686
  133.3 19.9 %collective-permute-start.31 = (f32[2,64,1024]{2,1,0:T(8,128)S(1)}, f32[2,64,1024]{2,1,0:T(8,128)S(1)}, u32[]{:S(2)}, u32[]{:S(2)}) collective-permute-start(f32[2,64,1024]{2,1,0:T(8,128)S(1)} %collective-permute-done.23.refs_0_), channel_id=1, source_target_pairs={{0,3},{1,2},{2,1},{3,0},{4,7},{5,6},{6,5},{7,4},{8,11},{9,10},{10,... | collective-permute-start | bytes 1572872 | tf_op jit(solution)/shard_map/ppermute | solution.py:686
  142.0 16.4 %collective-permute-start.30 = (f32[2,64,1024]{2,1,0:T(8,128)S(1)}, f32[2,64,1024]{2,1,0:T(8,128)S(1)}, u32[]{:S(2)}, u32[]{:S(2)}) collective-permute-start(f32[2,64,1024]{2,1,0:T(8,128)S(1)} %collective-permute-done.21.refs_0_), channel_id=1, source_target_pairs={{0,8},{1,9},{2,10},{3,11},{4,28},{5,29},{6,30},{7,31},{8,16},{9,17... | collective-permute-start | bytes 1572872 | tf_op jit(solution)/shard_map/ppermute | solution.py:686
  151.9 10.8 %collective-permute-start.32 = (f32[4,64,1024]{2,1,0:T(8,128)S(1)}, f32[4,64,1024]{2,1,0:T(8,128)S(1)}, u32[]{:S(2)}, u32[]{:S(2)}) collective-permute-start(f32[4,64,1024]{2,1,0:T(8,128)S(1)} %pad_maximum_fusion.2), channel_id=1, source_target_pairs={{0,1},{1,0},{2,3},{3,2},{4,5},{5,4},{6,7},{7,6},{8,9},{9,8},{10,11... | collective-permute-start | bytes 3145736 | tf_op jit(solution)/shard_map/ppermute | solution.py:686
  158.4 15.0 %collective-permute-start.36 = (f32[4,64,1024]{2,1,0:T(8,128)S(1)}, f32[4,64,1024]{2,1,0:T(8,128)S(1)}, u32[]{:S(2)}, u32[]{:S(2)}) collective-permute-start(f32[4,64,1024]{2,1,0:T(8,128)S(1)} %pad_maximum_fusion.3), channel_id=1, source_target_pairs={{0,1},{1,0},{2,3},{3,2},{4,5},{5,4},{6,7},{7,6},{8,9},{9,8},{10,11... | collective-permute-start | bytes 3145736 | tf_op jit(solution)/shard_map/ppermute | solution.py:686
  158.5 21.9 %collective-permute-start.29 = (f32[2,64,1024]{2,1,0:T(8,128)S(1)}, f32[2,64,1024]{2,1,0:T(8,128)S(1)}, u32[]{:S(2)}, u32[]{:S(2)}) collective-permute-start(f32[2,64,1024]{2,1,0:T(8,128)S(1)} %collective-permute-done.26.refs_0_.refs_4_), channel_id=1, source_target_pairs={{0,3},{1,2},{2,1},{3,0},{4,7},{5,6},{6,5},{7,4},{8,11},{9,10},{10,... | collective-permute-start | bytes 1572872 | tf_op jit(solution)/shard_map/ppermute | solution.py:686
  158.8 21.7 %collective-permute-start.28 = (f32[2,64,1024]{2,1,0:T(8,128)S(1)}, f32[2,64,1024]{2,1,0:T(8,128)S(1)}, u32[]{:S(2)}, u32[]{:S(2)}) collective-permute-start(f32[2,64,1024]{2,1,0:T(8,128)S(1)} %collective-permute-done.27.refs_1_), channel_id=1, source_target_pairs={{0,8},{1,9},{2,10},{3,11},{4,28},{5,29},{6,30},{7,31},{8,16},{9,17... | collective-permute-start | bytes 1572872 | tf_op jit(solution)/shard_map/ppermute | solution.py:686
  171.5 5.3 %collective-permute-start.33 = (f32[3]{0:T(128)S(1)}, f32[3]{0:T(128)S(1)}, u32[]{:S(2)}, u32[]{:S(2)}) collective-permute-start(f32[3]{0:T(128)S(1)} %get-tuple-element.143), channel_id=1, source_target_pairs={{0,1},{1,0},{2,3},{3,2},{4,5},{5,4},{6,7},{7,6},{8,9},{9,8},{10,11... | collective-permute-start | bytes 44 | tf_op jit(solution)/shard_map/ppermute | solution.py:654
  171.8 5.0 %collective-permute-start.34 = (f32[3]{0:T(128)S(1)}, f32[3]{0:T(128)S(1)}, u32[]{:S(2)}, u32[]{:S(2)}) collective-permute-start(f32[3]{0:T(128)S(1)} %get-tuple-element.143), channel_id=1, source_target_pairs={{0,2},{1,3},{2,0},{3,1},{4,6},{5,7},{6,4},{7,5},{8,10},{9,11},{10,... | collective-permute-start | bytes 44 | tf_op jit(solution)/shard_map/ppermute | solution.py:654
  173.5 3.3 %collective-permute-start.35 = (f32[3]{0:T(128)S(1)}, f32[3]{0:T(128)S(1)}, u32[]{:S(2)}, u32[]{:S(2)}) collective-permute-start(f32[3]{0:T(128)S(1)} %get-tuple-element.143), channel_id=1, source_target_pairs={{0,3},{1,2},{2,1},{3,0},{4,7},{5,6},{6,5},{7,4},{8,11},{9,10},{10,... | collective-permute-start | bytes 44 | tf_op jit(solution)/shard_map/ppermute | solution.py:654
  176.8 10.8 %collective-permute-start.37 = (f32[3]{0:T(128)S(1)}, f32[3]{0:T(128)S(1)}, u32[]{:S(2)}, u32[]{:S(2)}) collective-permute-start(f32[3]{0:T(128)S(1)} %add_add_fusion.1), channel_id=1, source_target_pairs={{0,4},{1,5},{2,6},{3,7},{4,0},{5,1},{6,2},{7,3},{8,12},{9,13},{10,... | collective-permute-start | bytes 44 | tf_op jit(solution)/shard_map/ppermute | solution.py:654
  178.9 8.7 %collective-permute-start.38 = (f32[3]{0:T(128)S(1)}, f32[3]{0:T(128)S(1)}, u32[]{:S(2)}, u32[]{:S(2)}) collective-permute-start(f32[3]{0:T(128)S(1)} %add_add_fusion.1), channel_id=1, source_target_pairs={{0,8},{1,9},{2,10},{3,11},{4,12},{5,13},{6,14},{7,15},{8,0},{9,1},... | collective-permute-start | bytes 44 | tf_op jit(solution)/shard_map/ppermute | solution.py:654
  179.1 8.6 %collective-permute-start.39 = (f32[3]{0:T(128)S(1)}, f32[3]{0:T(128)S(1)}, u32[]{:S(2)}, u32[]{:S(2)}) collective-permute-start(f32[3]{0:T(128)S(1)} %add_add_fusion.1), channel_id=1, source_target_pairs={{0,12},{1,13},{2,14},{3,15},{4,8},{5,9},{6,10},{7,11},{8,4},{9,5},... | collective-permute-start | bytes 44 | tf_op jit(solution)/shard_map/ppermute | solution.py:654
  187.7 4.5 %collective-permute-start.40 = (f32[3]{0:T(128)S(1)}, f32[3]{0:T(128)S(1)}, u32[]{:S(2)}, u32[]{:S(2)}) collective-permute-start(f32[3]{0:T(128)S(1)} %add_add_fusion), channel_id=1, source_target_pairs={{0,16},{1,17},{2,18},{3,19},{4,20},{5,21},{6,22},{7,23},{8,24},{9,... | collective-permute-start | bytes 44 | tf_op jit(solution)/shard_map/ppermute | solution.py:654
